TPU v7x, 32 devices: a whole 2x2x4 slice. The times are simulated.
32 devices in a mesh: gx: 4 (over x, core), gy: 8 (over z, y).
Axes of the slice: x: 2, y: 2, z: 4, core: 2. Of those that a mesh axis runs over, the one named last changes fastest.
Arguments:
- plate_motion: bfloat16 [8, 16, 128, 2, 128], P('gx', 'gy'), may hold values from -6 to 6
- adjoint_load: bfloat16 [8, 16, 128, 2, 128], P('gx', 'gy'), may hold values from -6 to 6
- excitation: bfloat16 [8, 16, 128, 2, 128], P('gx', 'gy'), may hold values from -6 to 6
- coupling: bfloat16 [8, 16, 5, 2, 128, 128], P('gx', 'gy'), may hold values from -0.25 to 0.25
- joints: int32 [8, 16, 4], P('gx', 'gy'), may hold values 0 or 1
- hydro: bfloat16 [2, 1024, 1024], P(None, 'gx', 'gy'), may hold values from -0.1875 to 0.1875
- panel_map: bfloat16 [1024, 2, 2, 128], P(('gx', 'gy')), may hold values from -0.25 to 0.25
Outputs:
- residual: float32 [8, 16, 128, 2, 128], P('gx', 'gy')
- multiplier: float32 [8, 16, 128, 2, 128], P('gx', 'gy')
- sensitivity: float32 [8, 16], P('gx', 'gy')
All inputs are finite; a program needn't handle non-finite values. No bound on the sum of `joints` on one device may be relied on, other than what follows from the above.
Results may differ from a plain program's by a relative error of at most 0.0031.
Values may be sent and summed in bfloat16 or wider, within the bound.
No kernel may reach another device: no remote copies, remote signals or barrier semaphores. Data moves between devices by JAX's collectives and lax.ppermute only.
A program may use at most 64 MiB of HBM per device.

v0:
```python
import math

import jax
import jax.numpy as jnp
from jax import lax
from jax.sharding import PartitionSpec as P


def extended(x, sides, width):
    for axis, dim in sides:
        size, length = (lax.axis_size(axis), x.shape[dim])
        up = [(i, (i + 1) % size) for i in range(size - 1)]
        down = [(j, i) for i, j in up]
        last = lax.slice_in_dim(x, length - width, length, axis=dim)
        first = lax.slice_in_dim(x, 0, width, axis=dim)
        before = lax.ppermute(last, axis, up)
        after = lax.ppermute(first, axis, down)
        x = jnp.concatenate([before, x, after], axis=dim)
    return x


def complex_apply(form, coupling, vector):
    real_c = coupling[..., 0, :, :]
    imag_c = coupling[..., 1, :, :]
    real_v = vector[..., 0, :]
    imag_v = vector[..., 1, :]

    def mult(matrix, values):
        return jnp.einsum(form, matrix, values, preferred_element_type=jnp.float32)

    return jnp.stack(
        [mult(real_c, real_v) - mult(imag_c, imag_v), mult(real_c, imag_v) + mult(imag_c, real_v)],
        axis=-2,
    )


def adjoint_apply(form, coupling, vector):
    real_c = coupling[..., 0, :, :]
    imag_c = coupling[..., 1, :, :]
    real_v = vector[..., 0, :]
    imag_v = vector[..., 1, :]

    def mult(matrix, values):
        return jnp.einsum(form, matrix, values, preferred_element_type=jnp.float32)

    return jnp.stack(
        [mult(real_c, real_v) + mult(imag_c, imag_v), mult(real_c, imag_v) - mult(imag_c, real_v)],
        axis=-2,
    )


def plain_product(matrix, values):
    return jnp.dot(matrix, values, preferred_element_type=jnp.float32)


def flipped_product(matrix, values):
    return lax.dot_general(
        matrix, values, (((0,), (0,)), ((), ())), preferred_element_type=jnp.float32
    )


def on_device(plate_motion, adjoint_load, excitation, coupling, joints, hydro, panel_map):
    rows_count = plate_motion.shape[0]
    cols_count = plate_motion.shape[1]
    panel_count = panel_map.shape[0]
    unknowns = plate_motion.shape[4]
    cases = plate_motion.shape[2]
    links = joints.astype(jnp.float32)[:, :, :, None, None, None]
    padded = extended(plate_motion, (("gx", 0), ("gy", 1)), 1)
    beside_all = jnp.stack(
        [
            padded[0:rows_count, 1:-1],
            padded[2:, 1:-1],
            padded[1:-1, 0:cols_count],
            padded[1:-1, 2:],
        ],
        axis=2,
    )
    own = complex_apply("xyij,xyhj->xyhi", coupling[:, :, 0], plate_motion)
    structural = own + jnp.sum(
        links * complex_apply("xydij,xydhj->xydhi", coupling[:, :, 1:], beside_all), axis=2
    )
    outgoing = links * adjoint_apply("xydji,xyhj->xydhi", coupling[:, :, 1:], adjoint_load)
    own_adjoint = adjoint_apply("xyji,xyhj->xyhi", coupling[:, :, 0], adjoint_load)
    layered = extended(outgoing, (("gx", 0), ("gy", 1)), 1)
    incoming = (
        layered[2:, 1:-1, 0] + layered[:-2, 1:-1, 1] + layered[1:-1, 2:, 2] + layered[1:-1, :-2, 3]
    )
    lift = math.sqrt(rows_count * cols_count * unknowns / panel_count)
    motion_panels = jnp.einsum(
        "nxyk,xyhck->cnh", panel_map, plate_motion, preferred_element_type=jnp.float32
    ).astype(jnp.bfloat16)
    load_panels = jnp.einsum(
        "nxyk,xyhck->cnh", panel_map, adjoint_load, preferred_element_type=jnp.float32
    ).astype(jnp.bfloat16)
    piece = lax.all_gather(motion_panels, "gx", axis=1, tiled=True)
    first = plain_product(hydro[0], piece[0]) - plain_product(hydro[1], piece[1])
    second = plain_product(hydro[0], piece[1]) + plain_product(hydro[1], piece[0])
    pressure_part = jnp.stack([first, second])
    piece = lax.all_gather(load_panels, "gy", axis=1, tiled=True)
    first = flipped_product(hydro[0], piece[0]) + flipped_product(hydro[1], piece[1])
    second = flipped_product(hydro[0], piece[1]) - flipped_product(hydro[1], piece[0])
    reaction_part = jnp.stack([first, second])
    pressure_band = lax.psum(pressure_part, "gy")
    pressure = lax.dynamic_slice_in_dim(
        pressure_band, lax.axis_index("gy") * panel_count, panel_count, 1
    )
    reaction_band = lax.psum(reaction_part, "gx")
    reaction = lax.dynamic_slice_in_dim(
        reaction_band, lax.axis_index("gx") * panel_count, panel_count, 1
    )
    pressure = pressure.astype(jnp.bfloat16)
    reaction = reaction.astype(jnp.bfloat16)
    pressure_force = jnp.einsum(
        "nxyk,cnh->xyhck", panel_map, pressure, preferred_element_type=jnp.float32
    )
    reaction_force = jnp.einsum(
        "nxyk,cnh->xyhck", panel_map, reaction, preferred_element_type=jnp.float32
    )
    residual = structural + lift * pressure_force - excitation.astype(jnp.float32)
    multiplier = own_adjoint + incoming + lift * reaction_force
    sensitivity = jnp.sum(multiplier * own, axis=(2, 3, 4)) / math.sqrt(cases * unknowns)
    return (residual, multiplier, sensitivity)


def solution(mesh):
    placed = (
        P("gx", "gy", None, None, None),
        P("gx", "gy", None, None, None),
        P("gx", "gy", None, None, None),
        P("gx", "gy", None, None, None, None),
        P("gx", "gy", None),
        P(None, "gx", "gy"),
        P(("gx", "gy"), None, None, None),
    )
    return jax.shard_map(
        on_device,
        mesh=mesh,
        in_specs=placed,
        out_specs=(P("gx", "gy", None, None, None), P("gx", "gy", None, None, None), P("gx", "gy")),
        check_vma=False,
    )
```

profile of v0, /device:TPU:0, one launch (start us, length us, event | category | flops | bytes accessed | tf_op | source)
XLA Modules:
  0.0 234.0 jit_solution(11795574891273521762)
XLA Ops:
  0.6 1.0 copy.43
  1.7 2.4 %collective-permute-start = (bf16[1,2,128,2,128]{4,2,1,0,3:T(8,128)(2,1)S(1)}, bf16[1,2,128,2,128]{4,2,1,0,3:T(8,128)(2,1)S(1)}, u32[]{:S(2)}, u32[]{:S(2)}) collective-permute-start(bf16[1,2,128,2,128]{4,2,1,0,3:T(8,128)(2,1)S(1)} %get-tuple-element.24), channel_id=1, source_target_pairs={{0,8},{8,16},{16,24},{1,9},{9,17},{17,25},{2,10},{10,18},{18,26},{... | collective-permute-start | bytes 393224 | tf_op jit(solution)/shard_map/ppermute | solution.py:16
  4.1 1.3 collective-permute-start.1
  5.4 1.3 slice_bitcast_fusion.2
  6.7 0.3 fusion.39
  7.0 0.3 fusion.37
  7.6 31.7 %all_gather.7 = bf16[2,256,128]{2,1,0:T(8,128)(2,1)S(1)} all-gather(bf16[2,32,128]{2,1,0:T(8,128)(2,1)S(1)} %fusion.19), channel_id=1, replica_groups=mesh['gx'=4,'gy'=8] {'gy'}, dimensions={1}, use_global_device_ids=true | all-gather | bytes 147456 | tf_op jit(solution)/shard_map/all_gather | solution.py:100
  39.3 0.2 fusion.71
  39.5 0.2 fusion.73
  39.8 0.8 fusion.20
  40.6 1.3 fusion.2
  41.8 1.3 fusion.1
  43.2 0.7 fusion.105
  44.0 3.5 %collective-permute-start.2 = (bf16[4,1,128,2,128]{4,2,1,0,3:T(8,128)(2,1)}, bf16[4,1,128,2,128]{4,2,1,0,3:T(8,128)(2,1)S(1)}, u32[]{:S(2)}, u32[]{:S(2)}) collective-permute-start(bf16[4,1,128,2,128]{4,2,1,0,3:T(8,128)(2,1)} %get-tuple-element.19), channel_id=1, source_target_pairs={{0,1},{1,2},{2,3},{3,4},{4,5},{5,6},{6,7},{8,9},{9,10},{10,11},{11... | collective-permute-start | bytes 786440 | tf_op jit(solution)/shard_map/ppermute | solution.py:16
  47.5 1.3 collective-permute-start.3
  48.8 0.2 fusion.15
  49.1 0.2 fusion.16
  49.4 5.7 %collective-permute-done.2 = bf16[4,1,128,2,128]{4,2,1,0,3:T(8,128)(2,1)S(1)} collective-permute-done((bf16[4,1,128,2,128]{4,2,1,0,3:T(8,128)(2,1)}, bf16[4,1,128,2,128]{4,2,1,0,3:T(8,128)(2,1)S(1)}, u32[]{:S(2)}, u32[]{:S(2)}) %collective-permute-start.2) | collective-permute-done | bytes 262176 | tf_op jit(solution)/shard_map/ppermute | solution.py:16
  55.1 0.7 collective-permute-done.3
  56.1 0.5 fusion.31
  56.5 0.5 fusion.27
  57.0 0.5 fusion.4
  57.5 0.5 fusion.3
  58.0 0.7 copy-done
  58.7 0.3 copy-done.1
  59.0 0.5 maximum_multiply_fusion.1
  59.5 1.5 fusion.104
  61.0 1.3 collective-permute-start.4
  62.3 4.0 %collective-permute-start.5 = (f32[1,2,4,128,2,128]{5,3,1,0,4,2:T(8,128)}, f32[1,2,4,128,2,128]{5,3,1,0,4,2:T(8,128)}, u32[]{:S(2)}, u32[]{:S(2)}) collective-permute-start(f32[1,2,4,128,2,128]{5,3,1,0,4,2:T(8,128)} %get-tuple-element.11), channel_id=1, source_target_pairs={{0,8},{8,16},{16,24},{1,9},{9,17},{17,25},{2,10},{10,18},{18,26},{... | collective-permute-start | bytes 3145736 | tf_op jit(solution)/shard_map/ppermute | solution.py:16
  66.3 0.7 pad_maximum_fusion.16
  67.0 14.0 %all_gather.6 = bf16[2,128,128]{2,1,0:T(8,128)(2,1)S(1)} all-gather(bf16[2,32,128]{2,1,0:T(8,128)(2,1)S(1)} %copy-done.8), channel_id=1, replica_groups=mesh['gx'=4,'gy'=8] {'gx'}, dimensions={1}, use_global_device_ids=true | all-gather | bytes 81920 | tf_op jit(solution)/shard_map/all_gather | solution.py:96
  81.7 15.5 %all-reduce.2 = bf16[2,128,128]{2,1,0:T(8,128)(2,1)} all-reduce(f32[2,128,128]{2,1,0:T(8,128)} %pad_maximum_fusion.16), channel_id=1, replica_groups=mesh['gx'=4,'gy'=8] {'gx'}, use_global_device_ids=true, to_apply=%region_2.0 | all-reduce | flops 32768 | bytes 196608 | tf_op jit(solution)/shard_map/psum | solution.py:108
  97.2 1.9 pad_maximum_fusion
  99.1 2.5 %fusion.103 = (f32[4,1,4,128,2,128]{5,3,1,0,4,2:T(8,128)}, f32[4,1,4,128,2,128]{5,3,1,0,4,2:T(8,128)}) fusion(f32[4,2,4,128,2,128]{5,3,1,0,4,2:T(8,128)S(1)} %pad_maximum_fusion), kind=kLoop, calls=%fused_computation.156 | loop fusion | bytes 8388608 | tf_op jit(solution)/shard_map/slice | solution.py:15
  101.6 1.3 collective-permute-start.6
  102.9 5.9 %collective-permute-start.7 = (f32[4,1,4,128,2,128]{5,3,1,0,4,2:T(8,128)}, f32[4,1,4,128,2,128]{5,3,1,0,4,2:T(8,128)}, u32[]{:S(2)}, u32[]{:S(2)}) collective-permute-start(f32[4,1,4,128,2,128]{5,3,1,0,4,2:T(8,128)} %get-tuple-element.10), channel_id=1, source_target_pairs={{0,1},{1,2},{2,3},{3,4},{4,5},{5,6},{6,7},{8,9},{9,10},{10,11},{11... | collective-permute-start | bytes 6291464 | tf_op jit(solution)/shard_map/ppermute | solution.py:16
  108.8 117.8 %all-reduce.3 = bf16[2,256,128]{2,1,0:T(8,128)(2,1)S(1)} all-reduce(f32[2,256,128]{2,1,0:T(8,128)S(1)} %pad_maximum_fusion.15), channel_id=1, replica_groups=mesh['gx'=4,'gy'=8] {'gy'}, use_global_device_ids=true, to_apply=%region_1.0 | all-reduce | flops 65536 | bytes 393216 | tf_op jit(solution)/shard_map/psum | solution.py:104
  226.5 1.0 copy_bitcast_fusion
  227.7 0.2 fusion.10
  228.3 0.2 fusion.58
  228.5 0.2 fusion.11
  228.7 0.2 fusion.57
  228.9 0.2 fusion.12
  229.2 0.3 fusion.8
  229.4 1.2 copy.80
  230.7 1.6 multiply_reduce_fusion
  232.2 1.2 copy.81
  233.5 0.6 broadcast_multiply_fusion
  (44 shorter events, 2.1 us)
Async XLA Ops:
  0.6 6.0 %copy-start.4 = (bf16[2,2,128,2,128]{4,3,2,1,0:T(2,128)(2,1)S(1)}, bf16[2,2,128,2,128]{4,3,2,1,0:T(2,128)(2,1)}, u32[]{:S(2)}) copy-start(bf16[2,2,128,2,128]{4,3,2,1,0:T(2,128)(2,1)} %param.8) | copy-start | bytes 786436
  1.7 41.4 %collective-permute-start = (bf16[1,2,128,2,128]{4,2,1,0,3:T(8,128)(2,1)S(1)}, bf16[1,2,128,2,128]{4,2,1,0,3:T(8,128)(2,1)S(1)}, u32[]{:S(2)}, u32[]{:S(2)}) collective-permute-start(bf16[1,2,128,2,128]{4,2,1,0,3:T(8,128)(2,1)S(1)} %get-tuple-element.24), channel_id=1, source_target_pairs={{0,8},{8,16},{16,24},{1,9},{9,17},{17,25},{2,10},{10,18},{18,26},{... | collective-permute-start | bytes 393224 | tf_op jit(solution)/shard_map/ppermute | solution.py:16
  4.1 39.1 %collective-permute-start.1 = (bf16[1,2,128,2,128]{4,2,1,0,3:T(8,128)(2,1)S(1)}, bf16[1,2,128,2,128]{4,2,1,0,3:T(8,128)(2,1)S(1)}, u32[]{:S(2)}, u32[]{:S(2)}) collective-permute-start(bf16[1,2,128,2,128]{4,2,1,0,3:T(8,128)(2,1)S(1)} %get-tuple-element.23), channel_id=1, source_target_pairs={{8,0},{16,8},{24,16},{9,1},{17,9},{25,17},{10,2},{18,10},{26,18},{... | collective-permute-start | bytes 393224 | tf_op jit(solution)/shard_map/ppermute | solution.py:17
  6.7 0.8 copy-start.6
  6.7 32.6 %copy-start.2 = (bf16[2,256,128]{2,1,0:T(8,128)(2,1)S(1)}, bf16[2,256,128]{2,1,0:T(8,128)(2,1)}, u32[]{:S(2)}) copy-start(bf16[2,256,128]{2,1,0:T(8,128)(2,1)} %param.12) | copy-start | bytes 393220
  6.7 33.0 %copy-start.3 = (bf16[2,2,128,2,128]{4,3,2,1,0:T(2,128)(2,1)S(1)}, bf16[2,2,128,2,128]{4,3,2,1,0:T(2,128)(2,1)}, u32[]{:S(2)}) copy-start(bf16[2,2,128,2,128]{4,3,2,1,0:T(2,128)(2,1)} %param.7) | copy-start | bytes 786436
  41.8 7.2 %copy-start.9 = (s32[2,2,4]{2,1,0:T(2,128)S(1)}, s32[2,2,4]{2,1,0:T(2,128)}, u32[]{:S(2)}) copy-start(s32[2,2,4]{2,1,0:T(2,128)} %param.11) | copy-start | bytes 196
  44.0 11.1 %collective-permute-start.2 = (bf16[4,1,128,2,128]{4,2,1,0,3:T(8,128)(2,1)}, bf16[4,1,128,2,128]{4,2,1,0,3:T(8,128)(2,1)S(1)}, u32[]{:S(2)}, u32[]{:S(2)}) collective-permute-start(bf16[4,1,128,2,128]{4,2,1,0,3:T(8,128)(2,1)} %get-tuple-element.19), channel_id=1, source_target_pairs={{0,1},{1,2},{2,3},{3,4},{4,5},{5,6},{6,7},{8,9},{9,10},{10,11},{11... | collective-permute-start | bytes 786440 | tf_op jit(solution)/shard_map/ppermute | solution.py:16
  47.5 8.3 %collective-permute-start.3 = (bf16[4,1,128,2,128]{4,2,1,0,3:T(8,128)(2,1)S(1)}, bf16[4,1,128,2,128]{4,2,1,0,3:T(8,128)(2,1)S(1)}, u32[]{:S(2)}, u32[]{:S(2)}) collective-permute-start(bf16[4,1,128,2,128]{4,2,1,0,3:T(8,128)(2,1)S(1)} %get-tuple-element.20), channel_id=1, source_target_pairs={{1,0},{2,1},{3,2},{4,3},{5,4},{6,5},{7,6},{9,8},{10,9},{11,10},{12... | collective-permute-start | bytes 786440 | tf_op jit(solution)/shard_map/ppermute | solution.py:17
  57.5 1.2 copy-start
  57.5 1.5 copy-start.1
  59.5 7.5 %copy-start.8 = (bf16[2,32,128]{2,1,0:T(8,128)(2,1)S(1)}, bf16[2,32,128]{2,1,0:T(8,128)(2,1)}, u32[]{:S(2)}) copy-start(bf16[2,32,128]{2,1,0:T(8,128)(2,1)} %fusion.20) | copy-start | bytes 49156
  61.0 36.2 %collective-permute-start.4 = (f32[1,2,4,128,2,128]{5,3,1,0,4,2:T(8,128)}, f32[1,2,4,128,2,128]{5,3,1,0,4,2:T(8,128)}, u32[]{:S(2)}, u32[]{:S(2)}) collective-permute-start(f32[1,2,4,128,2,128]{5,3,1,0,4,2:T(8,128)} %get-tuple-element.12), channel_id=1, source_target_pairs={{8,0},{16,8},{24,16},{9,1},{17,9},{25,17},{10,2},{18,10},{26,18},{... | collective-permute-start | bytes 3145736 | tf_op jit(solution)/shard_map/ppermute | solution.py:17
  62.3 34.9 %collective-permute-start.5 = (f32[1,2,4,128,2,128]{5,3,1,0,4,2:T(8,128)}, f32[1,2,4,128,2,128]{5,3,1,0,4,2:T(8,128)}, u32[]{:S(2)}, u32[]{:S(2)}) collective-permute-start(f32[1,2,4,128,2,128]{5,3,1,0,4,2:T(8,128)} %get-tuple-element.11), channel_id=1, source_target_pairs={{0,8},{8,16},{16,24},{1,9},{9,17},{17,25},{2,10},{10,18},{18,26},{... | collective-permute-start | bytes 3145736 | tf_op jit(solution)/shard_map/ppermute | solution.py:16
  101.6 129.1 %collective-permute-start.6 = (f32[4,1,4,128,2,128]{5,3,1,0,4,2:T(8,128)}, f32[4,1,4,128,2,128]{5,3,1,0,4,2:T(8,128)}, u32[]{:S(2)}, u32[]{:S(2)}) collective-permute-start(f32[4,1,4,128,2,128]{5,3,1,0,4,2:T(8,128)} %get-tuple-element.9), channel_id=1, source_target_pairs={{1,0},{2,1},{3,2},{4,3},{5,4},{6,5},{7,6},{9,8},{10,9},{11,10},{12... | collective-permute-start | bytes 6291464 | tf_op jit(solution)/shard_map/ppermute | solution.py:17
  102.9 127.8 %collective-permute-start.7 = (f32[4,1,4,128,2,128]{5,3,1,0,4,2:T(8,128)}, f32[4,1,4,128,2,128]{5,3,1,0,4,2:T(8,128)}, u32[]{:S(2)}, u32[]{:S(2)}) collective-permute-start(f32[4,1,4,128,2,128]{5,3,1,0,4,2:T(8,128)} %get-tuple-element.10), channel_id=1, source_target_pairs={{0,1},{1,2},{2,3},{3,4},{4,5},{5,6},{6,7},{8,9},{9,10},{10,11},{11... | collective-permute-start | bytes 6291464 | tf_op jit(solution)/shard_map/ppermute | solution.py:16
  227.9 1.3 copy-start.5
  227.9 1.3 copy-start.7
where the time goes:
time: 235 us; the launch traced here: 234 us
  blocking collectives  179 us (76%)
  starting transfers between devices  20.9 us (9%)
  local copies, waits for them, and re-layouts  11.9 us (5%)
  matrix products  10.8 us (5%)
  waiting for transfers between devices  6.36 us (3%)
  other arithmetic  3.85 us (2%)
    psum x1, blocking collectives, on_device(): pressure_band = lax.psum(pressure_part, 'gy')  118 us
    all_gather x1, blocking collectives, on_device(): piece = lax.all_gather(load_panels, 'gy', axis=1, tiled=True)  31.7 us
    ppermute x4, starting transfers between devices, extended(): before = lax.ppermute(last, axis, up)  15.8 us
    psum x1, blocking collectives, on_device(): reaction_band = lax.psum(reaction_part, 'gx')  15.5 us
    all_gather x1, blocking collectives, on_device(): piece = lax.all_gather(motion_panels, 'gx', axis=1, tiled=True)  14 us
    dot_general x16, matrix products, mult(): return jnp.einsum(form, matrix, values, preferred_element_type=jnp.float32)  6.56 us
    ppermute x4, waiting for transfers between devices, extended(): before = lax.ppermute(last, axis, up)  5.68 us
    ppermute x4, starting transfers between devices, extended(): after = lax.ppermute(first, axis, down)  5.14 us
  transfers between devices with their start and end apart: 8, of which 2 were waited for; matrix products, arithmetic and copies ran while one was open for 5% of the time, Pallas kernels for 0%

commit v1 on v0

v1 whole, which is shorter than its diff:
```python
import functools
import math

import jax
import jax.numpy as jnp
from jax import lax
from jax.experimental import pallas as pl
from jax.experimental.pallas import tpu as pltpu
from jax.sharding import PartitionSpec as P


F32 = jnp.float32
BF16 = jnp.bfloat16
OFFSETS = ((-1, 0), (1, 0), (0, -1), (0, 1))
WHOLE = pl.BlockSpec(memory_space=pltpu.VMEM)
SCALARS = pl.BlockSpec(memory_space=pltpu.SMEM)
FAR = pl.BlockSpec(memory_space=pltpu.HBM)


def dot(a, b, over):
    return lax.dot_general(a, b, ((over[:1], over[1:]), ((), ())), preferred_element_type=F32)


def times_i(field, axis):
    size = field.shape[axis]
    after = pltpu.roll(field, size - 1, axis)
    before = pltpu.roll(field, 1, axis)
    place = lax.broadcasted_iota(jnp.int32, field.shape, axis)
    return jnp.where(lax.rem(place, 2) == 0, -after, before)


def forward_parts(coupling, motion):
    return dot(motion, coupling.reshape(-1, coupling.shape[-1]), (1, 1))


def adjoint_parts(coupling, load):
    return dot(load, jnp.concatenate([coupling[0], coupling[1]], axis=1), (1, 0))


def joined(parts, sign):
    half = parts.shape[1] // 2
    turned = times_i(parts[:, half:], 0)
    return parts[:, :half] + turned if sign > 0 else parts[:, :half] - turned


def map_of_blocks(map_ref, blocks):
    rows = map_ref.shape[0]
    panels = rows // blocks
    row = lax.broadcasted_iota(jnp.int32, (panels, rows), 0)
    column = lax.broadcasted_iota(jnp.int32, (panels, rows), 1)
    whole = map_ref[...]
    out = []
    for b in range(blocks):
        pick = (column == row * blocks + b).astype(F32).astype(BF16)
        out.append(dot(pick, whole, (1, 0)).astype(BF16))
    return out


def target(i, step, n):
    if step == 0:
        return i
    if step == 1:
        return i ^ 1
    if step == 2:
        return (((i + 1) ^ 1) + n - 1) % n
    return (i + step - 1) % n


def source(i, step, n):
    return target(i, step, n) if step < 3 else (i + n + 1 - step) % n


def exchange(x, step):
    n = lax.axis_size("gx")
    return lax.ppermute(x, "gx", [(i, target(i, step, n)) for i in range(n)])


def panels_kernel(motion_far, load_far, map_far, motion_out, load_out, motion, load, maps, panels, arrive, leave):
    blocks = motion.shape[0]
    moves = [
        pltpu.make_async_copy(map_far, maps, arrive.at[0]),
        pltpu.make_async_copy(load_far, load, arrive.at[1]),
        pltpu.make_async_copy(motion_far, motion, arrive.at[2]),
    ]
    for move in moves:
        move.start()
    moves[0].wait()
    split = map_of_blocks(maps, blocks)
    moves[1].wait()
    panels[...] = sum(dot(split[b], load[b], (1, 1)) for b in range(blocks)).astype(BF16)
    outs = [pltpu.make_async_copy(panels, load_out.at[j], leave.at[j]) for j in range(load_out.shape[0])]
    for out in outs:
        out.start()
    moves[2].wait()
    motion_out[...] = sum(dot(split[b], motion[b], (1, 1)) for b in range(blocks)).astype(BF16)
    for out in outs:
        out.wait()


def edges(rows, cols, me):
    even = 1 - me % 2
    sides = []
    for d in (even, 1 - even):
        sides.append([(d * (rows - 1), y, d) for y in range(cols)])
    for d in (2, 3):
        sides.append([(x, (d - 2) * (cols - 1), d) for x in range(rows)])
    return sides


def edges_kernel(rows, cols, spot, joints, panels, motion_far, load_far, coupling_far, *refs):
    outs, (load, coupling, terms, arrive, pass_by, leave) = refs[:4], refs[4:]
    wide = load.shape[1]
    sides = edges(rows, cols, spot[0])
    spots = [(o, k) + place for o, side in enumerate(sides) for k, place in enumerate(side)]
    fetch = [pltpu.make_async_copy(load_far, load, arrive.at[len(spots)])]
    for i, (o, k, x, y, d) in enumerate(spots):
        fetch.append(pltpu.make_async_copy(coupling_far.at[x * cols + y, d + 1], coupling.at[i], arrive.at[i]))
    for move in fetch:
        move.start()
    direct = []
    for i, (o, k, x, y, d) in enumerate(spots):
        there = outs[o].at[pl.ds(k * wide, wide)]
        direct.append(pltpu.make_async_copy(motion_far.at[x * cols + y], there, pass_by.at[i]))
    size = panels.shape[0]
    for o in range(2):
        for h in range(wide // load.shape[2]):
            i = len(direct)
            there = outs[o].at[pl.ds(2 * len(sides[o]) * wide + h * size, size)]
            here = panels.at[:, pl.ds(h * load.shape[2], load.shape[2])]
            direct.append(pltpu.make_async_copy(here, there, pass_by.at[i]))
    for move in direct:
        move.start()
    fetch[0].wait()
    final = []
    for i, (o, k, x, y, d) in enumerate(spots):
        fetch[i + 1].wait()
        link = joints[x, y, d].astype(F32)
        term = joined(adjoint_parts(coupling[i], load[x * cols + y]), -1)
        terms[i] = (link * term).astype(BF16)
        there = outs[o].at[pl.ds((len(sides[o]) + k) * wide, wide)]
        final.append(pltpu.make_async_copy(terms.at[i], there, leave.at[i]))
        final[-1].start()
    for move in direct + final:
        move.wait()


def hydro_kernel(n_gx, spot, hydro_ref, loads_ref, *refs):
    pieces, (pressure_out, *reaction_outs, gathered, pressures, reacted, leave) = refs[:n_gx], refs[n_gx:]
    me = spot[0]
    panels, wide = pieces[0].shape
    for step in range(n_gx):
        start = pl.multiple_of(source(me, step, n_gx) * panels, panels)
        if step in (1, 2):
            narrow = pieces[step].shape[1]
            top = pieces[step].shape[0] - panels * wide // narrow
            for h in range(wide // narrow):
                part = pieces[step][pl.ds(top + h * panels, panels), :]
                gathered[pl.ds(start, panels), pl.ds(h * narrow, narrow)] = part
        else:
            gathered[pl.ds(start, panels), :] = pieces[step][...]
    hydro = hydro_ref[...]
    size, depth = hydro.shape[1:]
    both = dot(hydro.reshape(2 * size, depth), gathered[...], (1, 0))
    pressure = both[:size] + times_i(both[size:], 1)
    pressures[...] = pressure.astype(BF16).reshape(pressures.shape)
    out = pltpu.make_async_copy(pressures, pressure_out, leave)
    out.start()
    loads = loads_ref[...].reshape(size, -1)
    real = dot(hydro[0], loads, (0, 0))
    imag = dot(hydro[1], loads, (0, 0))
    reacted[...] = real - times_i(imag, 1)
    for step in range(n_gx):
        start = pl.multiple_of(target(me, step, n_gx) * panels, panels)
        reaction_outs[step][...] = reacted[pl.ds(start, panels), :]
    out.wait()


def local_kernel(rows, cols, n_gx, spot, joints, motion, load, excitation, coupling, *refs):
    first, second, before, after, residual_out, multiplier_out, own_out = refs
    wide = motion.shape[1]
    me = spot[0]
    even = me % 2 == 0
    valid = [(me > 0).astype(F32), (me < n_gx - 1).astype(F32), 1.0, 1.0]

    def received(d, k, kind):
        count = cols if d < 2 else rows
        here = pl.ds((kind * count + k) * wide, wide)
        if d >= 2:
            return (before if d == 2 else after)[here, :]
        return jnp.where(even, (second if d == 0 else first)[here, :], (first if d == 0 else second)[here, :])

    for x in range(rows):
        for y in range(cols):
            b = x * cols + y
            own = joined(forward_parts(coupling[b, 0], motion[b]), 1)
            own_out[b] = own
            parts = None
            adjoint = adjoint_parts(coupling[b, 0], load[b])
            extra = None
            for d in range(4):
                nx, ny = x + OFFSETS[d][0], y + OFFSETS[d][1]
                link = joints[x, y, d].astype(F32)
                if 0 <= nx < rows and 0 <= ny < cols:
                    n = nx * cols + ny
                    beside = motion[n]
                    back = joints[nx, ny, d ^ 1].astype(F32)
                    adjoint = adjoint + back * adjoint_parts(coupling[n, (d ^ 1) + 1], load[n])
                else:
                    k = y if d < 2 else x
                    beside = received(d, k, 0)
                    link = link * valid[d]
                    term = received(d, k, 1).astype(F32) * valid[d]
                    extra = term if extra is None else extra + term
                part = link * forward_parts(coupling[b, d + 1], beside)
                parts = part if parts is None else parts + part
            residual_out[b] = own + joined(parts, 1) - excitation[b].astype(F32)
            multiplier = joined(adjoint, -1)
            multiplier_out[b] = multiplier if extra is None else multiplier + extra


def final_kernel(rows, cols, lift, map_ref, residual, multiplier, own, pressures, *refs):
    reactions, (residual_out, multiplier_out, sensitivity_out) = refs[:-3], refs[-3:]
    blocks = rows * cols
    maps = map_of_blocks(map_ref, blocks)
    pressure = jnp.sum(pressures[...].astype(F32), axis=0).astype(BF16)
    reaction = sum(r[...].astype(F32) for r in reactions).astype(BF16)
    scale = 1.0 / math.sqrt(own.shape[1] // 2 * own.shape[2])
    for x in range(rows):
        for y in range(cols):
            b = x * cols + y
            residual_out[b] = residual[b] + lift * dot(pressure, maps[b], (0, 0))
            full = multiplier[b] + lift * dot(reaction, maps[b], (0, 0))
            multiplier_out[b] = full
            sensitivity_out[x, y] = jnp.sum(full * own[b]) * scale


def cost(flops, bytes_accessed):
    return pl.CostEstimate(flops=int(flops), bytes_accessed=int(bytes_accessed), transcendentals=0)


def shaped(dtype, *shape):
    return jax.ShapeDtypeStruct(shape, dtype)


PARAMS = pltpu.CompilerParams(vmem_limit_bytes=40 * 1024 * 1024)
DMA = pltpu.SemaphoreType.DMA


def on_device(plate_motion, adjoint_load, excitation, coupling, joints, hydro, panel_map):
    rows, cols, cases, _, unknowns = plate_motion.shape
    panels = panel_map.shape[0]
    blocks, wide = rows * cols, 2 * cases
    n_gx, n_gy = lax.axis_size("gx"), lax.axis_size("gy")
    spot = lax.axis_index("gx").reshape(1)
    motion = plate_motion.reshape(blocks, wide, unknowns)
    load = adjoint_load.reshape(blocks, wide, unknowns)
    force = excitation.reshape(blocks, wide, unknowns)
    coupling = coupling.reshape(blocks, 5, 2, unknowns, unknowns)
    panel_map = panel_map.reshape(panels * blocks, unknowns)
    lift = math.sqrt(blocks * unknowns / panels)
    block_flops = 2 * wide * unknowns * unknowns * 2
    field = (blocks, wide, unknowns)

    motion_panels, load_copies = pl.pallas_call(
        panels_kernel,
        name="panels",
        out_shape=[shaped(BF16, panels, wide), shaped(BF16, n_gy, panels, wide)],
        in_specs=[FAR] * 3,
        out_specs=[WHOLE, FAR],
        scratch_shapes=[
            pltpu.VMEM(field, BF16),
            pltpu.VMEM(field, BF16),
            pltpu.VMEM(panel_map.shape, BF16),
            pltpu.VMEM((panels, wide), BF16),
            DMA((3,)),
            DMA((n_gy,)),
        ],
        compiler_params=PARAMS,
        cost_estimate=cost(4 * blocks * wide * unknowns * panels, 4 * blocks * wide * unknowns),
    )(motion, load, panel_map)
    loads = lax.all_to_all(load_copies, "gy", 0, 0, tiled=True)

    counts = [cols, cols, rows, rows]
    extra = panels * wide // unknowns
    lengths = [2 * c * wide + (extra if o < 2 else 0) for o, c in enumerate(counts)]
    payloads = pl.pallas_call(
        functools.partial(edges_kernel, rows, cols),
        name="edges",
        out_shape=[shaped(BF16, length, unknowns) for length in lengths],
        in_specs=[SCALARS, SCALARS, WHOLE] + [FAR] * 3,
        out_specs=[FAR] * 4,
        scratch_shapes=[
            pltpu.VMEM(field, BF16),
            pltpu.VMEM((sum(counts), 2, unknowns, unknowns), BF16),
            pltpu.VMEM((sum(counts), wide, unknowns), BF16),
            DMA((sum(counts) + 1,)),
            DMA((sum(counts) + 2 * (wide // unknowns),)),
            DMA((sum(counts),)),
        ],
        compiler_params=PARAMS,
        cost_estimate=cost(sum(counts) * block_flops, 4 * blocks * wide * unknowns + 20 * blocks * unknowns**2),
    )(spot, joints, motion_panels, motion, load, coupling)
    first, second = exchange(payloads[0], 1), exchange(payloads[1], 2)
    pieces = [motion_panels, first, second] + [exchange(motion_panels, step) for step in range(3, n_gx)]
    before = lax.ppermute(payloads[3], "gy", [(i, i + 1) for i in range(n_gy - 1)])
    after = lax.ppermute(payloads[2], "gy", [(i + 1, i) for i in range(n_gy - 1)])

    pressure_parts, *reaction_parts = pl.pallas_call(
        functools.partial(hydro_kernel, n_gx),
        name="hydro",
        out_shape=[shaped(BF16, n_gy, panels, wide)] + [shaped(F32, panels, wide)] * n_gx,
        in_specs=[SCALARS] + [WHOLE] * (2 + n_gx),
        out_specs=[FAR] + [WHOLE] * n_gx,
        scratch_shapes=[
            pltpu.VMEM((n_gx * panels, wide), BF16),
            pltpu.VMEM((n_gy, panels, wide), BF16),
            pltpu.VMEM((n_gx * panels, wide), F32),
            DMA,
        ],
        compiler_params=PARAMS,
        cost_estimate=cost(4 * hydro.size * wide, 2 * hydro.size),
    )(spot, hydro, loads, *pieces)
    pressures = lax.all_to_all(pressure_parts, "gy", 0, 0, tiled=True)
    reactions = [reaction_parts[0]] + [exchange(reaction_parts[step], step) for step in range(1, n_gx)]

    residual, multiplier, own = pl.pallas_call(
        functools.partial(local_kernel, rows, cols, n_gx),
        name="local",
        out_shape=[shaped(F32, *field)] * 3,
        in_specs=[SCALARS] * 2 + [WHOLE] * 8,
        out_specs=[WHOLE] * 3,
        compiler_params=PARAMS,
        cost_estimate=cost(10 * blocks * block_flops, 20 * blocks * unknowns**2 + 20 * blocks * wide * unknowns),
    )(spot, joints, motion, load, force, coupling, first, second, before, after)

    residual, multiplier, sensitivity = pl.pallas_call(
        functools.partial(final_kernel, rows, cols, lift),
        name="final",
        out_shape=[shaped(F32, *field), shaped(F32, *field), shaped(F32, rows, cols)],
        in_specs=[WHOLE] * (5 + n_gx),
        out_specs=[WHOLE, WHOLE, SCALARS],
        compiler_params=PARAMS,
        cost_estimate=cost(4 * blocks * wide * unknowns * panels, 20 * blocks * wide * unknowns),
    )(panel_map, residual, multiplier, own, pressures, *reactions)
    shape = plate_motion.shape
    return residual.reshape(shape), multiplier.reshape(shape), sensitivity


def solution(mesh):
    field = P("gx", "gy", None, None, None)
    placed = (
        field,
        field,
        field,
        P("gx", "gy", None, None, None, None),
        P("gx", "gy", None),
        P(None, "gx", "gy"),
        P(("gx", "gy"), None, None, None),
    )
    return jax.shard_map(on_device, mesh=mesh, in_specs=placed, out_specs=(field, field, P("gx", "gy")), check_vma=False)
```

time: 235 us -> 51.5 us (0.22)
  blocking collectives: 179 us -> 0 us
  matrix products: 10.8 us -> 0 us
  Pallas kernels: 0 us -> 9.79 us
  other arithmetic: 3.85 us -> 0 us
  waiting for transfers between devices: 6.36 us -> 3.23 us
  starting transfers between devices: 20.9 us -> 23.5 us
    psum x2 -> x0, blocking collectives: 133 us -> none  [the longest x1 118 us: on_device(): pressure_band = lax.psum(pressure_part, 'gy')]
    all_gather x2 -> x0, blocking collectives: 45.7 us -> none  [the longest x1 31.7 us: on_device(): piece = lax.all_gather(load_panels, 'gy', axis=1, tiled=True)]
    all_to_all x0 -> x2, starting transfers between devices: none -> 12.5 us  [the longest x1 6.62 us: on_device(): pressures = lax.all_to_all(pressure_parts, 'gy', 0, 0, tiled=True)]
    dot_general x28 -> x0, matrix products: 10.8 us -> none  [the longest x16 6.56 us: mult(): return jnp.einsum(form, matrix, values, preferred_element_type=jnp.float32)]
    ppermute x8, starting transfers between devices: 20.9 us -> 11 us  [the longest x6 5.79 us: exchange(): return lax.ppermute(x, 'gx', [(i, target(i, step, n)) for i in range(n)])]
    pallas_call x0 -> x5, Pallas kernels: none -> 9.79 us  [the longest x1 4.14 us: on_device(): pl.pallas_call(functools.partial(edges_kernel, rows, cols), name='edges',...]
    unnamed x26 -> x46, local copies, waits for them, and re-layouts: 4.74 us -> 13.5 us
    slice x4 -> x0, local copies, waits for them, and re-layouts: 4.72 us -> none  [the longest x2 2.5 us: extended(): first = lax.slice_in_dim(x, 0, width, axis=dim)]
  transfers between devices with their start and end apart: 8 -> 10, of which waited for: 2 -> 1; matrix products, arithmetic and copies ran while one was open for 5% -> 0% of each run, Pallas kernels for 0% -> 6%
where the time goes in v1:
time: 51.5 us; the launch traced here: 50.8 us
  starting transfers between devices  23.5 us (46%)
  local copies, waits for them, and re-layouts  13.5 us (26%)
  Pallas kernels  9.79 us (19%)
  waiting for transfers between devices  3.23 us (6%)
  between operations  0.82 us (2%)
    unnamed x46, local copies, waits for them, and re-layouts  13.5 us
    all_to_all x1, starting transfers between devices, on_device(): pressures = lax.all_to_all(pressure_parts, 'gy', 0, 0, tiled=True)  6.62 us
    all_to_all x1, starting transfers between devices, on_device(): loads = lax.all_to_all(load_copies, 'gy', 0, 0, tiled=True)  5.84 us
    ppermute x6, starting transfers between devices, exchange(): return lax.ppermute(x, 'gx', [(i, target(i, step, n)) for i in range(n)])  5.79 us
    pallas_call x1, Pallas kernels, on_device(): pl.pallas_call(functools.partial(edges_kernel, rows, cols), name='edges',...  4.14 us
    ppermute x1, starting transfers between devices, on_device(): lax.ppermute(payloads[3], 'gy', [(i, i + 1) for i in range(n_gy - 1)])  3.93 us
    ppermute x6, waiting for transfers between devices, exchange(): return lax.ppermute(x, 'gx', [(i, target(i, step, n)) for i in range(n)])  3.22 us
    pallas_call x1, Pallas kernels, on_device(): pl.pallas_call(functools.partial(local_kernel, rows, cols, n_gx), name='l...  1.98 us
  transfers between devices with their start and end apart: 10, of which 1 were waited for; matrix products, arithmetic and copies ran while one was open for 0% of the time, Pallas kernels for 6%

profile of v1, /device:TPU:0, one launch (start us, length us, event | category | flops | bytes accessed | tf_op | source)
XLA Modules:
  0.0 50.8 jit_solution(11493554303709483394)
XLA Ops:
  0.6 0.0 copy-start.2
  0.6 0.9 %copy-done.2 = bf16[2,2,128,2,128]{4,3,2,1,0:T(2,128)(2,1)S(1)} copy-done((bf16[2,2,128,2,128]{4,3,2,1,0:T(2,128)(2,1)S(1)}, bf16[2,2,128,2,128]{4,3,2,1,0:T(2,128)(2,1)}, u32[]{:S(2)}) %copy-start.2) | copy-done | bytes 262168
  1.6 0.9 %copy-done.4 = bf16[2,2,128,2,128]{4,3,2,1,0:T(2,128)(2,1)S(1)} copy-done((bf16[2,2,128,2,128]{4,3,2,1,0:T(2,128)(2,1)S(1)}, bf16[2,2,128,2,128]{4,3,2,1,0:T(2,128)(2,1)}, u32[]{:S(2)}) %copy-start.4) | copy-done | bytes 262168
  2.5 0.8 %copy-done.15 = bf16[32,2,2,128]{3,2,1,0:T(2,128)(2,1)S(1)} copy-done((bf16[32,2,2,128]{3,2,1,0:T(2,128)(2,1)S(1)}, bf16[32,2,2,128]{3,2,1,0:T(2,128)(2,1)}, u32[]{:S(2)}) %copy-start.15) | copy-done | bytes 32792
  3.3 1.2 %panels.1 = (bf16[32,256]{1,0:T(8,128)(2,1)S(1)}, bf16[8,32,256]{2,1,0:T(8,128)(2,1)}) custom-call(bf16[4,256,128]{2,1,0:T(8,128)(2,1)S(1)} %bitcast.10, bf16[4,256,128]{2,1,0:T(8,128)(2,1)S(1)} %bitcast.13, bf16[128,128]{1,0:T(8,128)(2,1)S(1)} %bitcast.17), custom_call_target="tpu_custom_call" | custom-call | flops 16777216 | bytes 524288 | tf_op jit(solution)/shard_map/panels/pallas_call | solution.py:264
  4.5 0.0 copy-start
  4.5 1.3 %copy-done = bf16[2,2,5,2,128,128]{5,4,3,2,1,0:T(8,128)(2,1)S(1)} copy-done((bf16[2,2,5,2,128,128]{5,4,3,2,1,0:T(8,128)(2,1)S(1)}, bf16[2,2,5,2,128,128]{5,4,3,2,1,0:T(8,128)(2,1)}, u32[]{:S(2)}) %copy-start) | copy-done | bytes 1310744
  5.8 0.7 %copy-done.18 = s32[2,2,4]{2,1,0:T(2,128)S(1)} copy-done((s32[2,2,4]{2,1,0:T(2,128)S(1)}, s32[2,2,4]{2,1,0:T(2,128)}, u32[]{:S(2)}) %copy-start.18) | copy-done | bytes 88
  6.5 4.1 %edges.1 = (bf16[1088,128]{1,0:T(8,128)(2,1)}, bf16[1088,128]{1,0:T(8,128)(2,1)}, bf16[1024,128]{1,0:T(8,128)(2,1)S(1)}, bf16[1024,128]{1,0:T(8,128)(2,1)}) custom-call(s32[1]{0:T(128)} %bitcast.1.spot, s32[2,2,4]{2,1,0:T(2,128)S(1)} %copy-done.18, bf16[32,256]{1,0:T(8,128)(2,1)S(1)} %get-tuple-element.20.panels.refs_0_, bf16[4,256,128]{2,1,0:T(8,128)(2,1)S(1)} %bitcast.11, ...), custom_call_target="tpu_custom_call" | custom-call | flops 134217728 | bytes 1835008 | tf_op jit(solution)/shard_map/edges/pallas_call | solution.py:286
  10.7 0.7 %copy-done.20 = bf16[1024,128]{1,0:T(8,128)(2,1)} copy-done((bf16[1024,128]{1,0:T(8,128)(2,1)}, bf16[1024,128]{1,0:T(8,128)(2,1)S(1)}, u32[]{:S(2)}) %copy-start.20) | copy-done | bytes 262168
  11.4 0.5 collective-permute-start
  11.8 2.6 %collective-permute-start.1 = (bf16[1088,128]{1,0:T(8,128)(2,1)}, bf16[1088,128]{1,0:T(8,128)(2,1)S(1)}, u32[]{:S(2)}, u32[]{:S(2)}) collective-permute-start(bf16[1088,128]{1,0:T(8,128)(2,1)} %get-tuple-element.22), channel_id=1, source_target_pairs={{0,24},{8,16},{16,8},{24,0},{1,25},{9,17},{17,9},{25,1},{2,26},{10... | collective-permute-start | bytes 835592 | tf_op jit(solution)/shard_map/ppermute | solution.py:75
  14.4 5.8 %all-to-all-start = ((bf16[8,32,256]{2,1,0:T(8,128)(2,1)}), bf16[8,32,256]{2,1,0:T(8,128)(2,1)S(1)}, u32[]{:S(2)}, u32[]{:S(2)}) async-start(bf16[8,32,256]{2,1,0:T(8,128)(2,1)} %get-tuple-element.28), calls=%async_computation | async-start | bytes 262144 | tf_op jit(solution)/shard_map/all_to_all | solution.py:281
  20.3 3.9 %collective-permute-start.2 = (bf16[1024,128]{1,0:T(8,128)(2,1)}, bf16[1024,128]{1,0:T(8,128)(2,1)S(1)}, u32[]{:S(2)}, u32[]{:S(2)}) collective-permute-start(bf16[1024,128]{1,0:T(8,128)(2,1)} %get-tuple-element.23), channel_id=1, source_target_pairs={{0,1},{1,2},{2,3},{3,4},{4,5},{5,6},{6,7},{8,9},{9,10},{10,11},{11... | collective-permute-start | bytes 786440 | tf_op jit(solution)/shard_map/ppermute | solution.py:305
  24.2 1.3 %collective-permute-start.3 = (bf16[1024,128]{1,0:T(8,128)(2,1)}, bf16[1024,128]{1,0:T(8,128)(2,1)S(1)}, u32[]{:S(2)}, u32[]{:S(2)}) collective-permute-start(bf16[1024,128]{1,0:T(8,128)(2,1)} %copy-done.20), channel_id=1, source_target_pairs={{1,0},{2,1},{3,2},{4,3},{5,4},{6,5},{7,6},{9,8},{10,9},{11,10},{12... | collective-permute-start | bytes 786440 | tf_op jit(solution)/shard_map/ppermute | solution.py:306
  25.5 0.6 %collective-permute-start.4 = (bf16[32,256]{1,0:T(8,128)(2,1)S(1)}, bf16[32,256]{1,0:T(8,128)(2,1)S(1)}, u32[]{:S(2)}, u32[]{:S(2)}) collective-permute-start(bf16[32,256]{1,0:T(8,128)(2,1)S(1)} %get-tuple-element.20.panels.refs_0_), channel_id=1, source_target_pairs={{0,16},{8,24},{16,0},{24,8},{1,17},{9,25},{17,1},{25,9},{2,18},{10... | collective-permute-start | bytes 49160 | tf_op jit(solution)/shard_map/ppermute | solution.py:75
  26.1 3.2 %collective-permute-done.4.refs_3_ = bf16[32,256]{1,0:T(8,128)(2,1)S(1)} collective-permute-done((bf16[32,256]{1,0:T(8,128)(2,1)S(1)}, bf16[32,256]{1,0:T(8,128)(2,1)S(1)}, u32[]{:S(2)}, u32[]{:S(2)}) %collective-permute-start.4) | collective-permute-done | bytes 16416 | tf_op jit(solution)/shard_map/ppermute | solution.py:75
  29.3 0.0 all-to-all-done.loads_ref
  29.3 0.0 collective-permute-done.refs_0_.refs_1_
  29.3 0.0 collective-permute-done.1.refs_1_.refs_2_
  29.3 1.1 %hydro.1 = (bf16[8,32,256]{2,1,0:T(8,128)(2,1)}, f32[32,256]{1,0:T(8,128)S(1)}, f32[32,256]{1,0:T(8,128)S(1)}, f32[32,256]{1,0:T(8,128)S(1)}, f32[32,256]{1,0:T(8,128)S(1)}) custom-call(s32[1]{0:T(128)} %bitcast.1.spot, bf16[2,256,128]{2,1,0:T(8,128)(2,1)S(1)} %copy-done.17, bf16[8,32,256]{2,1,0:T(8,128)(2,1)S(1)} %all-to-all-done.loads_ref, ...), custom_call_target="tpu_custom_call" | custom-call | flops 67108864 | bytes 131072 | tf_op jit(solution)/shard_map/hydro/pallas_call | solution.py:308
  30.4 0.6 %copy-done.21 = f32[32,256]{1,0:T(8,128)} copy-done((f32[32,256]{1,0:T(8,128)}, f32[32,256]{1,0:T(8,128)S(1)}, u32[]{:S(2)}) %copy-start.21) | copy-done | bytes 32792
  31.0 0.6 %copy-done.22 = f32[32,256]{1,0:T(8,128)} copy-done((f32[32,256]{1,0:T(8,128)}, f32[32,256]{1,0:T(8,128)S(1)}, u32[]{:S(2)}) %copy-start.22) | copy-done | bytes 32792
  31.6 6.6 %all-to-all-start.1 = ((bf16[8,32,256]{2,1,0:T(8,128)(2,1)}), bf16[8,32,256]{2,1,0:T(8,128)(2,1)S(1)}, u32[]{:S(2)}, u32[]{:S(2)}) async-start(bf16[8,32,256]{2,1,0:T(8,128)(2,1)} %get-tuple-element.29), calls=%async_computation.1 | async-start | bytes 262144 | tf_op jit(solution)/shard_map/all_to_all | solution.py:323
  38.2 0.0 collective-permute-start.5
  38.3 0.6 %collective-permute-start.6 = (f32[32,256]{1,0:T(8,128)}, f32[32,256]{1,0:T(8,128)S(1)}, u32[]{:S(2)}, u32[]{:S(2)}) collective-permute-start(f32[32,256]{1,0:T(8,128)} %copy-done.21), channel_id=1, source_target_pairs={{0,24},{8,16},{16,8},{24,0},{1,25},{9,17},{17,9},{25,1},{2,26},{10... | collective-permute-start | bytes 98312 | tf_op jit(solution)/shard_map/ppermute | solution.py:75
  38.9 1.5 %collective-permute-start.7 = (f32[32,256]{1,0:T(8,128)S(1)}, f32[32,256]{1,0:T(8,128)S(1)}, u32[]{:S(2)}, u32[]{:S(2)}) collective-permute-start(f32[32,256]{1,0:T(8,128)S(1)} %get-tuple-element.33), channel_id=1, source_target_pairs={{0,16},{8,24},{16,0},{24,8},{1,17},{9,25},{17,1},{25,9},{2,18},{10... | collective-permute-start | bytes 98312 | tf_op jit(solution)/shard_map/ppermute | solution.py:75
  40.4 0.0 collective-permute-done.2.refs_2_
  40.4 0.7 %copy-done.11 = bf16[1024,128]{1,0:T(8,128)(2,1)} copy-done((bf16[1024,128]{1,0:T(8,128)(2,1)}, bf16[1024,128]{1,0:T(8,128)(2,1)S(1)}, u32[]{:S(2)}) %copy-start.11) | copy-done | bytes 262168
  41.1 0.0 collective-permute-done.3.refs_3_
  41.1 0.7 %copy-done.13 = bf16[1024,128]{1,0:T(8,128)(2,1)} copy-done((bf16[1024,128]{1,0:T(8,128)(2,1)}, bf16[1024,128]{1,0:T(8,128)(2,1)S(1)}, u32[]{:S(2)}) %copy-start.13) | copy-done | bytes 262168
  41.8 0.0 copy-done.5
  41.8 0.0 copy-start.12
  41.8 0.9 %copy-done.12 = bf16[1024,128]{1,0:T(8,128)(2,1)S(1)} copy-done((bf16[1024,128]{1,0:T(8,128)(2,1)S(1)}, bf16[1024,128]{1,0:T(8,128)(2,1)}, u32[]{:S(2)}) %copy-start.12) | copy-done | bytes 262168
  42.8 0.9 %copy-done.14 = bf16[1024,128]{1,0:T(8,128)(2,1)S(1)} copy-done((bf16[1024,128]{1,0:T(8,128)(2,1)S(1)}, bf16[1024,128]{1,0:T(8,128)(2,1)}, u32[]{:S(2)}) %copy-start.14) | copy-done | bytes 262168
  43.7 2.0 %local.1 = (f32[4,256,128]{2,1,0:T(8,128)S(1)}, f32[4,256,128]{2,1,0:T(8,128)S(1)}, f32[4,256,128]{2,1,0:T(8,128)S(1)}) custom-call(s32[1]{0:T(128)} %bitcast.1.spot, s32[2,2,4]{2,1,0:T(2,128)S(1)} %copy-done.19, bf16[4,256,128]{2,1,0:T(8,128)(2,1)S(1)} %bitcast.12, bf16[4,256,128]{2,1,0:T(8,128)(2,1)S(1)} %bitcast.15, bf16[4,256,128]{2,1,0:T(8,128)(2,1)S(1)} %bitcast.16, ...), custom_call_target="tpu_custom_call" | custom-call | flops 671088640 | bytes 3932160 | tf_op jit(solution)/shard_map/local/pallas_call | solution.py:326
  45.7 0.0 copy-start.6
  45.7 0.8 %copy-done.6 = f32[4,256,128]{2,1,0:T(8,128)} copy-done((f32[4,256,128]{2,1,0:T(8,128)}, f32[4,256,128]{2,1,0:T(8,128)S(1)}, u32[]{:S(2)}) %copy-start.6) | copy-done | bytes 524312
  46.5 0.8 %copy-done.8 = f32[4,256,128]{2,1,0:T(8,128)} copy-done((f32[4,256,128]{2,1,0:T(8,128)}, f32[4,256,128]{2,1,0:T(8,128)S(1)}, u32[]{:S(2)}) %copy-start.8) | copy-done | bytes 524312
  47.3 0.0 collective-permute-done.5.refs_1_
  47.3 0.0 collective-permute-done.6.refs_2_
  47.3 0.0 collective-permute-done.7.refs_3_
  47.3 0.0 all-to-all-done.1.pressures
  47.3 0.0 copy-done.16
  47.3 0.0 copy-start.7
  47.3 1.0 %copy-done.7 = f32[4,256,128]{2,1,0:T(8,128)S(1)} copy-done((f32[4,256,128]{2,1,0:T(8,128)S(1)}, f32[4,256,128]{2,1,0:T(8,128)}, u32[]{:S(2)}) %copy-start.7) | copy-done | bytes 524312
  48.4 1.0 %copy-done.9 = f32[4,256,128]{2,1,0:T(8,128)S(1)} copy-done((f32[4,256,128]{2,1,0:T(8,128)S(1)}, f32[4,256,128]{2,1,0:T(8,128)}, u32[]{:S(2)}) %copy-start.9) | copy-done | bytes 524312
  49.4 1.4 %final.1 = (f32[4,256,128]{2,1,0:T(8,128)}, f32[4,256,128]{2,1,0:T(8,128)}, f32[2,2]{1,0:T(2,128)}) custom-call(bf16[128,128]{1,0:T(8,128)(2,1)S(1)} %bitcast.18, f32[4,256,128]{2,1,0:T(8,128)S(1)} %get-tuple-element.25.residual, f32[4,256,128]{2,1,0:T(8,128)S(1)} %copy-done.7, f32[4,256,128]{2,1,0:T(8,128)S(1)} %copy-done.9, ...), custom_call_target="tpu_custom_call" | custom-call | flops 16777216 | bytes 2621440 | tf_op jit(solution)/shard_map/final/pallas_call | solution.py:336
  (23 shorter events, 0.0 us)
Async XLA Ops:
  0.6 1.0 %copy-start.2 = (bf16[2,2,128,2,128]{4,3,2,1,0:T(2,128)(2,1)S(1)}, bf16[2,2,128,2,128]{4,3,2,1,0:T(2,128)(2,1)}, u32[]{:S(2)}) copy-start(bf16[2,2,128,2,128]{4,3,2,1,0:T(2,128)(2,1)} %param.7) | copy-start | bytes 786436
  1.6 0.9 %copy-start.4 = (bf16[2,2,128,2,128]{4,3,2,1,0:T(2,128)(2,1)S(1)}, bf16[2,2,128,2,128]{4,3,2,1,0:T(2,128)(2,1)}, u32[]{:S(2)}) copy-start(bf16[2,2,128,2,128]{4,3,2,1,0:T(2,128)(2,1)} %param.8) | copy-start | bytes 786436
  2.5 0.8 %copy-start.15 = (bf16[32,2,2,128]{3,2,1,0:T(2,128)(2,1)S(1)}, bf16[32,2,2,128]{3,2,1,0:T(2,128)(2,1)}, u32[]{:S(2)}) copy-start(bf16[32,2,2,128]{3,2,1,0:T(2,128)(2,1)} %param.13) | copy-start | bytes 98308
  3.3 26.0 %copy-start.17 = (bf16[2,256,128]{2,1,0:T(8,128)(2,1)S(1)}, bf16[2,256,128]{2,1,0:T(8,128)(2,1)}, u32[]{:S(2)}) copy-start(bf16[2,256,128]{2,1,0:T(8,128)(2,1)} %hydro_ref.1) | copy-start | bytes 393220
  4.5 1.3 %copy-start = (bf16[2,2,5,2,128,128]{5,4,3,2,1,0:T(8,128)(2,1)S(1)}, bf16[2,2,5,2,128,128]{5,4,3,2,1,0:T(8,128)(2,1)}, u32[]{:S(2)}) copy-start(bf16[2,2,5,2,128,128]{5,4,3,2,1,0:T(8,128)(2,1)} %param.10) | copy-start | bytes 3932164
  5.8 0.7 %copy-start.18 = (s32[2,2,4]{2,1,0:T(2,128)S(1)}, s32[2,2,4]{2,1,0:T(2,128)}, u32[]{:S(2)}) copy-start(s32[2,2,4]{2,1,0:T(2,128)} %joints.3) | copy-start | bytes 196
  6.5 35.3 %copy-start.1 = (bf16[2,2,5,2,128,128]{5,4,3,2,1,0:T(8,128)(2,1)S(1)}, bf16[2,2,5,2,128,128]{5,4,3,2,1,0:T(8,128)(2,1)}, u32[]{:S(2)}) copy-start(bf16[2,2,5,2,128,128]{5,4,3,2,1,0:T(8,128)(2,1)} %param.10) | copy-start | bytes 3932164
  6.5 35.3 %copy-start.3 = (bf16[2,2,128,2,128]{4,3,2,1,0:T(2,128)(2,1)S(1)}, bf16[2,2,128,2,128]{4,3,2,1,0:T(2,128)(2,1)}, u32[]{:S(2)}) copy-start(bf16[2,2,128,2,128]{4,3,2,1,0:T(2,128)(2,1)} %param.7) | copy-start | bytes 786436
  6.5 35.3 %copy-start.5 = (bf16[2,2,128,2,128]{4,3,2,1,0:T(2,128)(2,1)S(1)}, bf16[2,2,128,2,128]{4,3,2,1,0:T(2,128)(2,1)}, u32[]{:S(2)}) copy-start(bf16[2,2,128,2,128]{4,3,2,1,0:T(2,128)(2,1)} %param.8) | copy-start | bytes 786436
  6.5 35.3 %copy-start.10 = (bf16[2,2,128,2,128]{4,3,2,1,0:T(2,128)(2,1)S(1)}, bf16[2,2,128,2,128]{4,3,2,1,0:T(2,128)(2,1)}, u32[]{:S(2)}) copy-start(bf16[2,2,128,2,128]{4,3,2,1,0:T(2,128)(2,1)} %param.9) | copy-start | bytes 786436
  6.5 35.3 %copy-start.19 = (s32[2,2,4]{2,1,0:T(2,128)S(1)}, s32[2,2,4]{2,1,0:T(2,128)}, u32[]{:S(2)}) copy-start(s32[2,2,4]{2,1,0:T(2,128)} %joints.3) | copy-start | bytes 196
  10.7 0.7 %copy-start.20 = (bf16[1024,128]{1,0:T(8,128)(2,1)}, bf16[1024,128]{1,0:T(8,128)(2,1)S(1)}, u32[]{:S(2)}) copy-start(bf16[1024,128]{1,0:T(8,128)(2,1)S(1)} %get-tuple-element.24) | copy-start | bytes 786436
  11.4 17.9 %collective-permute-start = (bf16[1088,128]{1,0:T(8,128)(2,1)}, bf16[1088,128]{1,0:T(8,128)(2,1)S(1)}, u32[]{:S(2)}, u32[]{:S(2)}) collective-permute-start(bf16[1088,128]{1,0:T(8,128)(2,1)} %get-tuple-element.21), channel_id=1, source_target_pairs={{0,8},{8,0},{16,24},{24,16},{1,9},{9,1},{17,25},{25,17},{2,10},{10... | collective-permute-start | bytes 835592 | tf_op jit(solution)/shard_map/ppermute | solution.py:75
  11.8 17.5 %collective-permute-start.1 = (bf16[1088,128]{1,0:T(8,128)(2,1)}, bf16[1088,128]{1,0:T(8,128)(2,1)S(1)}, u32[]{:S(2)}, u32[]{:S(2)}) collective-permute-start(bf16[1088,128]{1,0:T(8,128)(2,1)} %get-tuple-element.22), channel_id=1, source_target_pairs={{0,24},{8,16},{16,8},{24,0},{1,25},{9,17},{17,9},{25,1},{2,26},{10... | collective-permute-start | bytes 835592 | tf_op jit(solution)/shard_map/ppermute | solution.py:75
  14.4 14.9 %all-to-all-start = ((bf16[8,32,256]{2,1,0:T(8,128)(2,1)}), bf16[8,32,256]{2,1,0:T(8,128)(2,1)S(1)}, u32[]{:S(2)}, u32[]{:S(2)}) async-start(bf16[8,32,256]{2,1,0:T(8,128)(2,1)} %get-tuple-element.28), calls=%async_computation | async-start | bytes 262144 | tf_op jit(solution)/shard_map/all_to_all | solution.py:281
  20.3 20.1 %collective-permute-start.2 = (bf16[1024,128]{1,0:T(8,128)(2,1)}, bf16[1024,128]{1,0:T(8,128)(2,1)S(1)}, u32[]{:S(2)}, u32[]{:S(2)}) collective-permute-start(bf16[1024,128]{1,0:T(8,128)(2,1)} %get-tuple-element.23), channel_id=1, source_target_pairs={{0,1},{1,2},{2,3},{3,4},{4,5},{5,6},{6,7},{8,9},{9,10},{10,11},{11... | collective-permute-start | bytes 786440 | tf_op jit(solution)/shard_map/ppermute | solution.py:305
  24.2 16.9 %collective-permute-start.3 = (bf16[1024,128]{1,0:T(8,128)(2,1)}, bf16[1024,128]{1,0:T(8,128)(2,1)S(1)}, u32[]{:S(2)}, u32[]{:S(2)}) collective-permute-start(bf16[1024,128]{1,0:T(8,128)(2,1)} %copy-done.20), channel_id=1, source_target_pairs={{1,0},{2,1},{3,2},{4,3},{5,4},{6,5},{7,6},{9,8},{10,9},{11,10},{12... | collective-permute-start | bytes 786440 | tf_op jit(solution)/shard_map/ppermute | solution.py:306
  25.5 3.8 %collective-permute-start.4 = (bf16[32,256]{1,0:T(8,128)(2,1)S(1)}, bf16[32,256]{1,0:T(8,128)(2,1)S(1)}, u32[]{:S(2)}, u32[]{:S(2)}) collective-permute-start(bf16[32,256]{1,0:T(8,128)(2,1)S(1)} %get-tuple-element.20.panels.refs_0_), channel_id=1, source_target_pairs={{0,16},{8,24},{16,0},{24,8},{1,17},{9,25},{17,1},{25,9},{2,18},{10... | collective-permute-start | bytes 49160 | tf_op jit(solution)/shard_map/ppermute | solution.py:75
  30.4 0.6 %copy-start.21 = (f32[32,256]{1,0:T(8,128)}, f32[32,256]{1,0:T(8,128)S(1)}, u32[]{:S(2)}) copy-start(f32[32,256]{1,0:T(8,128)S(1)} %get-tuple-element.32) | copy-start | bytes 98308
  31.0 0.6 %copy-start.22 = (f32[32,256]{1,0:T(8,128)}, f32[32,256]{1,0:T(8,128)S(1)}, u32[]{:S(2)}) copy-start(f32[32,256]{1,0:T(8,128)S(1)} %get-tuple-element.31) | copy-start | bytes 98308
  31.6 15.7 %all-to-all-start.1 = ((bf16[8,32,256]{2,1,0:T(8,128)(2,1)}), bf16[8,32,256]{2,1,0:T(8,128)(2,1)S(1)}, u32[]{:S(2)}, u32[]{:S(2)}) async-start(bf16[8,32,256]{2,1,0:T(8,128)(2,1)} %get-tuple-element.29), calls=%async_computation.1 | async-start | bytes 262144 | tf_op jit(solution)/shard_map/all_to_all | solution.py:323
  38.2 9.1 %collective-permute-start.5 = (f32[32,256]{1,0:T(8,128)}, f32[32,256]{1,0:T(8,128)S(1)}, u32[]{:S(2)}, u32[]{:S(2)}) collective-permute-start(f32[32,256]{1,0:T(8,128)} %copy-done.22), channel_id=1, source_target_pairs={{0,8},{8,0},{16,24},{24,16},{1,9},{9,1},{17,25},{25,17},{2,10},{10... | collective-permute-start | bytes 98312 | tf_op jit(solution)/shard_map/ppermute | solution.py:75
  38.3 9.1 %collective-permute-start.6 = (f32[32,256]{1,0:T(8,128)}, f32[32,256]{1,0:T(8,128)S(1)}, u32[]{:S(2)}, u32[]{:S(2)}) collective-permute-start(f32[32,256]{1,0:T(8,128)} %copy-done.21), channel_id=1, source_target_pairs={{0,24},{8,16},{16,8},{24,0},{1,25},{9,17},{17,9},{25,1},{2,26},{10... | collective-permute-start | bytes 98312 | tf_op jit(solution)/shard_map/ppermute | solution.py:75
  38.9 8.4 %collective-permute-start.7 = (f32[32,256]{1,0:T(8,128)S(1)}, f32[32,256]{1,0:T(8,128)S(1)}, u32[]{:S(2)}, u32[]{:S(2)}) collective-permute-start(f32[32,256]{1,0:T(8,128)S(1)} %get-tuple-element.33), channel_id=1, source_target_pairs={{0,16},{8,24},{16,0},{24,8},{1,17},{9,25},{17,1},{25,9},{2,18},{10... | collective-permute-start | bytes 98312 | tf_op jit(solution)/shard_map/ppermute | solution.py:75
  40.4 0.7 %copy-start.11 = (bf16[1024,128]{1,0:T(8,128)(2,1)}, bf16[1024,128]{1,0:T(8,128)(2,1)S(1)}, u32[]{:S(2)}) copy-start(bf16[1024,128]{1,0:T(8,128)(2,1)S(1)} %collective-permute-done.2.refs_2_) | copy-start | bytes 786436
  41.1 0.7 %copy-start.13 = (bf16[1024,128]{1,0:T(8,128)(2,1)}, bf16[1024,128]{1,0:T(8,128)(2,1)S(1)}, u32[]{:S(2)}) copy-start(bf16[1024,128]{1,0:T(8,128)(2,1)S(1)} %collective-permute-done.3.refs_3_) | copy-start | bytes 786436
  41.8 1.0 %copy-start.12 = (bf16[1024,128]{1,0:T(8,128)(2,1)S(1)}, bf16[1024,128]{1,0:T(8,128)(2,1)}, u32[]{:S(2)}) copy-start(bf16[1024,128]{1,0:T(8,128)(2,1)} %copy-done.11) | copy-start | bytes 786436
  42.8 0.9 %copy-start.14 = (bf16[1024,128]{1,0:T(8,128)(2,1)S(1)}, bf16[1024,128]{1,0:T(8,128)(2,1)}, u32[]{:S(2)}) copy-start(bf16[1024,128]{1,0:T(8,128)(2,1)} %copy-done.13) | copy-start | bytes 786436
  43.7 3.6 %copy-start.16 = (bf16[32,2,2,128]{3,2,1,0:T(2,128)(2,1)S(1)}, bf16[32,2,2,128]{3,2,1,0:T(2,128)(2,1)}, u32[]{:S(2)}) copy-start(bf16[32,2,2,128]{3,2,1,0:T(2,128)(2,1)} %param.13) | copy-start | bytes 98308
  45.7 0.8 %copy-start.6 = (f32[4,256,128]{2,1,0:T(8,128)}, f32[4,256,128]{2,1,0:T(8,128)S(1)}, u32[]{:S(2)}) copy-start(f32[4,256,128]{2,1,0:T(8,128)S(1)} %get-tuple-element.26.multiplier) | copy-start | bytes 1572868
  46.5 0.8 %copy-start.8 = (f32[4,256,128]{2,1,0:T(8,128)}, f32[4,256,128]{2,1,0:T(8,128)S(1)}, u32[]{:S(2)}) copy-start(f32[4,256,128]{2,1,0:T(8,128)S(1)} %get-tuple-element.27.own) | copy-start | bytes 1572868
  47.3 1.0 %copy-start.7 = (f32[4,256,128]{2,1,0:T(8,128)S(1)}, f32[4,256,128]{2,1,0:T(8,128)}, u32[]{:S(2)}) copy-start(f32[4,256,128]{2,1,0:T(8,128)} %copy-done.6) | copy-start | bytes 1572868
  48.4 1.0 %copy-start.9 = (f32[4,256,128]{2,1,0:T(8,128)S(1)}, f32[4,256,128]{2,1,0:T(8,128)}, u32[]{:S(2)}) copy-start(f32[4,256,128]{2,1,0:T(8,128)} %copy-done.8) | copy-start | bytes 1572868

commit v2 on v1

--- a/solution.py
+++ b/solution.py
@@ -75,28 +75,6 @@
     return lax.ppermute(x, "gx", [(i, target(i, step, n)) for i in range(n)])
 
 
-def panels_kernel(motion_far, load_far, map_far, motion_out, load_out, motion, load, maps, panels, arrive, leave):
-    blocks = motion.shape[0]
-    moves = [
-        pltpu.make_async_copy(map_far, maps, arrive.at[0]),
-        pltpu.make_async_copy(load_far, load, arrive.at[1]),
-        pltpu.make_async_copy(motion_far, motion, arrive.at[2]),
-    ]
-    for move in moves:
-        move.start()
-    moves[0].wait()
-    split = map_of_blocks(maps, blocks)
-    moves[1].wait()
-    panels[...] = sum(dot(split[b], load[b], (1, 1)) for b in range(blocks)).astype(BF16)
-    outs = [pltpu.make_async_copy(panels, load_out.at[j], leave.at[j]) for j in range(load_out.shape[0])]
-    for out in outs:
-        out.start()
-    moves[2].wait()
-    motion_out[...] = sum(dot(split[b], motion[b], (1, 1)) for b in range(blocks)).astype(BF16)
-    for out in outs:
-        out.wait()
-
-
 def edges(rows, cols, me):
     even = 1 - me % 2
     sides = []
@@ -107,45 +85,62 @@
     return sides
 
 
-def edges_kernel(rows, cols, spot, joints, panels, motion_far, load_far, coupling_far, *refs):
-    outs, (load, coupling, terms, arrive, pass_by, leave) = refs[:4], refs[4:]
-    wide = load.shape[1]
+def send_kernel(rows, cols, spot, joints, motion_far, load_far, coupling_far, map_far, *refs):
+    load_out, motion_out, outs, refs = refs[0], refs[1], refs[2:6], refs[6:]
+    motion, load, coupling, maps, motion_panels, load_panels, terms, arrive, pass_by, leave = refs
+    blocks, wide, unknowns = motion.shape
     sides = edges(rows, cols, spot[0])
     spots = [(o, k) + place for o, side in enumerate(sides) for k, place in enumerate(side)]
-    fetch = [pltpu.make_async_copy(load_far, load, arrive.at[len(spots)])]
+    fetch = [
+        pltpu.make_async_copy(map_far, maps, arrive.at[0]),
+        pltpu.make_async_copy(load_far, load, arrive.at[1]),
+        pltpu.make_async_copy(motion_far, motion, arrive.at[2]),
+    ]
     for i, (o, k, x, y, d) in enumerate(spots):
-        fetch.append(pltpu.make_async_copy(coupling_far.at[x * cols + y, d + 1], coupling.at[i], arrive.at[i]))
+        fetch.append(pltpu.make_async_copy(coupling_far.at[x * cols + y, d + 1], coupling.at[i], arrive.at[i + 3]))
     for move in fetch:
         move.start()
-    direct = []
+    fetch[0].wait()
+    split = map_of_blocks(maps, blocks)
+    fetch[1].wait()
+    load_panels[...] = sum(dot(split[b], load[b], (1, 1)) for b in range(blocks)).astype(BF16)
+    sent = [pltpu.make_async_copy(load_panels, load_out.at[j], leave.at[j]) for j in range(load_out.shape[0])]
+    for move in sent:
+        move.start()
+    fetch[2].wait()
     for i, (o, k, x, y, d) in enumerate(spots):
         there = outs[o].at[pl.ds(k * wide, wide)]
-        direct.append(pltpu.make_async_copy(motion_far.at[x * cols + y], there, pass_by.at[i]))
-    size = panels.shape[0]
+        move = pltpu.make_async_copy(motion.at[x * cols + y], there, pass_by.at[i])
+        move.start()
+        sent.append(move)
+    motion_panels[...] = sum(dot(split[b], motion[b], (1, 1)) for b in range(blocks)).astype(BF16)
+    size, i = motion_panels.shape[0], len(spots)
+    move = pltpu.make_async_copy(motion_panels, motion_out, pass_by.at[i])
+    move.start()
+    sent.append(move)
     for o in range(2):
-        for h in range(wide // load.shape[2]):
-            i = len(direct)
+        for h in range(wide // unknowns):
+            i += 1
             there = outs[o].at[pl.ds(2 * len(sides[o]) * wide + h * size, size)]
-            here = panels.at[:, pl.ds(h * load.shape[2], load.shape[2])]
-            direct.append(pltpu.make_async_copy(here, there, pass_by.at[i]))
-    for move in direct:
-        move.start()
-    fetch[0].wait()
-    final = []
+            move = pltpu.make_async_copy(motion_panels.at[:, pl.ds(h * unknowns, unknowns)], there, pass_by.at[i])
+            move.start()
+            sent.append(move)
     for i, (o, k, x, y, d) in enumerate(spots):
-        fetch[i + 1].wait()
+        fetch[i + 3].wait()
         link = joints[x, y, d].astype(F32)
         term = joined(adjoint_parts(coupling[i], load[x * cols + y]), -1)
         terms[i] = (link * term).astype(BF16)
         there = outs[o].at[pl.ds((len(sides[o]) + k) * wide, wide)]
-        final.append(pltpu.make_async_copy(terms.at[i], there, leave.at[i]))
-        final[-1].start()
-    for move in direct + final:
+        move = pltpu.make_async_copy(terms.at[i], there, leave.at[load_out.shape[0] + i])
+        move.start()
+        sent.append(move)
+    for move in sent:
         move.wait()
 
 
 def hydro_kernel(n_gx, spot, hydro_ref, loads_ref, *refs):
     pieces, (pressure_out, *reaction_outs, gathered, pressures, reacted, leave) = refs[:n_gx], refs[n_gx:]
+    outs = [pltpu.make_async_copy(pressures, pressure_out, leave.at[0])]
     me = spot[0]
     panels, wide = pieces[0].shape
     for step in range(n_gx):
@@ -163,16 +158,17 @@
     both = dot(hydro.reshape(2 * size, depth), gathered[...], (1, 0))
     pressure = both[:size] + times_i(both[size:], 1)
     pressures[...] = pressure.astype(BF16).reshape(pressures.shape)
-    out = pltpu.make_async_copy(pressures, pressure_out, leave)
-    out.start()
+    outs[0].start()
     loads = loads_ref[...].reshape(size, -1)
     real = dot(hydro[0], loads, (0, 0))
     imag = dot(hydro[1], loads, (0, 0))
     reacted[...] = real - times_i(imag, 1)
     for step in range(n_gx):
         start = pl.multiple_of(target(me, step, n_gx) * panels, panels)
-        reaction_outs[step][...] = reacted[pl.ds(start, panels), :]
-    out.wait()
+        outs.append(pltpu.make_async_copy(reacted.at[pl.ds(start, panels)], reaction_outs[step], leave.at[step + 1]))
+        outs[-1].start()
+    for out in outs:
+        out.wait()
 
 
 def local_kernel(rows, cols, n_gx, spot, joints, motion, load, excitation, coupling, *refs):
@@ -242,7 +238,10 @@
     return jax.ShapeDtypeStruct(shape, dtype)
 
 
-PARAMS = pltpu.CompilerParams(vmem_limit_bytes=40 * 1024 * 1024)
+def params(mebibytes):
+    return pltpu.CompilerParams(vmem_limit_bytes=mebibytes * 1024 * 1024)
+
+
 DMA = pltpu.SemaphoreType.DMA
 
 
@@ -261,45 +260,32 @@
     block_flops = 2 * wide * unknowns * unknowns * 2
     field = (blocks, wide, unknowns)
 
-    motion_panels, load_copies = pl.pallas_call(
-        panels_kernel,
-        name="panels",
-        out_shape=[shaped(BF16, panels, wide), shaped(BF16, n_gy, panels, wide)],
-        in_specs=[FAR] * 3,
-        out_specs=[WHOLE, FAR],
+    counts = [cols, cols, rows, rows]
+    extra = panels * wide // unknowns
+    lengths = [2 * c * wide + (extra if o < 2 else 0) for o, c in enumerate(counts)]
+    load_copies, motion_panels, *payloads = pl.pallas_call(
+        functools.partial(send_kernel, rows, cols),
+        name="send",
+        out_shape=[shaped(BF16, n_gy, panels, wide), shaped(BF16, panels, wide)]
+        + [shaped(BF16, length, unknowns) for length in lengths],
+        in_specs=[SCALARS, SCALARS] + [FAR] * 4,
+        out_specs=[FAR] * 6,
         scratch_shapes=[
             pltpu.VMEM(field, BF16),
             pltpu.VMEM(field, BF16),
+            pltpu.VMEM((sum(counts), 2, unknowns, unknowns), BF16),
             pltpu.VMEM(panel_map.shape, BF16),
             pltpu.VMEM((panels, wide), BF16),
-            DMA((3,)),
-            DMA((n_gy,)),
+            pltpu.VMEM((panels, wide), BF16),
+            pltpu.VMEM((sum(counts), wide, unknowns), BF16),
+            DMA((sum(counts) + 3,)),
+            DMA((sum(counts) + 1 + 2 * (wide // unknowns),)),
+            DMA((n_gy + sum(counts),)),
         ],
-        compiler_params=PARAMS,
-        cost_estimate=cost(4 * blocks * wide * unknowns * panels, 4 * blocks * wide * unknowns),
-    )(motion, load, panel_map)
+        compiler_params=params(60),
+        cost_estimate=cost(sum(counts) * block_flops, 4 * blocks * wide * unknowns + 20 * blocks * unknowns**2),
+    )(spot, joints, motion, load, coupling, panel_map)
     loads = lax.all_to_all(load_copies, "gy", 0, 0, tiled=True)
-
-    counts = [cols, cols, rows, rows]
-    extra = panels * wide // unknowns
-    lengths = [2 * c * wide + (extra if o < 2 else 0) for o, c in enumerate(counts)]
-    payloads = pl.pallas_call(
-        functools.partial(edges_kernel, rows, cols),
-        name="edges",
-        out_shape=[shaped(BF16, length, unknowns) for length in lengths],
-        in_specs=[SCALARS, SCALARS, WHOLE] + [FAR] * 3,
-        out_specs=[FAR] * 4,
-        scratch_shapes=[
-            pltpu.VMEM(field, BF16),
-            pltpu.VMEM((sum(counts), 2, unknowns, unknowns), BF16),
-            pltpu.VMEM((sum(counts), wide, unknowns), BF16),
-            DMA((sum(counts) + 1,)),
-            DMA((sum(counts) + 2 * (wide // unknowns),)),
-            DMA((sum(counts),)),
-        ],
-        compiler_params=PARAMS,
-        cost_estimate=cost(sum(counts) * block_flops, 4 * blocks * wide * unknowns + 20 * blocks * unknowns**2),
-    )(spot, joints, motion_panels, motion, load, coupling)
     first, second = exchange(payloads[0], 1), exchange(payloads[1], 2)
     pieces = [motion_panels, first, second] + [exchange(motion_panels, step) for step in range(3, n_gx)]
     before = lax.ppermute(payloads[3], "gy", [(i, i + 1) for i in range(n_gy - 1)])
@@ -310,14 +296,14 @@
         name="hydro",
         out_shape=[shaped(BF16, n_gy, panels, wide)] + [shaped(F32, panels, wide)] * n_gx,
         in_specs=[SCALARS] + [WHOLE] * (2 + n_gx),
-        out_specs=[FAR] + [WHOLE] * n_gx,
+        out_specs=[FAR] * (1 + n_gx),
         scratch_shapes=[
             pltpu.VMEM((n_gx * panels, wide), BF16),
             pltpu.VMEM((n_gy, panels, wide), BF16),
             pltpu.VMEM((n_gx * panels, wide), F32),
-            DMA,
+            DMA((n_gx + 1,)),
         ],
-        compiler_params=PARAMS,
+        compiler_params=params(16),
         cost_estimate=cost(4 * hydro.size * wide, 2 * hydro.size),
     )(spot, hydro, loads, *pieces)
     pressures = lax.all_to_all(pressure_parts, "gy", 0, 0, tiled=True)
@@ -329,7 +315,7 @@
         out_shape=[shaped(F32, *field)] * 3,
         in_specs=[SCALARS] * 2 + [WHOLE] * 8,
         out_specs=[WHOLE] * 3,
-        compiler_params=PARAMS,
+        compiler_params=params(16),
         cost_estimate=cost(10 * blocks * block_flops, 20 * blocks * unknowns**2 + 20 * blocks * wide * unknowns),
     )(spot, joints, motion, load, force, coupling, first, second, before, after)
 
@@ -339,7 +325,7 @@
         out_shape=[shaped(F32, *field), shaped(F32, *field), shaped(F32, rows, cols)],
         in_specs=[WHOLE] * (5 + n_gx),
         out_specs=[WHOLE, WHOLE, SCALARS],
-        compiler_params=PARAMS,
+        compiler_params=params(16),
         cost_estimate=cost(4 * blocks * wide * unknowns * panels, 20 * blocks * wide * unknowns),
     )(panel_map, residual, multiplier, own, pressures, *reactions)
     shape = plate_motion.shape

time: 51.5 us -> 46.8 us (0.909)
  local copies, waits for them, and re-layouts: 13.5 us -> 8.97 us
    unnamed x46 -> x34, local copies, waits for them, and re-layouts: 13.5 us -> 8.97 us
    pallas_call x2 -> x1, Pallas kernels: 5.35 us -> 4.95 us  [on_device(): pl.pallas_call(functools.partial(send_kernel, rows, cols), name='send', o...]
  transfers between devices with their start and end apart: 10 -> 10, of which waited for: 1 -> 1; matrix products, arithmetic and copies ran while one was open for 0% -> 0% of each run, Pallas kernels for 6% -> 7%
where the time goes in v2:
time: 46.8 us; the launch traced here: 46.2 us
  starting transfers between devices  23.5 us (50%)
  Pallas kernels  9.41 us (20%)
  local copies, waits for them, and re-layouts  8.97 us (19%)
  waiting for transfers between devices  3.44 us (7%)
  between operations  0.81 us (2%)
    unnamed x34, local copies, waits for them, and re-layouts  8.97 us
    all_to_all x1, starting transfers between devices, on_device(): pressures = lax.all_to_all(pressure_parts, 'gy', 0, 0, tiled=True)  6.62 us
    ppermute x6, starting transfers between devices, exchange(): return lax.ppermute(x, 'gx', [(i, target(i, step, n)) for i in range(n)])  5.87 us
    all_to_all x1, starting transfers between devices, on_device(): loads = lax.all_to_all(load_copies, 'gy', 0, 0, tiled=True)  5.83 us
    pallas_call x1, Pallas kernels, on_device(): pl.pallas_call(functools.partial(send_kernel, rows, cols), name='send', o...  4.95 us
    ppermute x1, starting transfers between devices, on_device(): lax.ppermute(payloads[3], 'gy', [(i, i + 1) for i in range(n_gy - 1)])  3.93 us
    ppermute x6, waiting for transfers between devices, exchange(): return lax.ppermute(x, 'gx', [(i, target(i, step, n)) for i in range(n)])  3.43 us
    pallas_call x1, Pallas kernels, on_device(): pl.pallas_call(functools.partial(local_kernel, rows, cols, n_gx), name='l...  1.96 us
  transfers between devices with their start and end apart: 10, of which 1 were waited for; matrix products, arithmetic and copies ran while one was open for 0% of the time, Pallas kernels for 7%

profile of v2, /device:TPU:0, one launch (start us, length us, event | category | flops | bytes accessed | tf_op | source)
XLA Modules:
  0.0 46.2 jit_solution(5163473522081340503)
XLA Ops:
  0.6 0.0 copy-start.13
  0.6 0.0 copy-start
  0.7 0.0 copy-start.1
  0.7 0.0 copy-start.2
  0.7 0.0 copy-start.7
  0.7 4.9 %send.1 = (bf16[8,32,256]{2,1,0:T(8,128)(2,1)}, bf16[32,256]{1,0:T(8,128)(2,1)}, bf16[1088,128]{1,0:T(8,128)(2,1)}, bf16[1088,128]{1,0:T(8,128)(2,1)}, bf16[1024...) custom-call(s32[1]{0:T(128)} %bitcast.1.spot, s32[2,2,4]{2,1,0:T(2,128)} %joints.3, bf16[4,256,128]{2,1,0:T(8,128)(2,1)} %bitcast.10, ...), custom_call_target="tpu_custom_call" | custom-call | flops 134217728 | bytes 1835008 | tf_op jit(solution)/shard_map/send/pallas_call | solution.py:266
  5.6 0.5 %collective-permute-start = (bf16[1088,128]{1,0:T(8,128)(2,1)}, bf16[1088,128]{1,0:T(8,128)(2,1)S(1)}, u32[]{:S(2)}, u32[]{:S(2)}) collective-permute-start(bf16[1088,128]{1,0:T(8,128)(2,1)} %get-tuple-element.20), channel_id=1, source_target_pairs={{0,8},{8,0},{16,24},{24,16},{1,9},{9,1},{17,25},{25,17},{2,10},{10... | collective-permute-start | bytes 835592 | tf_op jit(solution)/shard_map/ppermute | solution.py:75
  6.2 2.6 %collective-permute-start.1 = (bf16[1088,128]{1,0:T(8,128)(2,1)}, bf16[1088,128]{1,0:T(8,128)(2,1)S(1)}, u32[]{:S(2)}, u32[]{:S(2)}) collective-permute-start(bf16[1088,128]{1,0:T(8,128)(2,1)} %get-tuple-element.21), channel_id=1, source_target_pairs={{0,24},{8,16},{16,8},{24,0},{1,25},{9,17},{17,9},{25,1},{2,26},{10... | collective-permute-start | bytes 835592 | tf_op jit(solution)/shard_map/ppermute | solution.py:75
  8.8 5.8 %all-to-all-start = ((bf16[8,32,256]{2,1,0:T(8,128)(2,1)}), bf16[8,32,256]{2,1,0:T(8,128)(2,1)S(1)}, u32[]{:S(2)}, u32[]{:S(2)}) async-start(bf16[8,32,256]{2,1,0:T(8,128)(2,1)} %get-tuple-element.27), calls=%async_computation | async-start | bytes 262144 | tf_op jit(solution)/shard_map/all_to_all | solution.py:288
  14.6 3.9 %collective-permute-start.2 = (bf16[1024,128]{1,0:T(8,128)(2,1)}, bf16[1024,128]{1,0:T(8,128)(2,1)S(1)}, u32[]{:S(2)}, u32[]{:S(2)}) collective-permute-start(bf16[1024,128]{1,0:T(8,128)(2,1)} %get-tuple-element.22), channel_id=1, source_target_pairs={{0,1},{1,2},{2,3},{3,4},{4,5},{5,6},{6,7},{8,9},{9,10},{10,11},{11... | collective-permute-start | bytes 786440 | tf_op jit(solution)/shard_map/ppermute | solution.py:291
  18.5 1.3 %collective-permute-start.3 = (bf16[1024,128]{1,0:T(8,128)(2,1)}, bf16[1024,128]{1,0:T(8,128)(2,1)S(1)}, u32[]{:S(2)}, u32[]{:S(2)}) collective-permute-start(bf16[1024,128]{1,0:T(8,128)(2,1)} %get-tuple-element.23), channel_id=1, source_target_pairs={{1,0},{2,1},{3,2},{4,3},{5,4},{6,5},{7,6},{9,8},{10,9},{11,10},{12... | collective-permute-start | bytes 786440 | tf_op jit(solution)/shard_map/ppermute | solution.py:292
  19.8 0.6 %collective-permute-start.4 = (bf16[32,256]{1,0:T(8,128)(2,1)}, bf16[32,256]{1,0:T(8,128)(2,1)S(1)}, u32[]{:S(2)}, u32[]{:S(2)}) collective-permute-start(bf16[32,256]{1,0:T(8,128)(2,1)} %get-tuple-element.28.refs_0_), channel_id=1, source_target_pairs={{0,16},{8,24},{16,0},{24,8},{1,17},{9,25},{17,1},{25,9},{2,18},{10... | collective-permute-start | bytes 49160 | tf_op jit(solution)/shard_map/ppermute | solution.py:75
  20.5 3.4 %collective-permute-done.4.refs_3_ = bf16[32,256]{1,0:T(8,128)(2,1)S(1)} collective-permute-done((bf16[32,256]{1,0:T(8,128)(2,1)}, bf16[32,256]{1,0:T(8,128)(2,1)S(1)}, u32[]{:S(2)}, u32[]{:S(2)}) %collective-permute-start.4) | collective-permute-done | bytes 16416 | tf_op jit(solution)/shard_map/ppermute | solution.py:75
  23.9 0.0 all-to-all-done.loads_ref
  23.9 0.0 collective-permute-done.refs_0_.refs_1_
  23.9 0.0 collective-permute-done.1.refs_1_.refs_2_
  23.9 0.0 copy-done.13
  23.9 0.0 copy-start.14
  23.9 0.7 %copy-done.14 = bf16[32,256]{1,0:T(8,128)(2,1)S(1)} copy-done((bf16[32,256]{1,0:T(8,128)(2,1)S(1)}, bf16[32,256]{1,0:T(8,128)(2,1)}, u32[]{:S(2)}) %copy-start.14) | copy-done | bytes 16408
  24.6 1.1 %hydro.1 = (bf16[8,32,256]{2,1,0:T(8,128)(2,1)}, f32[32,256]{1,0:T(8,128)S(1)}, f32[32,256]{1,0:T(8,128)S(1)}, f32[32,256]{1,0:T(8,128)S(1)}, f32[32,256]{1,0:T(8,128)S(1)}) custom-call(s32[1]{0:T(128)} %bitcast.1.spot, bf16[2,256,128]{2,1,0:T(8,128)(2,1)S(1)} %copy-done.13, bf16[8,32,256]{2,1,0:T(8,128)(2,1)S(1)} %all-to-all-done.loads_ref, ...), custom_call_target="tpu_custom_call" | custom-call | flops 67108864 | bytes 131072 | tf_op jit(solution)/shard_map/hydro/pallas_call | solution.py:294
  25.7 0.0 copy-start.16
  25.7 0.6 %copy-done.16 = f32[32,256]{1,0:T(8,128)} copy-done((f32[32,256]{1,0:T(8,128)}, f32[32,256]{1,0:T(8,128)S(1)}, u32[]{:S(2)}) %copy-start.16) | copy-done | bytes 32792
  26.3 6.6 %all-to-all-start.1 = ((bf16[8,32,256]{2,1,0:T(8,128)(2,1)}), bf16[8,32,256]{2,1,0:T(8,128)(2,1)S(1)}, u32[]{:S(2)}, u32[]{:S(2)}) async-start(bf16[8,32,256]{2,1,0:T(8,128)(2,1)} %get-tuple-element.29), calls=%async_computation.1 | async-start | bytes 262144 | tf_op jit(solution)/shard_map/all_to_all | solution.py:309
  33.0 0.0 collective-permute-start.5
  33.0 0.6 %collective-permute-start.6 = (f32[32,256]{1,0:T(8,128)S(1)}, f32[32,256]{1,0:T(8,128)S(1)}, u32[]{:S(2)}, u32[]{:S(2)}) collective-permute-start(f32[32,256]{1,0:T(8,128)S(1)} %get-tuple-element.32), channel_id=1, source_target_pairs={{0,24},{8,16},{16,8},{24,0},{1,25},{9,17},{17,9},{25,1},{2,26},{10... | collective-permute-start | bytes 98312 | tf_op jit(solution)/shard_map/ppermute | solution.py:75
  33.6 1.5 %collective-permute-start.7 = (f32[32,256]{1,0:T(8,128)S(1)}, f32[32,256]{1,0:T(8,128)S(1)}, u32[]{:S(2)}, u32[]{:S(2)}) collective-permute-start(f32[32,256]{1,0:T(8,128)S(1)} %get-tuple-element.33), channel_id=1, source_target_pairs={{0,16},{8,24},{16,0},{24,8},{1,17},{9,25},{17,1},{25,9},{2,18},{10... | collective-permute-start | bytes 98312 | tf_op jit(solution)/shard_map/ppermute | solution.py:75
  35.1 0.0 collective-permute-done.2.refs_2_
  35.1 0.7 %copy-done.8 = bf16[1024,128]{1,0:T(8,128)(2,1)} copy-done((bf16[1024,128]{1,0:T(8,128)(2,1)}, bf16[1024,128]{1,0:T(8,128)(2,1)S(1)}, u32[]{:S(2)}) %copy-start.8) | copy-done | bytes 262168
  35.8 0.0 collective-permute-done.3.refs_3_
  35.8 0.7 %copy-done.10 = bf16[1024,128]{1,0:T(8,128)(2,1)} copy-done((bf16[1024,128]{1,0:T(8,128)(2,1)}, bf16[1024,128]{1,0:T(8,128)(2,1)S(1)}, u32[]{:S(2)}) %copy-start.10) | copy-done | bytes 262168
  36.5 0.0 copy-done
  36.5 0.0 copy-done.1
  36.5 0.0 copy-done.2
  36.5 0.0 copy-start.9
  36.5 0.9 %copy-done.9 = bf16[1024,128]{1,0:T(8,128)(2,1)S(1)} copy-done((bf16[1024,128]{1,0:T(8,128)(2,1)S(1)}, bf16[1024,128]{1,0:T(8,128)(2,1)}, u32[]{:S(2)}) %copy-start.9) | copy-done | bytes 262168
  37.5 0.9 %copy-done.11 = bf16[1024,128]{1,0:T(8,128)(2,1)S(1)} copy-done((bf16[1024,128]{1,0:T(8,128)(2,1)S(1)}, bf16[1024,128]{1,0:T(8,128)(2,1)}, u32[]{:S(2)}) %copy-start.11) | copy-done | bytes 262168
  38.4 0.7 %copy-done.15 = s32[2,2,4]{2,1,0:T(2,128)S(1)} copy-done((s32[2,2,4]{2,1,0:T(2,128)S(1)}, s32[2,2,4]{2,1,0:T(2,128)}, u32[]{:S(2)}) %copy-start.15) | copy-done | bytes 88
  39.1 2.0 %local.1 = (f32[4,256,128]{2,1,0:T(8,128)S(1)}, f32[4,256,128]{2,1,0:T(8,128)S(1)}, f32[4,256,128]{2,1,0:T(8,128)S(1)}) custom-call(s32[1]{0:T(128)} %bitcast.1.spot, s32[2,2,4]{2,1,0:T(2,128)S(1)} %copy-done.15, bf16[4,256,128]{2,1,0:T(8,128)(2,1)S(1)} %bitcast.11, bf16[4,256,128]{2,1,0:T(8,128)(2,1)S(1)} %bitcast.13, bf16[4,256,128]{2,1,0:T(8,128)(2,1)S(1)} %bitcast.14, ...), custom_call_target="tpu_custom_call" | custom-call | flops 671088640 | bytes 3932160 | tf_op jit(solution)/shard_map/local/pallas_call | solution.py:312
  41.1 0.0 copy-start.3
  41.1 0.8 %copy-done.3 = f32[4,256,128]{2,1,0:T(8,128)} copy-done((f32[4,256,128]{2,1,0:T(8,128)}, f32[4,256,128]{2,1,0:T(8,128)S(1)}, u32[]{:S(2)}) %copy-start.3) | copy-done | bytes 524312
  41.9 0.8 %copy-done.5 = f32[4,256,128]{2,1,0:T(8,128)} copy-done((f32[4,256,128]{2,1,0:T(8,128)}, f32[4,256,128]{2,1,0:T(8,128)S(1)}, u32[]{:S(2)}) %copy-start.5) | copy-done | bytes 524312
  42.7 0.0 collective-permute-done.5.refs_1_
  42.7 0.0 collective-permute-done.6.refs_2_
  42.7 0.0 collective-permute-done.7.refs_3_
  42.7 0.0 all-to-all-done.1.pressures
  42.7 1.0 %copy-done.4 = f32[4,256,128]{2,1,0:T(8,128)S(1)} copy-done((f32[4,256,128]{2,1,0:T(8,128)S(1)}, f32[4,256,128]{2,1,0:T(8,128)}, u32[]{:S(2)}) %copy-start.4) | copy-done | bytes 524312
  43.8 1.0 %copy-done.6 = f32[4,256,128]{2,1,0:T(8,128)S(1)} copy-done((f32[4,256,128]{2,1,0:T(8,128)S(1)}, f32[4,256,128]{2,1,0:T(8,128)}, u32[]{:S(2)}) %copy-start.6) | copy-done | bytes 524312
  44.8 1.4 %final.1 = (f32[4,256,128]{2,1,0:T(8,128)}, f32[4,256,128]{2,1,0:T(8,128)}, f32[2,2]{1,0:T(2,128)}) custom-call(bf16[128,128]{1,0:T(8,128)(2,1)S(1)} %bitcast.16, f32[4,256,128]{2,1,0:T(8,128)S(1)} %get-tuple-element.24.residual, f32[4,256,128]{2,1,0:T(8,128)S(1)} %copy-done.4, f32[4,256,128]{2,1,0:T(8,128)S(1)} %copy-done.6, ...), custom_call_target="tpu_custom_call" | custom-call | flops 16777216 | bytes 2621440 | tf_op jit(solution)/shard_map/final/pallas_call | solution.py:322
  (10 shorter events, 0.0 us)
Async XLA Ops:
  0.6 23.2 %copy-start.13 = (bf16[2,256,128]{2,1,0:T(8,128)(2,1)S(1)}, bf16[2,256,128]{2,1,0:T(8,128)(2,1)}, u32[]{:S(2)}) copy-start(bf16[2,256,128]{2,1,0:T(8,128)(2,1)} %hydro_ref.1) | copy-start | bytes 393220
  0.6 35.9 %copy-start = (bf16[2,2,5,2,128,128]{5,4,3,2,1,0:T(8,128)(2,1)S(1)}, bf16[2,2,5,2,128,128]{5,4,3,2,1,0:T(8,128)(2,1)}, u32[]{:S(2)}) copy-start(bf16[2,2,5,2,128,128]{5,4,3,2,1,0:T(8,128)(2,1)} %param.10) | copy-start | bytes 3932164
  0.7 35.9 %copy-start.1 = (bf16[2,2,128,2,128]{4,3,2,1,0:T(2,128)(2,1)S(1)}, bf16[2,2,128,2,128]{4,3,2,1,0:T(2,128)(2,1)}, u32[]{:S(2)}) copy-start(bf16[2,2,128,2,128]{4,3,2,1,0:T(2,128)(2,1)} %param.7) | copy-start | bytes 786436
  0.7 35.9 %copy-start.2 = (bf16[2,2,128,2,128]{4,3,2,1,0:T(2,128)(2,1)S(1)}, bf16[2,2,128,2,128]{4,3,2,1,0:T(2,128)(2,1)}, u32[]{:S(2)}) copy-start(bf16[2,2,128,2,128]{4,3,2,1,0:T(2,128)(2,1)} %param.8) | copy-start | bytes 786436
  0.7 35.8 %copy-start.7 = (bf16[2,2,128,2,128]{4,3,2,1,0:T(2,128)(2,1)S(1)}, bf16[2,2,128,2,128]{4,3,2,1,0:T(2,128)(2,1)}, u32[]{:S(2)}) copy-start(bf16[2,2,128,2,128]{4,3,2,1,0:T(2,128)(2,1)} %param.9) | copy-start | bytes 786436
  5.6 18.2 %collective-permute-start = (bf16[1088,128]{1,0:T(8,128)(2,1)}, bf16[1088,128]{1,0:T(8,128)(2,1)S(1)}, u32[]{:S(2)}, u32[]{:S(2)}) collective-permute-start(bf16[1088,128]{1,0:T(8,128)(2,1)} %get-tuple-element.20), channel_id=1, source_target_pairs={{0,8},{8,0},{16,24},{24,16},{1,9},{9,1},{17,25},{25,17},{2,10},{10... | collective-permute-start | bytes 835592 | tf_op jit(solution)/shard_map/ppermute | solution.py:75
  6.2 17.7 %collective-permute-start.1 = (bf16[1088,128]{1,0:T(8,128)(2,1)}, bf16[1088,128]{1,0:T(8,128)(2,1)S(1)}, u32[]{:S(2)}, u32[]{:S(2)}) collective-permute-start(bf16[1088,128]{1,0:T(8,128)(2,1)} %get-tuple-element.21), channel_id=1, source_target_pairs={{0,24},{8,16},{16,8},{24,0},{1,25},{9,17},{17,9},{25,1},{2,26},{10... | collective-permute-start | bytes 835592 | tf_op jit(solution)/shard_map/ppermute | solution.py:75
  8.8 15.1 %all-to-all-start = ((bf16[8,32,256]{2,1,0:T(8,128)(2,1)}), bf16[8,32,256]{2,1,0:T(8,128)(2,1)S(1)}, u32[]{:S(2)}, u32[]{:S(2)}) async-start(bf16[8,32,256]{2,1,0:T(8,128)(2,1)} %get-tuple-element.27), calls=%async_computation | async-start | bytes 262144 | tf_op jit(solution)/shard_map/all_to_all | solution.py:288
  14.6 20.5 %collective-permute-start.2 = (bf16[1024,128]{1,0:T(8,128)(2,1)}, bf16[1024,128]{1,0:T(8,128)(2,1)S(1)}, u32[]{:S(2)}, u32[]{:S(2)}) collective-permute-start(bf16[1024,128]{1,0:T(8,128)(2,1)} %get-tuple-element.22), channel_id=1, source_target_pairs={{0,1},{1,2},{2,3},{3,4},{4,5},{5,6},{6,7},{8,9},{9,10},{10,11},{11... | collective-permute-start | bytes 786440 | tf_op jit(solution)/shard_map/ppermute | solution.py:291
  18.5 17.3 %collective-permute-start.3 = (bf16[1024,128]{1,0:T(8,128)(2,1)}, bf16[1024,128]{1,0:T(8,128)(2,1)S(1)}, u32[]{:S(2)}, u32[]{:S(2)}) collective-permute-start(bf16[1024,128]{1,0:T(8,128)(2,1)} %get-tuple-element.23), channel_id=1, source_target_pairs={{1,0},{2,1},{3,2},{4,3},{5,4},{6,5},{7,6},{9,8},{10,9},{11,10},{12... | collective-permute-start | bytes 786440 | tf_op jit(solution)/shard_map/ppermute | solution.py:292
  19.8 4.0 %collective-permute-start.4 = (bf16[32,256]{1,0:T(8,128)(2,1)}, bf16[32,256]{1,0:T(8,128)(2,1)S(1)}, u32[]{:S(2)}, u32[]{:S(2)}) collective-permute-start(bf16[32,256]{1,0:T(8,128)(2,1)} %get-tuple-element.28.refs_0_), channel_id=1, source_target_pairs={{0,16},{8,24},{16,0},{24,8},{1,17},{9,25},{17,1},{25,9},{2,18},{10... | collective-permute-start | bytes 49160 | tf_op jit(solution)/shard_map/ppermute | solution.py:75
  23.9 0.7 %copy-start.14 = (bf16[32,256]{1,0:T(8,128)(2,1)S(1)}, bf16[32,256]{1,0:T(8,128)(2,1)}, u32[]{:S(2)}) copy-start(bf16[32,256]{1,0:T(8,128)(2,1)} %get-tuple-element.28.refs_0_) | copy-start | bytes 49156
  25.7 0.6 %copy-start.16 = (f32[32,256]{1,0:T(8,128)}, f32[32,256]{1,0:T(8,128)S(1)}, u32[]{:S(2)}) copy-start(f32[32,256]{1,0:T(8,128)S(1)} %get-tuple-element.31) | copy-start | bytes 98308
  26.3 16.3 %all-to-all-start.1 = ((bf16[8,32,256]{2,1,0:T(8,128)(2,1)}), bf16[8,32,256]{2,1,0:T(8,128)(2,1)S(1)}, u32[]{:S(2)}, u32[]{:S(2)}) async-start(bf16[8,32,256]{2,1,0:T(8,128)(2,1)} %get-tuple-element.29), calls=%async_computation.1 | async-start | bytes 262144 | tf_op jit(solution)/shard_map/all_to_all | solution.py:309
  33.0 9.7 %collective-permute-start.5 = (f32[32,256]{1,0:T(8,128)}, f32[32,256]{1,0:T(8,128)S(1)}, u32[]{:S(2)}, u32[]{:S(2)}) collective-permute-start(f32[32,256]{1,0:T(8,128)} %copy-done.16), channel_id=1, source_target_pairs={{0,8},{8,0},{16,24},{24,16},{1,9},{9,1},{17,25},{25,17},{2,10},{10... | collective-permute-start | bytes 98312 | tf_op jit(solution)/shard_map/ppermute | solution.py:75
  33.0 9.7 %collective-permute-start.6 = (f32[32,256]{1,0:T(8,128)S(1)}, f32[32,256]{1,0:T(8,128)S(1)}, u32[]{:S(2)}, u32[]{:S(2)}) collective-permute-start(f32[32,256]{1,0:T(8,128)S(1)} %get-tuple-element.32), channel_id=1, source_target_pairs={{0,24},{8,16},{16,8},{24,0},{1,25},{9,17},{17,9},{25,1},{2,26},{10... | collective-permute-start | bytes 98312 | tf_op jit(solution)/shard_map/ppermute | solution.py:75
  33.6 9.1 %collective-permute-start.7 = (f32[32,256]{1,0:T(8,128)S(1)}, f32[32,256]{1,0:T(8,128)S(1)}, u32[]{:S(2)}, u32[]{:S(2)}) collective-permute-start(f32[32,256]{1,0:T(8,128)S(1)} %get-tuple-element.33), channel_id=1, source_target_pairs={{0,16},{8,24},{16,0},{24,8},{1,17},{9,25},{17,1},{25,9},{2,18},{10... | collective-permute-start | bytes 98312 | tf_op jit(solution)/shard_map/ppermute | solution.py:75
  35.1 0.7 %copy-start.8 = (bf16[1024,128]{1,0:T(8,128)(2,1)}, bf16[1024,128]{1,0:T(8,128)(2,1)S(1)}, u32[]{:S(2)}) copy-start(bf16[1024,128]{1,0:T(8,128)(2,1)S(1)} %collective-permute-done.2.refs_2_) | copy-start | bytes 786436
  35.8 0.7 %copy-start.10 = (bf16[1024,128]{1,0:T(8,128)(2,1)}, bf16[1024,128]{1,0:T(8,128)(2,1)S(1)}, u32[]{:S(2)}) copy-start(bf16[1024,128]{1,0:T(8,128)(2,1)S(1)} %collective-permute-done.3.refs_3_) | copy-start | bytes 786436
  36.5 1.0 %copy-start.9 = (bf16[1024,128]{1,0:T(8,128)(2,1)S(1)}, bf16[1024,128]{1,0:T(8,128)(2,1)}, u32[]{:S(2)}) copy-start(bf16[1024,128]{1,0:T(8,128)(2,1)} %copy-done.8) | copy-start | bytes 786436
  37.5 0.9 %copy-start.11 = (bf16[1024,128]{1,0:T(8,128)(2,1)S(1)}, bf16[1024,128]{1,0:T(8,128)(2,1)}, u32[]{:S(2)}) copy-start(bf16[1024,128]{1,0:T(8,128)(2,1)} %copy-done.10) | copy-start | bytes 786436
  38.4 0.7 %copy-start.15 = (s32[2,2,4]{2,1,0:T(2,128)S(1)}, s32[2,2,4]{2,1,0:T(2,128)}, u32[]{:S(2)}) copy-start(s32[2,2,4]{2,1,0:T(2,128)} %joints.3) | copy-start | bytes 196
  39.1 3.6 %copy-start.12 = (bf16[32,2,2,128]{3,2,1,0:T(2,128)(2,1)S(1)}, bf16[32,2,2,128]{3,2,1,0:T(2,128)(2,1)}, u32[]{:S(2)}) copy-start(bf16[32,2,2,128]{3,2,1,0:T(2,128)(2,1)} %param.13) | copy-start | bytes 98308
  41.1 0.8 %copy-start.3 = (f32[4,256,128]{2,1,0:T(8,128)}, f32[4,256,128]{2,1,0:T(8,128)S(1)}, u32[]{:S(2)}) copy-start(f32[4,256,128]{2,1,0:T(8,128)S(1)} %get-tuple-element.25.multiplier) | copy-start | bytes 1572868
  41.9 0.8 %copy-start.5 = (f32[4,256,128]{2,1,0:T(8,128)}, f32[4,256,128]{2,1,0:T(8,128)S(1)}, u32[]{:S(2)}) copy-start(f32[4,256,128]{2,1,0:T(8,128)S(1)} %get-tuple-element.26.own) | copy-start | bytes 1572868
  42.7 1.0 %copy-start.4 = (f32[4,256,128]{2,1,0:T(8,128)S(1)}, f32[4,256,128]{2,1,0:T(8,128)}, u32[]{:S(2)}) copy-start(f32[4,256,128]{2,1,0:T(8,128)} %copy-done.3) | copy-start | bytes 1572868
  43.8 1.0 %copy-start.6 = (f32[4,256,128]{2,1,0:T(8,128)S(1)}, f32[4,256,128]{2,1,0:T(8,128)}, u32[]{:S(2)}) copy-start(f32[4,256,128]{2,1,0:T(8,128)} %copy-done.5) | copy-start | bytes 1572868

commit v3 on v2

--- a/solution.py
+++ b/solution.py
@@ -70,26 +70,37 @@
     return target(i, step, n) if step < 3 else (i + n + 1 - step) % n
 
 
-def exchange(x, step):
-    n = lax.axis_size("gx")
-    return lax.ppermute(x, "gx", [(i, target(i, step, n)) for i in range(n)])
-
-
-def edges(rows, cols, me):
-    even = 1 - me % 2
+def exchange(x, step, axis="gx", wrap=True):
+    n = lax.axis_size(axis)
+    pairs = [(i, target(i, step, n)) for i in range(n)]
+    return lax.ppermute(x, axis, [(i, j) for i, j in pairs if wrap or abs(i - j) < n - 1 or n == 2])
+
+
+def near(x):
+    return pltpu.with_memory_space_constraint(x, pltpu.VMEM)
+
+
+def far(x):
+    return pltpu.with_memory_space_constraint(x, pltpu.HBM)
+
+
+def edges(rows, cols, spot):
     sides = []
-    for d in (even, 1 - even):
-        sides.append([(d * (rows - 1), y, d) for y in range(cols)])
-    for d in (2, 3):
-        sides.append([(x, (d - 2) * (cols - 1), d) for x in range(rows)])
+    for axis in range(2):
+        even = 1 - spot[axis] % 2
+        for up in (even, 1 - even):
+            if axis == 0:
+                sides.append([(up * (rows - 1), y, up) for y in range(cols)])
+            else:
+                sides.append([(x, up * (cols - 1), 2 + up) for x in range(rows)])
     return sides
 
 
 def send_kernel(rows, cols, spot, joints, motion_far, load_far, coupling_far, map_far, *refs):
     load_out, motion_out, outs, refs = refs[0], refs[1], refs[2:6], refs[6:]
-    motion, load, coupling, maps, motion_panels, load_panels, terms, arrive, pass_by, leave = refs
+    motion, load, coupling, maps, load_panels, arrive, leave = refs
     blocks, wide, unknowns = motion.shape
-    sides = edges(rows, cols, spot[0])
+    sides = edges(rows, cols, spot)
     spots = [(o, k) + place for o, side in enumerate(sides) for k, place in enumerate(side)]
     fetch = [
         pltpu.make_async_copy(map_far, maps, arrive.at[0]),
@@ -108,39 +119,25 @@
     for move in sent:
         move.start()
     fetch[2].wait()
-    for i, (o, k, x, y, d) in enumerate(spots):
-        there = outs[o].at[pl.ds(k * wide, wide)]
-        move = pltpu.make_async_copy(motion.at[x * cols + y], there, pass_by.at[i])
-        move.start()
-        sent.append(move)
-    motion_panels[...] = sum(dot(split[b], motion[b], (1, 1)) for b in range(blocks)).astype(BF16)
-    size, i = motion_panels.shape[0], len(spots)
-    move = pltpu.make_async_copy(motion_panels, motion_out, pass_by.at[i])
-    move.start()
-    sent.append(move)
+    panels = sum(dot(split[b], motion[b], (1, 1)) for b in range(blocks)).astype(BF16)
+    motion_out[...] = panels
     for o in range(2):
         for h in range(wide // unknowns):
-            i += 1
-            there = outs[o].at[pl.ds(2 * len(sides[o]) * wide + h * size, size)]
-            move = pltpu.make_async_copy(motion_panels.at[:, pl.ds(h * unknowns, unknowns)], there, pass_by.at[i])
-            move.start()
-            sent.append(move)
+            top = 2 * len(sides[o]) * wide + h * panels.shape[0]
+            outs[o][pl.ds(top, panels.shape[0]), :] = panels[:, h * unknowns : (h + 1) * unknowns]
     for i, (o, k, x, y, d) in enumerate(spots):
+        outs[o][pl.ds(k * wide, wide), :] = motion[x * cols + y]
         fetch[i + 3].wait()
         link = joints[x, y, d].astype(F32)
         term = joined(adjoint_parts(coupling[i], load[x * cols + y]), -1)
-        terms[i] = (link * term).astype(BF16)
-        there = outs[o].at[pl.ds((len(sides[o]) + k) * wide, wide)]
-        move = pltpu.make_async_copy(terms.at[i], there, leave.at[load_out.shape[0] + i])
-        move.start()
-        sent.append(move)
+        outs[o][pl.ds((len(sides[o]) + k) * wide, wide), :] = (link * term).astype(BF16)
     for move in sent:
         move.wait()
 
 
 def hydro_kernel(n_gx, spot, hydro_ref, loads_ref, *refs):
     pieces, (pressure_out, *reaction_outs, gathered, pressures, reacted, leave) = refs[:n_gx], refs[n_gx:]
-    outs = [pltpu.make_async_copy(pressures, pressure_out, leave.at[0])]
+    outs = [pltpu.make_async_copy(pressures, pressure_out, leave)]
     me = spot[0]
     panels, wide = pieces[0].shape
     for step in range(n_gx):
@@ -165,26 +162,37 @@
     reacted[...] = real - times_i(imag, 1)
     for step in range(n_gx):
         start = pl.multiple_of(target(me, step, n_gx) * panels, panels)
-        outs.append(pltpu.make_async_copy(reacted.at[pl.ds(start, panels)], reaction_outs[step], leave.at[step + 1]))
-        outs[-1].start()
-    for out in outs:
-        out.wait()
-
-
-def local_kernel(rows, cols, n_gx, spot, joints, motion, load, excitation, coupling, *refs):
-    first, second, before, after, residual_out, multiplier_out, own_out = refs
+        reaction_outs[step][...] = reacted[pl.ds(start, panels), :]
+    outs[0].wait()
+
+
+def local_kernel(rows, cols, sizes, spot, joints, motion_far, load_far, excitation_far, coupling_far, *refs):
+    received_refs, (residual_out, multiplier_out, own_out), refs = refs[:4], refs[4:7], refs[7:]
+    motion, load, excitation, coupling, arrive = refs
+    moves = [
+        pltpu.make_async_copy(motion_far, motion, arrive.at[0]),
+        pltpu.make_async_copy(load_far, load, arrive.at[1]),
+        pltpu.make_async_copy(coupling_far, coupling, arrive.at[2]),
+        pltpu.make_async_copy(excitation_far, excitation, arrive.at[3]),
+    ]
+    for move in moves:
+        move.start()
     wide = motion.shape[1]
-    me = spot[0]
-    even = me % 2 == 0
-    valid = [(me > 0).astype(F32), (me < n_gx - 1).astype(F32), 1.0, 1.0]
+    even = [spot[axis] % 2 == 0 for axis in range(2)]
+    valid = []
+    for axis in range(2):
+        valid += [(spot[axis] > 0).astype(F32), (spot[axis] < sizes[axis] - 1).astype(F32)]
 
     def received(d, k, kind):
         count = cols if d < 2 else rows
         here = pl.ds((kind * count + k) * wide, wide)
-        if d >= 2:
-            return (before if d == 2 else after)[here, :]
-        return jnp.where(even, (second if d == 0 else first)[here, :], (first if d == 0 else second)[here, :])
-
+        first, second = received_refs[d // 2 * 2], received_refs[d // 2 * 2 + 1]
+        if d % 2:
+            first, second = second, first
+        return jnp.where(even[d // 2], second[here, :], first[here, :])
+
+    for move in moves:
+        move.wait()
     for x in range(rows):
         for y in range(cols):
             b = x * cols + y
@@ -215,19 +223,25 @@
 
 
 def final_kernel(rows, cols, lift, map_ref, residual, multiplier, own, pressures, *refs):
-    reactions, (residual_out, multiplier_out, sensitivity_out) = refs[:-3], refs[-3:]
+    reactions, (residual_out, multiplier_out, sensitivity_out, full, leave) = refs[:-5], refs[-5:]
     blocks = rows * cols
     maps = map_of_blocks(map_ref, blocks)
     pressure = jnp.sum(pressures[...].astype(F32), axis=0).astype(BF16)
     reaction = sum(r[...].astype(F32) for r in reactions).astype(BF16)
     scale = 1.0 / math.sqrt(own.shape[1] // 2 * own.shape[2])
-    for x in range(rows):
-        for y in range(cols):
-            b = x * cols + y
-            residual_out[b] = residual[b] + lift * dot(pressure, maps[b], (0, 0))
-            full = multiplier[b] + lift * dot(reaction, maps[b], (0, 0))
-            multiplier_out[b] = full
-            sensitivity_out[x, y] = jnp.sum(full * own[b]) * scale
+    sent = []
+    for b in range(blocks):
+        full[0, b] = residual[b] + lift * dot(pressure, maps[b], (0, 0))
+        sent.append(pltpu.make_async_copy(full.at[0, b], residual_out.at[b], leave.at[0, b]))
+        sent[-1].start()
+    for b in range(blocks):
+        value = multiplier[b] + lift * dot(reaction, maps[b], (0, 0))
+        full[1, b] = value
+        sent.append(pltpu.make_async_copy(full.at[1, b], multiplier_out.at[b], leave.at[1, b]))
+        sent[-1].start()
+        sensitivity_out[b // cols, b % cols] = jnp.sum(value * own[b]) * scale
+    for move in sent:
+        move.wait()
 
 
 def cost(flops, bytes_accessed):
@@ -250,7 +264,7 @@
     panels = panel_map.shape[0]
     blocks, wide = rows * cols, 2 * cases
     n_gx, n_gy = lax.axis_size("gx"), lax.axis_size("gy")
-    spot = lax.axis_index("gx").reshape(1)
+    spot = jnp.stack([lax.axis_index("gx"), lax.axis_index("gy")])
     motion = plate_motion.reshape(blocks, wide, unknowns)
     load = adjoint_load.reshape(blocks, wide, unknowns)
     force = excitation.reshape(blocks, wide, unknowns)
@@ -266,42 +280,40 @@
     load_copies, motion_panels, *payloads = pl.pallas_call(
         functools.partial(send_kernel, rows, cols),
         name="send",
-        out_shape=[shaped(BF16, n_gy, panels, wide), shaped(BF16, panels, wide)]
-        + [shaped(BF16, length, unknowns) for length in lengths],
+        out_shape=[pltpu.HBM((n_gy, panels, wide), BF16), pltpu.VMEM((panels, wide), BF16)]
+        + [pltpu.VMEM((length, unknowns), BF16) for length in lengths],
         in_specs=[SCALARS, SCALARS] + [FAR] * 4,
-        out_specs=[FAR] * 6,
+        out_specs=[FAR] + [WHOLE] * 5,
         scratch_shapes=[
             pltpu.VMEM(field, BF16),
             pltpu.VMEM(field, BF16),
             pltpu.VMEM((sum(counts), 2, unknowns, unknowns), BF16),
             pltpu.VMEM(panel_map.shape, BF16),
             pltpu.VMEM((panels, wide), BF16),
-            pltpu.VMEM((panels, wide), BF16),
-            pltpu.VMEM((sum(counts), wide, unknowns), BF16),
             DMA((sum(counts) + 3,)),
-            DMA((sum(counts) + 1 + 2 * (wide // unknowns),)),
-            DMA((n_gy + sum(counts),)),
+            DMA((n_gy,)),
         ],
-        compiler_params=params(60),
+        compiler_params=params(16),
         cost_estimate=cost(sum(counts) * block_flops, 4 * blocks * wide * unknowns + 20 * blocks * unknowns**2),
-    )(spot, joints, motion, load, coupling, panel_map)
+    )(spot, joints, far(motion), far(load), far(coupling), far(panel_map))
     loads = lax.all_to_all(load_copies, "gy", 0, 0, tiled=True)
+    further = [exchange(motion_panels, step) for step in range(3, n_gx)]
+    (*payloads, further) = lax.optimization_barrier((*payloads, further))
     first, second = exchange(payloads[0], 1), exchange(payloads[1], 2)
-    pieces = [motion_panels, first, second] + [exchange(motion_panels, step) for step in range(3, n_gx)]
-    before = lax.ppermute(payloads[3], "gy", [(i, i + 1) for i in range(n_gy - 1)])
-    after = lax.ppermute(payloads[2], "gy", [(i + 1, i) for i in range(n_gy - 1)])
+    third, fourth = exchange(payloads[2], 1, "gy"), exchange(payloads[3], 2, "gy", wrap=False)
+    pieces = [motion_panels, first, second] + further
 
     pressure_parts, *reaction_parts = pl.pallas_call(
         functools.partial(hydro_kernel, n_gx),
         name="hydro",
-        out_shape=[shaped(BF16, n_gy, panels, wide)] + [shaped(F32, panels, wide)] * n_gx,
+        out_shape=[pltpu.HBM((n_gy, panels, wide), BF16)] + [pltpu.VMEM((panels, wide), F32)] * n_gx,
         in_specs=[SCALARS] + [WHOLE] * (2 + n_gx),
-        out_specs=[FAR] * (1 + n_gx),
+        out_specs=[FAR] + [WHOLE] * n_gx,
         scratch_shapes=[
             pltpu.VMEM((n_gx * panels, wide), BF16),
             pltpu.VMEM((n_gy, panels, wide), BF16),
             pltpu.VMEM((n_gx * panels, wide), F32),
-            DMA((n_gx + 1,)),
+            DMA,
         ],
         compiler_params=params(16),
         cost_estimate=cost(4 * hydro.size * wide, 2 * hydro.size),
@@ -310,21 +322,23 @@
     reactions = [reaction_parts[0]] + [exchange(reaction_parts[step], step) for step in range(1, n_gx)]
 
     residual, multiplier, own = pl.pallas_call(
-        functools.partial(local_kernel, rows, cols, n_gx),
+        functools.partial(local_kernel, rows, cols, (n_gx, n_gy)),
         name="local",
-        out_shape=[shaped(F32, *field)] * 3,
-        in_specs=[SCALARS] * 2 + [WHOLE] * 8,
+        out_shape=[pltpu.VMEM(field, F32)] * 3,
+        in_specs=[SCALARS] * 2 + [FAR] * 4 + [WHOLE] * 4,
         out_specs=[WHOLE] * 3,
+        scratch_shapes=[pltpu.VMEM(field, BF16)] * 3 + [pltpu.VMEM(coupling.shape, BF16), DMA((4,))],
         compiler_params=params(16),
         cost_estimate=cost(10 * blocks * block_flops, 20 * blocks * unknowns**2 + 20 * blocks * wide * unknowns),
-    )(spot, joints, motion, load, force, coupling, first, second, before, after)
+    )(spot, joints, far(motion), far(load), far(force), far(coupling), first, second, third, fourth)
 
     residual, multiplier, sensitivity = pl.pallas_call(
         functools.partial(final_kernel, rows, cols, lift),
         name="final",
-        out_shape=[shaped(F32, *field), shaped(F32, *field), shaped(F32, rows, cols)],
+        out_shape=[pltpu.HBM(field, F32), pltpu.HBM(field, F32), shaped(F32, rows, cols)],
         in_specs=[WHOLE] * (5 + n_gx),
-        out_specs=[WHOLE, WHOLE, SCALARS],
+        out_specs=[FAR, FAR, SCALARS],
+        scratch_shapes=[pltpu.VMEM((2,) + field, F32), DMA((2, blocks))],
         compiler_params=params(16),
         cost_estimate=cost(4 * blocks * wide * unknowns * panels, 20 * blocks * wide * unknowns),
     )(panel_map, residual, multiplier, own, pressures, *reactions)

time: 46.8 us -> 40.1 us (0.86)
  local copies, waits for them, and re-layouts: 8.97 us -> 0.7 us
  waiting for transfers between devices: 3.44 us -> 7.9 us
  starting transfers between devices: 23.5 us -> 19.3 us
  Pallas kernels: 9.41 us -> 11 us
    unnamed x34 -> x8, local copies, waits for them, and re-layouts: 8.97 us -> 0.7 us
    all_to_all x1, waiting for transfers between devices: 0.01 us -> 4.76 us  [on_device(): loads = lax.all_to_all(load_copies, 'gy', 0, 0, tiled=True)]
    all_to_all x1, starting transfers between devices: 6.62 us -> 3.38 us  [on_device(): pressures = lax.all_to_all(pressure_parts, 'gy', 0, 0, tiled=True)]
    ppermute x8, waiting for transfers between devices: 3.43 us -> 1.74 us  [exchange(): lax.ppermute(x, axis, [(i, j) for i, j in pairs if wrap or abs(i - j) < n...]
    pallas_call x1, Pallas kernels: 1.96 us -> 3.59 us  [on_device(): pl.pallas_call(functools.partial(local_kernel, rows, cols, (n_gx, n_gy)),...]
    all_to_all x1, waiting for transfers between devices: 0.01 us -> 1.4 us  [on_device(): pressures = lax.all_to_all(pressure_parts, 'gy', 0, 0, tiled=True)]
    ppermute x8, starting transfers between devices: 11.1 us -> 10 us  [exchange(): lax.ppermute(x, axis, [(i, j) for i, j in pairs if wrap or abs(i - j) < n...]
    pallas_call x1, Pallas kernels: 4.95 us -> 3.9 us  [on_device(): pl.pallas_call(functools.partial(send_kernel, rows, cols), name='send', o...]
  transfers between devices with their start and end apart: 10 -> 10, of which waited for: 1 -> 3; matrix products, arithmetic and copies ran while one was open for 0% -> 0% of each run, Pallas kernels for 7% -> 13%
where the time goes in v3:
time: 40.1 us; the launch traced here: 39.7 us
  starting transfers between devices  19.3 us (48%)
  Pallas kernels  11 us (27%)
  waiting for transfers between devices  7.9 us (20%)
  between operations  0.74 us (2%)
  local copies, waits for them, and re-layouts  0.7 us (2%)
    ppermute x8, starting transfers between devices, exchange(): lax.ppermute(x, axis, [(i, j) for i, j in pairs if wrap or abs(i - j) < n...  10 us
    all_to_all x1, starting transfers between devices, on_device(): loads = lax.all_to_all(load_copies, 'gy', 0, 0, tiled=True)  5.84 us
    all_to_all x1, waiting for transfers between devices, on_device(): loads = lax.all_to_all(load_copies, 'gy', 0, 0, tiled=True)  4.76 us
    pallas_call x1, Pallas kernels, on_device(): pl.pallas_call(functools.partial(send_kernel, rows, cols), name='send', o...  3.9 us
    pallas_call x1, Pallas kernels, on_device(): pl.pallas_call(functools.partial(local_kernel, rows, cols, (n_gx, n_gy)),...  3.59 us
    all_to_all x1, starting transfers between devices, on_device(): pressures = lax.all_to_all(pressure_parts, 'gy', 0, 0, tiled=True)  3.38 us
    pallas_call x1, Pallas kernels, on_device(): pl.pallas_call(functools.partial(final_kernel, rows, cols, lift), name='f...  1.9 us
    ppermute x8, waiting for transfers between devices, exchange(): lax.ppermute(x, axis, [(i, j) for i, j in pairs if wrap or abs(i - j) < n...  1.74 us
  transfers between devices with their start and end apart: 10, of which 3 were waited for; matrix products, arithmetic and copies ran while one was open for 0% of the time, Pallas kernels for 13%

profile of v3, /device:TPU:0, one launch (start us, length us, event | category | flops | bytes accessed | tf_op | source)
XLA Modules:
  0.0 39.7 jit_solution(11451559027056466750)
XLA Ops:
  0.6 0.0 copy-start.1
  0.6 0.1 pad_add_fusion.spot
  0.7 0.0 copy-start.2
  0.7 0.7 %copy-done.2 = s32[2,2,4]{2,1,0:T(2,128)S(1)} copy-done((s32[2,2,4]{2,1,0:T(2,128)S(1)}, s32[2,2,4]{2,1,0:T(2,128)}, u32[]{:S(2)}) %copy-start.2) | copy-done | bytes 88
  1.4 0.0 copy-start.3
  1.4 3.9 %send.1 = (bf16[8,32,256]{2,1,0:T(8,128)(2,1)}, bf16[32,256]{1,0:T(8,128)(2,1)S(1)}, bf16[1088,128]{1,0:T(8,128)(2,1)S(1)}, bf16[1088,128]{1,0:T(8,128)(2,1)S(1)...) custom-call(s32[2]{0:T(128)S(1)} %pad_add_fusion.spot, s32[2,2,4]{2,1,0:T(2,128)S(1)} %copy-done.2, ...), custom_call_target="tpu_custom_call" | custom-call | flops 134217728 | bytes 1835008 | tf_op jit(solution)/shard_map/send/pallas_call | solution.py:280
  5.3 3.0 %collective-permute-start = (bf16[32,256]{1,0:T(8,128)(2,1)S(1)}, bf16[32,256]{1,0:T(8,128)(2,1)S(1)}, u32[]{:S(2)}, u32[]{:S(2)}) collective-permute-start(bf16[32,256]{1,0:T(8,128)(2,1)S(1)} %get-tuple-element.29.refs_0_), channel_id=1, source_target_pairs={{0,16},{8,24},{16,0},{24,8},{1,17},{9,25},{17,1},{25,9},{2,18},{10... | collective-permute-start | bytes 49160 | tf_op jit(solution)/shard_map/ppermute | solution.py:76
  8.3 1.7 %collective-permute-done.refs_3_ = bf16[32,256]{1,0:T(8,128)(2,1)S(1)} collective-permute-done((bf16[32,256]{1,0:T(8,128)(2,1)S(1)}, bf16[32,256]{1,0:T(8,128)(2,1)S(1)}, u32[]{:S(2)}, u32[]{:S(2)}) %collective-permute-start) | collective-permute-done | bytes 16416 | tf_op jit(solution)/shard_map/ppermute | solution.py:76
  10.0 0.0 collective-permute-start.1
  10.0 2.1 %collective-permute-start.2 = (bf16[1088,128]{1,0:T(8,128)(2,1)S(1)}, bf16[1088,128]{1,0:T(8,128)(2,1)S(1)}, u32[]{:S(2)}, u32[]{:S(2)}) collective-permute-start(bf16[1088,128]{1,0:T(8,128)(2,1)S(1)} %get-tuple-element.31), channel_id=1, source_target_pairs={{0,24},{8,16},{16,8},{24,0},{1,25},{9,17},{17,9},{25,1},{2,26},{10... | collective-permute-start | bytes 835592 | tf_op jit(solution)/shard_map/ppermute | solution.py:76
  12.2 5.8 %all-to-all-start = ((bf16[8,32,256]{2,1,0:T(8,128)(2,1)}), bf16[8,32,256]{2,1,0:T(8,128)(2,1)S(1)}, u32[]{:S(2)}, u32[]{:S(2)}) async-start(bf16[8,32,256]{2,1,0:T(8,128)(2,1)} %get-tuple-element.37), calls=%async_computation | async-start | bytes 262144 | tf_op jit(solution)/shard_map/all_to_all | solution.py:299
  18.0 2.0 %collective-permute-start.3 = (bf16[1024,128]{1,0:T(8,128)(2,1)S(1)}, bf16[1024,128]{1,0:T(8,128)(2,1)S(1)}, u32[]{:S(2)}, u32[]{:S(2)}) collective-permute-start(bf16[1024,128]{1,0:T(8,128)(2,1)S(1)} %get-tuple-element.32), channel_id=1, source_target_pairs={{0,1},{1,0},{2,3},{3,2},{4,5},{5,4},{6,7},{7,6},{8,9},{9,8},{10,11... | collective-permute-start | bytes 786440 | tf_op jit(solution)/shard_map/ppermute | solution.py:76
  20.0 0.7 %collective-permute-start.4 = (bf16[1024,128]{1,0:T(8,128)(2,1)S(1)}, bf16[1024,128]{1,0:T(8,128)(2,1)S(1)}, u32[]{:S(2)}, u32[]{:S(2)}) collective-permute-start(bf16[1024,128]{1,0:T(8,128)(2,1)S(1)} %get-tuple-element.33), channel_id=1, source_target_pairs={{1,2},{2,1},{3,4},{4,3},{5,6},{6,5},{9,10},{10,9},{11,12},{12,11},... | collective-permute-start | bytes 786440 | tf_op jit(solution)/shard_map/ppermute | solution.py:76
  20.7 4.8 %all-to-all-done.loads_ref = bf16[8,32,256]{2,1,0:T(8,128)(2,1)S(1)} async-done(((bf16[8,32,256]{2,1,0:T(8,128)(2,1)}), bf16[8,32,256]{2,1,0:T(8,128)(2,1)S(1)}, u32[]{:S(2)}, u32[]{:S(2)}) %all-to-all-start) | async-done | bytes 131104 | tf_op jit(solution)/shard_map/all_to_all | solution.py:299
  25.5 0.0 collective-permute-done.1.refs_0_.refs_1_
  25.5 0.0 collective-permute-done.2.refs_1_.refs_2_
  25.5 0.0 copy-done.1
  25.5 1.6 %hydro.1 = (bf16[8,32,256]{2,1,0:T(8,128)(2,1)}, f32[32,256]{1,0:T(8,128)S(1)}, f32[32,256]{1,0:T(8,128)S(1)}, f32[32,256]{1,0:T(8,128)S(1)}, f32[32,256]{1,0:T(8,128)S(1)}) custom-call(s32[2]{0:T(128)S(1)} %pad_add_fusion.spot, bf16[2,256,128]{2,1,0:T(8,128)(2,1)S(1)} %copy-done.1, bf16[8,32,256]{2,1,0:T(8,128)(2,1)S(1)} %all-to-all-done.loads_ref, ...), custom_call_target="tpu_custom_call" | custom-call | flops 67108864 | bytes 131072 | tf_op jit(solution)/shard_map/hydro/pallas_call | solution.py:306
  27.1 3.4 %all-to-all-start.1 = ((bf16[8,32,256]{2,1,0:T(8,128)(2,1)}), bf16[8,32,256]{2,1,0:T(8,128)(2,1)S(1)}, u32[]{:S(2)}, u32[]{:S(2)}) async-start(bf16[8,32,256]{2,1,0:T(8,128)(2,1)} %get-tuple-element.39), calls=%async_computation.1 | async-start | bytes 262144 | tf_op jit(solution)/shard_map/all_to_all | solution.py:321
  30.5 0.1 collective-permute-start.5
  30.6 0.6 %collective-permute-start.6 = (f32[32,256]{1,0:T(8,128)S(1)}, f32[32,256]{1,0:T(8,128)S(1)}, u32[]{:S(2)}, u32[]{:S(2)}) collective-permute-start(f32[32,256]{1,0:T(8,128)S(1)} %get-tuple-element.42), channel_id=1, source_target_pairs={{0,24},{8,16},{16,8},{24,0},{1,25},{9,17},{17,9},{25,1},{2,26},{10... | collective-permute-start | bytes 98312 | tf_op jit(solution)/shard_map/ppermute | solution.py:76
  31.2 1.5 %collective-permute-start.7 = (f32[32,256]{1,0:T(8,128)S(1)}, f32[32,256]{1,0:T(8,128)S(1)}, u32[]{:S(2)}, u32[]{:S(2)}) collective-permute-start(f32[32,256]{1,0:T(8,128)S(1)} %get-tuple-element.43), channel_id=1, source_target_pairs={{0,16},{8,24},{16,0},{24,8},{1,17},{9,25},{17,1},{25,9},{2,18},{10... | collective-permute-start | bytes 98312 | tf_op jit(solution)/shard_map/ppermute | solution.py:76
  32.7 0.0 collective-permute-done.3.refs_2_
  32.7 0.0 collective-permute-done.4.refs_3_
  32.7 0.0 copy-done.3
  32.7 0.0 copy-start
  32.7 3.6 %local.1 = (f32[4,256,128]{2,1,0:T(8,128)S(1)}, f32[4,256,128]{2,1,0:T(8,128)S(1)}, f32[4,256,128]{2,1,0:T(8,128)S(1)}) custom-call(s32[2]{0:T(128)S(1)} %pad_add_fusion.spot, s32[2,2,4]{2,1,0:T(2,128)S(1)} %copy-done.3, bf16[4,256,128]{2,1,0:T(8,128)(2,1)} %bitcast.14, bf16[4,256,128]{2,1,0:T(8,128)(2,1)} %bitcast.16, bf16[4,256,128]{2,1,0:T(8,128)(2,1)} %bitcast.17, ...), custom_call_target="tpu_custom_call" | custom-call | flops 671088640 | bytes 3932160 | tf_op jit(solution)/shard_map/local/pallas_call | solution.py:324
  36.3 0.0 collective-permute-done.5.refs_1_
  36.4 0.0 collective-permute-done.6.refs_2_
  36.4 0.0 collective-permute-done.7.refs_3_
  36.4 1.4 %all-to-all-done.1.pressures = bf16[8,32,256]{2,1,0:T(8,128)(2,1)S(1)} async-done(((bf16[8,32,256]{2,1,0:T(8,128)(2,1)}), bf16[8,32,256]{2,1,0:T(8,128)(2,1)S(1)}, u32[]{:S(2)}, u32[]{:S(2)}) %all-to-all-start.1) | async-done | bytes 131104 | tf_op jit(solution)/shard_map/all_to_all | solution.py:321
  37.8 0.0 copy-done
  37.8 1.9 %final.1 = (f32[4,256,128]{2,1,0:T(8,128)}, f32[4,256,128]{2,1,0:T(8,128)}, f32[2,2]{1,0:T(2,128)}) custom-call(bf16[128,128]{1,0:T(8,128)(2,1)S(1)} %bitcast.10, f32[4,256,128]{2,1,0:T(8,128)S(1)} %get-tuple-element.34.residual, f32[4,256,128]{2,1,0:T(8,128)S(1)} %get-tuple-element.35.multiplier, f32[4,256,128]{2,1,0:T(8,128)S(1)} %get-tuple-element.36.own, ...), custom_call_target="tpu_custom_call" | custom-call | flops 16777216 | bytes 2621440 | tf_op jit(solution)/shard_map/final/pallas_call | solution.py:335
Async XLA Ops:
  0.6 24.8 %copy-start.1 = (bf16[2,256,128]{2,1,0:T(8,128)(2,1)S(1)}, bf16[2,256,128]{2,1,0:T(8,128)(2,1)}, u32[]{:S(2)}) copy-start(bf16[2,256,128]{2,1,0:T(8,128)(2,1)} %hydro_ref.1) | copy-start | bytes 393220
  0.7 0.7 %copy-start.2 = (s32[2,2,4]{2,1,0:T(2,128)S(1)}, s32[2,2,4]{2,1,0:T(2,128)}, u32[]{:S(2)}) copy-start(s32[2,2,4]{2,1,0:T(2,128)} %joints.3) | copy-start | bytes 196
  1.4 31.3 %copy-start.3 = (s32[2,2,4]{2,1,0:T(2,128)S(1)}, s32[2,2,4]{2,1,0:T(2,128)}, u32[]{:S(2)}) copy-start(s32[2,2,4]{2,1,0:T(2,128)} %joints.3) | copy-start | bytes 196
  5.3 4.7 %collective-permute-start = (bf16[32,256]{1,0:T(8,128)(2,1)S(1)}, bf16[32,256]{1,0:T(8,128)(2,1)S(1)}, u32[]{:S(2)}, u32[]{:S(2)}) collective-permute-start(bf16[32,256]{1,0:T(8,128)(2,1)S(1)} %get-tuple-element.29.refs_0_), channel_id=1, source_target_pairs={{0,16},{8,24},{16,0},{24,8},{1,17},{9,25},{17,1},{25,9},{2,18},{10... | collective-permute-start | bytes 49160 | tf_op jit(solution)/shard_map/ppermute | solution.py:76
  10.0 15.4 %collective-permute-start.1 = (bf16[1088,128]{1,0:T(8,128)(2,1)S(1)}, bf16[1088,128]{1,0:T(8,128)(2,1)S(1)}, u32[]{:S(2)}, u32[]{:S(2)}) collective-permute-start(bf16[1088,128]{1,0:T(8,128)(2,1)S(1)} %get-tuple-element.30), channel_id=1, source_target_pairs={{0,8},{8,0},{16,24},{24,16},{1,9},{9,1},{17,25},{25,17},{2,10},{10... | collective-permute-start | bytes 835592 | tf_op jit(solution)/shard_map/ppermute | solution.py:76
  10.0 15.4 %collective-permute-start.2 = (bf16[1088,128]{1,0:T(8,128)(2,1)S(1)}, bf16[1088,128]{1,0:T(8,128)(2,1)S(1)}, u32[]{:S(2)}, u32[]{:S(2)}) collective-permute-start(bf16[1088,128]{1,0:T(8,128)(2,1)S(1)} %get-tuple-element.31), channel_id=1, source_target_pairs={{0,24},{8,16},{16,8},{24,0},{1,25},{9,17},{17,9},{25,1},{2,26},{10... | collective-permute-start | bytes 835592 | tf_op jit(solution)/shard_map/ppermute | solution.py:76
  12.2 13.3 %all-to-all-start = ((bf16[8,32,256]{2,1,0:T(8,128)(2,1)}), bf16[8,32,256]{2,1,0:T(8,128)(2,1)S(1)}, u32[]{:S(2)}, u32[]{:S(2)}) async-start(bf16[8,32,256]{2,1,0:T(8,128)(2,1)} %get-tuple-element.37), calls=%async_computation | async-start | bytes 262144 | tf_op jit(solution)/shard_map/all_to_all | solution.py:299
  18.0 14.7 %collective-permute-start.3 = (bf16[1024,128]{1,0:T(8,128)(2,1)S(1)}, bf16[1024,128]{1,0:T(8,128)(2,1)S(1)}, u32[]{:S(2)}, u32[]{:S(2)}) collective-permute-start(bf16[1024,128]{1,0:T(8,128)(2,1)S(1)} %get-tuple-element.32), channel_id=1, source_target_pairs={{0,1},{1,0},{2,3},{3,2},{4,5},{5,4},{6,7},{7,6},{8,9},{9,8},{10,11... | collective-permute-start | bytes 786440 | tf_op jit(solution)/shard_map/ppermute | solution.py:76
  20.0 12.7 %collective-permute-start.4 = (bf16[1024,128]{1,0:T(8,128)(2,1)S(1)}, bf16[1024,128]{1,0:T(8,128)(2,1)S(1)}, u32[]{:S(2)}, u32[]{:S(2)}) collective-permute-start(bf16[1024,128]{1,0:T(8,128)(2,1)S(1)} %get-tuple-element.33), channel_id=1, source_target_pairs={{1,2},{2,1},{3,4},{4,3},{5,6},{6,5},{9,10},{10,9},{11,12},{12,11},... | collective-permute-start | bytes 786440 | tf_op jit(solution)/shard_map/ppermute | solution.py:76
  27.1 10.7 %all-to-all-start.1 = ((bf16[8,32,256]{2,1,0:T(8,128)(2,1)}), bf16[8,32,256]{2,1,0:T(8,128)(2,1)S(1)}, u32[]{:S(2)}, u32[]{:S(2)}) async-start(bf16[8,32,256]{2,1,0:T(8,128)(2,1)} %get-tuple-element.39), calls=%async_computation.1 | async-start | bytes 262144 | tf_op jit(solution)/shard_map/all_to_all | solution.py:321
  30.5 5.8 %collective-permute-start.5 = (f32[32,256]{1,0:T(8,128)S(1)}, f32[32,256]{1,0:T(8,128)S(1)}, u32[]{:S(2)}, u32[]{:S(2)}) collective-permute-start(f32[32,256]{1,0:T(8,128)S(1)} %get-tuple-element.41), channel_id=1, source_target_pairs={{0,8},{8,0},{16,24},{24,16},{1,9},{9,1},{17,25},{25,17},{2,10},{10... | collective-permute-start | bytes 98312 | tf_op jit(solution)/shard_map/ppermute | solution.py:76
  30.6 5.8 %collective-permute-start.6 = (f32[32,256]{1,0:T(8,128)S(1)}, f32[32,256]{1,0:T(8,128)S(1)}, u32[]{:S(2)}, u32[]{:S(2)}) collective-permute-start(f32[32,256]{1,0:T(8,128)S(1)} %get-tuple-element.42), channel_id=1, source_target_pairs={{0,24},{8,16},{16,8},{24,0},{1,25},{9,17},{17,9},{25,1},{2,26},{10... | collective-permute-start | bytes 98312 | tf_op jit(solution)/shard_map/ppermute | solution.py:76
  31.2 5.1 %collective-permute-start.7 = (f32[32,256]{1,0:T(8,128)S(1)}, f32[32,256]{1,0:T(8,128)S(1)}, u32[]{:S(2)}, u32[]{:S(2)}) collective-permute-start(f32[32,256]{1,0:T(8,128)S(1)} %get-tuple-element.43), channel_id=1, source_target_pairs={{0,16},{8,24},{16,0},{24,8},{1,17},{9,25},{17,1},{25,9},{2,18},{10... | collective-permute-start | bytes 98312 | tf_op jit(solution)/shard_map/ppermute | solution.py:76
  32.7 5.0 %copy-start = (bf16[32,2,2,128]{3,2,1,0:T(2,128)(2,1)S(1)}, bf16[32,2,2,128]{3,2,1,0:T(2,128)(2,1)}, u32[]{:S(2)}) copy-start(bf16[32,2,2,128]{3,2,1,0:T(2,128)(2,1)} %param.13) | copy-start | bytes 98308

commit v4 on v3

--- a/solution.py
+++ b/solution.py
@@ -22,11 +22,14 @@
 
 
 def times_i(field, axis):
+    shape = field.shape
+    if axis == 0:
+        field, axis = field.reshape(-1, 8, shape[1]), 1
     size = field.shape[axis]
     after = pltpu.roll(field, size - 1, axis)
     before = pltpu.roll(field, 1, axis)
     place = lax.broadcasted_iota(jnp.int32, field.shape, axis)
-    return jnp.where(lax.rem(place, 2) == 0, -after, before)
+    return jnp.where(lax.rem(place, 2) == 0, -after, before).reshape(shape)
 
 
 def forward_parts(coupling, motion):
@@ -96,74 +99,95 @@
     return sides
 
 
-def send_kernel(rows, cols, spot, joints, motion_far, load_far, coupling_far, map_far, *refs):
-    load_out, motion_out, outs, refs = refs[0], refs[1], refs[2:6], refs[6:]
-    motion, load, coupling, maps, load_panels, arrive, leave = refs
-    blocks, wide, unknowns = motion.shape
+def fetch_edges(which, sides, cols, coupling_far, coupling, arrive, first):
+    moves = []
+    for o in which:
+        for x, y, d in sides[o]:
+            i = len(moves)
+            moves.append(pltpu.make_async_copy(coupling_far.at[x * cols + y, d + 1], coupling.at[i], arrive.at[first + i]))
+            moves[-1].start()
+    return moves
+
+
+def fill_edges(which, sides, cols, joints, motion, load, coupling, moves, outs):
+    wide = motion.shape[1]
+    i = 0
+    for o, out in zip(which, outs):
+        for k, (x, y, d) in enumerate(sides[o]):
+            out[pl.ds(k * wide, wide), :] = motion[x * cols + y]
+            moves[i].wait()
+            link = joints[x, y, d].astype(F32)
+            term = joined(adjoint_parts(coupling[i], load[x * cols + y]), -1)
+            out[pl.ds((len(sides[o]) + k) * wide, wide), :] = (link * term).astype(BF16)
+            i += 1
+
+
+def panels_kernel(rows, cols, which, spot, joints, motion_far, load_far, coupling_far, map_far, *refs):
+    motion_out, load_out, outs, refs = refs[0], refs[1], refs[2 : 2 + len(which)], refs[2 + len(which) :]
+    motion, load, coupling, maps, arrive = refs
+    moves = [
+        pltpu.make_async_copy(map_far, maps, arrive.at[0]),
+        pltpu.make_async_copy(motion_far, motion, arrive.at[1]),
+        pltpu.make_async_copy(load_far, load, arrive.at[2]),
+    ]
+    for move in moves:
+        move.start()
     sides = edges(rows, cols, spot)
-    spots = [(o, k) + place for o, side in enumerate(sides) for k, place in enumerate(side)]
-    fetch = [
-        pltpu.make_async_copy(map_far, maps, arrive.at[0]),
-        pltpu.make_async_copy(load_far, load, arrive.at[1]),
-        pltpu.make_async_copy(motion_far, motion, arrive.at[2]),
+    more = fetch_edges(which, sides, cols, coupling_far, coupling, arrive, 3)
+    blocks = motion.shape[0]
+    moves[0].wait()
+    split = map_of_blocks(maps, blocks)
+    for move, field, out in ((moves[1], motion, motion_out), (moves[2], load, load_out)):
+        move.wait()
+        out[...] = sum(dot(split[b], field[b], (1, 1)) for b in range(blocks)).astype(BF16)
+    fill_edges(which, sides, cols, joints, motion, load, coupling, more, outs)
+
+
+def edges_kernel(rows, cols, which, spot, joints, motion_far, load_far, coupling_far, *refs):
+    outs, (motion, load, coupling, arrive) = refs[: len(which)], refs[len(which) :]
+    moves = [
+        pltpu.make_async_copy(load_far, load, arrive.at[0]),
+        pltpu.make_async_copy(motion_far, motion, arrive.at[1]),
     ]
-    for i, (o, k, x, y, d) in enumerate(spots):
-        fetch.append(pltpu.make_async_copy(coupling_far.at[x * cols + y, d + 1], coupling.at[i], arrive.at[i + 3]))
-    for move in fetch:
+    for move in moves:
         move.start()
-    fetch[0].wait()
-    split = map_of_blocks(maps, blocks)
-    fetch[1].wait()
-    load_panels[...] = sum(dot(split[b], load[b], (1, 1)) for b in range(blocks)).astype(BF16)
-    sent = [pltpu.make_async_copy(load_panels, load_out.at[j], leave.at[j]) for j in range(load_out.shape[0])]
-    for move in sent:
-        move.start()
-    fetch[2].wait()
-    panels = sum(dot(split[b], motion[b], (1, 1)) for b in range(blocks)).astype(BF16)
-    motion_out[...] = panels
-    for o in range(2):
-        for h in range(wide // unknowns):
-            top = 2 * len(sides[o]) * wide + h * panels.shape[0]
-            outs[o][pl.ds(top, panels.shape[0]), :] = panels[:, h * unknowns : (h + 1) * unknowns]
-    for i, (o, k, x, y, d) in enumerate(spots):
-        outs[o][pl.ds(k * wide, wide), :] = motion[x * cols + y]
-        fetch[i + 3].wait()
-        link = joints[x, y, d].astype(F32)
-        term = joined(adjoint_parts(coupling[i], load[x * cols + y]), -1)
-        outs[o][pl.ds((len(sides[o]) + k) * wide, wide), :] = (link * term).astype(BF16)
-    for move in sent:
+    sides = edges(rows, cols, spot)
+    more = fetch_edges(which, sides, cols, coupling_far, coupling, arrive, 2)
+    for move in moves:
         move.wait()
-
-
-def hydro_kernel(n_gx, spot, hydro_ref, loads_ref, *refs):
-    pieces, (pressure_out, *reaction_outs, gathered, pressures, reacted, leave) = refs[:n_gx], refs[n_gx:]
-    outs = [pltpu.make_async_copy(pressures, pressure_out, leave)]
+    fill_edges(which, sides, cols, joints, motion, load, coupling, more, outs)
+
+
+def pressure_kernel(n_gx, spot, hydro_ref, load_panels, *refs):
+    pieces, (out_far, gathered, out, leave) = refs[:n_gx], refs[n_gx:]
     me = spot[0]
-    panels, wide = pieces[0].shape
+    panels, wide = load_panels.shape
     for step in range(n_gx):
         start = pl.multiple_of(source(me, step, n_gx) * panels, panels)
-        if step in (1, 2):
-            narrow = pieces[step].shape[1]
-            top = pieces[step].shape[0] - panels * wide // narrow
-            for h in range(wide // narrow):
-                part = pieces[step][pl.ds(top + h * panels, panels), :]
-                gathered[pl.ds(start, panels), pl.ds(h * narrow, narrow)] = part
-        else:
-            gathered[pl.ds(start, panels), :] = pieces[step][...]
+        gathered[pl.ds(start, panels), :] = pieces[step][...]
     hydro = hydro_ref[...]
     size, depth = hydro.shape[1:]
     both = dot(hydro.reshape(2 * size, depth), gathered[...], (1, 0))
     pressure = both[:size] + times_i(both[size:], 1)
-    pressures[...] = pressure.astype(BF16).reshape(pressures.shape)
-    outs[0].start()
-    loads = loads_ref[...].reshape(size, -1)
+    out[:, :panels, :] = pressure.astype(BF16).reshape(-1, panels, wide)
+    out[:, panels:, :] = jnp.broadcast_to(load_panels[...], (out.shape[0], panels, wide))
+    move = pltpu.make_async_copy(out, out_far, leave)
+    move.start()
+    move.wait()
+
+
+def reaction_kernel(n_gx, spot, hydro_ref, arrived, *refs):
+    outs, (reacted,) = refs[:n_gx], refs[n_gx:]
+    me = spot[0]
+    panels = outs[0].shape[0]
+    hydro = hydro_ref[...]
+    loads = arrived[:, panels:, :].reshape(hydro.shape[1], -1)
     real = dot(hydro[0], loads, (0, 0))
     imag = dot(hydro[1], loads, (0, 0))
     reacted[...] = real - times_i(imag, 1)
     for step in range(n_gx):
         start = pl.multiple_of(target(me, step, n_gx) * panels, panels)
-        reaction_outs[step][...] = reacted[pl.ds(start, panels), :]
-    outs[0].wait()
+        outs[step][...] = reacted[pl.ds(start, panels), :]
 
 
 def local_kernel(rows, cols, sizes, spot, joints, motion_far, load_far, excitation_far, coupling_far, *refs):
@@ -226,7 +250,8 @@
     reactions, (residual_out, multiplier_out, sensitivity_out, full, leave) = refs[:-5], refs[-5:]
     blocks = rows * cols
     maps = map_of_blocks(map_ref, blocks)
-    pressure = jnp.sum(pressures[...].astype(F32), axis=0).astype(BF16)
+    panels = reactions[0].shape[0]
+    pressure = jnp.sum(pressures[:, :panels, :].astype(F32), axis=0).astype(BF16)
     reaction = sum(r[...].astype(F32) for r in reactions).astype(BF16)
     scale = 1.0 / math.sqrt(own.shape[1] // 2 * own.shape[2])
     sent = []
@@ -275,50 +300,69 @@
     field = (blocks, wide, unknowns)
 
     counts = [cols, cols, rows, rows]
-    extra = panels * wide // unknowns
-    lengths = [2 * c * wide + (extra if o < 2 else 0) for o, c in enumerate(counts)]
-    load_copies, motion_panels, *payloads = pl.pallas_call(
-        functools.partial(send_kernel, rows, cols),
-        name="send",
-        out_shape=[pltpu.HBM((n_gy, panels, wide), BF16), pltpu.VMEM((panels, wide), BF16)]
-        + [pltpu.VMEM((length, unknowns), BF16) for length in lengths],
+    early, late = (2,), (0, 1, 3)
+    motion_panels, load_panels, *payloads = pl.pallas_call(
+        functools.partial(panels_kernel, rows, cols, early),
+        name="panels",
+        out_shape=[pltpu.VMEM((panels, wide), BF16)] * 2
+        + [pltpu.VMEM((2 * counts[o] * wide, unknowns), BF16) for o in early],
         in_specs=[SCALARS, SCALARS] + [FAR] * 4,
-        out_specs=[FAR] + [WHOLE] * 5,
+        out_specs=[WHOLE] * (2 + len(early)),
         scratch_shapes=[
             pltpu.VMEM(field, BF16),
             pltpu.VMEM(field, BF16),
-            pltpu.VMEM((sum(counts), 2, unknowns, unknowns), BF16),
+            pltpu.VMEM((sum(counts[o] for o in early), 2, unknowns, unknowns), BF16),
             pltpu.VMEM(panel_map.shape, BF16),
-            pltpu.VMEM((panels, wide), BF16),
-            DMA((sum(counts) + 3,)),
-            DMA((n_gy,)),
+            DMA((3 + sum(counts[o] for o in early),)),
         ],
         compiler_params=params(16),
+        cost_estimate=cost(4 * blocks * wide * unknowns * panels, 4 * blocks * wide * unknowns),
+    )(spot, far(joints), far(motion), far(load), far(coupling), far(panel_map))
+    pieces = [motion_panels] + [exchange(motion_panels, step) for step in range(1, n_gx)]
+    third = exchange(payloads[0], 1, "gy")
+
+    payloads = pl.pallas_call(
+        functools.partial(edges_kernel, rows, cols, late),
+        name="edges",
+        out_shape=[pltpu.VMEM((2 * counts[o] * wide, unknowns), BF16) for o in late],
+        in_specs=[SCALARS, SCALARS] + [FAR] * 3,
+        out_specs=[WHOLE] * len(late),
+        scratch_shapes=[
+            pltpu.VMEM(field, BF16),
+            pltpu.VMEM(field, BF16),
+            pltpu.VMEM((sum(counts[o] for o in late), 2, unknowns, unknowns), BF16),
+            DMA((2 + sum(counts[o] for o in late),)),
+        ],
+        compiler_params=params(16),
         cost_estimate=cost(sum(counts) * block_flops, 4 * blocks * wide * unknowns + 20 * blocks * unknowns**2),
-    )(spot, joints, far(motion), far(load), far(coupling), far(panel_map))
-    loads = lax.all_to_all(load_copies, "gy", 0, 0, tiled=True)
-    further = [exchange(motion_panels, step) for step in range(3, n_gx)]
-    (*payloads, further) = lax.optimization_barrier((*payloads, further))
-    first, second = exchange(payloads[0], 1), exchange(payloads[1], 2)
-    third, fourth = exchange(payloads[2], 1, "gy"), exchange(payloads[3], 2, "gy", wrap=False)
-    pieces = [motion_panels, first, second] + further
-
-    pressure_parts, *reaction_parts = pl.pallas_call(
-        functools.partial(hydro_kernel, n_gx),
-        name="hydro",
-        out_shape=[pltpu.HBM((n_gy, panels, wide), BF16)] + [pltpu.VMEM((panels, wide), F32)] * n_gx,
+    )(spot, far(joints), far(motion), far(load), far(coupling))
+    (*payloads, load_panels) = lax.optimization_barrier((*payloads, load_panels))
+    first, second = exchange(payloads[0], 1), exchange(payloads[1], 2, wrap=False)
+    fourth = exchange(payloads[2], 2, "gy", wrap=False)
+
+    parts = pl.pallas_call(
+        functools.partial(pressure_kernel, n_gx),
+        name="pressure",
+        out_shape=pltpu.HBM((n_gy, 2 * panels, wide), BF16),
         in_specs=[SCALARS] + [WHOLE] * (2 + n_gx),
-        out_specs=[FAR] + [WHOLE] * n_gx,
-        scratch_shapes=[
-            pltpu.VMEM((n_gx * panels, wide), BF16),
-            pltpu.VMEM((n_gy, panels, wide), BF16),
-            pltpu.VMEM((n_gx * panels, wide), F32),
-            DMA,
-        ],
-        compiler_params=params(16),
-        cost_estimate=cost(4 * hydro.size * wide, 2 * hydro.size),
-    )(spot, hydro, loads, *pieces)
-    pressures = lax.all_to_all(pressure_parts, "gy", 0, 0, tiled=True)
+        out_specs=FAR,
+        scratch_shapes=[pltpu.VMEM((n_gx * panels, wide), BF16), pltpu.VMEM((n_gy, 2 * panels, wide), BF16), DMA],
+        compiler_params=params(16),
+        cost_estimate=cost(2 * hydro.size * wide, 2 * hydro.size),
+    )(spot, hydro, load_panels, *pieces)
+    parts, third = lax.optimization_barrier((parts, third))
+    arrived = lax.all_to_all(parts, "gy", 0, 0, tiled=True)
+
+    reaction_parts = pl.pallas_call(
+        functools.partial(reaction_kernel, n_gx),
+        name="reaction",
+        out_shape=[pltpu.VMEM((panels, wide), F32)] * n_gx,
+        in_specs=[SCALARS] + [WHOLE] * 2,
+        out_specs=[WHOLE] * n_gx,
+        scratch_shapes=[pltpu.VMEM((n_gx * panels, wide), F32)],
+        compiler_params=params(16),
+        cost_estimate=cost(2 * hydro.size * wide, 2 * hydro.size),
+    )(spot, hydro, arrived)
     reactions = [reaction_parts[0]] + [exchange(reaction_parts[step], step) for step in range(1, n_gx)]
 
     residual, multiplier, own = pl.pallas_call(
@@ -330,7 +374,7 @@
         scratch_shapes=[pltpu.VMEM(field, BF16)] * 3 + [pltpu.VMEM(coupling.shape, BF16), DMA((4,))],
         compiler_params=params(16),
         cost_estimate=cost(10 * blocks * block_flops, 20 * blocks * unknowns**2 + 20 * blocks * wide * unknowns),
-    )(spot, joints, far(motion), far(load), far(force), far(coupling), first, second, third, fourth)
+    )(spot, far(joints), far(motion), far(load), far(force), far(coupling), first, second, third, fourth)
 
     residual, multiplier, sensitivity = pl.pallas_call(
         functools.partial(final_kernel, rows, cols, lift),
@@ -341,7 +385,7 @@
         scratch_shapes=[pltpu.VMEM((2,) + field, F32), DMA((2, blocks))],
         compiler_params=params(16),
         cost_estimate=cost(4 * blocks * wide * unknowns * panels, 20 * blocks * wide * unknowns),
-    )(panel_map, residual, multiplier, own, pressures, *reactions)
+    )(panel_map, residual, multiplier, own, arrived, *reactions)
     shape = plate_motion.shape
     return residual.reshape(shape), multiplier.reshape(shape), sensitivity
 

time: 40.1 us -> 37.2 us (0.928)
  the two profiles are of different devices: /device:TPU:0 before, /device:TPU:5 now
where the time goes in v4:
time: 37.2 us; the launch traced here: 36.7 us
  starting transfers between devices  19.8 us (53%)
  Pallas kernels  13.8 us (37%)
  waiting for transfers between devices  2.24 us (6%)
  between operations  0.79 us (2%)
    ppermute x10, starting transfers between devices, exchange(): lax.ppermute(x, axis, [(i, j) for i, j in pairs if wrap or abs(i - j) < n...  13.8 us
    all_to_all x1, starting transfers between devices, on_device(): arrived = lax.all_to_all(parts, 'gy', 0, 0, tiled=True)  5.99 us
    pallas_call x1, Pallas kernels, on_device(): pl.pallas_call(functools.partial(local_kernel, rows, cols, (n_gx, n_gy)),...  3.77 us
    pallas_call x1, Pallas kernels, on_device(): pl.pallas_call(functools.partial(edges_kernel, rows, cols, late), name='e...  3.05 us
    pallas_call x1, Pallas kernels, on_device(): pl.pallas_call(functools.partial(panels_kernel, rows, cols, early), name=...  2.64 us
    ppermute x10, waiting for transfers between devices, exchange(): lax.ppermute(x, axis, [(i, j) for i, j in pairs if wrap or abs(i - j) < n...  2.23 us
    pallas_call x1, Pallas kernels, on_device(): pl.pallas_call(functools.partial(final_kernel, rows, cols, lift), name='f...  1.9 us
    pallas_call x1, Pallas kernels, on_device(): pl.pallas_call(functools.partial(pressure_kernel, n_gx), name='pressure',...  1.62 us
  transfers between devices with their start and end apart: 11, of which 1 were waited for; matrix products, arithmetic and copies ran while one was open for 0% of the time, Pallas kernels for 25%

profile of v4, /device:TPU:5, one launch (start us, length us, event | category | flops | bytes accessed | tf_op | source)
XLA Modules:
  0.0 36.7 jit_solution(15313660050276166812)
XLA Ops:
  0.6 0.1 pad_add_fusion.spot
  0.7 2.6 %panels.1 = (bf16[32,256]{1,0:T(8,128)(2,1)S(1)}, bf16[32,256]{1,0:T(8,128)(2,1)S(1)}, bf16[1024,128]{1,0:T(8,128)(2,1)S(1)}) custom-call(s32[2]{0:T(128)S(1)} %pad_add_fusion.spot, s32[2,2,4]{2,1,0:T(2,128)} %joints.5, bf16[4,256,128]{2,1,0:T(8,128)(2,1)} %bitcast.14, bf16[4,256,128]{2,1,0:T(8,128)(2,1)} %bitcast.17, bf16[4,5,2,128,128]{4,3,2,1,0:T(8,128)(2,1)} %bitcast.11, ...), custom_call_target="tpu_custom_call" | custom-call | flops 16777216 | bytes 524288 | tf_op jit(solution)/shard_map/panels/pallas_call | solution.py:304
  3.4 0.0 copy-start
  3.4 0.1 collective-permute-start.5
  3.5 1.4 %collective-permute-start.4 = (bf16[32,256]{1,0:T(8,128)(2,1)S(1)}, bf16[32,256]{1,0:T(8,128)(2,1)S(1)}, u32[]{:S(2)}, u32[]{:S(2)}) collective-permute-start(bf16[32,256]{1,0:T(8,128)(2,1)S(1)} %get-tuple-element.32.refs_0_), channel_id=1, source_target_pairs={{0,16},{8,24},{16,0},{24,8},{1,17},{9,25},{17,1},{25,9},{2,18},{10... | collective-permute-start | bytes 49160 | tf_op jit(solution)/shard_map/ppermute | solution.py:79
  4.9 0.9 %collective-permute-start.3 = (bf16[32,256]{1,0:T(8,128)(2,1)S(1)}, bf16[32,256]{1,0:T(8,128)(2,1)S(1)}, u32[]{:S(2)}, u32[]{:S(2)}) collective-permute-start(bf16[32,256]{1,0:T(8,128)(2,1)S(1)} %get-tuple-element.32.refs_0_), channel_id=1, source_target_pairs={{0,24},{8,16},{16,8},{24,0},{1,25},{9,17},{17,9},{25,1},{2,26},{10... | collective-permute-start | bytes 49160 | tf_op jit(solution)/shard_map/ppermute | solution.py:79
  5.8 0.3 collective-permute-start.2
  6.1 3.0 %edges.1 = (bf16[1024,128]{1,0:T(8,128)(2,1)S(1)}, bf16[1024,128]{1,0:T(8,128)(2,1)S(1)}, bf16[1024,128]{1,0:T(8,128)(2,1)S(1)}) custom-call(s32[2]{0:T(128)S(1)} %pad_add_fusion.spot, s32[2,2,4]{2,1,0:T(2,128)} %joints.5, bf16[4,256,128]{2,1,0:T(8,128)(2,1)} %bitcast.15, bf16[4,256,128]{2,1,0:T(8,128)(2,1)} %bitcast.18, bf16[4,5,2,128,128]{4,3,2,1,0:T(8,128)(2,1)} %bitcast.12), custom_call_target="tpu_custom_call" | custom-call | flops 134217728 | bytes 1835008 | tf_op jit(solution)/shard_map/edges/pallas_call | solution.py:324
  9.2 0.0 collective-permute-done.4.refs_3_
  9.2 0.0 collective-permute-done.3.refs_2_
  9.2 0.0 collective-permute-done.2.refs_1_
  9.2 0.0 copy-done
  9.2 1.6 %pressure.1 = bf16[8,64,256]{2,1,0:T(8,128)(2,1)} custom-call(s32[2]{0:T(128)S(1)} %pad_add_fusion.spot, bf16[2,256,128]{2,1,0:T(8,128)(2,1)S(1)} %copy-done, bf16[32,256]{1,0:T(8,128)(2,1)S(1)} %get-tuple-element.31.load_panels, bf16[32,256]{1,0:T(8,128)(2,1)S(1)} %get-tuple-element.32.refs_0_, bf16[32,256]{1,0:T(8,128)(2,1)S(1)} %collective-permute-done.2.refs_1_, ...), custom_call_target="tpu_custom_call" | custom-call | flops 33554432 | bytes 131072 | tf_op jit(solution)/shard_map/pressure/pallas_call | solution.py:343
  10.8 0.0 collective-permute-done.5.refs_2_
  10.9 6.0 %all-to-all-start = ((bf16[8,64,256]{2,1,0:T(8,128)(2,1)}), bf16[8,64,256]{2,1,0:T(8,128)(2,1)S(1)}, u32[]{:S(2)}, u32[]{:S(2)}) async-start(bf16[8,64,256]{2,1,0:T(8,128)(2,1)} %pressure.1), calls=%async_computation | async-start | bytes 524288 | tf_op jit(solution)/shard_map/all_to_all | solution.py:354
  16.8 1.6 %collective-permute-start = (bf16[1024,128]{1,0:T(8,128)(2,1)S(1)}, bf16[1024,128]{1,0:T(8,128)(2,1)S(1)}, u32[]{:S(2)}, u32[]{:S(2)}) collective-permute-start(bf16[1024,128]{1,0:T(8,128)(2,1)S(1)} %get-tuple-element.29), channel_id=1, source_target_pairs={{0,8},{8,0},{16,24},{24,16},{1,9},{9,1},{17,25},{25,17},{2,10},{10... | collective-permute-start | bytes 786440 | tf_op jit(solution)/shard_map/ppermute | solution.py:79
  18.5 3.0 %collective-permute-start.1 = (bf16[1024,128]{1,0:T(8,128)(2,1)S(1)}, bf16[1024,128]{1,0:T(8,128)(2,1)S(1)}, u32[]{:S(2)}, u32[]{:S(2)}) collective-permute-start(bf16[1024,128]{1,0:T(8,128)(2,1)S(1)} %get-tuple-element.30), channel_id=1, source_target_pairs={{8,16},{16,8},{9,17},{17,9},{10,18},{18,10},{11,19},{19,11},{12,20... | collective-permute-start | bytes 786440 | tf_op jit(solution)/shard_map/ppermute | solution.py:79
  21.5 3.1 %collective-permute-start.6 = (bf16[1024,128]{1,0:T(8,128)(2,1)S(1)}, bf16[1024,128]{1,0:T(8,128)(2,1)S(1)}, u32[]{:S(2)}, u32[]{:S(2)}) collective-permute-start(bf16[1024,128]{1,0:T(8,128)(2,1)S(1)} %get-tuple-element.35), channel_id=1, source_target_pairs={{1,2},{2,1},{3,4},{4,3},{5,6},{6,5},{9,10},{10,9},{11,12},{12,11},... | collective-permute-start | bytes 786440 | tf_op jit(solution)/shard_map/ppermute | solution.py:79
  24.6 0.0 all-to-all-done.arrived.pressures
  24.6 0.9 %reaction.1 = (f32[32,256]{1,0:T(8,128)S(1)}, f32[32,256]{1,0:T(8,128)S(1)}, f32[32,256]{1,0:T(8,128)S(1)}, f32[32,256]{1,0:T(8,128)S(1)}) custom-call(s32[2]{0:T(128)S(1)} %pad_add_fusion.spot, bf16[2,256,128]{2,1,0:T(8,128)(2,1)S(1)} %copy-done, bf16[8,64,256]{2,1,0:T(8,128)(2,1)S(1)} %all-to-all-done.arrived.pressures), custom_call_target="tpu_custom_call" | custom-call | flops 33554432 | bytes 131072 | tf_op jit(solution)/shard_map/reaction/pallas_call | solution.py:356
  25.5 1.9 %collective-permute-start.7 = (f32[32,256]{1,0:T(8,128)S(1)}, f32[32,256]{1,0:T(8,128)S(1)}, u32[]{:S(2)}, u32[]{:S(2)}) collective-permute-start(f32[32,256]{1,0:T(8,128)S(1)} %get-tuple-element.41), channel_id=1, source_target_pairs={{0,8},{8,0},{16,24},{24,16},{1,9},{9,1},{17,25},{25,17},{2,10},{10... | collective-permute-start | bytes 98312 | tf_op jit(solution)/shard_map/ppermute | solution.py:79
  27.4 1.2 %collective-permute-start.8 = (f32[32,256]{1,0:T(8,128)S(1)}, f32[32,256]{1,0:T(8,128)S(1)}, u32[]{:S(2)}, u32[]{:S(2)}) collective-permute-start(f32[32,256]{1,0:T(8,128)S(1)} %get-tuple-element.42), channel_id=1, source_target_pairs={{0,24},{8,16},{16,8},{24,0},{1,25},{9,17},{17,9},{25,1},{2,26},{10... | collective-permute-start | bytes 98312 | tf_op jit(solution)/shard_map/ppermute | solution.py:79
  28.6 0.0 collective-permute-done.refs_0_
  28.6 0.3 collective-permute-start.9
  28.8 0.0 collective-permute-done.1.refs_1_
  28.8 2.2 %collective-permute-done.6.refs_3_ = bf16[1024,128]{1,0:T(8,128)(2,1)S(1)} collective-permute-done((bf16[1024,128]{1,0:T(8,128)(2,1)S(1)}, bf16[1024,128]{1,0:T(8,128)(2,1)S(1)}, u32[]{:S(2)}, u32[]{:S(2)}) %collective-permute-start.6) | collective-permute-done | bytes 262176 | tf_op jit(solution)/shard_map/ppermute | solution.py:79
  31.0 0.0 copy-start.1
  31.0 3.8 %local.1 = (f32[4,256,128]{2,1,0:T(8,128)S(1)}, f32[4,256,128]{2,1,0:T(8,128)S(1)}, f32[4,256,128]{2,1,0:T(8,128)S(1)}) custom-call(s32[2]{0:T(128)S(1)} %pad_add_fusion.spot, s32[2,2,4]{2,1,0:T(2,128)} %joints.5, bf16[4,256,128]{2,1,0:T(8,128)(2,1)} %bitcast.16, bf16[4,256,128]{2,1,0:T(8,128)(2,1)} %bitcast.19, bf16[4,256,128]{2,1,0:T(8,128)(2,1)} %bitcast.20, ...), custom_call_target="tpu_custom_call" | custom-call | flops 671088640 | bytes 3932160 | tf_op jit(solution)/shard_map/local/pallas_call | solution.py:368
  34.8 0.0 collective-permute-done.7.refs_1_
  34.8 0.0 collective-permute-done.8.refs_2_
  34.8 0.0 collective-permute-done.9.refs_3_
  34.8 0.0 copy-done.1
  34.8 1.9 %final.1 = (f32[4,256,128]{2,1,0:T(8,128)}, f32[4,256,128]{2,1,0:T(8,128)}, f32[2,2]{1,0:T(2,128)}) custom-call(bf16[128,128]{1,0:T(8,128)(2,1)S(1)} %bitcast.10, f32[4,256,128]{2,1,0:T(8,128)S(1)} %get-tuple-element.36.residual, f32[4,256,128]{2,1,0:T(8,128)S(1)} %get-tuple-element.37.multiplier, f32[4,256,128]{2,1,0:T(8,128)S(1)} %get-tuple-element.38.own, ...), custom_call_target="tpu_custom_call" | custom-call | flops 16777216 | bytes 2621440 | tf_op jit(solution)/shard_map/final/pallas_call | solution.py:379
Async XLA Ops:
  3.4 5.8 %copy-start = (bf16[2,256,128]{2,1,0:T(8,128)(2,1)S(1)}, bf16[2,256,128]{2,1,0:T(8,128)(2,1)}, u32[]{:S(2)}) copy-start(bf16[2,256,128]{2,1,0:T(8,128)(2,1)} %hydro_ref.3) | copy-start | bytes 393220
  3.4 7.5 %collective-permute-start.5 = (bf16[1024,128]{1,0:T(8,128)(2,1)S(1)}, bf16[1024,128]{1,0:T(8,128)(2,1)S(1)}, u32[]{:S(2)}, u32[]{:S(2)}) collective-permute-start(bf16[1024,128]{1,0:T(8,128)(2,1)S(1)} %get-tuple-element.33), channel_id=1, source_target_pairs={{0,1},{1,0},{2,3},{3,2},{4,5},{5,4},{6,7},{7,6},{8,9},{9,8},{10,11... | collective-permute-start | bytes 786440 | tf_op jit(solution)/shard_map/ppermute | solution.py:79
  3.5 5.7 %collective-permute-start.4 = (bf16[32,256]{1,0:T(8,128)(2,1)S(1)}, bf16[32,256]{1,0:T(8,128)(2,1)S(1)}, u32[]{:S(2)}, u32[]{:S(2)}) collective-permute-start(bf16[32,256]{1,0:T(8,128)(2,1)S(1)} %get-tuple-element.32.refs_0_), channel_id=1, source_target_pairs={{0,16},{8,24},{16,0},{24,8},{1,17},{9,25},{17,1},{25,9},{2,18},{10... | collective-permute-start | bytes 49160 | tf_op jit(solution)/shard_map/ppermute | solution.py:79
  4.9 4.3 %collective-permute-start.3 = (bf16[32,256]{1,0:T(8,128)(2,1)S(1)}, bf16[32,256]{1,0:T(8,128)(2,1)S(1)}, u32[]{:S(2)}, u32[]{:S(2)}) collective-permute-start(bf16[32,256]{1,0:T(8,128)(2,1)S(1)} %get-tuple-element.32.refs_0_), channel_id=1, source_target_pairs={{0,24},{8,16},{16,8},{24,0},{1,25},{9,17},{17,9},{25,1},{2,26},{10... | collective-permute-start | bytes 49160 | tf_op jit(solution)/shard_map/ppermute | solution.py:79
  5.8 3.4 %collective-permute-start.2 = (bf16[32,256]{1,0:T(8,128)(2,1)S(1)}, bf16[32,256]{1,0:T(8,128)(2,1)S(1)}, u32[]{:S(2)}, u32[]{:S(2)}) collective-permute-start(bf16[32,256]{1,0:T(8,128)(2,1)S(1)} %get-tuple-element.32.refs_0_), channel_id=1, source_target_pairs={{0,8},{8,0},{16,24},{24,16},{1,9},{9,1},{17,25},{25,17},{2,10},{10... | collective-permute-start | bytes 49160 | tf_op jit(solution)/shard_map/ppermute | solution.py:79
  10.9 13.7 %all-to-all-start = ((bf16[8,64,256]{2,1,0:T(8,128)(2,1)}), bf16[8,64,256]{2,1,0:T(8,128)(2,1)S(1)}, u32[]{:S(2)}, u32[]{:S(2)}) async-start(bf16[8,64,256]{2,1,0:T(8,128)(2,1)} %pressure.1), calls=%async_computation | async-start | bytes 524288 | tf_op jit(solution)/shard_map/all_to_all | solution.py:354
  16.8 11.7 %collective-permute-start = (bf16[1024,128]{1,0:T(8,128)(2,1)S(1)}, bf16[1024,128]{1,0:T(8,128)(2,1)S(1)}, u32[]{:S(2)}, u32[]{:S(2)}) collective-permute-start(bf16[1024,128]{1,0:T(8,128)(2,1)S(1)} %get-tuple-element.29), channel_id=1, source_target_pairs={{0,8},{8,0},{16,24},{24,16},{1,9},{9,1},{17,25},{25,17},{2,10},{10... | collective-permute-start | bytes 786440 | tf_op jit(solution)/shard_map/ppermute | solution.py:79
  18.5 10.3 %collective-permute-start.1 = (bf16[1024,128]{1,0:T(8,128)(2,1)S(1)}, bf16[1024,128]{1,0:T(8,128)(2,1)S(1)}, u32[]{:S(2)}, u32[]{:S(2)}) collective-permute-start(bf16[1024,128]{1,0:T(8,128)(2,1)S(1)} %get-tuple-element.30), channel_id=1, source_target_pairs={{8,16},{16,8},{9,17},{17,9},{10,18},{18,10},{11,19},{19,11},{12,20... | collective-permute-start | bytes 786440 | tf_op jit(solution)/shard_map/ppermute | solution.py:79
  21.5 9.5 %collective-permute-start.6 = (bf16[1024,128]{1,0:T(8,128)(2,1)S(1)}, bf16[1024,128]{1,0:T(8,128)(2,1)S(1)}, u32[]{:S(2)}, u32[]{:S(2)}) collective-permute-start(bf16[1024,128]{1,0:T(8,128)(2,1)S(1)} %get-tuple-element.35), channel_id=1, source_target_pairs={{1,2},{2,1},{3,4},{4,3},{5,6},{6,5},{9,10},{10,9},{11,12},{12,11},... | collective-permute-start | bytes 786440 | tf_op jit(solution)/shard_map/ppermute | solution.py:79
  25.5 9.3 %collective-permute-start.7 = (f32[32,256]{1,0:T(8,128)S(1)}, f32[32,256]{1,0:T(8,128)S(1)}, u32[]{:S(2)}, u32[]{:S(2)}) collective-permute-start(f32[32,256]{1,0:T(8,128)S(1)} %get-tuple-element.41), channel_id=1, source_target_pairs={{0,8},{8,0},{16,24},{24,16},{1,9},{9,1},{17,25},{25,17},{2,10},{10... | collective-permute-start | bytes 98312 | tf_op jit(solution)/shard_map/ppermute | solution.py:79
  27.4 7.4 %collective-permute-start.8 = (f32[32,256]{1,0:T(8,128)S(1)}, f32[32,256]{1,0:T(8,128)S(1)}, u32[]{:S(2)}, u32[]{:S(2)}) collective-permute-start(f32[32,256]{1,0:T(8,128)S(1)} %get-tuple-element.42), channel_id=1, source_target_pairs={{0,24},{8,16},{16,8},{24,0},{1,25},{9,17},{17,9},{25,1},{2,26},{10... | collective-permute-start | bytes 98312 | tf_op jit(solution)/shard_map/ppermute | solution.py:79
  28.6 6.3 %collective-permute-start.9 = (f32[32,256]{1,0:T(8,128)S(1)}, f32[32,256]{1,0:T(8,128)S(1)}, u32[]{:S(2)}, u32[]{:S(2)}) collective-permute-start(f32[32,256]{1,0:T(8,128)S(1)} %get-tuple-element.43), channel_id=1, source_target_pairs={{0,16},{8,24},{16,0},{24,8},{1,17},{9,25},{17,1},{25,9},{2,18},{10... | collective-permute-start | bytes 98312 | tf_op jit(solution)/shard_map/ppermute | solution.py:79
  31.0 3.8 %copy-start.1 = (bf16[32,2,2,128]{3,2,1,0:T(2,128)(2,1)S(1)}, bf16[32,2,2,128]{3,2,1,0:T(2,128)(2,1)}, u32[]{:S(2)}) copy-start(bf16[32,2,2,128]{3,2,1,0:T(2,128)(2,1)} %param.13) | copy-start | bytes 98308

commit v5 on v4

v5 whole, which is shorter than its diff:
```python
import functools
import math

import jax
import jax.numpy as jnp
from jax import lax
from jax.experimental import pallas as pl
from jax.experimental.pallas import tpu as pltpu
from jax.sharding import PartitionSpec as P


F32 = jnp.float32
BF16 = jnp.bfloat16
OFFSETS = ((-1, 0), (1, 0), (0, -1), (0, 1))
WHOLE = pl.BlockSpec(memory_space=pltpu.VMEM)
SCALARS = pl.BlockSpec(memory_space=pltpu.SMEM)
FAR = pl.BlockSpec(memory_space=pltpu.HBM)


def dot(a, b, over):
    return lax.dot_general(a, b, ((over[:1], over[1:]), ((), ())), preferred_element_type=F32)


def times_i(field, axis):
    shape = field.shape
    if axis == 0:
        field, axis = field.reshape(-1, 8, shape[1]), 1
        place = lax.broadcasted_iota(jnp.int32, (1, 8, shape[1]), 1)
    else:
        place = lax.broadcasted_iota(jnp.int32, (1, shape[1]), 1)
    size = field.shape[axis]
    after = pltpu.roll(field, size - 1, axis)
    before = pltpu.roll(field, 1, axis)
    return jnp.where((place & 1) == 0, -after, before).reshape(shape)


def forward_parts(coupling, motion):
    return dot(motion, coupling.reshape(-1, coupling.shape[-1]), (1, 1))


def adjoint_parts(coupling, load):
    return dot(load, jnp.concatenate([coupling[0], coupling[1]], axis=1), (1, 0))


def beside_turned(field, sign):
    turned = times_i(field.astype(F32), 0)
    return jnp.concatenate([field, (turned if sign > 0 else -turned).astype(BF16)], axis=1)


def forward_product(coupling, both):
    return dot(both, jnp.concatenate([coupling[0], coupling[1]], axis=1), (1, 1))


def adjoint_product(coupling, both):
    return dot(both, coupling.reshape(-1, coupling.shape[-1]), (1, 0))


def joined(parts, sign):
    half = parts.shape[1] // 2
    turned = times_i(parts[:, half:], 0)
    return parts[:, :half] + turned if sign > 0 else parts[:, :half] - turned


def map_of_blocks(map_ref, blocks):
    rows = map_ref.shape[0]
    panels = rows // blocks
    row = lax.broadcasted_iota(jnp.int32, (panels, rows), 0)
    column = lax.broadcasted_iota(jnp.int32, (panels, rows), 1)
    whole = map_ref[...]
    out = []
    for b in range(blocks):
        pick = (column == row * blocks + b).astype(F32).astype(BF16)
        out.append(dot(pick, whole, (1, 0)).astype(BF16))
    return out


def target(i, step, n):
    if step == 0:
        return i
    if step == 1:
        return i ^ 1
    if step == 2:
        return (((i + 1) ^ 1) + n - 1) % n
    return (i + step - 1) % n


def source(i, step, n):
    return target(i, step, n) if step < 3 else (i + n + 1 - step) % n


def exchange(x, step):
    n = lax.axis_size("gx")
    return lax.ppermute(x, "gx", [(i, target(i, step, n)) for i in range(n)])


def exchange_sides(x, axis, step):
    sizes = lax.axis_size("gx"), lax.axis_size("gy")
    pairs = []
    for x_at in range(sizes[0]):
        for y_at in range(sizes[1]):
            there = [x_at, y_at]
            other = target(there[axis], step, sizes[axis])
            if axis == 0 or abs(other - there[axis]) == 1:
                there[axis] = other
            else:
                there[0] ^= 1
            pairs.append((x_at * sizes[1] + y_at, there[0] * sizes[1] + there[1]))
    return lax.ppermute(x, ("gx", "gy"), pairs)


def far(x):
    return pltpu.with_memory_space_constraint(x, pltpu.HBM)


def edges(rows, cols, spot):
    sides = []
    for axis in range(2):
        even = 1 - spot[axis] % 2
        for up in (even, 1 - even):
            if axis == 0:
                sides.append([(up * (rows - 1), y, up) for y in range(cols)])
            else:
                sides.append([(x, up * (cols - 1), 2 + up) for x in range(rows)])
    return sides


def fetch_edges(which, sides, cols, coupling_far, coupling, arrive, first):
    moves = []
    for o in which:
        for x, y, d in sides[o]:
            i = len(moves)
            moves.append(pltpu.make_async_copy(coupling_far.at[x * cols + y, d + 1], coupling.at[i], arrive.at[first + i]))
            moves[-1].start()
    return moves


def panels_kernel(rows, cols, early, late, spot, joints, motion_far, load_far, coupling_far, map_far, *refs):
    motion_out, outs, refs = refs[0], refs[1 : 1 + len(early)], refs[1 + len(early) :]
    motion, load, maps, near_coupling, coupling, arrive = refs
    moves = [
        pltpu.make_async_copy(map_far, maps, arrive.at[0]),
        pltpu.make_async_copy(motion_far, motion, arrive.at[1]),
        pltpu.make_async_copy(load_far, load, arrive.at[2]),
    ]
    for move in moves:
        move.start()
    sides = edges(rows, cols, spot)
    more = fetch_edges(early, sides, cols, coupling_far, coupling, arrive, 3)
    later = fetch_edges(late, sides, cols, coupling_far, near_coupling, arrive, 3 + len(more))
    blocks, wide = motion.shape[:2]
    moves[0].wait()
    split = map_of_blocks(maps, blocks)
    moves[1].wait()
    motion_out[...] = sum(dot(split[b], motion[b], (1, 1)) for b in range(blocks)).astype(BF16)
    moves[2].wait()
    i = 0
    for o, out in zip(early, outs):
        for k, (x, y, d) in enumerate(sides[o]):
            out[pl.ds(k * wide, wide), :] = motion[x * cols + y]
            more[i].wait()
            link = joints[x, y, d].astype(F32)
            term = joined(adjoint_parts(coupling[i], load[x * cols + y]), -1)
            out[pl.ds((len(sides[o]) + k) * wide, wide), :] = (link * term).astype(BF16)
            i += 1
    for move in later:
        move.wait()


def edges_kernel(rows, cols, late, spot, joints, motion, load, maps, coupling, *refs):
    load_out, outs, (both,) = refs[0], refs[1 : 1 + len(late)], refs[1 + len(late) :]
    blocks, wide = motion.shape[:2]
    sides = edges(rows, cols, spot)
    split = map_of_blocks(maps, blocks)
    load_out[...] = sum(dot(split[b], load[b], (1, 1)) for b in range(blocks)).astype(BF16)
    for b in range(blocks):
        both[b] = beside_turned(load[b], -1)
    i = 0
    for o, out in zip(late, outs):
        for k, (x, y, d) in enumerate(sides[o]):
            out[pl.ds(k * wide, wide), :] = motion[x * cols + y]
            matrix = coupling[i] * joints[x, y, d].astype(BF16)
            term = adjoint_product(matrix, both[x * cols + y])
            out[pl.ds((len(sides[o]) + k) * wide, wide), :] = term.astype(BF16)
            i += 1


def pressure_kernel(n_gx, spot, hydro_ref, load_panels, *refs):
    pieces, (out_far, gathered, out, leave) = refs[:n_gx], refs[n_gx:]
    me = spot[0]
    panels, wide = load_panels.shape
    for step in range(n_gx):
        start = pl.multiple_of(source(me, step, n_gx) * panels, panels)
        gathered[0, pl.ds(start, panels), :] = pieces[step][...]
        gathered[1, pl.ds(start, panels), :] = times_i(pieces[step][...].astype(F32), 1).astype(BF16)
    fields = gathered[...].reshape(-1, wide)
    tiles = out.shape[0]
    moves = []
    for i in range(2):
        here = pl.ds(i * tiles // 2, tiles // 2)
        rows = pl.ds(i * tiles // 2 * panels, tiles // 2 * panels)
        hydro = jnp.concatenate([hydro_ref[0, rows, :], hydro_ref[1, rows, :]], axis=1)
        out[here, :panels, :] = dot(hydro, fields, (1, 0)).astype(BF16).reshape(-1, panels, wide)
        out[here, panels:, :] = jnp.broadcast_to(load_panels[...], (tiles // 2, panels, wide))
        moves.append(pltpu.make_async_copy(out.at[here], out_far.at[here], leave.at[i]))
        moves[-1].start()
    for move in moves:
        move.wait()


def reaction_kernel(n_gx, spot, hydro_ref, arrived, *refs):
    outs, (reacted,) = refs[:n_gx], refs[n_gx:]
    me = spot[0]
    panels = outs[0].shape[0]
    hydro = hydro_ref[...]
    loads = arrived[:, panels:, :].reshape(hydro.shape[1], -1)
    real = dot(hydro[0], loads, (0, 0))
    imag = dot(hydro[1], loads, (0, 0))
    reacted[...] = real - times_i(imag, 1)
    for step in range(n_gx):
        start = pl.multiple_of(target(me, step, n_gx) * panels, panels)
        outs[step][...] = reacted[pl.ds(start, panels), :]


def add_side(side, joints, valid, received, couplings, residual, multiplier):
    wide = residual.shape[1]
    for k, (b, x, y, d) in enumerate(side):
        matrix = couplings(k, b, d) * (joints[x, y, d].astype(F32) * valid).astype(BF16)
        motion = received[pl.ds(k * wide, wide), :]
        residual[b] += joined(forward_parts(matrix, motion), 1)
        terms = received[pl.ds((len(side) + k) * wide, wide), :]
        multiplier[b] += valid * terms.astype(F32)


def placed(cols, sides):
    return [[(x * cols + y, x, y, d) for x, y, d in side] for side in sides]


def beyond(spot, sizes, o):
    n, me = sizes[o // 2], spot[o // 2]
    other = target(me, 1 + o % 2, n)
    return (abs(me - other) <= 1).astype(F32) if n > 2 else F32(1 - o % 2)


def interior_kernel(rows, cols, sizes, early, late, spot, joints, motion_far, load_far, excitation_far, *refs):
    coupling_far, received, refs = refs[0], refs[1 : 1 + len(early)], refs[1 + len(early) :]
    residual_out, multiplier_out, own_far, outer, motion, load, excitation, coupling, own, arrive, leave = refs
    blocks = rows * cols
    moves = [
        pltpu.make_async_copy(motion_far, motion, arrive.at[0]),
        pltpu.make_async_copy(load_far, load, arrive.at[1]),
    ]
    for b in range(blocks):
        moves.append(pltpu.make_async_copy(coupling_far.at[b], coupling.at[b], arrive.at[2 + b]))
    moves.append(pltpu.make_async_copy(excitation_far, excitation, arrive.at[2 + blocks]))
    for move in moves:
        move.start()
    sides = edges(rows, cols, spot)
    later = fetch_edges(late, sides, cols, coupling_far, outer, arrive, 3 + blocks)
    moves[0].wait()
    moving = [beside_turned(motion[b], 1) for b in range(blocks)]
    moves[1].wait()
    loads = [beside_turned(load[b], -1) for b in range(blocks)]
    sent = []
    for b in range(blocks):
        moves[2 + b].wait()
        own[b] = forward_product(coupling[b, 0], moving[b])
        sent.append(pltpu.make_async_copy(own.at[b], own_far.at[b], leave.at[b]))
        sent[-1].start()
    moves[2 + blocks].wait()
    for x in range(rows):
        for y in range(cols):
            b = x * cols + y
            forward, adjoint = [], [(loads[b], coupling[b, 0])]
            for d in range(4):
                nx, ny = x + OFFSETS[d][0], y + OFFSETS[d][1]
                if 0 <= nx < rows and 0 <= ny < cols:
                    n = nx * cols + ny
                    forward.append((moving[n], coupling[b, d + 1] * joints[x, y, d].astype(BF16)))
                    adjoint.append((loads[n], coupling[n, (d ^ 1) + 1] * joints[nx, ny, d ^ 1].astype(BF16)))
            residual = own[b] - excitation[b].astype(F32)
            if forward:
                fields = jnp.concatenate([f for f, _ in forward], axis=1)
                matrix = jnp.concatenate([c[part] for _, c in forward for part in range(2)], axis=1)
                residual = residual + dot(fields, matrix, (1, 1))
            residual_out[b] = residual
            fields = jnp.concatenate([f for f, _ in adjoint], axis=1)
            matrix = jnp.concatenate([c[part] for _, c in adjoint for part in range(2)], axis=0)
            multiplier_out[b] = dot(fields, matrix, (1, 0))
    for o, ref in zip(early, received):
        side = placed(cols, sides)[o]
        add_side(side, joints, beyond(spot, sizes, o), ref, lambda k, b, d: coupling[b, d + 1], residual_out, multiplier_out)
    for move in sent + later:
        move.wait()


def boundary_kernel(rows, cols, sizes, lift, late, spot, joints, map_ref, coupling, residual, multiplier, arrived, *refs):
    received, (residual_out, multiplier_out, full, leave) = refs[: len(late)], refs[len(late) :]
    blocks, unknowns = rows * cols, residual.shape[2]
    panels = map_ref.shape[0] // blocks
    maps = jnp.concatenate(map_of_blocks(map_ref, blocks), axis=1)
    pressure = jnp.sum(arrived[:, :panels, :].astype(F32), axis=0).astype(BF16)
    forces = lift * dot(pressure, maps, (0, 0))
    for b in range(blocks):
        full[b] = residual[b] + forces[:, b * unknowns : (b + 1) * unknowns]
        multiplier_out[b] = multiplier[b]
    sides, first = placed(cols, edges(rows, cols, spot)), 0
    for o, ref in zip(late, received):
        at = first
        add_side(sides[o], joints, beyond(spot, sizes, o), ref, lambda k, b, d: coupling[at + k], full, multiplier_out)
        first += len(sides[o])
    move = pltpu.make_async_copy(full, residual_out, leave)
    move.start()
    move.wait()


def final_kernel(rows, cols, lift, map_ref, multiplier, own, *refs):
    reactions, (multiplier_out, sensitivity_out, full, leave) = refs[:-4], refs[-4:]
    blocks = rows * cols
    unknowns = own.shape[2]
    maps = jnp.concatenate(map_of_blocks(map_ref, blocks), axis=1)
    reaction = sum(r[...].astype(F32) for r in reactions).astype(BF16)
    scale = 1.0 / math.sqrt(own.shape[1] // 2 * unknowns)
    forces = lift * dot(reaction, maps, (0, 0))
    sent, sums = [], []
    for b in range(blocks):
        value = multiplier[b] + forces[:, b * unknowns : (b + 1) * unknowns]
        full[b] = value
        sent.append(pltpu.make_async_copy(full.at[b], multiplier_out.at[b], leave.at[b]))
        sent[-1].start()
        sums.append(jnp.sum((value * own[b]).reshape(-1, 8, unknowns), axis=0))
    for b in range(blocks):
        sensitivity_out[b // cols, b % cols] = jnp.sum(sums[b]) * scale
    for move in sent:
        move.wait()


def cost(flops, bytes_accessed):
    return pl.CostEstimate(flops=int(flops), bytes_accessed=int(bytes_accessed), transcendentals=0)


def shaped(dtype, *shape):
    return jax.ShapeDtypeStruct(shape, dtype)


def params(mebibytes):
    return pltpu.CompilerParams(vmem_limit_bytes=mebibytes * 1024 * 1024)


DMA = pltpu.SemaphoreType.DMA


def on_device(plate_motion, adjoint_load, excitation, coupling, joints, hydro, panel_map):
    rows, cols, cases, _, unknowns = plate_motion.shape
    panels = panel_map.shape[0]
    blocks, wide = rows * cols, 2 * cases
    n_gx, n_gy = lax.axis_size("gx"), lax.axis_size("gy")
    spot = jnp.stack([lax.axis_index("gx"), lax.axis_index("gy")])
    motion = plate_motion.reshape(blocks, wide, unknowns)
    load = adjoint_load.reshape(blocks, wide, unknowns)
    force = excitation.reshape(blocks, wide, unknowns)
    coupling = coupling.reshape(blocks, 5, 2, unknowns, unknowns)
    panel_map = panel_map.reshape(panels * blocks, unknowns)
    lift = math.sqrt(blocks * unknowns / panels)
    block_flops = 2 * wide * unknowns * unknowns * 2
    field = (blocks, wide, unknowns)

    counts = [cols, cols, rows, rows]
    early, late = (3,), (0, 1, 2)
    few, many = sum(counts[o] for o in early), sum(counts[o] for o in late)
    pair = (2, unknowns, unknowns)
    motion_panels, *payloads, near_motion, near_load, near_map, near_coupling = pl.pallas_call(
        functools.partial(panels_kernel, rows, cols, early, late),
        name="panels",
        out_shape=[pltpu.VMEM((panels, wide), BF16)]
        + [pltpu.VMEM((2 * counts[o] * wide, unknowns), BF16) for o in early]
        + [pltpu.VMEM(field, BF16)] * 2
        + [pltpu.VMEM(panel_map.shape, BF16), pltpu.VMEM((many,) + pair, BF16)],
        in_specs=[SCALARS, SCALARS] + [FAR] * 4,
        out_specs=[WHOLE] * (5 + len(early)),
        scratch_shapes=[pltpu.VMEM((few,) + pair, BF16), DMA((3 + few + many,))],
        compiler_params=params(16),
        cost_estimate=cost(4 * blocks * wide * unknowns * panels, 4 * blocks * wide * unknowns),
    )(spot, far(joints), far(motion), far(load), far(coupling), far(panel_map))
    pieces = [motion_panels] + [exchange(motion_panels, step) for step in range(1, n_gx)]
    fourth = exchange_sides(payloads[0], 1, 2)

    load_panels, *payloads = pl.pallas_call(
        functools.partial(edges_kernel, rows, cols, late),
        name="edges",
        out_shape=[pltpu.VMEM((panels, wide), BF16)]
        + [pltpu.VMEM((2 * counts[o] * wide, unknowns), BF16) for o in late],
        in_specs=[SCALARS, SCALARS] + [WHOLE] * 4,
        out_specs=[WHOLE] * (1 + len(late)),
        scratch_shapes=[pltpu.VMEM((blocks, wide, 2 * unknowns), BF16)],
        compiler_params=params(16),
        cost_estimate=cost(many * block_flops, 4 * blocks * wide * unknowns + 12 * blocks * unknowns**2),
    )(spot, far(joints), near_motion, near_load, near_map, near_coupling)
    (*payloads, load_panels) = lax.optimization_barrier((*payloads, load_panels))
    first, second = exchange_sides(payloads[0], 0, 1), exchange_sides(payloads[1], 0, 2)
    third = exchange_sides(payloads[2], 1, 1)

    parts = pl.pallas_call(
        functools.partial(pressure_kernel, n_gx),
        name="pressure",
        out_shape=pltpu.HBM((n_gy, 2 * panels, wide), BF16),
        in_specs=[SCALARS] + [WHOLE] * (2 + n_gx),
        out_specs=FAR,
        scratch_shapes=[pltpu.VMEM((2, n_gx * panels, wide), BF16), pltpu.VMEM((n_gy, 2 * panels, wide), BF16), DMA((2,))],
        compiler_params=params(16),
        cost_estimate=cost(2 * hydro.size * wide, 2 * hydro.size),
    )(spot, hydro, load_panels, *pieces)
    parts, fourth = lax.optimization_barrier((parts, fourth))
    arrived = lax.all_to_all(parts, "gy", 0, 0, tiled=True)

    residual, multiplier, own, outer = pl.pallas_call(
        functools.partial(interior_kernel, rows, cols, (n_gx, n_gy), early, late),
        name="interior",
        out_shape=[pltpu.VMEM(field, F32)] * 2
        + [pltpu.HBM(field, F32), pltpu.VMEM((many,) + pair, BF16)],
        in_specs=[SCALARS] * 2 + [FAR] * 4 + [WHOLE] * len(early),
        out_specs=[WHOLE] * 2 + [FAR, WHOLE],
        scratch_shapes=[pltpu.VMEM(field, BF16)] * 3
        + [pltpu.VMEM(coupling.shape, BF16), pltpu.VMEM(field, F32), DMA((3 + blocks + many,)), DMA((blocks,))],
        compiler_params=params(16),
        cost_estimate=cost(6 * blocks * block_flops, 20 * blocks * unknowns**2 + 18 * blocks * wide * unknowns),
    )(spot, far(joints), far(motion), far(load), far(force), far(coupling), fourth)
    arrived, residual, multiplier, own, outer = lax.optimization_barrier((arrived, residual, multiplier, own, outer))

    reaction_parts = pl.pallas_call(
        functools.partial(reaction_kernel, n_gx),
        name="reaction",
        out_shape=[pltpu.VMEM((panels, wide), F32)] * n_gx,
        in_specs=[SCALARS] + [WHOLE] * 2,
        out_specs=[WHOLE] * n_gx,
        scratch_shapes=[pltpu.VMEM((n_gx * panels, wide), F32)],
        compiler_params=params(16),
        cost_estimate=cost(2 * hydro.size * wide, 2 * hydro.size),
    )(spot, hydro, arrived)
    reactions = [reaction_parts[0]] + [exchange(reaction_parts[step], step) for step in range(1, n_gx)]

    residual, multiplier = pl.pallas_call(
        functools.partial(boundary_kernel, rows, cols, (n_gx, n_gy), lift, late),
        name="boundary",
        out_shape=[pltpu.HBM(field, F32), pltpu.VMEM(field, F32)],
        in_specs=[SCALARS] * 2 + [WHOLE] * (5 + len(late)),
        out_specs=[FAR, WHOLE],
        scratch_shapes=[pltpu.VMEM(field, F32), DMA],
        compiler_params=params(16),
        cost_estimate=cost(4 * blocks * block_flops, 10 * blocks * unknowns**2 + 18 * blocks * wide * unknowns),
    )(spot, far(joints), panel_map, outer, residual, multiplier, arrived, first, second, third)

    multiplier, sensitivity = pl.pallas_call(
        functools.partial(final_kernel, rows, cols, lift),
        name="final",
        out_shape=[pltpu.HBM(field, F32), shaped(F32, rows, cols)],
        in_specs=[WHOLE] * (3 + n_gx),
        out_specs=[FAR, SCALARS],
        scratch_shapes=[pltpu.VMEM(field, F32), DMA((blocks,))],
        compiler_params=params(16),
        cost_estimate=cost(4 * blocks * wide * unknowns * panels, 20 * blocks * wide * unknowns),
    )(panel_map, multiplier, own, *reactions)
    shape = plate_motion.shape
    return residual.reshape(shape), multiplier.reshape(shape), sensitivity


def solution(mesh):
    field = P("gx", "gy", None, None, None)
    placed = (
        field,
        field,
        field,
        P("gx", "gy", None, None, None, None),
        P("gx", "gy", None),
        P(None, "gx", "gy"),
        P(("gx", "gy"), None, None, None),
    )
    return jax.shard_map(on_device, mesh=mesh, in_specs=placed, out_specs=(field, field, P("gx", "gy")), check_vma=False)
```

time: 37.2 us -> 35.6 us (0.957)
  the two profiles are of different devices: /device:TPU:5 before, /device:TPU:0 now
where the time goes in v5:
time: 35.6 us; the launch traced here: 35.2 us
  starting transfers between devices  16.6 us (47%)
  Pallas kernels  14.8 us (42%)
  waiting for transfers between devices  2.93 us (8%)
  between operations  0.73 us (2%)
    all_to_all x1, starting transfers between devices, on_device(): arrived = lax.all_to_all(parts, 'gy', 0, 0, tiled=True)  7.5 us
    ppermute x6, starting transfers between devices, exchange(): return lax.ppermute(x, 'gx', [(i, target(i, step, n)) for i in range(n)])  4.99 us
    ppermute x4, starting transfers between devices, exchange_sides(): return lax.ppermute(x, ('gx', 'gy'), pairs)  4.14 us
    pallas_call x1, Pallas kernels, on_device(): pl.pallas_call(functools.partial(interior_kernel, rows, cols, (n_gx, n_gy...  4.04 us
    pallas_call x1, Pallas kernels, on_device(): pl.pallas_call(functools.partial(panels_kernel, rows, cols, early, late),...  2.59 us
    ppermute x6, waiting for transfers between devices, exchange(): return lax.ppermute(x, 'gx', [(i, target(i, step, n)) for i in range(n)])  2.21 us
    pallas_call x1, Pallas kernels, on_device(): pl.pallas_call(functools.partial(boundary_kernel, rows, cols, (n_gx, n_gy...  2.16 us
    pallas_call x1, Pallas kernels, on_device(): pl.pallas_call(functools.partial(edges_kernel, rows, cols, late), name='e...  1.88 us
  transfers between devices with their start and end apart: 11, of which 4 were waited for; matrix products, arithmetic and copies ran while one was open for 0% of the time, Pallas kernels for 30%

profile of v5, /device:TPU:0, one launch (start us, length us, event | category | flops | bytes accessed | tf_op | source)
XLA Modules:
  0.0 35.2 jit_solution(9644336362756250528)
XLA Ops:
  0.6 0.1 pad_add_fusion.spot
  0.7 0.0 copy-start.1
  0.7 2.6 %panels.1 = (bf16[32,256]{1,0:T(8,128)(2,1)S(1)}, bf16[1024,128]{1,0:T(8,128)(2,1)S(1)}, bf16[4,256,128]{2,1,0:T(8,128)(2,1)S(1)}, bf16[4,256,128]{2,1,0:T(8,128...) custom-call(s32[2]{0:T(128)S(1)} %pad_add_fusion.spot, s32[2,2,4]{2,1,0:T(2,128)} %joints.7, ...), custom_call_target="tpu_custom_call" | custom-call | flops 16777216 | bytes 524288 | tf_op jit(solution)/shard_map/panels/pallas_call | solution.py:371
  3.3 0.5 %collective-permute-start.3 = (bf16[1024,128]{1,0:T(8,128)(2,1)S(1)}, bf16[1024,128]{1,0:T(8,128)(2,1)S(1)}, u32[]{:S(2)}, u32[]{:S(2)}) collective-permute-start(bf16[1024,128]{1,0:T(8,128)(2,1)S(1)} %get-tuple-element.46), channel_id=1, source_target_pairs={{0,8},{1,2},{2,1},{3,4},{4,3},{5,6},{6,5},{7,15},{8,0},{9,10},{10,... | collective-permute-start | bytes 786440 | tf_op jit(solution)/shard_map/ppermute | solution.py:108
  3.8 2.6 %collective-permute-start.2 = (bf16[32,256]{1,0:T(8,128)(2,1)S(1)}, bf16[32,256]{1,0:T(8,128)(2,1)S(1)}, u32[]{:S(2)}, u32[]{:S(2)}) collective-permute-start(bf16[32,256]{1,0:T(8,128)(2,1)S(1)} %get-tuple-element.45.refs_0_), channel_id=1, source_target_pairs={{0,16},{8,24},{16,0},{24,8},{1,17},{9,25},{17,1},{25,9},{2,18},{10... | collective-permute-start | bytes 49160 | tf_op jit(solution)/shard_map/ppermute | solution.py:93
  6.4 0.1 collective-permute-start.1
  6.5 0.1 collective-permute-start
  6.6 1.9 %edges.1 = (bf16[32,256]{1,0:T(8,128)(2,1)S(1)}, bf16[1024,128]{1,0:T(8,128)(2,1)}, bf16[1024,128]{1,0:T(8,128)(2,1)S(1)}, bf16[1024,128]{1,0:T(8,128)(2,1)S(1)}) custom-call(s32[2]{0:T(128)S(1)} %pad_add_fusion.spot, s32[2,2,4]{2,1,0:T(2,128)} %joints.7, bf16[4,256,128]{2,1,0:T(8,128)(2,1)S(1)} %get-tuple-element.36.motion, ...), custom_call_target="tpu_custom_call" | custom-call | flops 100663296 | bytes 1310720 | tf_op jit(solution)/shard_map/edges/pallas_call | solution.py:387
  8.5 0.0 collective-permute-done.2.refs_3_
  8.5 1.1 %collective-permute-done.1.refs_2_ = bf16[32,256]{1,0:T(8,128)(2,1)S(1)} collective-permute-done((bf16[32,256]{1,0:T(8,128)(2,1)S(1)}, bf16[32,256]{1,0:T(8,128)(2,1)S(1)}, u32[]{:S(2)}, u32[]{:S(2)}) %collective-permute-start.1) | collective-permute-done | bytes 16416 | tf_op jit(solution)/shard_map/ppermute | solution.py:93
  9.6 0.0 collective-permute-done.refs_1_
  9.6 0.0 copy-done.1
  9.6 1.6 %pressure.1 = bf16[8,64,256]{2,1,0:T(8,128)(2,1)} custom-call(s32[2]{0:T(128)S(1)} %pad_add_fusion.spot, bf16[2,256,128]{2,1,0:T(8,128)(2,1)S(1)} %copy-done.1, bf16[32,256]{1,0:T(8,128)(2,1)S(1)} %get-tuple-element.44.load_panels, bf16[32,256]{1,0:T(8,128)(2,1)S(1)} %get-tuple-element.45.refs_0_, bf16[32,256]{1,0:T(8,128)(2,1)S(1)} %collective-permute-done.refs_1_, ...), custom_call_target="tpu_custom_call" | custom-call | flops 33554432 | bytes 131072 | tf_op jit(solution)/shard_map/pressure/pallas_call | solution.py:402
  11.1 0.0 collective-permute-done.3.refs_1_
  11.1 7.5 %all-to-all-start = ((bf16[8,64,256]{2,1,0:T(8,128)(2,1)}), bf16[8,64,256]{2,1,0:T(8,128)(2,1)S(1)}, u32[]{:S(2)}, u32[]{:S(2)}) async-start(bf16[8,64,256]{2,1,0:T(8,128)(2,1)} %pressure.1), calls=%async_computation | async-start | bytes 524288 | tf_op jit(solution)/shard_map/all_to_all | solution.py:413
  18.6 0.0 collective-permute-start.4
  18.7 1.6 %collective-permute-start.5 = (bf16[1024,128]{1,0:T(8,128)(2,1)S(1)}, bf16[1024,128]{1,0:T(8,128)(2,1)S(1)}, u32[]{:S(2)}, u32[]{:S(2)}) collective-permute-start(bf16[1024,128]{1,0:T(8,128)(2,1)S(1)} %get-tuple-element.58), channel_id=1, source_target_pairs={{0,24},{1,25},{2,26},{3,27},{4,28},{5,29},{6,30},{7,31},{8,16},{9,... | collective-permute-start | bytes 786440 | tf_op jit(solution)/shard_map/ppermute | solution.py:108
  20.3 2.0 %collective-permute-start.6 = (bf16[1024,128]{1,0:T(8,128)(2,1)S(1)}, bf16[1024,128]{1,0:T(8,128)(2,1)S(1)}, u32[]{:S(2)}, u32[]{:S(2)}) collective-permute-start(bf16[1024,128]{1,0:T(8,128)(2,1)S(1)} %get-tuple-element.59), channel_id=1, source_target_pairs={{0,1},{1,0},{2,3},{3,2},{4,5},{5,4},{6,7},{7,6},{8,9},{9,8},{10,11... | collective-permute-start | bytes 786440 | tf_op jit(solution)/shard_map/ppermute | solution.py:108
  22.3 0.0 copy-start.2
  22.3 4.0 %interior.1 = (f32[4,256,128]{2,1,0:T(8,128)S(1)}, f32[4,256,128]{2,1,0:T(8,128)S(1)}, f32[4,256,128]{2,1,0:T(8,128)}, bf16[6,2,128,128]{3,2,1,0:T(8,128)(2,1)S(1)}) custom-call(s32[2]{0:T(128)S(1)} %pad_add_fusion.spot, s32[2,2,4]{2,1,0:T(2,128)} %joints.7, bf16[4,256,128]{2,1,0:T(8,128)(2,1)} %bitcast.15, bf16[4,256,128]{2,1,0:T(8,128)(2,1)} %bitcast.17, ...), custom_call_target="tpu_custom_call" | custom-call | flops 402653184 | bytes 3670016 | tf_op jit(solution)/shard_map/interior/pallas_call | solution.py:415
  26.3 0.7 %all-to-all-done.arrived = bf16[8,64,256]{2,1,0:T(8,128)(2,1)S(1)} async-done(((bf16[8,64,256]{2,1,0:T(8,128)(2,1)}), bf16[8,64,256]{2,1,0:T(8,128)(2,1)S(1)}, u32[]{:S(2)}, u32[]{:S(2)}) %all-to-all-start) | async-done | bytes 262176 | tf_op jit(solution)/shard_map/all_to_all | solution.py:413
  27.0 0.9 %reaction.1 = (f32[32,256]{1,0:T(8,128)S(1)}, f32[32,256]{1,0:T(8,128)S(1)}, f32[32,256]{1,0:T(8,128)S(1)}, f32[32,256]{1,0:T(8,128)S(1)}) custom-call(s32[2]{0:T(128)S(1)} %pad_add_fusion.spot, bf16[2,256,128]{2,1,0:T(8,128)(2,1)S(1)} %copy-done.1, bf16[8,64,256]{2,1,0:T(8,128)(2,1)S(1)} %all-to-all-done.arrived), custom_call_target="tpu_custom_call" | custom-call | flops 33554432 | bytes 131072 | tf_op jit(solution)/shard_map/reaction/pallas_call | solution.py:429
  27.9 0.0 copy-start
  27.9 0.1 collective-permute-start.7
  27.9 1.6 %collective-permute-start.8 = (f32[32,256]{1,0:T(8,128)S(1)}, f32[32,256]{1,0:T(8,128)S(1)}, u32[]{:S(2)}, u32[]{:S(2)}) collective-permute-start(f32[32,256]{1,0:T(8,128)S(1)} %get-tuple-element.65), channel_id=1, source_target_pairs={{0,24},{8,16},{16,8},{24,0},{1,25},{9,17},{17,9},{25,1},{2,26},{10... | collective-permute-start | bytes 98312 | tf_op jit(solution)/shard_map/ppermute | solution.py:93
  29.5 0.0 collective-permute-done.4.refs_0_
  29.5 0.5 %collective-permute-start.9 = (f32[32,256]{1,0:T(8,128)S(1)}, f32[32,256]{1,0:T(8,128)S(1)}, u32[]{:S(2)}, u32[]{:S(2)}) collective-permute-start(f32[32,256]{1,0:T(8,128)S(1)} %get-tuple-element.66), channel_id=1, source_target_pairs={{0,16},{8,24},{16,0},{24,8},{1,17},{9,25},{17,1},{25,9},{2,18},{10... | collective-permute-start | bytes 98312 | tf_op jit(solution)/shard_map/ppermute | solution.py:93
  30.1 0.0 collective-permute-done.5.refs_1_
  30.1 0.1 collective-permute-done.6.refs_2_
  30.1 0.0 copy-done.2
  30.2 2.2 %boundary.1 = (f32[4,256,128]{2,1,0:T(8,128)}, f32[4,256,128]{2,1,0:T(8,128)S(1)}) custom-call(s32[2]{0:T(128)S(1)} %pad_add_fusion.spot, s32[2,2,4]{2,1,0:T(2,128)} %joints.7, bf16[128,128]{1,0:T(8,128)(2,1)S(1)} %bitcast.10, bf16[6,2,128,128]{3,2,1,0:T(8,128)(2,1)S(1)} %get-tuple-element.53.coupling, f32[4,256,128]{2,1,0:T(8,128)S(1)} %get-tuple-element.54.residual, ...), custom_call_target="tpu_custom_call" | custom-call | flops 268435456 | bytes 3014656 | tf_op jit(solution)/shard_map/boundary/pallas_call | solution.py:441
  32.3 0.0 collective-permute-done.7.refs_1_
  32.3 0.0 collective-permute-done.8.refs_2_
  32.3 1.1 %collective-permute-done.9.refs_3_ = f32[32,256]{1,0:T(8,128)S(1)} collective-permute-done((f32[32,256]{1,0:T(8,128)S(1)}, f32[32,256]{1,0:T(8,128)S(1)}, u32[]{:S(2)}, u32[]{:S(2)}) %collective-permute-start.9) | collective-permute-done | bytes 32800 | tf_op jit(solution)/shard_map/ppermute | solution.py:93
  33.5 0.0 copy-done
  33.5 1.7 %final.1 = (f32[4,256,128]{2,1,0:T(8,128)}, f32[2,2]{1,0:T(2,128)}) custom-call(bf16[128,128]{1,0:T(8,128)(2,1)S(1)} %bitcast.11, f32[4,256,128]{2,1,0:T(8,128)S(1)} %get-tuple-element.61.multiplier, f32[4,256,128]{2,1,0:T(8,128)S(1)} %copy-done, f32[32,256]{1,0:T(8,128)S(1)} %get-tuple-element.63.refs_0_, f32[32,256]{1,0:T(8,128)S(1)} %collective-permute-done.7.refs_1_, ...), custom_call_target="tpu_custom_call" | custom-call | flops 16777216 | bytes 2621440 | tf_op jit(solution)/shard_map/final/pallas_call | solution.py:452
Async XLA Ops:
  0.7 8.9 %copy-start.1 = (bf16[2,256,128]{2,1,0:T(8,128)(2,1)S(1)}, bf16[2,256,128]{2,1,0:T(8,128)(2,1)}, u32[]{:S(2)}) copy-start(bf16[2,256,128]{2,1,0:T(8,128)(2,1)} %hydro_ref.3) | copy-start | bytes 393220
  3.3 7.8 %collective-permute-start.3 = (bf16[1024,128]{1,0:T(8,128)(2,1)S(1)}, bf16[1024,128]{1,0:T(8,128)(2,1)S(1)}, u32[]{:S(2)}, u32[]{:S(2)}) collective-permute-start(bf16[1024,128]{1,0:T(8,128)(2,1)S(1)} %get-tuple-element.46), channel_id=1, source_target_pairs={{0,8},{1,2},{2,1},{3,4},{4,3},{5,6},{6,5},{7,15},{8,0},{9,10},{10,... | collective-permute-start | bytes 786440 | tf_op jit(solution)/shard_map/ppermute | solution.py:108
  3.8 4.7 %collective-permute-start.2 = (bf16[32,256]{1,0:T(8,128)(2,1)S(1)}, bf16[32,256]{1,0:T(8,128)(2,1)S(1)}, u32[]{:S(2)}, u32[]{:S(2)}) collective-permute-start(bf16[32,256]{1,0:T(8,128)(2,1)S(1)} %get-tuple-element.45.refs_0_), channel_id=1, source_target_pairs={{0,16},{8,24},{16,0},{24,8},{1,17},{9,25},{17,1},{25,9},{2,18},{10... | collective-permute-start | bytes 49160 | tf_op jit(solution)/shard_map/ppermute | solution.py:93
  6.4 3.2 %collective-permute-start.1 = (bf16[32,256]{1,0:T(8,128)(2,1)S(1)}, bf16[32,256]{1,0:T(8,128)(2,1)S(1)}, u32[]{:S(2)}, u32[]{:S(2)}) collective-permute-start(bf16[32,256]{1,0:T(8,128)(2,1)S(1)} %get-tuple-element.45.refs_0_), channel_id=1, source_target_pairs={{0,24},{8,16},{16,8},{24,0},{1,25},{9,17},{17,9},{25,1},{2,26},{10... | collective-permute-start | bytes 49160 | tf_op jit(solution)/shard_map/ppermute | solution.py:93
  6.5 3.1 %collective-permute-start = (bf16[32,256]{1,0:T(8,128)(2,1)S(1)}, bf16[32,256]{1,0:T(8,128)(2,1)S(1)}, u32[]{:S(2)}, u32[]{:S(2)}) collective-permute-start(bf16[32,256]{1,0:T(8,128)(2,1)S(1)} %get-tuple-element.45.refs_0_), channel_id=1, source_target_pairs={{0,8},{8,0},{16,24},{24,16},{1,9},{9,1},{17,25},{25,17},{2,10},{10... | collective-permute-start | bytes 49160 | tf_op jit(solution)/shard_map/ppermute | solution.py:93
  11.1 15.8 %all-to-all-start = ((bf16[8,64,256]{2,1,0:T(8,128)(2,1)}), bf16[8,64,256]{2,1,0:T(8,128)(2,1)S(1)}, u32[]{:S(2)}, u32[]{:S(2)}) async-start(bf16[8,64,256]{2,1,0:T(8,128)(2,1)} %pressure.1), calls=%async_computation | async-start | bytes 524288 | tf_op jit(solution)/shard_map/all_to_all | solution.py:413
  18.6 10.9 %collective-permute-start.4 = (bf16[1024,128]{1,0:T(8,128)(2,1)}, bf16[1024,128]{1,0:T(8,128)(2,1)S(1)}, u32[]{:S(2)}, u32[]{:S(2)}) collective-permute-start(bf16[1024,128]{1,0:T(8,128)(2,1)} %get-tuple-element.57), channel_id=1, source_target_pairs={{0,8},{1,9},{2,10},{3,11},{4,12},{5,13},{6,14},{7,15},{8,0},{9,1},... | collective-permute-start | bytes 786440 | tf_op jit(solution)/shard_map/ppermute | solution.py:108
  18.7 11.4 %collective-permute-start.5 = (bf16[1024,128]{1,0:T(8,128)(2,1)S(1)}, bf16[1024,128]{1,0:T(8,128)(2,1)S(1)}, u32[]{:S(2)}, u32[]{:S(2)}) collective-permute-start(bf16[1024,128]{1,0:T(8,128)(2,1)S(1)} %get-tuple-element.58), channel_id=1, source_target_pairs={{0,24},{1,25},{2,26},{3,27},{4,28},{5,29},{6,30},{7,31},{8,16},{9,... | collective-permute-start | bytes 786440 | tf_op jit(solution)/shard_map/ppermute | solution.py:108
  20.3 9.9 %collective-permute-start.6 = (bf16[1024,128]{1,0:T(8,128)(2,1)S(1)}, bf16[1024,128]{1,0:T(8,128)(2,1)S(1)}, u32[]{:S(2)}, u32[]{:S(2)}) collective-permute-start(bf16[1024,128]{1,0:T(8,128)(2,1)S(1)} %get-tuple-element.59), channel_id=1, source_target_pairs={{0,1},{1,0},{2,3},{3,2},{4,5},{5,4},{6,7},{7,6},{8,9},{9,8},{10,11... | collective-permute-start | bytes 786440 | tf_op jit(solution)/shard_map/ppermute | solution.py:108
  22.3 7.9 %copy-start.2 = (bf16[32,2,2,128]{3,2,1,0:T(2,128)(2,1)S(1)}, bf16[32,2,2,128]{3,2,1,0:T(2,128)(2,1)}, u32[]{:S(2)}) copy-start(bf16[32,2,2,128]{3,2,1,0:T(2,128)(2,1)} %param.13) | copy-start | bytes 98308
  27.9 5.6 %copy-start = (f32[4,256,128]{2,1,0:T(8,128)S(1)}, f32[4,256,128]{2,1,0:T(8,128)}, u32[]{:S(2)}) copy-start(f32[4,256,128]{2,1,0:T(8,128)} %get-tuple-element.62.own) | copy-start | bytes 1572868
  27.9 4.5 %collective-permute-start.7 = (f32[32,256]{1,0:T(8,128)S(1)}, f32[32,256]{1,0:T(8,128)S(1)}, u32[]{:S(2)}, u32[]{:S(2)}) collective-permute-start(f32[32,256]{1,0:T(8,128)S(1)} %get-tuple-element.64), channel_id=1, source_target_pairs={{0,8},{8,0},{16,24},{24,16},{1,9},{9,1},{17,25},{25,17},{2,10},{10... | collective-permute-start | bytes 98312 | tf_op jit(solution)/shard_map/ppermute | solution.py:93
  27.9 4.4 %collective-permute-start.8 = (f32[32,256]{1,0:T(8,128)S(1)}, f32[32,256]{1,0:T(8,128)S(1)}, u32[]{:S(2)}, u32[]{:S(2)}) collective-permute-start(f32[32,256]{1,0:T(8,128)S(1)} %get-tuple-element.65), channel_id=1, source_target_pairs={{0,24},{8,16},{16,8},{24,0},{1,25},{9,17},{17,9},{25,1},{2,26},{10... | collective-permute-start | bytes 98312 | tf_op jit(solution)/shard_map/ppermute | solution.py:93
  29.5 3.9 %collective-permute-start.9 = (f32[32,256]{1,0:T(8,128)S(1)}, f32[32,256]{1,0:T(8,128)S(1)}, u32[]{:S(2)}, u32[]{:S(2)}) collective-permute-start(f32[32,256]{1,0:T(8,128)S(1)} %get-tuple-element.66), channel_id=1, source_target_pairs={{0,16},{8,24},{16,0},{24,8},{1,17},{9,25},{17,1},{25,9},{2,18},{10... | collective-permute-start | bytes 98312 | tf_op jit(solution)/shard_map/ppermute | solution.py:93

commit v6 on v5

--- a/solution.py
+++ b/solution.py
@@ -13,7 +13,6 @@
 BF16 = jnp.bfloat16
 OFFSETS = ((-1, 0), (1, 0), (0, -1), (0, 1))
 WHOLE = pl.BlockSpec(memory_space=pltpu.VMEM)
-SCALARS = pl.BlockSpec(memory_space=pltpu.SMEM)
 FAR = pl.BlockSpec(memory_space=pltpu.HBM)
 
 
@@ -124,6 +123,10 @@
     return sides
 
 
+def here_on_mesh():
+    return lax.axis_index("gx"), lax.axis_index("gy")
+
+
 def fetch_edges(which, sides, cols, coupling_far, coupling, arrive, first):
     moves = []
     for o in which:
@@ -134,42 +137,48 @@
     return moves
 
 
-def panels_kernel(rows, cols, early, late, spot, joints, motion_far, load_far, coupling_far, map_far, *refs):
+def panels_kernel(rows, cols, early, late, joints_far, motion_far, load_far, coupling_far, map_far, *refs):
     motion_out, outs, refs = refs[0], refs[1 : 1 + len(early)], refs[1 + len(early) :]
-    motion, load, maps, near_coupling, coupling, arrive = refs
+    motion, load, maps, near_coupling, coupling, joints, arrive = refs
     moves = [
         pltpu.make_async_copy(map_far, maps, arrive.at[0]),
         pltpu.make_async_copy(motion_far, motion, arrive.at[1]),
         pltpu.make_async_copy(load_far, load, arrive.at[2]),
+        pltpu.make_async_copy(joints_far, joints, arrive.at[3]),
     ]
     for move in moves:
         move.start()
-    sides = edges(rows, cols, spot)
-    more = fetch_edges(early, sides, cols, coupling_far, coupling, arrive, 3)
-    later = fetch_edges(late, sides, cols, coupling_far, near_coupling, arrive, 3 + len(more))
+    sides = edges(rows, cols, here_on_mesh())
+    more = fetch_edges(early, sides, cols, coupling_far, coupling, arrive, 4)
+    later = fetch_edges(late, sides, cols, coupling_far, near_coupling, arrive, 4 + len(more))
     blocks, wide = motion.shape[:2]
     moves[0].wait()
     split = map_of_blocks(maps, blocks)
     moves[1].wait()
     motion_out[...] = sum(dot(split[b], motion[b], (1, 1)) for b in range(blocks)).astype(BF16)
     moves[2].wait()
+    moves[3].wait()
     i = 0
     for o, out in zip(early, outs):
         for k, (x, y, d) in enumerate(sides[o]):
             out[pl.ds(k * wide, wide), :] = motion[x * cols + y]
             more[i].wait()
-            link = joints[x, y, d].astype(F32)
-            term = joined(adjoint_parts(coupling[i], load[x * cols + y]), -1)
-            out[pl.ds((len(sides[o]) + k) * wide, wide), :] = (link * term).astype(BF16)
+            matrix = coupling[i] * joints[x, y, d].astype(BF16)
+            term = joined(adjoint_parts(matrix, load[x * cols + y]), -1)
+            out[pl.ds((len(sides[o]) + k) * wide, wide), :] = term.astype(BF16)
             i += 1
-    for move in later:
-        move.wait()
-
-
-def edges_kernel(rows, cols, late, spot, joints, motion, load, maps, coupling, *refs):
+    i = 0
+    for o in late:
+        for x, y, d in sides[o]:
+            later[i].wait()
+            near_coupling[i] = near_coupling[i] * joints[x, y, d].astype(BF16)
+            i += 1
+
+
+def edges_kernel(rows, cols, late, motion, load, maps, coupling, *refs):
     load_out, outs, (both,) = refs[0], refs[1 : 1 + len(late)], refs[1 + len(late) :]
     blocks, wide = motion.shape[:2]
-    sides = edges(rows, cols, spot)
+    sides = edges(rows, cols, here_on_mesh())
     split = map_of_blocks(maps, blocks)
     load_out[...] = sum(dot(split[b], load[b], (1, 1)) for b in range(blocks)).astype(BF16)
     for b in range(blocks):
@@ -178,15 +187,14 @@
     for o, out in zip(late, outs):
         for k, (x, y, d) in enumerate(sides[o]):
             out[pl.ds(k * wide, wide), :] = motion[x * cols + y]
-            matrix = coupling[i] * joints[x, y, d].astype(BF16)
-            term = adjoint_product(matrix, both[x * cols + y])
+            term = adjoint_product(coupling[i], both[x * cols + y])
             out[pl.ds((len(sides[o]) + k) * wide, wide), :] = term.astype(BF16)
             i += 1
 
 
-def pressure_kernel(n_gx, spot, hydro_ref, load_panels, *refs):
+def pressure_kernel(n_gx, hydro_ref, load_panels, *refs):
     pieces, (out_far, gathered, out, leave) = refs[:n_gx], refs[n_gx:]
-    me = spot[0]
+    me = lax.axis_index("gx")
     panels, wide = load_panels.shape
     for step in range(n_gx):
         start = pl.multiple_of(source(me, step, n_gx) * panels, panels)
@@ -207,9 +215,9 @@
         move.wait()
 
 
-def reaction_kernel(n_gx, spot, hydro_ref, arrived, *refs):
+def reaction_kernel(n_gx, hydro_ref, arrived, *refs):
     outs, (reacted,) = refs[:n_gx], refs[n_gx:]
-    me = spot[0]
+    me = lax.axis_index("gx")
     panels = outs[0].shape[0]
     hydro = hydro_ref[...]
     loads = arrived[:, panels:, :].reshape(hydro.shape[1], -1)
@@ -221,12 +229,11 @@
         outs[step][...] = reacted[pl.ds(start, panels), :]
 
 
-def add_side(side, joints, valid, received, couplings, residual, multiplier):
+def add_side(side, valid, received, couplings, residual, multiplier):
     wide = residual.shape[1]
     for k, (b, x, y, d) in enumerate(side):
-        matrix = couplings(k, b, d) * (joints[x, y, d].astype(F32) * valid).astype(BF16)
         motion = received[pl.ds(k * wide, wide), :]
-        residual[b] += joined(forward_parts(matrix, motion), 1)
+        residual[b] += joined(forward_parts(couplings(k, x, y, d), motion), 1)
         terms = received[pl.ds((len(side) + k) * wide, wide), :]
         multiplier[b] += valid * terms.astype(F32)
 
@@ -241,10 +248,10 @@
     return (abs(me - other) <= 1).astype(F32) if n > 2 else F32(1 - o % 2)
 
 
-def interior_kernel(rows, cols, sizes, early, late, spot, joints, motion_far, load_far, excitation_far, *refs):
+def interior_kernel(rows, cols, sizes, early, late, joints_far, motion_far, load_far, excitation_far, *refs):
     coupling_far, received, refs = refs[0], refs[1 : 1 + len(early)], refs[1 + len(early) :]
-    residual_out, multiplier_out, own_far, outer, motion, load, excitation, coupling, own, arrive, leave = refs
-    blocks = rows * cols
+    residual_out, multiplier_out, own_far, outer, motion, load, excitation, coupling, own, joints, arrive, leave = refs
+    blocks, spot = rows * cols, here_on_mesh()
     moves = [
         pltpu.make_async_copy(motion_far, motion, arrive.at[0]),
         pltpu.make_async_copy(load_far, load, arrive.at[1]),
@@ -252,10 +259,11 @@
     for b in range(blocks):
         moves.append(pltpu.make_async_copy(coupling_far.at[b], coupling.at[b], arrive.at[2 + b]))
     moves.append(pltpu.make_async_copy(excitation_far, excitation, arrive.at[2 + blocks]))
+    moves.append(pltpu.make_async_copy(joints_far, joints, arrive.at[3 + blocks]))
     for move in moves:
         move.start()
     sides = edges(rows, cols, spot)
-    later = fetch_edges(late, sides, cols, coupling_far, outer, arrive, 3 + blocks)
+    later = fetch_edges(late, sides, cols, coupling_far, outer, arrive, 4 + blocks)
     moves[0].wait()
     moving = [beside_turned(motion[b], 1) for b in range(blocks)]
     moves[1].wait()
@@ -267,6 +275,7 @@
         sent.append(pltpu.make_async_copy(own.at[b], own_far.at[b], leave.at[b]))
         sent[-1].start()
     moves[2 + blocks].wait()
+    moves[3 + blocks].wait()
     for x in range(rows):
         for y in range(cols):
             b = x * cols + y
@@ -287,15 +296,26 @@
             matrix = jnp.concatenate([c[part] for _, c in adjoint for part in range(2)], axis=0)
             multiplier_out[b] = dot(fields, matrix, (1, 0))
     for o, ref in zip(early, received):
-        side = placed(cols, sides)[o]
-        add_side(side, joints, beyond(spot, sizes, o), ref, lambda k, b, d: coupling[b, d + 1], residual_out, multiplier_out)
-    for move in sent + later:
+        valid = beyond(spot, sizes, o)
+
+        def linked(k, x, y, d, valid=valid):
+            return coupling[x * cols + y, d + 1] * (valid * joints[x, y, d].astype(F32)).astype(BF16)
+
+        add_side(placed(cols, sides)[o], valid, ref, linked, residual_out, multiplier_out)
+    i = 0
+    for o in late:
+        valid = beyond(spot, sizes, o)
+        for x, y, d in sides[o]:
+            later[i].wait()
+            outer[i] = outer[i] * (valid * joints[x, y, d].astype(F32)).astype(BF16)
+            i += 1
+    for move in sent:
         move.wait()
 
 
-def boundary_kernel(rows, cols, sizes, lift, late, spot, joints, map_ref, coupling, residual, multiplier, arrived, *refs):
+def boundary_kernel(rows, cols, sizes, lift, late, map_ref, coupling, residual, multiplier, arrived, *refs):
     received, (residual_out, multiplier_out, full, leave) = refs[: len(late)], refs[len(late) :]
-    blocks, unknowns = rows * cols, residual.shape[2]
+    blocks, unknowns, spot = rows * cols, residual.shape[2], here_on_mesh()
     panels = map_ref.shape[0] // blocks
     maps = jnp.concatenate(map_of_blocks(map_ref, blocks), axis=1)
     pressure = jnp.sum(arrived[:, :panels, :].astype(F32), axis=0).astype(BF16)
@@ -306,7 +326,7 @@
     sides, first = placed(cols, edges(rows, cols, spot)), 0
     for o, ref in zip(late, received):
         at = first
-        add_side(sides[o], joints, beyond(spot, sizes, o), ref, lambda k, b, d: coupling[at + k], full, multiplier_out)
+        add_side(sides[o], beyond(spot, sizes, o), ref, lambda k, x, y, d: coupling[at + k], full, multiplier_out)
         first += len(sides[o])
     move = pltpu.make_async_copy(full, residual_out, leave)
     move.start()
@@ -314,7 +334,7 @@
 
 
 def final_kernel(rows, cols, lift, map_ref, multiplier, own, *refs):
-    reactions, (multiplier_out, sensitivity_out, full, leave) = refs[:-4], refs[-4:]
+    reactions, (multiplier_out, sensitivity_out, full, sensitivity, leave) = refs[:-5], refs[-5:]
     blocks = rows * cols
     unknowns = own.shape[2]
     maps = jnp.concatenate(map_of_blocks(map_ref, blocks), axis=1)
@@ -329,7 +349,9 @@
         sent[-1].start()
         sums.append(jnp.sum((value * own[b]).reshape(-1, 8, unknowns), axis=0))
     for b in range(blocks):
-        sensitivity_out[b // cols, b % cols] = jnp.sum(sums[b]) * scale
+        sensitivity[b // cols, b % cols] = jnp.sum(sums[b]) * scale
+    sent.append(pltpu.make_async_copy(sensitivity, sensitivity_out, leave.at[blocks]))
+    sent[-1].start()
     for move in sent:
         move.wait()
 
@@ -354,7 +376,6 @@
     panels = panel_map.shape[0]
     blocks, wide = rows * cols, 2 * cases
     n_gx, n_gy = lax.axis_size("gx"), lax.axis_size("gy")
-    spot = jnp.stack([lax.axis_index("gx"), lax.axis_index("gy")])
     motion = plate_motion.reshape(blocks, wide, unknowns)
     load = adjoint_load.reshape(blocks, wide, unknowns)
     force = excitation.reshape(blocks, wide, unknowns)
@@ -375,12 +396,16 @@
         + [pltpu.VMEM((2 * counts[o] * wide, unknowns), BF16) for o in early]
         + [pltpu.VMEM(field, BF16)] * 2
         + [pltpu.VMEM(panel_map.shape, BF16), pltpu.VMEM((many,) + pair, BF16)],
-        in_specs=[SCALARS, SCALARS] + [FAR] * 4,
+        in_specs=[FAR] * 5,
         out_specs=[WHOLE] * (5 + len(early)),
-        scratch_shapes=[pltpu.VMEM((few,) + pair, BF16), DMA((3 + few + many,))],
+        scratch_shapes=[
+            pltpu.VMEM((few,) + pair, BF16),
+            pltpu.SMEM(joints.shape, jnp.int32),
+            DMA((4 + few + many,)),
+        ],
         compiler_params=params(16),
         cost_estimate=cost(4 * blocks * wide * unknowns * panels, 4 * blocks * wide * unknowns),
-    )(spot, far(joints), far(motion), far(load), far(coupling), far(panel_map))
+    )(far(joints), far(motion), far(load), far(coupling), far(panel_map))
     pieces = [motion_panels] + [exchange(motion_panels, step) for step in range(1, n_gx)]
     fourth = exchange_sides(payloads[0], 1, 2)
 
@@ -389,12 +414,12 @@
         name="edges",
         out_shape=[pltpu.VMEM((panels, wide), BF16)]
         + [pltpu.VMEM((2 * counts[o] * wide, unknowns), BF16) for o in late],
-        in_specs=[SCALARS, SCALARS] + [WHOLE] * 4,
+        in_specs=[WHOLE] * 4,
         out_specs=[WHOLE] * (1 + len(late)),
         scratch_shapes=[pltpu.VMEM((blocks, wide, 2 * unknowns), BF16)],
         compiler_params=params(16),
         cost_estimate=cost(many * block_flops, 4 * blocks * wide * unknowns + 12 * blocks * unknowns**2),
-    )(spot, far(joints), near_motion, near_load, near_map, near_coupling)
+    )(near_motion, near_load, near_map, near_coupling)
     (*payloads, load_panels) = lax.optimization_barrier((*payloads, load_panels))
     first, second = exchange_sides(payloads[0], 0, 1), exchange_sides(payloads[1], 0, 2)
     third = exchange_sides(payloads[2], 1, 1)
@@ -403,12 +428,12 @@
         functools.partial(pressure_kernel, n_gx),
         name="pressure",
         out_shape=pltpu.HBM((n_gy, 2 * panels, wide), BF16),
-        in_specs=[SCALARS] + [WHOLE] * (2 + n_gx),
+        in_specs=[WHOLE] * (2 + n_gx),
         out_specs=FAR,
         scratch_shapes=[pltpu.VMEM((2, n_gx * panels, wide), BF16), pltpu.VMEM((n_gy, 2 * panels, wide), BF16), DMA((2,))],
         compiler_params=params(16),
         cost_estimate=cost(2 * hydro.size * wide, 2 * hydro.size),
-    )(spot, hydro, load_panels, *pieces)
+    )(hydro, load_panels, *pieces)
     parts, fourth = lax.optimization_barrier((parts, fourth))
     arrived = lax.all_to_all(parts, "gy", 0, 0, tiled=True)
 
@@ -417,45 +442,51 @@
         name="interior",
         out_shape=[pltpu.VMEM(field, F32)] * 2
         + [pltpu.HBM(field, F32), pltpu.VMEM((many,) + pair, BF16)],
-        in_specs=[SCALARS] * 2 + [FAR] * 4 + [WHOLE] * len(early),
+        in_specs=[FAR] * 5 + [WHOLE] * len(early),
         out_specs=[WHOLE] * 2 + [FAR, WHOLE],
         scratch_shapes=[pltpu.VMEM(field, BF16)] * 3
-        + [pltpu.VMEM(coupling.shape, BF16), pltpu.VMEM(field, F32), DMA((3 + blocks + many,)), DMA((blocks,))],
+        + [
+            pltpu.VMEM(coupling.shape, BF16),
+            pltpu.VMEM(field, F32),
+            pltpu.SMEM(joints.shape, jnp.int32),
+            DMA((4 + blocks + many,)),
+            DMA((blocks,)),
+        ],
         compiler_params=params(16),
         cost_estimate=cost(6 * blocks * block_flops, 20 * blocks * unknowns**2 + 18 * blocks * wide * unknowns),
-    )(spot, far(joints), far(motion), far(load), far(force), far(coupling), fourth)
+    )(far(joints), far(motion), far(load), far(force), far(coupling), fourth)
     arrived, residual, multiplier, own, outer = lax.optimization_barrier((arrived, residual, multiplier, own, outer))
 
     reaction_parts = pl.pallas_call(
         functools.partial(reaction_kernel, n_gx),
         name="reaction",
         out_shape=[pltpu.VMEM((panels, wide), F32)] * n_gx,
-        in_specs=[SCALARS] + [WHOLE] * 2,
+        in_specs=[WHOLE] * 2,
         out_specs=[WHOLE] * n_gx,
         scratch_shapes=[pltpu.VMEM((n_gx * panels, wide), F32)],
         compiler_params=params(16),
         cost_estimate=cost(2 * hydro.size * wide, 2 * hydro.size),
-    )(spot, hydro, arrived)
+    )(hydro, arrived)
     reactions = [reaction_parts[0]] + [exchange(reaction_parts[step], step) for step in range(1, n_gx)]
 
     residual, multiplier = pl.pallas_call(
         functools.partial(boundary_kernel, rows, cols, (n_gx, n_gy), lift, late),
         name="boundary",
         out_shape=[pltpu.HBM(field, F32), pltpu.VMEM(field, F32)],
-        in_specs=[SCALARS] * 2 + [WHOLE] * (5 + len(late)),
+        in_specs=[WHOLE] * (5 + len(late)),
         out_specs=[FAR, WHOLE],
         scratch_shapes=[pltpu.VMEM(field, F32), DMA],
         compiler_params=params(16),
         cost_estimate=cost(4 * blocks * block_flops, 10 * blocks * unknowns**2 + 18 * blocks * wide * unknowns),
-    )(spot, far(joints), panel_map, outer, residual, multiplier, arrived, first, second, third)
+    )(panel_map, outer, residual, multiplier, arrived, first, second, third)
 
     multiplier, sensitivity = pl.pallas_call(
         functools.partial(final_kernel, rows, cols, lift),
         name="final",
-        out_shape=[pltpu.HBM(field, F32), shaped(F32, rows, cols)],
+        out_shape=[pltpu.HBM(field, F32), pltpu.HBM((rows, cols), F32)],
         in_specs=[WHOLE] * (3 + n_gx),
-        out_specs=[FAR, SCALARS],
-        scratch_shapes=[pltpu.VMEM(field, F32), DMA((blocks,))],
+        out_specs=[FAR, FAR],
+        scratch_shapes=[pltpu.VMEM(field, F32), pltpu.SMEM((rows, cols), F32), DMA((blocks + 1,))],
         compiler_params=params(16),
         cost_estimate=cost(4 * blocks * wide * unknowns * panels, 20 * blocks * wide * unknowns),
     )(panel_map, multiplier, own, *reactions)

time: 35.6 us -> 33.6 us (0.944)
  Pallas kernels: 14.8 us -> 10.4 us
  waiting for transfers between devices: 2.93 us -> 5.05 us
  starting transfers between devices: 16.6 us -> 17.2 us
    ppermute x6, waiting for transfers between devices: 2.21 us -> 3.09 us  [exchange(): return lax.ppermute(x, 'gx', [(i, target(i, step, n)) for i in range(n)])]
    pallas_call x1, Pallas kernels: 2.16 us -> 1.43 us  [on_device(): pl.pallas_call(functools.partial(boundary_kernel, rows, cols, (n_gx, n_gy...]
    pallas_call x1, Pallas kernels: 4.04 us -> 3.34 us  [on_device(): pl.pallas_call(functools.partial(interior_kernel, rows, cols, (n_gx, n_gy...]
    pallas_call x1, Pallas kernels: 1.88 us -> 1.18 us  [on_device(): pl.pallas_call(functools.partial(edges_kernel, rows, cols, late), name='e...]
    all_to_all x1, waiting for transfers between devices: 0.66 us -> 1.35 us  [on_device(): arrived = lax.all_to_all(parts, 'gy', 0, 0, tiled=True)]
    pallas_call x1, Pallas kernels: 2.59 us -> 1.93 us  [on_device(): pl.pallas_call(functools.partial(panels_kernel, rows, cols, early, late),...]
    pallas_call x1, Pallas kernels: 1.71 us -> 1.16 us  [on_device(): pl.pallas_call(functools.partial(final_kernel, rows, cols, lift), name='f...]
    all_to_all x1, starting transfers between devices: 7.5 us -> 8.05 us  [on_device(): arrived = lax.all_to_all(parts, 'gy', 0, 0, tiled=True)]
  transfers between devices with their start and end apart: 11 -> 11, of which waited for: 4 -> 5; matrix products, arithmetic and copies ran while one was open for 0% -> 0% of each run, Pallas kernels for 30% -> 22%
where the time goes in v6:
time: 33.6 us; the launch traced here: 33.4 us
  starting transfers between devices  17.2 us (51%)
  Pallas kernels  10.4 us (31%)
  waiting for transfers between devices  5.05 us (15%)
  between operations  0.73 us (2%)
    all_to_all x1, starting transfers between devices, on_device(): arrived = lax.all_to_all(parts, 'gy', 0, 0, tiled=True)  8.05 us
    ppermute x6, starting transfers between devices, exchange(): return lax.ppermute(x, 'gx', [(i, target(i, step, n)) for i in range(n)])  4.98 us
    ppermute x4, starting transfers between devices, exchange_sides(): return lax.ppermute(x, ('gx', 'gy'), pairs)  4.14 us
    pallas_call x1, Pallas kernels, on_device(): pl.pallas_call(functools.partial(interior_kernel, rows, cols, (n_gx, n_gy...  3.34 us
    ppermute x6, waiting for transfers between devices, exchange(): return lax.ppermute(x, 'gx', [(i, target(i, step, n)) for i in range(n)])  3.09 us
    pallas_call x1, Pallas kernels, on_device(): pl.pallas_call(functools.partial(panels_kernel, rows, cols, early, late),...  1.93 us
    pallas_call x1, Pallas kernels, on_device(): pl.pallas_call(functools.partial(boundary_kernel, rows, cols, (n_gx, n_gy...  1.43 us
    all_to_all x1, waiting for transfers between devices, on_device(): arrived = lax.all_to_all(parts, 'gy', 0, 0, tiled=True)  1.35 us
  transfers between devices with their start and end apart: 11, of which 5 were waited for; matrix products, arithmetic and copies ran while one was open for 0% of the time, Pallas kernels for 22%

profile of v6, /device:TPU:0, one launch (start us, length us, event | category | flops | bytes accessed | tf_op | source)
XLA Modules:
  0.0 33.4 jit_solution(1897741592118940997)
XLA Ops:
  0.6 0.0 copy-start.1
  0.6 1.9 %panels.1 = (bf16[32,256]{1,0:T(8,128)(2,1)S(1)}, bf16[1024,128]{1,0:T(8,128)(2,1)S(1)}, bf16[4,256,128]{2,1,0:T(8,128)(2,1)S(1)}, bf16[4,256,128]{2,1,0:T(8,128...) custom-call(s32[2,2,4]{2,1,0:T(2,128)} %joints_far.3, bf16[4,256,128]{2,1,0:T(8,128)(2,1)} %bitcast.12, ...), custom_call_target="tpu_custom_call" | custom-call | flops 16777216 | bytes 524288 | tf_op jit(solution)/shard_map/panels/pallas_call | solution.py:392
  2.6 0.5 %collective-permute-start.3 = (bf16[1024,128]{1,0:T(8,128)(2,1)S(1)}, bf16[1024,128]{1,0:T(8,128)(2,1)S(1)}, u32[]{:S(2)}, u32[]{:S(2)}) collective-permute-start(bf16[1024,128]{1,0:T(8,128)(2,1)S(1)} %get-tuple-element.46), channel_id=1, source_target_pairs={{0,8},{1,2},{2,1},{3,4},{4,3},{5,6},{6,5},{7,15},{8,0},{9,10},{10,... | collective-permute-start | bytes 786440 | tf_op jit(solution)/shard_map/ppermute | solution.py:107
  3.1 2.6 %collective-permute-start.2 = (bf16[32,256]{1,0:T(8,128)(2,1)S(1)}, bf16[32,256]{1,0:T(8,128)(2,1)S(1)}, u32[]{:S(2)}, u32[]{:S(2)}) collective-permute-start(bf16[32,256]{1,0:T(8,128)(2,1)S(1)} %get-tuple-element.45.refs_0_), channel_id=1, source_target_pairs={{0,16},{8,24},{16,0},{24,8},{1,17},{9,25},{17,1},{25,9},{2,18},{10... | collective-permute-start | bytes 49160 | tf_op jit(solution)/shard_map/ppermute | solution.py:92
  5.7 0.1 collective-permute-start.1
  5.7 0.1 collective-permute-start
  5.9 1.2 %edges.1 = (bf16[32,256]{1,0:T(8,128)(2,1)S(1)}, bf16[1024,128]{1,0:T(8,128)(2,1)}, bf16[1024,128]{1,0:T(8,128)(2,1)S(1)}, bf16[1024,128]{1,0:T(8,128)(2,1)S(1)}) custom-call(bf16[4,256,128]{2,1,0:T(8,128)(2,1)S(1)} %get-tuple-element.36.motion, bf16[4,256,128]{2,1,0:T(8,128)(2,1)S(1)} %get-tuple-element.37.load, ...), custom_call_target="tpu_custom_call" | custom-call | flops 100663296 | bytes 1310720 | tf_op jit(solution)/shard_map/edges/pallas_call | solution.py:412
  7.1 0.3 collective-permute-done.2.refs_3_
  7.4 1.4 %collective-permute-done.1.refs_2_ = bf16[32,256]{1,0:T(8,128)(2,1)S(1)} collective-permute-done((bf16[32,256]{1,0:T(8,128)(2,1)S(1)}, bf16[32,256]{1,0:T(8,128)(2,1)S(1)}, u32[]{:S(2)}, u32[]{:S(2)}) %collective-permute-start.1) | collective-permute-done | bytes 16416 | tf_op jit(solution)/shard_map/ppermute | solution.py:92
  8.8 0.0 collective-permute-done.refs_1_
  8.8 0.0 copy-done.1
  8.8 1.0 %pressure.1 = bf16[8,64,256]{2,1,0:T(8,128)(2,1)} custom-call(bf16[2,256,128]{2,1,0:T(8,128)(2,1)S(1)} %copy-done.1, bf16[32,256]{1,0:T(8,128)(2,1)S(1)} %get-tuple-element.44.load_panels, bf16[32,256]{1,0:T(8,128)(2,1)S(1)} %get-tuple-element.45.refs_0_, bf16[32,256]{1,0:T(8,128)(2,1)S(1)} %collective-permute-done.refs_1_, ...), custom_call_target="tpu_custom_call" | custom-call | flops 33554432 | bytes 131072 | tf_op jit(solution)/shard_map/pressure/pallas_call | solution.py:427
  9.9 0.0 collective-permute-done.3.refs_1_
  9.9 8.1 %all-to-all-start = ((bf16[8,64,256]{2,1,0:T(8,128)(2,1)}), bf16[8,64,256]{2,1,0:T(8,128)(2,1)S(1)}, u32[]{:S(2)}, u32[]{:S(2)}) async-start(bf16[8,64,256]{2,1,0:T(8,128)(2,1)} %pressure.1), calls=%async_computation | async-start | bytes 524288 | tf_op jit(solution)/shard_map/all_to_all | solution.py:438
  17.9 0.0 collective-permute-start.4
  17.9 1.6 %collective-permute-start.5 = (bf16[1024,128]{1,0:T(8,128)(2,1)S(1)}, bf16[1024,128]{1,0:T(8,128)(2,1)S(1)}, u32[]{:S(2)}, u32[]{:S(2)}) collective-permute-start(bf16[1024,128]{1,0:T(8,128)(2,1)S(1)} %get-tuple-element.58), channel_id=1, source_target_pairs={{0,24},{1,25},{2,26},{3,27},{4,28},{5,29},{6,30},{7,31},{8,16},{9,... | collective-permute-start | bytes 786440 | tf_op jit(solution)/shard_map/ppermute | solution.py:107
  19.5 2.0 %collective-permute-start.6 = (bf16[1024,128]{1,0:T(8,128)(2,1)S(1)}, bf16[1024,128]{1,0:T(8,128)(2,1)S(1)}, u32[]{:S(2)}, u32[]{:S(2)}) collective-permute-start(bf16[1024,128]{1,0:T(8,128)(2,1)S(1)} %get-tuple-element.59), channel_id=1, source_target_pairs={{0,1},{1,0},{2,3},{3,2},{4,5},{5,4},{6,7},{7,6},{8,9},{9,8},{10,11... | collective-permute-start | bytes 786440 | tf_op jit(solution)/shard_map/ppermute | solution.py:107
  21.5 0.0 copy-start.2
  21.5 3.3 %interior.1 = (f32[4,256,128]{2,1,0:T(8,128)S(1)}, f32[4,256,128]{2,1,0:T(8,128)S(1)}, f32[4,256,128]{2,1,0:T(8,128)}, bf16[6,2,128,128]{3,2,1,0:T(8,128)(2,1)S(1)}) custom-call(s32[2,2,4]{2,1,0:T(2,128)} %joints_far.3, bf16[4,256,128]{2,1,0:T(8,128)(2,1)} %bitcast.13, bf16[4,256,128]{2,1,0:T(8,128)(2,1)} %bitcast.15, bf16[4,256,128]{2,1,0:T(8,128)(2,1)} %bitcast.16, ...), custom_call_target="tpu_custom_call" | custom-call | flops 402653184 | bytes 3670016 | tf_op jit(solution)/shard_map/interior/pallas_call | solution.py:440
  24.9 1.4 %all-to-all-done.arrived = bf16[8,64,256]{2,1,0:T(8,128)(2,1)S(1)} async-done(((bf16[8,64,256]{2,1,0:T(8,128)(2,1)}), bf16[8,64,256]{2,1,0:T(8,128)(2,1)S(1)}, u32[]{:S(2)}, u32[]{:S(2)}) %all-to-all-start) | async-done | bytes 262176 | tf_op jit(solution)/shard_map/all_to_all | solution.py:438
  26.3 0.3 reaction.1
  26.6 0.0 copy-start
  26.6 0.1 collective-permute-start.7
  26.7 1.6 %collective-permute-start.8 = (f32[32,256]{1,0:T(8,128)S(1)}, f32[32,256]{1,0:T(8,128)S(1)}, u32[]{:S(2)}, u32[]{:S(2)}) collective-permute-start(f32[32,256]{1,0:T(8,128)S(1)} %get-tuple-element.65), channel_id=1, source_target_pairs={{0,24},{8,16},{16,8},{24,0},{1,25},{9,17},{17,9},{25,1},{2,26},{10... | collective-permute-start | bytes 98312 | tf_op jit(solution)/shard_map/ppermute | solution.py:92
  28.3 0.0 collective-permute-done.4.refs_0_
  28.3 0.5 %collective-permute-start.9 = (f32[32,256]{1,0:T(8,128)S(1)}, f32[32,256]{1,0:T(8,128)S(1)}, u32[]{:S(2)}, u32[]{:S(2)}) collective-permute-start(f32[32,256]{1,0:T(8,128)S(1)} %get-tuple-element.66), channel_id=1, source_target_pairs={{0,16},{8,24},{16,0},{24,8},{1,17},{9,25},{17,1},{25,9},{2,18},{10... | collective-permute-start | bytes 98312 | tf_op jit(solution)/shard_map/ppermute | solution.py:92
  28.8 0.0 collective-permute-done.5.refs_1_
  28.8 0.6 %collective-permute-done.6.refs_2_ = bf16[1024,128]{1,0:T(8,128)(2,1)S(1)} collective-permute-done((bf16[1024,128]{1,0:T(8,128)(2,1)S(1)}, bf16[1024,128]{1,0:T(8,128)(2,1)S(1)}, u32[]{:S(2)}, u32[]{:S(2)}) %collective-permute-start.6) | collective-permute-done | bytes 262176 | tf_op jit(solution)/shard_map/ppermute | solution.py:107
  29.4 0.0 copy-done.2
  29.4 1.4 %boundary.1 = (f32[4,256,128]{2,1,0:T(8,128)}, f32[4,256,128]{2,1,0:T(8,128)S(1)}) custom-call(bf16[128,128]{1,0:T(8,128)(2,1)S(1)} %bitcast.8, bf16[6,2,128,128]{3,2,1,0:T(8,128)(2,1)S(1)} %get-tuple-element.53.coupling, f32[4,256,128]{2,1,0:T(8,128)S(1)} %get-tuple-element.54.residual, f32[4,256,128]{2,1,0:T(8,128)S(1)} %get-tuple-element.55.multiplier, ...), custom_call_target="tpu_custom_call" | custom-call | flops 268435456 | bytes 3014656 | tf_op jit(solution)/shard_map/boundary/pallas_call | solution.py:472
  30.9 0.0 collective-permute-done.7.refs_1_
  30.9 0.0 collective-permute-done.8.refs_2_
  30.9 1.3 %collective-permute-done.9.refs_3_ = f32[32,256]{1,0:T(8,128)S(1)} collective-permute-done((f32[32,256]{1,0:T(8,128)S(1)}, f32[32,256]{1,0:T(8,128)S(1)}, u32[]{:S(2)}, u32[]{:S(2)}) %collective-permute-start.9) | collective-permute-done | bytes 32800 | tf_op jit(solution)/shard_map/ppermute | solution.py:92
  32.2 0.0 copy-done
  32.2 1.2 %final.1 = (f32[4,256,128]{2,1,0:T(8,128)}, f32[2,2]{1,0:T(2,128)}) custom-call(bf16[128,128]{1,0:T(8,128)(2,1)S(1)} %bitcast.9, f32[4,256,128]{2,1,0:T(8,128)S(1)} %get-tuple-element.61.multiplier, f32[4,256,128]{2,1,0:T(8,128)S(1)} %copy-done, f32[32,256]{1,0:T(8,128)S(1)} %get-tuple-element.63.refs_0_, f32[32,256]{1,0:T(8,128)S(1)} %collective-permute-done.7.refs_1_, ...), custom_call_target="tpu_custom_call" | custom-call | flops 16777216 | bytes 2621440 | tf_op jit(solution)/shard_map/final/pallas_call | solution.py:483
Async XLA Ops:
  0.6 8.2 %copy-start.1 = (bf16[2,256,128]{2,1,0:T(8,128)(2,1)S(1)}, bf16[2,256,128]{2,1,0:T(8,128)(2,1)}, u32[]{:S(2)}) copy-start(bf16[2,256,128]{2,1,0:T(8,128)(2,1)} %hydro_ref.3) | copy-start | bytes 393220
  2.6 7.3 %collective-permute-start.3 = (bf16[1024,128]{1,0:T(8,128)(2,1)S(1)}, bf16[1024,128]{1,0:T(8,128)(2,1)S(1)}, u32[]{:S(2)}, u32[]{:S(2)}) collective-permute-start(bf16[1024,128]{1,0:T(8,128)(2,1)S(1)} %get-tuple-element.46), channel_id=1, source_target_pairs={{0,8},{1,2},{2,1},{3,4},{4,3},{5,6},{6,5},{7,15},{8,0},{9,10},{10,... | collective-permute-start | bytes 786440 | tf_op jit(solution)/shard_map/ppermute | solution.py:107
  3.1 4.3 %collective-permute-start.2 = (bf16[32,256]{1,0:T(8,128)(2,1)S(1)}, bf16[32,256]{1,0:T(8,128)(2,1)S(1)}, u32[]{:S(2)}, u32[]{:S(2)}) collective-permute-start(bf16[32,256]{1,0:T(8,128)(2,1)S(1)} %get-tuple-element.45.refs_0_), channel_id=1, source_target_pairs={{0,16},{8,24},{16,0},{24,8},{1,17},{9,25},{17,1},{25,9},{2,18},{10... | collective-permute-start | bytes 49160 | tf_op jit(solution)/shard_map/ppermute | solution.py:92
  5.7 3.2 %collective-permute-start.1 = (bf16[32,256]{1,0:T(8,128)(2,1)S(1)}, bf16[32,256]{1,0:T(8,128)(2,1)S(1)}, u32[]{:S(2)}, u32[]{:S(2)}) collective-permute-start(bf16[32,256]{1,0:T(8,128)(2,1)S(1)} %get-tuple-element.45.refs_0_), channel_id=1, source_target_pairs={{0,24},{8,16},{16,8},{24,0},{1,25},{9,17},{17,9},{25,1},{2,26},{10... | collective-permute-start | bytes 49160 | tf_op jit(solution)/shard_map/ppermute | solution.py:92
  5.7 3.1 %collective-permute-start = (bf16[32,256]{1,0:T(8,128)(2,1)S(1)}, bf16[32,256]{1,0:T(8,128)(2,1)S(1)}, u32[]{:S(2)}, u32[]{:S(2)}) collective-permute-start(bf16[32,256]{1,0:T(8,128)(2,1)S(1)} %get-tuple-element.45.refs_0_), channel_id=1, source_target_pairs={{0,8},{8,0},{16,24},{24,16},{1,9},{9,1},{17,25},{25,17},{2,10},{10... | collective-permute-start | bytes 49160 | tf_op jit(solution)/shard_map/ppermute | solution.py:92
  9.9 16.4 %all-to-all-start = ((bf16[8,64,256]{2,1,0:T(8,128)(2,1)}), bf16[8,64,256]{2,1,0:T(8,128)(2,1)S(1)}, u32[]{:S(2)}, u32[]{:S(2)}) async-start(bf16[8,64,256]{2,1,0:T(8,128)(2,1)} %pressure.1), calls=%async_computation | async-start | bytes 524288 | tf_op jit(solution)/shard_map/all_to_all | solution.py:438
  17.9 10.4 %collective-permute-start.4 = (bf16[1024,128]{1,0:T(8,128)(2,1)}, bf16[1024,128]{1,0:T(8,128)(2,1)S(1)}, u32[]{:S(2)}, u32[]{:S(2)}) collective-permute-start(bf16[1024,128]{1,0:T(8,128)(2,1)} %get-tuple-element.57), channel_id=1, source_target_pairs={{0,8},{1,9},{2,10},{3,11},{4,12},{5,13},{6,14},{7,15},{8,0},{9,1},... | collective-permute-start | bytes 786440 | tf_op jit(solution)/shard_map/ppermute | solution.py:107
  17.9 10.9 %collective-permute-start.5 = (bf16[1024,128]{1,0:T(8,128)(2,1)S(1)}, bf16[1024,128]{1,0:T(8,128)(2,1)S(1)}, u32[]{:S(2)}, u32[]{:S(2)}) collective-permute-start(bf16[1024,128]{1,0:T(8,128)(2,1)S(1)} %get-tuple-element.58), channel_id=1, source_target_pairs={{0,24},{1,25},{2,26},{3,27},{4,28},{5,29},{6,30},{7,31},{8,16},{9,... | collective-permute-start | bytes 786440 | tf_op jit(solution)/shard_map/ppermute | solution.py:107
  19.5 9.9 %collective-permute-start.6 = (bf16[1024,128]{1,0:T(8,128)(2,1)S(1)}, bf16[1024,128]{1,0:T(8,128)(2,1)S(1)}, u32[]{:S(2)}, u32[]{:S(2)}) collective-permute-start(bf16[1024,128]{1,0:T(8,128)(2,1)S(1)} %get-tuple-element.59), channel_id=1, source_target_pairs={{0,1},{1,0},{2,3},{3,2},{4,5},{5,4},{6,7},{7,6},{8,9},{9,8},{10,11... | collective-permute-start | bytes 786440 | tf_op jit(solution)/shard_map/ppermute | solution.py:107
  21.5 7.9 %copy-start.2 = (bf16[32,2,2,128]{3,2,1,0:T(2,128)(2,1)S(1)}, bf16[32,2,2,128]{3,2,1,0:T(2,128)(2,1)}, u32[]{:S(2)}) copy-start(bf16[32,2,2,128]{3,2,1,0:T(2,128)(2,1)} %param.13) | copy-start | bytes 98308
  26.6 5.6 %copy-start = (f32[4,256,128]{2,1,0:T(8,128)S(1)}, f32[4,256,128]{2,1,0:T(8,128)}, u32[]{:S(2)}) copy-start(f32[4,256,128]{2,1,0:T(8,128)} %get-tuple-element.62.own) | copy-start | bytes 1572868
  26.6 4.3 %collective-permute-start.7 = (f32[32,256]{1,0:T(8,128)S(1)}, f32[32,256]{1,0:T(8,128)S(1)}, u32[]{:S(2)}, u32[]{:S(2)}) collective-permute-start(f32[32,256]{1,0:T(8,128)S(1)} %get-tuple-element.64), channel_id=1, source_target_pairs={{0,8},{8,0},{16,24},{24,16},{1,9},{9,1},{17,25},{25,17},{2,10},{10... | collective-permute-start | bytes 98312 | tf_op jit(solution)/shard_map/ppermute | solution.py:92
  26.7 4.2 %collective-permute-start.8 = (f32[32,256]{1,0:T(8,128)S(1)}, f32[32,256]{1,0:T(8,128)S(1)}, u32[]{:S(2)}, u32[]{:S(2)}) collective-permute-start(f32[32,256]{1,0:T(8,128)S(1)} %get-tuple-element.65), channel_id=1, source_target_pairs={{0,24},{8,16},{16,8},{24,0},{1,25},{9,17},{17,9},{25,1},{2,26},{10... | collective-permute-start | bytes 98312 | tf_op jit(solution)/shard_map/ppermute | solution.py:92
  28.3 3.9 %collective-permute-start.9 = (f32[32,256]{1,0:T(8,128)S(1)}, f32[32,256]{1,0:T(8,128)S(1)}, u32[]{:S(2)}, u32[]{:S(2)}) collective-permute-start(f32[32,256]{1,0:T(8,128)S(1)} %get-tuple-element.66), channel_id=1, source_target_pairs={{0,16},{8,24},{16,0},{24,8},{1,17},{9,25},{17,1},{25,9},{2,18},{10... | collective-permute-start | bytes 98312 | tf_op jit(solution)/shard_map/ppermute | solution.py:92

commit v7 on v6

--- a/solution.py
+++ b/solution.py
@@ -313,44 +313,50 @@
         move.wait()
 
 
-def boundary_kernel(rows, cols, sizes, lift, late, map_ref, coupling, residual, multiplier, arrived, *refs):
-    received, (residual_out, multiplier_out, full, leave) = refs[: len(late)], refs[len(late) :]
+def boundary_kernel(rows, cols, sizes, lift, which, map_ref, coupling, residual, multiplier, arrived, *refs):
+    received, (residual_out, multiplier_out) = refs[: len(which)], refs[len(which) :]
     blocks, unknowns, spot = rows * cols, residual.shape[2], here_on_mesh()
     panels = map_ref.shape[0] // blocks
     maps = jnp.concatenate(map_of_blocks(map_ref, blocks), axis=1)
     pressure = jnp.sum(arrived[:, :panels, :].astype(F32), axis=0).astype(BF16)
     forces = lift * dot(pressure, maps, (0, 0))
     for b in range(blocks):
-        full[b] = residual[b] + forces[:, b * unknowns : (b + 1) * unknowns]
+        residual_out[b] = residual[b] + forces[:, b * unknowns : (b + 1) * unknowns]
         multiplier_out[b] = multiplier[b]
     sides, first = placed(cols, edges(rows, cols, spot)), 0
-    for o, ref in zip(late, received):
+    for o, ref in zip(which, received):
         at = first
-        add_side(sides[o], beyond(spot, sizes, o), ref, lambda k, x, y, d: coupling[at + k], full, multiplier_out)
+        add_side(sides[o], beyond(spot, sizes, o), ref, lambda k, x, y, d: coupling[at + k], residual_out, multiplier_out)
         first += len(sides[o])
-    move = pltpu.make_async_copy(full, residual_out, leave)
-    move.start()
-    move.wait()
-
-
-def final_kernel(rows, cols, lift, map_ref, multiplier, own, *refs):
-    reactions, (multiplier_out, sensitivity_out, full, sensitivity, leave) = refs[:-5], refs[-5:]
-    blocks = rows * cols
+
+
+def final_kernel(rows, cols, sizes, lift, which, first, map_ref, coupling, residual, multiplier, own, *refs):
+    received, refs = refs[: len(which)], refs[len(which) :]
+    reactions, (residual_out, multiplier_out, sensitivity_out, full, sensitivity, leave) = refs[:-6], refs[-6:]
+    blocks, spot = rows * cols, here_on_mesh()
     unknowns = own.shape[2]
     maps = jnp.concatenate(map_of_blocks(map_ref, blocks), axis=1)
     reaction = sum(r[...].astype(F32) for r in reactions).astype(BF16)
     scale = 1.0 / math.sqrt(own.shape[1] // 2 * unknowns)
     forces = lift * dot(reaction, maps, (0, 0))
-    sent, sums = [], []
-    for b in range(blocks):
-        value = multiplier[b] + forces[:, b * unknowns : (b + 1) * unknowns]
-        full[b] = value
-        sent.append(pltpu.make_async_copy(full.at[b], multiplier_out.at[b], leave.at[b]))
-        sent[-1].start()
-        sums.append(jnp.sum((value * own[b]).reshape(-1, 8, unknowns), axis=0))
-    for b in range(blocks):
-        sensitivity[b // cols, b % cols] = jnp.sum(sums[b]) * scale
-    sent.append(pltpu.make_async_copy(sensitivity, sensitivity_out, leave.at[blocks]))
+    for b in range(blocks):
+        full[0, b] = residual[b]
+        full[1, b] = multiplier[b] + forces[:, b * unknowns : (b + 1) * unknowns]
+    sides = placed(cols, edges(rows, cols, spot))
+    for o, ref in zip(which, received):
+        at = first
+        add_side(sides[o], beyond(spot, sizes, o), ref, lambda k, x, y, d: coupling[at + k], full.at[0], full.at[1])
+        first += len(sides[o])
+    sent = [
+        pltpu.make_async_copy(full.at[0], residual_out, leave.at[0]),
+        pltpu.make_async_copy(full.at[1], multiplier_out, leave.at[1]),
+    ]
+    for move in sent:
+        move.start()
+    for b in range(blocks):
+        total = jnp.sum((full[1, b] * own[b]).reshape(-1, 8, unknowns), axis=0)
+        sensitivity[b // cols, b % cols] = jnp.sum(total) * scale
+    sent.append(pltpu.make_async_copy(sensitivity, sensitivity_out, leave.at[2]))
     sent[-1].start()
     for move in sent:
         move.wait()
@@ -421,9 +427,6 @@
         cost_estimate=cost(many * block_flops, 4 * blocks * wide * unknowns + 12 * blocks * unknowns**2),
     )(near_motion, near_load, near_map, near_coupling)
     (*payloads, load_panels) = lax.optimization_barrier((*payloads, load_panels))
-    first, second = exchange_sides(payloads[0], 0, 1), exchange_sides(payloads[1], 0, 2)
-    third = exchange_sides(payloads[2], 1, 1)
-
     parts = pl.pallas_call(
         functools.partial(pressure_kernel, n_gx),
         name="pressure",
@@ -434,8 +437,11 @@
         compiler_params=params(16),
         cost_estimate=cost(2 * hydro.size * wide, 2 * hydro.size),
     )(hydro, load_panels, *pieces)
-    parts, fourth = lax.optimization_barrier((parts, fourth))
     arrived = lax.all_to_all(parts, "gy", 0, 0, tiled=True)
+    (*payloads, fourth) = lax.optimization_barrier((*payloads, fourth))
+    third = exchange_sides(payloads[2], 1, 1)
+    second = exchange_sides(payloads[1], 0, 2)
+    first = exchange_sides(payloads[0], 0, 1)
 
     residual, multiplier, own, outer = pl.pallas_call(
         functools.partial(interior_kernel, rows, cols, (n_gx, n_gy), early, late),
@@ -467,29 +473,29 @@
         compiler_params=params(16),
         cost_estimate=cost(2 * hydro.size * wide, 2 * hydro.size),
     )(hydro, arrived)
-    reactions = [reaction_parts[0]] + [exchange(reaction_parts[step], step) for step in range(1, n_gx)]
+    reactions = [exchange(reaction_parts[step], step) for step in reversed(range(1, n_gx))] + [reaction_parts[0]]
 
     residual, multiplier = pl.pallas_call(
-        functools.partial(boundary_kernel, rows, cols, (n_gx, n_gy), lift, late),
+        functools.partial(boundary_kernel, rows, cols, (n_gx, n_gy), lift, late[:2]),
         name="boundary",
-        out_shape=[pltpu.HBM(field, F32), pltpu.VMEM(field, F32)],
-        in_specs=[WHOLE] * (5 + len(late)),
-        out_specs=[FAR, WHOLE],
-        scratch_shapes=[pltpu.VMEM(field, F32), DMA],
+        out_shape=[pltpu.VMEM(field, F32)] * 2,
+        in_specs=[WHOLE] * 7,
+        out_specs=[WHOLE] * 2,
         compiler_params=params(16),
         cost_estimate=cost(4 * blocks * block_flops, 10 * blocks * unknowns**2 + 18 * blocks * wide * unknowns),
-    )(panel_map, outer, residual, multiplier, arrived, first, second, third)
-
-    multiplier, sensitivity = pl.pallas_call(
-        functools.partial(final_kernel, rows, cols, lift),
+    )(panel_map, outer, residual, multiplier, arrived, first, second)
+
+    done = counts[late[0]] + counts[late[1]]
+    residual, multiplier, sensitivity = pl.pallas_call(
+        functools.partial(final_kernel, rows, cols, (n_gx, n_gy), lift, late[2:], done),
         name="final",
-        out_shape=[pltpu.HBM(field, F32), pltpu.HBM((rows, cols), F32)],
-        in_specs=[WHOLE] * (3 + n_gx),
-        out_specs=[FAR, FAR],
-        scratch_shapes=[pltpu.VMEM(field, F32), pltpu.SMEM((rows, cols), F32), DMA((blocks + 1,))],
+        out_shape=[pltpu.HBM(field, F32), pltpu.HBM(field, F32), pltpu.HBM((rows, cols), F32)],
+        in_specs=[WHOLE] * (6 + n_gx),
+        out_specs=[FAR] * 3,
+        scratch_shapes=[pltpu.VMEM((2,) + field, F32), pltpu.SMEM((rows, cols), F32), DMA((3,))],
         compiler_params=params(16),
         cost_estimate=cost(4 * blocks * wide * unknowns * panels, 20 * blocks * wide * unknowns),
-    )(panel_map, multiplier, own, *reactions)
+    )(panel_map, outer, residual, multiplier, own, third, *reactions)
     shape = plate_motion.shape
     return residual.reshape(shape), multiplier.reshape(shape), sensitivity
 

time: 33.6 us -> 31.9 us (0.949)
  starting transfers between devices: 17.2 us -> 14.6 us
  waiting for transfers between devices: 5.05 us -> 6.42 us
  Pallas kernels: 10.4 us -> 9.87 us
    all_to_all x1, starting transfers between devices: 8.05 us -> 6.28 us  [on_device(): arrived = lax.all_to_all(parts, 'gy', 0, 0, tiled=True)]
    all_to_all x1, waiting for transfers between devices: 1.35 us -> 2.72 us  [on_device(): arrived = lax.all_to_all(parts, 'gy', 0, 0, tiled=True)]
    pallas_call x1, Pallas kernels: 1.43 us -> 0.54 us  [on_device(): pl.pallas_call(functools.partial(boundary_kernel, rows, cols, (n_gx, n_gy...]
    ppermute x4, starting transfers between devices: 4.14 us -> 3.36 us  [exchange_sides(): return lax.ppermute(x, ('gx', 'gy'), pairs)]
    ppermute x6, waiting for transfers between devices: 3.09 us -> 3.7 us  [exchange(): return lax.ppermute(x, 'gx', [(i, target(i, step, n)) for i in range(n)])]
    ppermute x4, waiting for transfers between devices: 0.61 us -> 0.01 us  [exchange_sides(): return lax.ppermute(x, ('gx', 'gy'), pairs)]
    pallas_call x1, Pallas kernels: 1.16 us -> 1.54 us  [on_device(): pl.pallas_call(functools.partial(final_kernel, rows, cols, (n_gx, n_gy),...]
  transfers between devices with their start and end apart: 11 -> 11, of which waited for: 5 -> 5; matrix products, arithmetic and copies ran while one was open for 0% -> 0% of each run, Pallas kernels for 22% -> 20%
where the time goes in v7:
time: 31.9 us; the launch traced here: 31.6 us
  starting transfers between devices  14.6 us (46%)
  Pallas kernels  9.87 us (31%)
  waiting for transfers between devices  6.42 us (20%)
  between operations  0.7 us (2%)
    all_to_all x1, starting transfers between devices, on_device(): arrived = lax.all_to_all(parts, 'gy', 0, 0, tiled=True)  6.28 us
    ppermute x6, starting transfers between devices, exchange(): return lax.ppermute(x, 'gx', [(i, target(i, step, n)) for i in range(n)])  4.98 us
    ppermute x6, waiting for transfers between devices, exchange(): return lax.ppermute(x, 'gx', [(i, target(i, step, n)) for i in range(n)])  3.7 us
    ppermute x4, starting transfers between devices, exchange_sides(): return lax.ppermute(x, ('gx', 'gy'), pairs)  3.36 us
    pallas_call x1, Pallas kernels, on_device(): pl.pallas_call(functools.partial(interior_kernel, rows, cols, (n_gx, n_gy...  3.34 us
    all_to_all x1, waiting for transfers between devices, on_device(): arrived = lax.all_to_all(parts, 'gy', 0, 0, tiled=True)  2.72 us
    pallas_call x1, Pallas kernels, on_device(): pl.pallas_call(functools.partial(panels_kernel, rows, cols, early, late),...  1.93 us
    pallas_call x1, Pallas kernels, on_device(): pl.pallas_call(functools.partial(final_kernel, rows, cols, (n_gx, n_gy),...  1.54 us
  transfers between devices with their start and end apart: 11, of which 5 were waited for; matrix products, arithmetic and copies ran while one was open for 0% of the time, Pallas kernels for 20%

profile of v7, /device:TPU:0, one launch (start us, length us, event | category | flops | bytes accessed | tf_op | source)
XLA Modules:
  0.0 31.6 jit_solution(9456110599599634198)
XLA Ops:
  0.6 0.0 copy-start
  0.6 1.9 %panels.1 = (bf16[32,256]{1,0:T(8,128)(2,1)S(1)}, bf16[1024,128]{1,0:T(8,128)(2,1)S(1)}, bf16[4,256,128]{2,1,0:T(8,128)(2,1)S(1)}, bf16[4,256,128]{2,1,0:T(8,128...) custom-call(s32[2,2,4]{2,1,0:T(2,128)} %joints_far.3, bf16[4,256,128]{2,1,0:T(8,128)(2,1)} %bitcast.12, ...), custom_call_target="tpu_custom_call" | custom-call | flops 16777216 | bytes 524288 | tf_op jit(solution)/shard_map/panels/pallas_call | solution.py:398
  2.6 0.5 %collective-permute-start.3 = (bf16[1024,128]{1,0:T(8,128)(2,1)S(1)}, bf16[1024,128]{1,0:T(8,128)(2,1)S(1)}, u32[]{:S(2)}, u32[]{:S(2)}) collective-permute-start(bf16[1024,128]{1,0:T(8,128)(2,1)S(1)} %get-tuple-element.52), channel_id=1, source_target_pairs={{0,8},{1,2},{2,1},{3,4},{4,3},{5,6},{6,5},{7,15},{8,0},{9,10},{10,... | collective-permute-start | bytes 786440 | tf_op jit(solution)/shard_map/ppermute | solution.py:107
  3.1 2.6 %collective-permute-start.2 = (bf16[32,256]{1,0:T(8,128)(2,1)S(1)}, bf16[32,256]{1,0:T(8,128)(2,1)S(1)}, u32[]{:S(2)}, u32[]{:S(2)}) collective-permute-start(bf16[32,256]{1,0:T(8,128)(2,1)S(1)} %get-tuple-element.48.refs_0_), channel_id=1, source_target_pairs={{0,16},{8,24},{16,0},{24,8},{1,17},{9,25},{17,1},{25,9},{2,18},{10... | collective-permute-start | bytes 49160 | tf_op jit(solution)/shard_map/ppermute | solution.py:92
  5.7 0.1 collective-permute-start.1
  5.7 0.1 collective-permute-start
  5.9 1.2 %edges.1 = (bf16[32,256]{1,0:T(8,128)(2,1)S(1)}, bf16[1024,128]{1,0:T(8,128)(2,1)}, bf16[1024,128]{1,0:T(8,128)(2,1)S(1)}, bf16[1024,128]{1,0:T(8,128)(2,1)S(1)}) custom-call(bf16[4,256,128]{2,1,0:T(8,128)(2,1)S(1)} %get-tuple-element.39.motion, bf16[4,256,128]{2,1,0:T(8,128)(2,1)S(1)} %get-tuple-element.40.load, ...), custom_call_target="tpu_custom_call" | custom-call | flops 100663296 | bytes 1310720 | tf_op jit(solution)/shard_map/edges/pallas_call | solution.py:418
  7.1 0.3 %collective-permute-done.2.refs_3_ = bf16[32,256]{1,0:T(8,128)(2,1)S(1)} collective-permute-done((bf16[32,256]{1,0:T(8,128)(2,1)S(1)}, bf16[32,256]{1,0:T(8,128)(2,1)S(1)}, u32[]{:S(2)}, u32[]{:S(2)}) %collective-permute-start.2) | collective-permute-done | bytes 16416 | tf_op jit(solution)/shard_map/ppermute | solution.py:92
  7.4 1.4 %collective-permute-done.1.refs_2_ = bf16[32,256]{1,0:T(8,128)(2,1)S(1)} collective-permute-done((bf16[32,256]{1,0:T(8,128)(2,1)S(1)}, bf16[32,256]{1,0:T(8,128)(2,1)S(1)}, u32[]{:S(2)}, u32[]{:S(2)}) %collective-permute-start.1) | collective-permute-done | bytes 16416 | tf_op jit(solution)/shard_map/ppermute | solution.py:92
  8.8 0.0 collective-permute-done.refs_1_
  8.8 0.0 copy-done
  8.8 1.0 %pressure.1 = bf16[8,64,256]{2,1,0:T(8,128)(2,1)} custom-call(bf16[2,256,128]{2,1,0:T(8,128)(2,1)S(1)} %copy-done, bf16[32,256]{1,0:T(8,128)(2,1)S(1)} %get-tuple-element.47.load_panels, bf16[32,256]{1,0:T(8,128)(2,1)S(1)} %get-tuple-element.48.refs_0_, bf16[32,256]{1,0:T(8,128)(2,1)S(1)} %collective-permute-done.refs_1_, ...), custom_call_target="tpu_custom_call" | custom-call | flops 33554432 | bytes 131072 | tf_op jit(solution)/shard_map/pressure/pallas_call | solution.py:430
  9.9 6.3 %all-to-all-start = ((bf16[8,64,256]{2,1,0:T(8,128)(2,1)}), bf16[8,64,256]{2,1,0:T(8,128)(2,1)S(1)}, u32[]{:S(2)}, u32[]{:S(2)}) async-start(bf16[8,64,256]{2,1,0:T(8,128)(2,1)} %pressure.1), calls=%async_computation | async-start | bytes 524288 | tf_op jit(solution)/shard_map/all_to_all | solution.py:440
  16.1 0.0 collective-permute-done.3.refs_1_
  16.1 0.1 collective-permute-start.4
  16.2 0.8 %collective-permute-start.5 = (bf16[1024,128]{1,0:T(8,128)(2,1)S(1)}, bf16[1024,128]{1,0:T(8,128)(2,1)S(1)}, u32[]{:S(2)}, u32[]{:S(2)}) collective-permute-start(bf16[1024,128]{1,0:T(8,128)(2,1)S(1)} %get-tuple-element.63), channel_id=1, source_target_pairs={{0,24},{1,25},{2,26},{3,27},{4,28},{5,29},{6,30},{7,31},{8,16},{9,... | collective-permute-start | bytes 786440 | tf_op jit(solution)/shard_map/ppermute | solution.py:107
  17.1 1.9 %collective-permute-start.6 = (bf16[1024,128]{1,0:T(8,128)(2,1)S(1)}, bf16[1024,128]{1,0:T(8,128)(2,1)S(1)}, u32[]{:S(2)}, u32[]{:S(2)}) collective-permute-start(bf16[1024,128]{1,0:T(8,128)(2,1)S(1)} %get-tuple-element.67), channel_id=1, source_target_pairs={{0,1},{1,0},{2,3},{3,2},{4,5},{5,4},{6,7},{7,6},{8,9},{9,8},{10,11... | collective-permute-start | bytes 786440 | tf_op jit(solution)/shard_map/ppermute | solution.py:107
  19.0 0.0 copy-start.2
  19.0 3.3 %interior.1 = (f32[4,256,128]{2,1,0:T(8,128)S(1)}, f32[4,256,128]{2,1,0:T(8,128)S(1)}, f32[4,256,128]{2,1,0:T(8,128)}, bf16[6,2,128,128]{3,2,1,0:T(8,128)(2,1)S(1)}) custom-call(s32[2,2,4]{2,1,0:T(2,128)} %joints_far.3, bf16[4,256,128]{2,1,0:T(8,128)(2,1)} %bitcast.13, bf16[4,256,128]{2,1,0:T(8,128)(2,1)} %bitcast.15, bf16[4,256,128]{2,1,0:T(8,128)(2,1)} %bitcast.16, ...), custom_call_target="tpu_custom_call" | custom-call | flops 402653184 | bytes 3670016 | tf_op jit(solution)/shard_map/interior/pallas_call | solution.py:446
  22.3 2.7 %all-to-all-done.arrived = bf16[8,64,256]{2,1,0:T(8,128)(2,1)S(1)} async-done(((bf16[8,64,256]{2,1,0:T(8,128)(2,1)}), bf16[8,64,256]{2,1,0:T(8,128)(2,1)S(1)}, u32[]{:S(2)}, u32[]{:S(2)}) %all-to-all-start) | async-done | bytes 262176 | tf_op jit(solution)/shard_map/all_to_all | solution.py:440
  25.1 0.0 copy-start.1
  25.1 0.3 %reaction.1 = (f32[32,256]{1,0:T(8,128)S(1)}, f32[32,256]{1,0:T(8,128)S(1)}, f32[32,256]{1,0:T(8,128)S(1)}, f32[32,256]{1,0:T(8,128)S(1)}) custom-call(bf16[2,256,128]{2,1,0:T(8,128)(2,1)S(1)} %copy-done, bf16[8,64,256]{2,1,0:T(8,128)(2,1)S(1)} %all-to-all-done.arrived), custom_call_target="tpu_custom_call" | custom-call | flops 33554432 | bytes 131072 | tf_op jit(solution)/shard_map/reaction/pallas_call | solution.py:466
  25.4 1.3 %collective-permute-start.7 = (f32[32,256]{1,0:T(8,128)S(1)}, f32[32,256]{1,0:T(8,128)S(1)}, u32[]{:S(2)}, u32[]{:S(2)}) collective-permute-start(f32[32,256]{1,0:T(8,128)S(1)} %get-tuple-element.68), channel_id=1, source_target_pairs={{0,16},{8,24},{16,0},{24,8},{1,17},{9,25},{17,1},{25,9},{2,18},{10... | collective-permute-start | bytes 98312 | tf_op jit(solution)/shard_map/ppermute | solution.py:92
  26.7 0.0 collective-permute-start.8
  26.7 0.0 collective-permute-done.4.refs_0_
  26.7 0.9 %collective-permute-start.9 = (f32[32,256]{1,0:T(8,128)S(1)}, f32[32,256]{1,0:T(8,128)S(1)}, u32[]{:S(2)}, u32[]{:S(2)}) collective-permute-start(f32[32,256]{1,0:T(8,128)S(1)} %get-tuple-element.70), channel_id=1, source_target_pairs={{0,8},{8,0},{16,24},{24,16},{1,9},{9,1},{17,25},{25,17},{2,10},{10... | collective-permute-start | bytes 98312 | tf_op jit(solution)/shard_map/ppermute | solution.py:92
  27.6 0.0 collective-permute-done.5.refs_1_
  27.6 0.0 copy-done.2
  27.6 0.5 %boundary.1 = (f32[4,256,128]{2,1,0:T(8,128)S(1)}, f32[4,256,128]{2,1,0:T(8,128)S(1)}) custom-call(bf16[128,128]{1,0:T(8,128)(2,1)S(1)} %bitcast.8, bf16[6,2,128,128]{3,2,1,0:T(8,128)(2,1)S(1)} %get-tuple-element.58.coupling, f32[4,256,128]{2,1,0:T(8,128)S(1)} %get-tuple-element.59.residual, f32[4,256,128]{2,1,0:T(8,128)S(1)} %get-tuple-element.60.multiplier, ...), custom_call_target="tpu_custom_call" | custom-call | flops 268435456 | bytes 3014656 | tf_op jit(solution)/shard_map/boundary/pallas_call | solution.py:478
  28.2 1.2 %collective-permute-done.7.refs_1_ = f32[32,256]{1,0:T(8,128)S(1)} collective-permute-done((f32[32,256]{1,0:T(8,128)S(1)}, f32[32,256]{1,0:T(8,128)S(1)}, u32[]{:S(2)}, u32[]{:S(2)}) %collective-permute-start.7) | collective-permute-done | bytes 32800 | tf_op jit(solution)/shard_map/ppermute | solution.py:92
  29.4 0.7 %collective-permute-done.8.refs_2_ = f32[32,256]{1,0:T(8,128)S(1)} collective-permute-done((f32[32,256]{1,0:T(8,128)S(1)}, f32[32,256]{1,0:T(8,128)S(1)}, u32[]{:S(2)}, u32[]{:S(2)}) %collective-permute-start.8) | collective-permute-done | bytes 32800 | tf_op jit(solution)/shard_map/ppermute | solution.py:92
  30.1 0.0 collective-permute-done.9.refs_3_
  30.1 0.0 collective-permute-done.6.refs_0_
  30.1 0.0 copy-done.1
  30.1 1.5 %final.1 = (f32[4,256,128]{2,1,0:T(8,128)}, f32[4,256,128]{2,1,0:T(8,128)}, f32[2,2]{1,0:T(2,128)}) custom-call(bf16[128,128]{1,0:T(8,128)(2,1)S(1)} %bitcast.9, bf16[6,2,128,128]{3,2,1,0:T(8,128)(2,1)S(1)} %get-tuple-element.58.coupling, f32[4,256,128]{2,1,0:T(8,128)S(1)} %get-tuple-element.64.residual, f32[4,256,128]{2,1,0:T(8,128)S(1)} %get-tuple-element.65.multiplier, ...), custom_call_target="tpu_custom_call" | custom-call | flops 16777216 | bytes 2621440 | tf_op jit(solution)/shard_map/final/pallas_call | solution.py:489
Async XLA Ops:
  0.6 8.2 %copy-start = (bf16[2,256,128]{2,1,0:T(8,128)(2,1)S(1)}, bf16[2,256,128]{2,1,0:T(8,128)(2,1)}, u32[]{:S(2)}) copy-start(bf16[2,256,128]{2,1,0:T(8,128)(2,1)} %hydro_ref.3) | copy-start | bytes 393220
  2.6 13.6 %collective-permute-start.3 = (bf16[1024,128]{1,0:T(8,128)(2,1)S(1)}, bf16[1024,128]{1,0:T(8,128)(2,1)S(1)}, u32[]{:S(2)}, u32[]{:S(2)}) collective-permute-start(bf16[1024,128]{1,0:T(8,128)(2,1)S(1)} %get-tuple-element.52), channel_id=1, source_target_pairs={{0,8},{1,2},{2,1},{3,4},{4,3},{5,6},{6,5},{7,15},{8,0},{9,10},{10,... | collective-permute-start | bytes 786440 | tf_op jit(solution)/shard_map/ppermute | solution.py:107
  3.1 4.3 %collective-permute-start.2 = (bf16[32,256]{1,0:T(8,128)(2,1)S(1)}, bf16[32,256]{1,0:T(8,128)(2,1)S(1)}, u32[]{:S(2)}, u32[]{:S(2)}) collective-permute-start(bf16[32,256]{1,0:T(8,128)(2,1)S(1)} %get-tuple-element.48.refs_0_), channel_id=1, source_target_pairs={{0,16},{8,24},{16,0},{24,8},{1,17},{9,25},{17,1},{25,9},{2,18},{10... | collective-permute-start | bytes 49160 | tf_op jit(solution)/shard_map/ppermute | solution.py:92
  5.7 3.2 %collective-permute-start.1 = (bf16[32,256]{1,0:T(8,128)(2,1)S(1)}, bf16[32,256]{1,0:T(8,128)(2,1)S(1)}, u32[]{:S(2)}, u32[]{:S(2)}) collective-permute-start(bf16[32,256]{1,0:T(8,128)(2,1)S(1)} %get-tuple-element.48.refs_0_), channel_id=1, source_target_pairs={{0,24},{8,16},{16,8},{24,0},{1,25},{9,17},{17,9},{25,1},{2,26},{10... | collective-permute-start | bytes 49160 | tf_op jit(solution)/shard_map/ppermute | solution.py:92
  5.7 3.1 %collective-permute-start = (bf16[32,256]{1,0:T(8,128)(2,1)S(1)}, bf16[32,256]{1,0:T(8,128)(2,1)S(1)}, u32[]{:S(2)}, u32[]{:S(2)}) collective-permute-start(bf16[32,256]{1,0:T(8,128)(2,1)S(1)} %get-tuple-element.48.refs_0_), channel_id=1, source_target_pairs={{0,8},{8,0},{16,24},{24,16},{1,9},{9,1},{17,25},{25,17},{2,10},{10... | collective-permute-start | bytes 49160 | tf_op jit(solution)/shard_map/ppermute | solution.py:92
  9.9 15.2 %all-to-all-start = ((bf16[8,64,256]{2,1,0:T(8,128)(2,1)}), bf16[8,64,256]{2,1,0:T(8,128)(2,1)S(1)}, u32[]{:S(2)}, u32[]{:S(2)}) async-start(bf16[8,64,256]{2,1,0:T(8,128)(2,1)} %pressure.1), calls=%async_computation | async-start | bytes 524288 | tf_op jit(solution)/shard_map/all_to_all | solution.py:440
  16.1 10.6 %collective-permute-start.4 = (bf16[1024,128]{1,0:T(8,128)(2,1)}, bf16[1024,128]{1,0:T(8,128)(2,1)S(1)}, u32[]{:S(2)}, u32[]{:S(2)}) collective-permute-start(bf16[1024,128]{1,0:T(8,128)(2,1)} %get-tuple-element.62), channel_id=1, source_target_pairs={{0,8},{1,9},{2,10},{3,11},{4,12},{5,13},{6,14},{7,15},{8,0},{9,1},... | collective-permute-start | bytes 786440 | tf_op jit(solution)/shard_map/ppermute | solution.py:107
  16.2 11.4 %collective-permute-start.5 = (bf16[1024,128]{1,0:T(8,128)(2,1)S(1)}, bf16[1024,128]{1,0:T(8,128)(2,1)S(1)}, u32[]{:S(2)}, u32[]{:S(2)}) collective-permute-start(bf16[1024,128]{1,0:T(8,128)(2,1)S(1)} %get-tuple-element.63), channel_id=1, source_target_pairs={{0,24},{1,25},{2,26},{3,27},{4,28},{5,29},{6,30},{7,31},{8,16},{9,... | collective-permute-start | bytes 786440 | tf_op jit(solution)/shard_map/ppermute | solution.py:107
  17.1 13.0 %collective-permute-start.6 = (bf16[1024,128]{1,0:T(8,128)(2,1)S(1)}, bf16[1024,128]{1,0:T(8,128)(2,1)S(1)}, u32[]{:S(2)}, u32[]{:S(2)}) collective-permute-start(bf16[1024,128]{1,0:T(8,128)(2,1)S(1)} %get-tuple-element.67), channel_id=1, source_target_pairs={{0,1},{1,0},{2,3},{3,2},{4,5},{5,4},{6,7},{7,6},{8,9},{9,8},{10,11... | collective-permute-start | bytes 786440 | tf_op jit(solution)/shard_map/ppermute | solution.py:107
  19.0 8.6 %copy-start.2 = (bf16[32,2,2,128]{3,2,1,0:T(2,128)(2,1)S(1)}, bf16[32,2,2,128]{3,2,1,0:T(2,128)(2,1)}, u32[]{:S(2)}) copy-start(bf16[32,2,2,128]{3,2,1,0:T(2,128)(2,1)} %param.13) | copy-start | bytes 98308
  25.1 5.0 %copy-start.1 = (f32[4,256,128]{2,1,0:T(8,128)S(1)}, f32[4,256,128]{2,1,0:T(8,128)}, u32[]{:S(2)}) copy-start(f32[4,256,128]{2,1,0:T(8,128)} %get-tuple-element.66.own) | copy-start | bytes 1572868
  25.4 4.0 %collective-permute-start.7 = (f32[32,256]{1,0:T(8,128)S(1)}, f32[32,256]{1,0:T(8,128)S(1)}, u32[]{:S(2)}, u32[]{:S(2)}) collective-permute-start(f32[32,256]{1,0:T(8,128)S(1)} %get-tuple-element.68), channel_id=1, source_target_pairs={{0,16},{8,24},{16,0},{24,8},{1,17},{9,25},{17,1},{25,9},{2,18},{10... | collective-permute-start | bytes 98312 | tf_op jit(solution)/shard_map/ppermute | solution.py:92
  26.7 3.4 %collective-permute-start.8 = (f32[32,256]{1,0:T(8,128)S(1)}, f32[32,256]{1,0:T(8,128)S(1)}, u32[]{:S(2)}, u32[]{:S(2)}) collective-permute-start(f32[32,256]{1,0:T(8,128)S(1)} %get-tuple-element.69), channel_id=1, source_target_pairs={{0,24},{8,16},{16,8},{24,0},{1,25},{9,17},{17,9},{25,1},{2,26},{10... | collective-permute-start | bytes 98312 | tf_op jit(solution)/shard_map/ppermute | solution.py:92
  26.7 3.4 %collective-permute-start.9 = (f32[32,256]{1,0:T(8,128)S(1)}, f32[32,256]{1,0:T(8,128)S(1)}, u32[]{:S(2)}, u32[]{:S(2)}) collective-permute-start(f32[32,256]{1,0:T(8,128)S(1)} %get-tuple-element.70), channel_id=1, source_target_pairs={{0,8},{8,0},{16,24},{24,16},{1,9},{9,1},{17,25},{25,17},{2,10},{10... | collective-permute-start | bytes 98312 | tf_op jit(solution)/shard_map/ppermute | solution.py:92

commit v8 on v7

--- a/solution.py
+++ b/solution.py
@@ -139,7 +139,7 @@
 
 def panels_kernel(rows, cols, early, late, joints_far, motion_far, load_far, coupling_far, map_far, *refs):
     motion_out, outs, refs = refs[0], refs[1 : 1 + len(early)], refs[1 + len(early) :]
-    motion, load, maps, near_coupling, coupling, joints, arrive = refs
+    motion, load, spread, near_coupling, coupling, maps, joints, arrive = refs
     moves = [
         pltpu.make_async_copy(map_far, maps, arrive.at[0]),
         pltpu.make_async_copy(motion_far, motion, arrive.at[1]),
@@ -154,6 +154,7 @@
     blocks, wide = motion.shape[:2]
     moves[0].wait()
     split = map_of_blocks(maps, blocks)
+    spread[...] = jnp.concatenate(split, axis=1)
     moves[1].wait()
     motion_out[...] = sum(dot(split[b], motion[b], (1, 1)) for b in range(blocks)).astype(BF16)
     moves[2].wait()
@@ -179,7 +180,8 @@
     load_out, outs, (both,) = refs[0], refs[1 : 1 + len(late)], refs[1 + len(late) :]
     blocks, wide = motion.shape[:2]
     sides = edges(rows, cols, here_on_mesh())
-    split = map_of_blocks(maps, blocks)
+    width = load.shape[2]
+    split = [maps[:, b * width : (b + 1) * width] for b in range(blocks)]
     load_out[...] = sum(dot(split[b], load[b], (1, 1)) for b in range(blocks)).astype(BF16)
     for b in range(blocks):
         both[b] = beside_turned(load[b], -1)
@@ -313,13 +315,12 @@
         move.wait()
 
 
-def boundary_kernel(rows, cols, sizes, lift, which, map_ref, coupling, residual, multiplier, arrived, *refs):
+def boundary_kernel(rows, cols, sizes, lift, which, maps, coupling, residual, multiplier, arrived, *refs):
     received, (residual_out, multiplier_out) = refs[: len(which)], refs[len(which) :]
     blocks, unknowns, spot = rows * cols, residual.shape[2], here_on_mesh()
-    panels = map_ref.shape[0] // blocks
-    maps = jnp.concatenate(map_of_blocks(map_ref, blocks), axis=1)
+    panels = maps.shape[0]
     pressure = jnp.sum(arrived[:, :panels, :].astype(F32), axis=0).astype(BF16)
-    forces = lift * dot(pressure, maps, (0, 0))
+    forces = lift * dot(pressure, maps[...], (0, 0))
     for b in range(blocks):
         residual_out[b] = residual[b] + forces[:, b * unknowns : (b + 1) * unknowns]
         multiplier_out[b] = multiplier[b]
@@ -330,33 +331,25 @@
         first += len(sides[o])
 
 
-def final_kernel(rows, cols, sizes, lift, which, first, map_ref, coupling, residual, multiplier, own, *refs):
-    received, refs = refs[: len(which)], refs[len(which) :]
+def final_kernel(rows, cols, lift, maps, residual, multiplier, own, *refs):
     reactions, (residual_out, multiplier_out, sensitivity_out, full, sensitivity, leave) = refs[:-6], refs[-6:]
-    blocks, spot = rows * cols, here_on_mesh()
+    blocks = rows * cols
     unknowns = own.shape[2]
-    maps = jnp.concatenate(map_of_blocks(map_ref, blocks), axis=1)
+    sent = [pltpu.make_async_copy(residual, residual_out, leave.at[blocks + 1])]
+    sent[0].start()
     reaction = sum(r[...].astype(F32) for r in reactions).astype(BF16)
     scale = 1.0 / math.sqrt(own.shape[1] // 2 * unknowns)
-    forces = lift * dot(reaction, maps, (0, 0))
-    for b in range(blocks):
-        full[0, b] = residual[b]
-        full[1, b] = multiplier[b] + forces[:, b * unknowns : (b + 1) * unknowns]
-    sides = placed(cols, edges(rows, cols, spot))
-    for o, ref in zip(which, received):
-        at = first
-        add_side(sides[o], beyond(spot, sizes, o), ref, lambda k, x, y, d: coupling[at + k], full.at[0], full.at[1])
-        first += len(sides[o])
-    sent = [
-        pltpu.make_async_copy(full.at[0], residual_out, leave.at[0]),
-        pltpu.make_async_copy(full.at[1], multiplier_out, leave.at[1]),
-    ]
-    for move in sent:
-        move.start()
-    for b in range(blocks):
-        total = jnp.sum((full[1, b] * own[b]).reshape(-1, 8, unknowns), axis=0)
-        sensitivity[b // cols, b % cols] = jnp.sum(total) * scale
-    sent.append(pltpu.make_async_copy(sensitivity, sensitivity_out, leave.at[2]))
+    forces = lift * dot(reaction, maps[...], (0, 0))
+    sums = []
+    for b in range(blocks):
+        value = multiplier[b] + forces[:, b * unknowns : (b + 1) * unknowns]
+        full[b] = value
+        sent.append(pltpu.make_async_copy(full.at[b], multiplier_out.at[b], leave.at[b]))
+        sent[-1].start()
+        sums.append(jnp.sum((value * own[b]).reshape(-1, 8, unknowns), axis=0))
+    for b in range(blocks):
+        sensitivity[b // cols, b % cols] = jnp.sum(sums[b]) * scale
+    sent.append(pltpu.make_async_copy(sensitivity, sensitivity_out, leave.at[blocks]))
     sent[-1].start()
     for move in sent:
         move.wait()
@@ -395,17 +388,18 @@
     early, late = (3,), (0, 1, 2)
     few, many = sum(counts[o] for o in early), sum(counts[o] for o in late)
     pair = (2, unknowns, unknowns)
-    motion_panels, *payloads, near_motion, near_load, near_map, near_coupling = pl.pallas_call(
+    motion_panels, *payloads, near_motion, near_load, maps, near_coupling = pl.pallas_call(
         functools.partial(panels_kernel, rows, cols, early, late),
         name="panels",
         out_shape=[pltpu.VMEM((panels, wide), BF16)]
         + [pltpu.VMEM((2 * counts[o] * wide, unknowns), BF16) for o in early]
         + [pltpu.VMEM(field, BF16)] * 2
-        + [pltpu.VMEM(panel_map.shape, BF16), pltpu.VMEM((many,) + pair, BF16)],
+        + [pltpu.VMEM((panels, blocks * unknowns), BF16), pltpu.VMEM((many,) + pair, BF16)],
         in_specs=[FAR] * 5,
         out_specs=[WHOLE] * (5 + len(early)),
         scratch_shapes=[
             pltpu.VMEM((few,) + pair, BF16),
+            pltpu.VMEM(panel_map.shape, BF16),
             pltpu.SMEM(joints.shape, jnp.int32),
             DMA((4 + few + many,)),
         ],
@@ -425,7 +419,7 @@
         scratch_shapes=[pltpu.VMEM((blocks, wide, 2 * unknowns), BF16)],
         compiler_params=params(16),
         cost_estimate=cost(many * block_flops, 4 * blocks * wide * unknowns + 12 * blocks * unknowns**2),
-    )(near_motion, near_load, near_map, near_coupling)
+    )(near_motion, near_load, maps, near_coupling)
     (*payloads, load_panels) = lax.optimization_barrier((*payloads, load_panels))
     parts = pl.pallas_call(
         functools.partial(pressure_kernel, n_gx),
@@ -476,26 +470,25 @@
     reactions = [exchange(reaction_parts[step], step) for step in reversed(range(1, n_gx))] + [reaction_parts[0]]
 
     residual, multiplier = pl.pallas_call(
-        functools.partial(boundary_kernel, rows, cols, (n_gx, n_gy), lift, late[:2]),
+        functools.partial(boundary_kernel, rows, cols, (n_gx, n_gy), lift, late),
         name="boundary",
         out_shape=[pltpu.VMEM(field, F32)] * 2,
-        in_specs=[WHOLE] * 7,
+        in_specs=[WHOLE] * (5 + len(late)),
         out_specs=[WHOLE] * 2,
         compiler_params=params(16),
         cost_estimate=cost(4 * blocks * block_flops, 10 * blocks * unknowns**2 + 18 * blocks * wide * unknowns),
-    )(panel_map, outer, residual, multiplier, arrived, first, second)
-
-    done = counts[late[0]] + counts[late[1]]
+    )(maps, outer, residual, multiplier, arrived, first, second, third)
+
     residual, multiplier, sensitivity = pl.pallas_call(
-        functools.partial(final_kernel, rows, cols, (n_gx, n_gy), lift, late[2:], done),
+        functools.partial(final_kernel, rows, cols, lift),
         name="final",
         out_shape=[pltpu.HBM(field, F32), pltpu.HBM(field, F32), pltpu.HBM((rows, cols), F32)],
-        in_specs=[WHOLE] * (6 + n_gx),
+        in_specs=[WHOLE] * (4 + n_gx),
         out_specs=[FAR] * 3,
-        scratch_shapes=[pltpu.VMEM((2,) + field, F32), pltpu.SMEM((rows, cols), F32), DMA((3,))],
+        scratch_shapes=[pltpu.VMEM(field, F32), pltpu.SMEM((rows, cols), F32), DMA((blocks + 2,))],
         compiler_params=params(16),
         cost_estimate=cost(4 * blocks * wide * unknowns * panels, 20 * blocks * wide * unknowns),
-    )(panel_map, outer, residual, multiplier, own, third, *reactions)
+    )(maps, residual, multiplier, own, *reactions)
     shape = plate_motion.shape
     return residual.reshape(shape), multiplier.reshape(shape), sensitivity
 

time: 31.9 us -> 31.4 us (0.984)
  Pallas kernels: 9.87 us -> 9.44 us
    pallas_call x1, Pallas kernels: 1.54 us -> 1.1 us  [on_device(): pl.pallas_call(functools.partial(final_kernel, rows, cols, lift), name='f...]
  transfers between devices with their start and end apart: 11 -> 11, of which waited for: 5 -> 6; matrix products, arithmetic and copies ran while one was open for 0% -> 0% of each run, Pallas kernels for 20% -> 21%
where the time goes in v8:
time: 31.4 us; the launch traced here: 31.2 us
  starting transfers between devices  14.6 us (46%)
  Pallas kernels  9.44 us (30%)
  waiting for transfers between devices  6.41 us (20%)
  between operations  0.71 us (2%)
    all_to_all x1, starting transfers between devices, on_device(): arrived = lax.all_to_all(parts, 'gy', 0, 0, tiled=True)  6.28 us
    ppermute x6, starting transfers between devices, exchange(): return lax.ppermute(x, 'gx', [(i, target(i, step, n)) for i in range(n)])  4.98 us
    ppermute x6, waiting for transfers between devices, exchange(): return lax.ppermute(x, 'gx', [(i, target(i, step, n)) for i in range(n)])  3.58 us
    ppermute x4, starting transfers between devices, exchange_sides(): return lax.ppermute(x, ('gx', 'gy'), pairs)  3.36 us
    pallas_call x1, Pallas kernels, on_device(): pl.pallas_call(functools.partial(interior_kernel, rows, cols, (n_gx, n_gy...  3.34 us
    all_to_all x1, waiting for transfers between devices, on_device(): arrived = lax.all_to_all(parts, 'gy', 0, 0, tiled=True)  2.72 us
    pallas_call x1, Pallas kernels, on_device(): pl.pallas_call(functools.partial(panels_kernel, rows, cols, early, late),...  1.93 us
    pallas_call x1, Pallas kernels, on_device(): pl.pallas_call(functools.partial(edges_kernel, rows, cols, late), name='e...  1.13 us
  transfers between devices with their start and end apart: 11, of which 6 were waited for; matrix products, arithmetic and copies ran while one was open for 0% of the time, Pallas kernels for 21%

profile of v8, /device:TPU:0, one launch (start us, length us, event | category | flops | bytes accessed | tf_op | source)
XLA Modules:
  0.0 31.2 jit_solution(3293748121301133855)
XLA Ops:
  0.6 0.0 copy-start.1
  0.6 1.9 %panels.1 = (bf16[32,256]{1,0:T(8,128)(2,1)S(1)}, bf16[1024,128]{1,0:T(8,128)(2,1)S(1)}, bf16[4,256,128]{2,1,0:T(8,128)(2,1)S(1)}, bf16[4,256,128]{2,1,0:T(8,128...) custom-call(s32[2,2,4]{2,1,0:T(2,128)} %joints_far.3, bf16[4,256,128]{2,1,0:T(8,128)(2,1)} %bitcast.9, ...), custom_call_target="tpu_custom_call" | custom-call | flops 16777216 | bytes 524288 | tf_op jit(solution)/shard_map/panels/pallas_call | solution.py:391
  2.6 0.5 %collective-permute-start.3 = (bf16[1024,128]{1,0:T(8,128)(2,1)S(1)}, bf16[1024,128]{1,0:T(8,128)(2,1)S(1)}, u32[]{:S(2)}, u32[]{:S(2)}) collective-permute-start(bf16[1024,128]{1,0:T(8,128)(2,1)S(1)} %get-tuple-element.52), channel_id=1, source_target_pairs={{0,8},{1,2},{2,1},{3,4},{4,3},{5,6},{6,5},{7,15},{8,0},{9,10},{10,... | collective-permute-start | bytes 786440 | tf_op jit(solution)/shard_map/ppermute | solution.py:107
  3.1 2.6 %collective-permute-start.2 = (bf16[32,256]{1,0:T(8,128)(2,1)S(1)}, bf16[32,256]{1,0:T(8,128)(2,1)S(1)}, u32[]{:S(2)}, u32[]{:S(2)}) collective-permute-start(bf16[32,256]{1,0:T(8,128)(2,1)S(1)} %get-tuple-element.48.refs_0_), channel_id=1, source_target_pairs={{0,16},{8,24},{16,0},{24,8},{1,17},{9,25},{17,1},{25,9},{2,18},{10... | collective-permute-start | bytes 49160 | tf_op jit(solution)/shard_map/ppermute | solution.py:92
  5.7 0.1 collective-permute-start.1
  5.7 0.1 collective-permute-start
  5.9 1.1 %edges.1 = (bf16[32,256]{1,0:T(8,128)(2,1)S(1)}, bf16[1024,128]{1,0:T(8,128)(2,1)}, bf16[1024,128]{1,0:T(8,128)(2,1)S(1)}, bf16[1024,128]{1,0:T(8,128)(2,1)S(1)}) custom-call(bf16[4,256,128]{2,1,0:T(8,128)(2,1)S(1)} %get-tuple-element.40.motion, bf16[4,256,128]{2,1,0:T(8,128)(2,1)S(1)} %get-tuple-element.41.load, ...), custom_call_target="tpu_custom_call" | custom-call | flops 100663296 | bytes 1310720 | tf_op jit(solution)/shard_map/edges/pallas_call | solution.py:412
  7.0 0.4 %collective-permute-done.2.refs_3_ = bf16[32,256]{1,0:T(8,128)(2,1)S(1)} collective-permute-done((bf16[32,256]{1,0:T(8,128)(2,1)S(1)}, bf16[32,256]{1,0:T(8,128)(2,1)S(1)}, u32[]{:S(2)}, u32[]{:S(2)}) %collective-permute-start.2) | collective-permute-done | bytes 16416 | tf_op jit(solution)/shard_map/ppermute | solution.py:92
  7.4 1.4 %collective-permute-done.1.refs_2_ = bf16[32,256]{1,0:T(8,128)(2,1)S(1)} collective-permute-done((bf16[32,256]{1,0:T(8,128)(2,1)S(1)}, bf16[32,256]{1,0:T(8,128)(2,1)S(1)}, u32[]{:S(2)}, u32[]{:S(2)}) %collective-permute-start.1) | collective-permute-done | bytes 16416 | tf_op jit(solution)/shard_map/ppermute | solution.py:92
  8.8 0.0 collective-permute-done.refs_1_
  8.8 0.0 copy-done.1
  8.8 1.0 %pressure.1 = bf16[8,64,256]{2,1,0:T(8,128)(2,1)} custom-call(bf16[2,256,128]{2,1,0:T(8,128)(2,1)S(1)} %copy-done.1, bf16[32,256]{1,0:T(8,128)(2,1)S(1)} %get-tuple-element.47.load_panels, bf16[32,256]{1,0:T(8,128)(2,1)S(1)} %get-tuple-element.48.refs_0_, bf16[32,256]{1,0:T(8,128)(2,1)S(1)} %collective-permute-done.refs_1_, ...), custom_call_target="tpu_custom_call" | custom-call | flops 33554432 | bytes 131072 | tf_op jit(solution)/shard_map/pressure/pallas_call | solution.py:424
  9.8 6.3 %all-to-all-start = ((bf16[8,64,256]{2,1,0:T(8,128)(2,1)}), bf16[8,64,256]{2,1,0:T(8,128)(2,1)S(1)}, u32[]{:S(2)}, u32[]{:S(2)}) async-start(bf16[8,64,256]{2,1,0:T(8,128)(2,1)} %pressure.1), calls=%async_computation | async-start | bytes 524288 | tf_op jit(solution)/shard_map/all_to_all | solution.py:434
  16.1 0.0 collective-permute-done.3.refs_1_
  16.1 0.1 collective-permute-start.4
  16.2 0.8 %collective-permute-start.5 = (bf16[1024,128]{1,0:T(8,128)(2,1)S(1)}, bf16[1024,128]{1,0:T(8,128)(2,1)S(1)}, u32[]{:S(2)}, u32[]{:S(2)}) collective-permute-start(bf16[1024,128]{1,0:T(8,128)(2,1)S(1)} %get-tuple-element.63), channel_id=1, source_target_pairs={{0,24},{1,25},{2,26},{3,27},{4,28},{5,29},{6,30},{7,31},{8,16},{9,... | collective-permute-start | bytes 786440 | tf_op jit(solution)/shard_map/ppermute | solution.py:107
  17.0 1.9 %collective-permute-start.6 = (bf16[1024,128]{1,0:T(8,128)(2,1)S(1)}, bf16[1024,128]{1,0:T(8,128)(2,1)S(1)}, u32[]{:S(2)}, u32[]{:S(2)}) collective-permute-start(bf16[1024,128]{1,0:T(8,128)(2,1)S(1)} %get-tuple-element.64), channel_id=1, source_target_pairs={{0,1},{1,0},{2,3},{3,2},{4,5},{5,4},{6,7},{7,6},{8,9},{9,8},{10,11... | collective-permute-start | bytes 786440 | tf_op jit(solution)/shard_map/ppermute | solution.py:107
  19.0 3.3 %interior.1 = (f32[4,256,128]{2,1,0:T(8,128)S(1)}, f32[4,256,128]{2,1,0:T(8,128)S(1)}, f32[4,256,128]{2,1,0:T(8,128)}, bf16[6,2,128,128]{3,2,1,0:T(8,128)(2,1)S(1)}) custom-call(s32[2,2,4]{2,1,0:T(2,128)} %joints_far.3, bf16[4,256,128]{2,1,0:T(8,128)(2,1)} %bitcast.10, bf16[4,256,128]{2,1,0:T(8,128)(2,1)} %bitcast.12, bf16[4,256,128]{2,1,0:T(8,128)(2,1)} %bitcast.13, ...), custom_call_target="tpu_custom_call" | custom-call | flops 402653184 | bytes 3670016 | tf_op jit(solution)/shard_map/interior/pallas_call | solution.py:440
  22.3 2.7 %all-to-all-done.arrived = bf16[8,64,256]{2,1,0:T(8,128)(2,1)S(1)} async-done(((bf16[8,64,256]{2,1,0:T(8,128)(2,1)}), bf16[8,64,256]{2,1,0:T(8,128)(2,1)S(1)}, u32[]{:S(2)}, u32[]{:S(2)}) %all-to-all-start) | async-done | bytes 262176 | tf_op jit(solution)/shard_map/all_to_all | solution.py:434
  25.1 0.3 %reaction.1 = (f32[32,256]{1,0:T(8,128)S(1)}, f32[32,256]{1,0:T(8,128)S(1)}, f32[32,256]{1,0:T(8,128)S(1)}, f32[32,256]{1,0:T(8,128)S(1)}) custom-call(bf16[2,256,128]{2,1,0:T(8,128)(2,1)S(1)} %copy-done.1, bf16[8,64,256]{2,1,0:T(8,128)(2,1)S(1)} %all-to-all-done.arrived), custom_call_target="tpu_custom_call" | custom-call | flops 33554432 | bytes 131072 | tf_op jit(solution)/shard_map/reaction/pallas_call | solution.py:460
  25.4 0.0 copy-start
  25.4 1.3 %collective-permute-start.7 = (f32[32,256]{1,0:T(8,128)S(1)}, f32[32,256]{1,0:T(8,128)S(1)}, u32[]{:S(2)}, u32[]{:S(2)}) collective-permute-start(f32[32,256]{1,0:T(8,128)S(1)} %get-tuple-element.68), channel_id=1, source_target_pairs={{0,16},{8,24},{16,0},{24,8},{1,17},{9,25},{17,1},{25,9},{2,18},{10... | collective-permute-start | bytes 98312 | tf_op jit(solution)/shard_map/ppermute | solution.py:92
  26.7 0.0 collective-permute-start.8
  26.7 0.0 collective-permute-done.4.refs_0_
  26.7 0.9 %collective-permute-start.9 = (f32[32,256]{1,0:T(8,128)S(1)}, f32[32,256]{1,0:T(8,128)S(1)}, u32[]{:S(2)}, u32[]{:S(2)}) collective-permute-start(f32[32,256]{1,0:T(8,128)S(1)} %get-tuple-element.70), channel_id=1, source_target_pairs={{0,8},{8,0},{16,24},{24,16},{1,9},{9,1},{17,25},{25,17},{2,10},{10... | collective-permute-start | bytes 98312 | tf_op jit(solution)/shard_map/ppermute | solution.py:92
  27.6 0.0 collective-permute-done.5.refs_1_
  27.6 0.1 collective-permute-done.6.refs_2_
  27.7 0.6 %boundary.1 = (f32[4,256,128]{2,1,0:T(8,128)S(1)}, f32[4,256,128]{2,1,0:T(8,128)S(1)}) custom-call(bf16[32,512]{1,0:T(8,128)(2,1)S(1)} %get-tuple-element.39.maps, bf16[6,2,128,128]{3,2,1,0:T(8,128)(2,1)S(1)} %get-tuple-element.58.coupling, f32[4,256,128]{2,1,0:T(8,128)S(1)} %get-tuple-element.59.residual, f32[4,256,128]{2,1,0:T(8,128)S(1)} %get-tuple-element.60.multiplier, ...), custom_call_target="tpu_custom_call" | custom-call | flops 268435456 | bytes 3014656 | tf_op jit(solution)/shard_map/boundary/pallas_call | solution.py:472
  28.3 1.0 %collective-permute-done.7.refs_0_ = f32[32,256]{1,0:T(8,128)S(1)} collective-permute-done((f32[32,256]{1,0:T(8,128)S(1)}, f32[32,256]{1,0:T(8,128)S(1)}, u32[]{:S(2)}, u32[]{:S(2)}) %collective-permute-start.7) | collective-permute-done | bytes 32800 | tf_op jit(solution)/shard_map/ppermute | solution.py:92
  29.4 0.7 %collective-permute-done.8.refs_1_ = f32[32,256]{1,0:T(8,128)S(1)} collective-permute-done((f32[32,256]{1,0:T(8,128)S(1)}, f32[32,256]{1,0:T(8,128)S(1)}, u32[]{:S(2)}, u32[]{:S(2)}) %collective-permute-start.8) | collective-permute-done | bytes 32800 | tf_op jit(solution)/shard_map/ppermute | solution.py:92
  30.1 0.0 collective-permute-done.9.refs_2_
  30.1 0.0 copy-done
  30.1 1.1 %final.1 = (f32[4,256,128]{2,1,0:T(8,128)}, f32[4,256,128]{2,1,0:T(8,128)}, f32[2,2]{1,0:T(2,128)}) custom-call(bf16[32,512]{1,0:T(8,128)(2,1)S(1)} %get-tuple-element.39.maps, f32[4,256,128]{2,1,0:T(8,128)S(1)} %get-tuple-element.65.residual, f32[4,256,128]{2,1,0:T(8,128)S(1)} %get-tuple-element.66.multiplier, f32[4,256,128]{2,1,0:T(8,128)S(1)} %copy-done, ...), custom_call_target="tpu_custom_call" | custom-call | flops 16777216 | bytes 2621440 | tf_op jit(solution)/shard_map/final/pallas_call | solution.py:482
Async XLA Ops:
  0.6 8.2 %copy-start.1 = (bf16[2,256,128]{2,1,0:T(8,128)(2,1)S(1)}, bf16[2,256,128]{2,1,0:T(8,128)(2,1)}, u32[]{:S(2)}) copy-start(bf16[2,256,128]{2,1,0:T(8,128)(2,1)} %hydro_ref.3) | copy-start | bytes 393220
  2.6 13.6 %collective-permute-start.3 = (bf16[1024,128]{1,0:T(8,128)(2,1)S(1)}, bf16[1024,128]{1,0:T(8,128)(2,1)S(1)}, u32[]{:S(2)}, u32[]{:S(2)}) collective-permute-start(bf16[1024,128]{1,0:T(8,128)(2,1)S(1)} %get-tuple-element.52), channel_id=1, source_target_pairs={{0,8},{1,2},{2,1},{3,4},{4,3},{5,6},{6,5},{7,15},{8,0},{9,10},{10,... | collective-permute-start | bytes 786440 | tf_op jit(solution)/shard_map/ppermute | solution.py:107
  3.1 4.3 %collective-permute-start.2 = (bf16[32,256]{1,0:T(8,128)(2,1)S(1)}, bf16[32,256]{1,0:T(8,128)(2,1)S(1)}, u32[]{:S(2)}, u32[]{:S(2)}) collective-permute-start(bf16[32,256]{1,0:T(8,128)(2,1)S(1)} %get-tuple-element.48.refs_0_), channel_id=1, source_target_pairs={{0,16},{8,24},{16,0},{24,8},{1,17},{9,25},{17,1},{25,9},{2,18},{10... | collective-permute-start | bytes 49160 | tf_op jit(solution)/shard_map/ppermute | solution.py:92
  5.7 3.2 %collective-permute-start.1 = (bf16[32,256]{1,0:T(8,128)(2,1)S(1)}, bf16[32,256]{1,0:T(8,128)(2,1)S(1)}, u32[]{:S(2)}, u32[]{:S(2)}) collective-permute-start(bf16[32,256]{1,0:T(8,128)(2,1)S(1)} %get-tuple-element.48.refs_0_), channel_id=1, source_target_pairs={{0,24},{8,16},{16,8},{24,0},{1,25},{9,17},{17,9},{25,1},{2,26},{10... | collective-permute-start | bytes 49160 | tf_op jit(solution)/shard_map/ppermute | solution.py:92
  5.7 3.1 %collective-permute-start = (bf16[32,256]{1,0:T(8,128)(2,1)S(1)}, bf16[32,256]{1,0:T(8,128)(2,1)S(1)}, u32[]{:S(2)}, u32[]{:S(2)}) collective-permute-start(bf16[32,256]{1,0:T(8,128)(2,1)S(1)} %get-tuple-element.48.refs_0_), channel_id=1, source_target_pairs={{0,8},{8,0},{16,24},{24,16},{1,9},{9,1},{17,25},{25,17},{2,10},{10... | collective-permute-start | bytes 49160 | tf_op jit(solution)/shard_map/ppermute | solution.py:92
  9.8 15.2 %all-to-all-start = ((bf16[8,64,256]{2,1,0:T(8,128)(2,1)}), bf16[8,64,256]{2,1,0:T(8,128)(2,1)S(1)}, u32[]{:S(2)}, u32[]{:S(2)}) async-start(bf16[8,64,256]{2,1,0:T(8,128)(2,1)} %pressure.1), calls=%async_computation | async-start | bytes 524288 | tf_op jit(solution)/shard_map/all_to_all | solution.py:434
  16.1 10.6 %collective-permute-start.4 = (bf16[1024,128]{1,0:T(8,128)(2,1)}, bf16[1024,128]{1,0:T(8,128)(2,1)S(1)}, u32[]{:S(2)}, u32[]{:S(2)}) collective-permute-start(bf16[1024,128]{1,0:T(8,128)(2,1)} %get-tuple-element.62), channel_id=1, source_target_pairs={{0,8},{1,9},{2,10},{3,11},{4,12},{5,13},{6,14},{7,15},{8,0},{9,1},... | collective-permute-start | bytes 786440 | tf_op jit(solution)/shard_map/ppermute | solution.py:107
  16.2 11.4 %collective-permute-start.5 = (bf16[1024,128]{1,0:T(8,128)(2,1)S(1)}, bf16[1024,128]{1,0:T(8,128)(2,1)S(1)}, u32[]{:S(2)}, u32[]{:S(2)}) collective-permute-start(bf16[1024,128]{1,0:T(8,128)(2,1)S(1)} %get-tuple-element.63), channel_id=1, source_target_pairs={{0,24},{1,25},{2,26},{3,27},{4,28},{5,29},{6,30},{7,31},{8,16},{9,... | collective-permute-start | bytes 786440 | tf_op jit(solution)/shard_map/ppermute | solution.py:107
  17.0 10.7 %collective-permute-start.6 = (bf16[1024,128]{1,0:T(8,128)(2,1)S(1)}, bf16[1024,128]{1,0:T(8,128)(2,1)S(1)}, u32[]{:S(2)}, u32[]{:S(2)}) collective-permute-start(bf16[1024,128]{1,0:T(8,128)(2,1)S(1)} %get-tuple-element.64), channel_id=1, source_target_pairs={{0,1},{1,0},{2,3},{3,2},{4,5},{5,4},{6,7},{7,6},{8,9},{9,8},{10,11... | collective-permute-start | bytes 786440 | tf_op jit(solution)/shard_map/ppermute | solution.py:107
  25.4 4.7 %copy-start = (f32[4,256,128]{2,1,0:T(8,128)S(1)}, f32[4,256,128]{2,1,0:T(8,128)}, u32[]{:S(2)}) copy-start(f32[4,256,128]{2,1,0:T(8,128)} %get-tuple-element.67.own) | copy-start | bytes 1572868
  25.4 4.0 %collective-permute-start.7 = (f32[32,256]{1,0:T(8,128)S(1)}, f32[32,256]{1,0:T(8,128)S(1)}, u32[]{:S(2)}, u32[]{:S(2)}) collective-permute-start(f32[32,256]{1,0:T(8,128)S(1)} %get-tuple-element.68), channel_id=1, source_target_pairs={{0,16},{8,24},{16,0},{24,8},{1,17},{9,25},{17,1},{25,9},{2,18},{10... | collective-permute-start | bytes 98312 | tf_op jit(solution)/shard_map/ppermute | solution.py:92
  26.7 3.4 %collective-permute-start.8 = (f32[32,256]{1,0:T(8,128)S(1)}, f32[32,256]{1,0:T(8,128)S(1)}, u32[]{:S(2)}, u32[]{:S(2)}) collective-permute-start(f32[32,256]{1,0:T(8,128)S(1)} %get-tuple-element.69), channel_id=1, source_target_pairs={{0,24},{8,16},{16,8},{24,0},{1,25},{9,17},{17,9},{25,1},{2,26},{10... | collective-permute-start | bytes 98312 | tf_op jit(solution)/shard_map/ppermute | solution.py:92
  26.7 3.4 %collective-permute-start.9 = (f32[32,256]{1,0:T(8,128)S(1)}, f32[32,256]{1,0:T(8,128)S(1)}, u32[]{:S(2)}, u32[]{:S(2)}) collective-permute-start(f32[32,256]{1,0:T(8,128)S(1)} %get-tuple-element.70), channel_id=1, source_target_pairs={{0,8},{8,0},{16,24},{24,16},{1,9},{9,1},{17,25},{25,17},{2,10},{10... | collective-permute-start | bytes 98312 | tf_op jit(solution)/shard_map/ppermute | solution.py:92

commit v9 on v8

--- a/solution.py
+++ b/solution.py
@@ -85,6 +85,14 @@
 
 def source(i, step, n):
     return target(i, step, n) if step < 3 else (i + n + 1 - step) % n
+
+
+def places_along_gy(n):
+    return list(range(n // 2, n)) + list(range(n // 2))
+
+
+def all_steps(n):
+    return [0, 1] + list(range(3, n)) + [2] if n > 2 else list(range(n))
 
 
 def exchange(x, step):
@@ -198,19 +206,22 @@
     pieces, (out_far, gathered, out, leave) = refs[:n_gx], refs[n_gx:]
     me = lax.axis_index("gx")
     panels, wide = load_panels.shape
-    for step in range(n_gx):
+    for step, piece in zip(all_steps(n_gx), pieces):
         start = pl.multiple_of(source(me, step, n_gx) * panels, panels)
-        gathered[0, pl.ds(start, panels), :] = pieces[step][...]
-        gathered[1, pl.ds(start, panels), :] = times_i(pieces[step][...].astype(F32), 1).astype(BF16)
+        gathered[0, pl.ds(start, panels), :] = piece[...]
+        gathered[1, pl.ds(start, panels), :] = times_i(piece[...].astype(F32), 1).astype(BF16)
     fields = gathered[...].reshape(-1, wide)
     tiles = out.shape[0]
+    places, half = places_along_gy(tiles), tiles // 2
     moves = []
     for i in range(2):
-        here = pl.ds(i * tiles // 2, tiles // 2)
-        rows = pl.ds(i * tiles // 2 * panels, tiles // 2 * panels)
-        hydro = jnp.concatenate([hydro_ref[0, rows, :], hydro_ref[1, rows, :]], axis=1)
+        here = pl.ds(i * half, half)
+        tops = [places[k] * panels for k in range(i * half, (i + 1) * half)]
+        hydro = jnp.concatenate(
+            [jnp.concatenate([hydro_ref[part, pl.ds(top, panels), :] for part in range(2)], axis=1) for top in tops], axis=0
+        )
         out[here, :panels, :] = dot(hydro, fields, (1, 0)).astype(BF16).reshape(-1, panels, wide)
-        out[here, panels:, :] = jnp.broadcast_to(load_panels[...], (tiles // 2, panels, wide))
+        out[here, panels:, :] = jnp.broadcast_to(load_panels[...], (half, panels, wide))
         moves.append(pltpu.make_async_copy(out.at[here], out_far.at[here], leave.at[i]))
         moves[-1].start()
     for move in moves:
@@ -222,7 +233,8 @@
     me = lax.axis_index("gx")
     panels = outs[0].shape[0]
     hydro = hydro_ref[...]
-    loads = arrived[:, panels:, :].reshape(hydro.shape[1], -1)
+    places = places_along_gy(arrived.shape[0])
+    loads = jnp.concatenate([arrived[places.index(j), panels:, :] for j in range(len(places))], axis=0)
     real = dot(hydro[0], loads, (0, 0))
     imag = dot(hydro[1], loads, (0, 0))
     reacted[...] = real - times_i(imag, 1)
@@ -406,7 +418,7 @@
         compiler_params=params(16),
         cost_estimate=cost(4 * blocks * wide * unknowns * panels, 4 * blocks * wide * unknowns),
     )(far(joints), far(motion), far(load), far(coupling), far(panel_map))
-    pieces = [motion_panels] + [exchange(motion_panels, step) for step in range(1, n_gx)]
+    pieces = [motion_panels] + [exchange(motion_panels, step) for step in all_steps(n_gx)[1:]]
     fourth = exchange_sides(payloads[0], 1, 2)
 
     load_panels, *payloads = pl.pallas_call(
@@ -431,7 +443,7 @@
         compiler_params=params(16),
         cost_estimate=cost(2 * hydro.size * wide, 2 * hydro.size),
     )(hydro, load_panels, *pieces)
-    arrived = lax.all_to_all(parts, "gy", 0, 0, tiled=True)
+    arrived = lax.all_to_all(parts, "gy", 0, 0, axis_index_groups=[places_along_gy(n_gy)], tiled=True)
     (*payloads, fourth) = lax.optimization_barrier((*payloads, fourth))
     third = exchange_sides(payloads[2], 1, 1)
     second = exchange_sides(payloads[1], 0, 2)

time: 31.4 us -> 30.1 us (0.959)
  waiting for transfers between devices: 6.41 us -> 5.34 us
    all_to_all x1, waiting for transfers between devices: 2.72 us -> 1.55 us  [on_device(): lax.all_to_all(parts, 'gy', 0, 0, axis_index_groups=[places_along_gy(n_gy...]
    ppermute x4, waiting for transfers between devices: 0.11 us -> 1 us  [exchange_sides(): return lax.ppermute(x, ('gx', 'gy'), pairs)]
    ppermute x6, waiting for transfers between devices: 3.58 us -> 2.8 us  [exchange(): return lax.ppermute(x, 'gx', [(i, target(i, step, n)) for i in range(n)])]
    ppermute x4, starting transfers between devices: 3.36 us -> 2.81 us  [exchange_sides(): return lax.ppermute(x, ('gx', 'gy'), pairs)]
  transfers between devices with their start and end apart: 11 -> 11, of which waited for: 6 -> 5; matrix products, arithmetic and copies ran while one was open for 0% -> 0% of each run, Pallas kernels for 21% -> 22%
where the time goes in v9:
time: 30.1 us; the launch traced here: 29.8 us
  starting transfers between devices  14.3 us (48%)
  Pallas kernels  9.45 us (31%)
  waiting for transfers between devices  5.34 us (18%)
  between operations  0.71 us (2%)
    all_to_all x1, starting transfers between devices, on_device(): lax.all_to_all(parts, 'gy', 0, 0, axis_index_groups=[places_along_gy(n_gy...  6.53 us
    ppermute x6, starting transfers between devices, exchange(): return lax.ppermute(x, 'gx', [(i, target(i, step, n)) for i in range(n)])  4.95 us
    pallas_call x1, Pallas kernels, on_device(): pl.pallas_call(functools.partial(interior_kernel, rows, cols, (n_gx, n_gy...  3.34 us
    ppermute x4, starting transfers between devices, exchange_sides(): return lax.ppermute(x, ('gx', 'gy'), pairs)  2.81 us
    ppermute x6, waiting for transfers between devices, exchange(): return lax.ppermute(x, 'gx', [(i, target(i, step, n)) for i in range(n)])  2.8 us
    pallas_call x1, Pallas kernels, on_device(): pl.pallas_call(functools.partial(panels_kernel, rows, cols, early, late),...  1.93 us
    all_to_all x1, waiting for transfers between devices, on_device(): lax.all_to_all(parts, 'gy', 0, 0, axis_index_groups=[places_along_gy(n_gy...  1.55 us
    pallas_call x1, Pallas kernels, on_device(): pl.pallas_call(functools.partial(edges_kernel, rows, cols, late), name='e...  1.13 us
  transfers between devices with their start and end apart: 11, of which 5 were waited for; matrix products, arithmetic and copies ran while one was open for 0% of the time, Pallas kernels for 22%

profile of v9, /device:TPU:0, one launch (start us, length us, event | category | flops | bytes accessed | tf_op | source)
XLA Modules:
  0.0 29.8 jit_solution(9444099917039811510)
XLA Ops:
  0.6 0.0 copy-start.1
  0.6 1.9 %panels.1 = (bf16[32,256]{1,0:T(8,128)(2,1)S(1)}, bf16[1024,128]{1,0:T(8,128)(2,1)S(1)}, bf16[4,256,128]{2,1,0:T(8,128)(2,1)S(1)}, bf16[4,256,128]{2,1,0:T(8,128...) custom-call(s32[2,2,4]{2,1,0:T(2,128)} %joints_far.3, bf16[4,256,128]{2,1,0:T(8,128)(2,1)} %bitcast.9, ...), custom_call_target="tpu_custom_call" | custom-call | flops 16777216 | bytes 524288 | tf_op jit(solution)/shard_map/panels/pallas_call | solution.py:403
  2.6 0.5 %collective-permute-start.3 = (bf16[1024,128]{1,0:T(8,128)(2,1)S(1)}, bf16[1024,128]{1,0:T(8,128)(2,1)S(1)}, u32[]{:S(2)}, u32[]{:S(2)}) collective-permute-start(bf16[1024,128]{1,0:T(8,128)(2,1)S(1)} %get-tuple-element.52), channel_id=1, source_target_pairs={{0,8},{1,2},{2,1},{3,4},{4,3},{5,6},{6,5},{7,15},{8,0},{9,10},{10,... | collective-permute-start | bytes 786440 | tf_op jit(solution)/shard_map/ppermute | solution.py:115
  3.1 2.6 %collective-permute-start.2 = (bf16[32,256]{1,0:T(8,128)(2,1)S(1)}, bf16[32,256]{1,0:T(8,128)(2,1)S(1)}, u32[]{:S(2)}, u32[]{:S(2)}) collective-permute-start(bf16[32,256]{1,0:T(8,128)(2,1)S(1)} %get-tuple-element.48.refs_0_), channel_id=1, source_target_pairs={{0,24},{8,16},{16,8},{24,0},{1,25},{9,17},{17,9},{25,1},{2,26},{10... | collective-permute-start | bytes 49160 | tf_op jit(solution)/shard_map/ppermute | solution.py:100
  5.7 0.0 collective-permute-start.1
  5.8 0.1 collective-permute-start
  5.8 1.1 %edges.1 = (bf16[32,256]{1,0:T(8,128)(2,1)S(1)}, bf16[1024,128]{1,0:T(8,128)(2,1)}, bf16[1024,128]{1,0:T(8,128)(2,1)S(1)}, bf16[1024,128]{1,0:T(8,128)(2,1)S(1)}) custom-call(bf16[4,256,128]{2,1,0:T(8,128)(2,1)S(1)} %get-tuple-element.40.motion, bf16[4,256,128]{2,1,0:T(8,128)(2,1)S(1)} %get-tuple-element.41.load, ...), custom_call_target="tpu_custom_call" | custom-call | flops 100663296 | bytes 1310720 | tf_op jit(solution)/shard_map/edges/pallas_call | solution.py:424
  7.0 0.2 collective-permute-done.2.refs_3_
  7.2 2.3 %collective-permute-done.1.refs_2_ = bf16[32,256]{1,0:T(8,128)(2,1)S(1)} collective-permute-done((bf16[32,256]{1,0:T(8,128)(2,1)S(1)}, bf16[32,256]{1,0:T(8,128)(2,1)S(1)}, u32[]{:S(2)}, u32[]{:S(2)}) %collective-permute-start.1) | collective-permute-done | bytes 16416 | tf_op jit(solution)/shard_map/ppermute | solution.py:100
  9.5 0.0 collective-permute-done.refs_1_
  9.5 0.0 copy-done.1
  9.5 1.0 %pressure.1 = bf16[8,64,256]{2,1,0:T(8,128)(2,1)} custom-call(bf16[2,256,128]{2,1,0:T(8,128)(2,1)S(1)} %copy-done.1, bf16[32,256]{1,0:T(8,128)(2,1)S(1)} %get-tuple-element.47.load_panels, bf16[32,256]{1,0:T(8,128)(2,1)S(1)} %get-tuple-element.48.refs_0_, bf16[32,256]{1,0:T(8,128)(2,1)S(1)} %collective-permute-done.refs_1_, ...), custom_call_target="tpu_custom_call" | custom-call | flops 33554432 | bytes 131072 | tf_op jit(solution)/shard_map/pressure/pallas_call | solution.py:436
  10.5 6.5 %all-to-all-start = ((bf16[8,64,256]{2,1,0:T(8,128)(2,1)}), bf16[8,64,256]{2,1,0:T(8,128)(2,1)S(1)}, u32[]{:S(2)}, u32[]{:S(2)}) async-start(bf16[8,64,256]{2,1,0:T(8,128)(2,1)} %pressure.1), calls=%async_computation | async-start | bytes 524288 | tf_op jit(solution)/shard_map/all_to_all | solution.py:446
  17.0 0.0 collective-permute-done.3.refs_1_
  17.0 0.0 collective-permute-start.4
  17.0 0.8 %collective-permute-start.5 = (bf16[1024,128]{1,0:T(8,128)(2,1)S(1)}, bf16[1024,128]{1,0:T(8,128)(2,1)S(1)}, u32[]{:S(2)}, u32[]{:S(2)}) collective-permute-start(bf16[1024,128]{1,0:T(8,128)(2,1)S(1)} %get-tuple-element.63), channel_id=1, source_target_pairs={{0,24},{1,25},{2,26},{3,27},{4,28},{5,29},{6,30},{7,31},{8,16},{9,... | collective-permute-start | bytes 786440 | tf_op jit(solution)/shard_map/ppermute | solution.py:115
  17.8 1.5 %collective-permute-start.6 = (bf16[1024,128]{1,0:T(8,128)(2,1)S(1)}, bf16[1024,128]{1,0:T(8,128)(2,1)S(1)}, u32[]{:S(2)}, u32[]{:S(2)}) collective-permute-start(bf16[1024,128]{1,0:T(8,128)(2,1)S(1)} %get-tuple-element.64), channel_id=1, source_target_pairs={{0,1},{1,0},{2,3},{3,2},{4,5},{5,4},{6,7},{7,6},{8,9},{9,8},{10,11... | collective-permute-start | bytes 786440 | tf_op jit(solution)/shard_map/ppermute | solution.py:115
  19.3 3.3 %interior.1 = (f32[4,256,128]{2,1,0:T(8,128)S(1)}, f32[4,256,128]{2,1,0:T(8,128)S(1)}, f32[4,256,128]{2,1,0:T(8,128)}, bf16[6,2,128,128]{3,2,1,0:T(8,128)(2,1)S(1)}) custom-call(s32[2,2,4]{2,1,0:T(2,128)} %joints_far.3, bf16[4,256,128]{2,1,0:T(8,128)(2,1)} %bitcast.10, bf16[4,256,128]{2,1,0:T(8,128)(2,1)} %bitcast.12, bf16[4,256,128]{2,1,0:T(8,128)(2,1)} %bitcast.13, ...), custom_call_target="tpu_custom_call" | custom-call | flops 402653184 | bytes 3670016 | tf_op jit(solution)/shard_map/interior/pallas_call | solution.py:452
  22.7 1.5 %all-to-all-done.arrived = bf16[8,64,256]{2,1,0:T(8,128)(2,1)S(1)} async-done(((bf16[8,64,256]{2,1,0:T(8,128)(2,1)}), bf16[8,64,256]{2,1,0:T(8,128)(2,1)S(1)}, u32[]{:S(2)}, u32[]{:S(2)}) %all-to-all-start) | async-done | bytes 262176 | tf_op jit(solution)/shard_map/all_to_all | solution.py:446
  24.2 0.3 %reaction.1 = (f32[32,256]{1,0:T(8,128)S(1)}, f32[32,256]{1,0:T(8,128)S(1)}, f32[32,256]{1,0:T(8,128)S(1)}, f32[32,256]{1,0:T(8,128)S(1)}) custom-call(bf16[2,256,128]{2,1,0:T(8,128)(2,1)S(1)} %copy-done.1, bf16[8,64,256]{2,1,0:T(8,128)(2,1)S(1)} %all-to-all-done.arrived), custom_call_target="tpu_custom_call" | custom-call | flops 33554432 | bytes 131072 | tf_op jit(solution)/shard_map/reaction/pallas_call | solution.py:472
  24.5 0.0 copy-start
  24.5 0.4 %collective-permute-start.7 = (f32[32,256]{1,0:T(8,128)S(1)}, f32[32,256]{1,0:T(8,128)S(1)}, u32[]{:S(2)}, u32[]{:S(2)}) collective-permute-start(f32[32,256]{1,0:T(8,128)S(1)} %get-tuple-element.68), channel_id=1, source_target_pairs={{0,16},{8,24},{16,0},{24,8},{1,17},{9,25},{17,1},{25,9},{2,18},{10... | collective-permute-start | bytes 98312 | tf_op jit(solution)/shard_map/ppermute | solution.py:100
  25.0 0.0 collective-permute-start.8
  25.0 0.0 collective-permute-done.4.refs_0_
  25.0 1.8 %collective-permute-start.9 = (f32[32,256]{1,0:T(8,128)S(1)}, f32[32,256]{1,0:T(8,128)S(1)}, u32[]{:S(2)}, u32[]{:S(2)}) collective-permute-start(f32[32,256]{1,0:T(8,128)S(1)} %get-tuple-element.70), channel_id=1, source_target_pairs={{0,8},{8,0},{16,24},{24,16},{1,9},{9,1},{17,25},{25,17},{2,10},{10... | collective-permute-start | bytes 98312 | tf_op jit(solution)/shard_map/ppermute | solution.py:100
  26.8 0.0 collective-permute-done.5.refs_1_
  26.8 1.0 %collective-permute-done.6.refs_2_ = bf16[1024,128]{1,0:T(8,128)(2,1)S(1)} collective-permute-done((bf16[1024,128]{1,0:T(8,128)(2,1)S(1)}, bf16[1024,128]{1,0:T(8,128)(2,1)S(1)}, u32[]{:S(2)}, u32[]{:S(2)}) %collective-permute-start.6) | collective-permute-done | bytes 262176 | tf_op jit(solution)/shard_map/ppermute | solution.py:115
  27.7 0.6 %boundary.1 = (f32[4,256,128]{2,1,0:T(8,128)S(1)}, f32[4,256,128]{2,1,0:T(8,128)S(1)}) custom-call(bf16[32,512]{1,0:T(8,128)(2,1)S(1)} %get-tuple-element.39.maps, bf16[6,2,128,128]{3,2,1,0:T(8,128)(2,1)S(1)} %get-tuple-element.58.coupling, f32[4,256,128]{2,1,0:T(8,128)S(1)} %get-tuple-element.59.residual, f32[4,256,128]{2,1,0:T(8,128)S(1)} %get-tuple-element.60.multiplier, ...), custom_call_target="tpu_custom_call" | custom-call | flops 268435456 | bytes 3014656 | tf_op jit(solution)/shard_map/boundary/pallas_call | solution.py:484
  28.4 0.3 %collective-permute-done.7.refs_0_ = f32[32,256]{1,0:T(8,128)S(1)} collective-permute-done((f32[32,256]{1,0:T(8,128)S(1)}, f32[32,256]{1,0:T(8,128)S(1)}, u32[]{:S(2)}, u32[]{:S(2)}) %collective-permute-start.7) | collective-permute-done | bytes 32800 | tf_op jit(solution)/shard_map/ppermute | solution.py:100
  28.7 0.0 collective-permute-done.8.refs_1_
  28.7 0.0 collective-permute-done.9.refs_2_
  28.7 0.0 copy-done
  28.7 1.1 %final.1 = (f32[4,256,128]{2,1,0:T(8,128)}, f32[4,256,128]{2,1,0:T(8,128)}, f32[2,2]{1,0:T(2,128)}) custom-call(bf16[32,512]{1,0:T(8,128)(2,1)S(1)} %get-tuple-element.39.maps, f32[4,256,128]{2,1,0:T(8,128)S(1)} %get-tuple-element.65.residual, f32[4,256,128]{2,1,0:T(8,128)S(1)} %get-tuple-element.66.multiplier, f32[4,256,128]{2,1,0:T(8,128)S(1)} %copy-done, ...), custom_call_target="tpu_custom_call" | custom-call | flops 16777216 | bytes 2621440 | tf_op jit(solution)/shard_map/final/pallas_call | solution.py:494
Async XLA Ops:
  0.6 8.8 %copy-start.1 = (bf16[2,256,128]{2,1,0:T(8,128)(2,1)S(1)}, bf16[2,256,128]{2,1,0:T(8,128)(2,1)}, u32[]{:S(2)}) copy-start(bf16[2,256,128]{2,1,0:T(8,128)(2,1)} %hydro_ref.3) | copy-start | bytes 393220
  2.6 14.4 %collective-permute-start.3 = (bf16[1024,128]{1,0:T(8,128)(2,1)S(1)}, bf16[1024,128]{1,0:T(8,128)(2,1)S(1)}, u32[]{:S(2)}, u32[]{:S(2)}) collective-permute-start(bf16[1024,128]{1,0:T(8,128)(2,1)S(1)} %get-tuple-element.52), channel_id=1, source_target_pairs={{0,8},{1,2},{2,1},{3,4},{4,3},{5,6},{6,5},{7,15},{8,0},{9,10},{10,... | collective-permute-start | bytes 786440 | tf_op jit(solution)/shard_map/ppermute | solution.py:115
  3.1 4.1 %collective-permute-start.2 = (bf16[32,256]{1,0:T(8,128)(2,1)S(1)}, bf16[32,256]{1,0:T(8,128)(2,1)S(1)}, u32[]{:S(2)}, u32[]{:S(2)}) collective-permute-start(bf16[32,256]{1,0:T(8,128)(2,1)S(1)} %get-tuple-element.48.refs_0_), channel_id=1, source_target_pairs={{0,24},{8,16},{16,8},{24,0},{1,25},{9,17},{17,9},{25,1},{2,26},{10... | collective-permute-start | bytes 49160 | tf_op jit(solution)/shard_map/ppermute | solution.py:100
  5.7 3.7 %collective-permute-start.1 = (bf16[32,256]{1,0:T(8,128)(2,1)S(1)}, bf16[32,256]{1,0:T(8,128)(2,1)S(1)}, u32[]{:S(2)}, u32[]{:S(2)}) collective-permute-start(bf16[32,256]{1,0:T(8,128)(2,1)S(1)} %get-tuple-element.48.refs_0_), channel_id=1, source_target_pairs={{0,16},{8,24},{16,0},{24,8},{1,17},{9,25},{17,1},{25,9},{2,18},{10... | collective-permute-start | bytes 49160 | tf_op jit(solution)/shard_map/ppermute | solution.py:100
  5.8 3.7 %collective-permute-start = (bf16[32,256]{1,0:T(8,128)(2,1)S(1)}, bf16[32,256]{1,0:T(8,128)(2,1)S(1)}, u32[]{:S(2)}, u32[]{:S(2)}) collective-permute-start(bf16[32,256]{1,0:T(8,128)(2,1)S(1)} %get-tuple-element.48.refs_0_), channel_id=1, source_target_pairs={{0,8},{8,0},{16,24},{24,16},{1,9},{9,1},{17,25},{25,17},{2,10},{10... | collective-permute-start | bytes 49160 | tf_op jit(solution)/shard_map/ppermute | solution.py:100
  10.5 13.7 %all-to-all-start = ((bf16[8,64,256]{2,1,0:T(8,128)(2,1)}), bf16[8,64,256]{2,1,0:T(8,128)(2,1)S(1)}, u32[]{:S(2)}, u32[]{:S(2)}) async-start(bf16[8,64,256]{2,1,0:T(8,128)(2,1)} %pressure.1), calls=%async_computation | async-start | bytes 524288 | tf_op jit(solution)/shard_map/all_to_all | solution.py:446
  17.0 8.0 %collective-permute-start.4 = (bf16[1024,128]{1,0:T(8,128)(2,1)}, bf16[1024,128]{1,0:T(8,128)(2,1)S(1)}, u32[]{:S(2)}, u32[]{:S(2)}) collective-permute-start(bf16[1024,128]{1,0:T(8,128)(2,1)} %get-tuple-element.62), channel_id=1, source_target_pairs={{0,8},{1,9},{2,10},{3,11},{4,12},{5,13},{6,14},{7,15},{8,0},{9,1},... | collective-permute-start | bytes 786440 | tf_op jit(solution)/shard_map/ppermute | solution.py:115
  17.0 9.7 %collective-permute-start.5 = (bf16[1024,128]{1,0:T(8,128)(2,1)S(1)}, bf16[1024,128]{1,0:T(8,128)(2,1)S(1)}, u32[]{:S(2)}, u32[]{:S(2)}) collective-permute-start(bf16[1024,128]{1,0:T(8,128)(2,1)S(1)} %get-tuple-element.63), channel_id=1, source_target_pairs={{0,24},{1,25},{2,26},{3,27},{4,28},{5,29},{6,30},{7,31},{8,16},{9,... | collective-permute-start | bytes 786440 | tf_op jit(solution)/shard_map/ppermute | solution.py:115
  17.8 9.9 %collective-permute-start.6 = (bf16[1024,128]{1,0:T(8,128)(2,1)S(1)}, bf16[1024,128]{1,0:T(8,128)(2,1)S(1)}, u32[]{:S(2)}, u32[]{:S(2)}) collective-permute-start(bf16[1024,128]{1,0:T(8,128)(2,1)S(1)} %get-tuple-element.64), channel_id=1, source_target_pairs={{0,1},{1,0},{2,3},{3,2},{4,5},{5,4},{6,7},{7,6},{8,9},{9,8},{10,11... | collective-permute-start | bytes 786440 | tf_op jit(solution)/shard_map/ppermute | solution.py:115
  24.5 4.2 %copy-start = (f32[4,256,128]{2,1,0:T(8,128)S(1)}, f32[4,256,128]{2,1,0:T(8,128)}, u32[]{:S(2)}) copy-start(f32[4,256,128]{2,1,0:T(8,128)} %get-tuple-element.67.own) | copy-start | bytes 1572868
  24.5 4.1 %collective-permute-start.7 = (f32[32,256]{1,0:T(8,128)S(1)}, f32[32,256]{1,0:T(8,128)S(1)}, u32[]{:S(2)}, u32[]{:S(2)}) collective-permute-start(f32[32,256]{1,0:T(8,128)S(1)} %get-tuple-element.68), channel_id=1, source_target_pairs={{0,16},{8,24},{16,0},{24,8},{1,17},{9,25},{17,1},{25,9},{2,18},{10... | collective-permute-start | bytes 98312 | tf_op jit(solution)/shard_map/ppermute | solution.py:100
  25.0 3.7 %collective-permute-start.8 = (f32[32,256]{1,0:T(8,128)S(1)}, f32[32,256]{1,0:T(8,128)S(1)}, u32[]{:S(2)}, u32[]{:S(2)}) collective-permute-start(f32[32,256]{1,0:T(8,128)S(1)} %get-tuple-element.69), channel_id=1, source_target_pairs={{0,24},{8,16},{16,8},{24,0},{1,25},{9,17},{17,9},{25,1},{2,26},{10... | collective-permute-start | bytes 98312 | tf_op jit(solution)/shard_map/ppermute | solution.py:100
  25.0 3.7 %collective-permute-start.9 = (f32[32,256]{1,0:T(8,128)S(1)}, f32[32,256]{1,0:T(8,128)S(1)}, u32[]{:S(2)}, u32[]{:S(2)}) collective-permute-start(f32[32,256]{1,0:T(8,128)S(1)} %get-tuple-element.70), channel_id=1, source_target_pairs={{0,8},{8,0},{16,24},{24,16},{1,9},{9,1},{17,25},{25,17},{2,10},{10... | collective-permute-start | bytes 98312 | tf_op jit(solution)/shard_map/ppermute | solution.py:100

commit v10 on v9

--- a/solution.py
+++ b/solution.py
@@ -430,7 +430,7 @@
         out_specs=[WHOLE] * (1 + len(late)),
         scratch_shapes=[pltpu.VMEM((blocks, wide, 2 * unknowns), BF16)],
         compiler_params=params(16),
-        cost_estimate=cost(many * block_flops, 4 * blocks * wide * unknowns + 12 * blocks * unknowns**2),
+        cost_estimate=cost(30 * many * block_flops, 4 * blocks * wide * unknowns + 12 * blocks * unknowns**2),
     )(near_motion, near_load, maps, near_coupling)
     (*payloads, load_panels) = lax.optimization_barrier((*payloads, load_panels))
     parts = pl.pallas_call(
@@ -441,7 +441,7 @@
         out_specs=FAR,
         scratch_shapes=[pltpu.VMEM((2, n_gx * panels, wide), BF16), pltpu.VMEM((n_gy, 2 * panels, wide), BF16), DMA((2,))],
         compiler_params=params(16),
-        cost_estimate=cost(2 * hydro.size * wide, 2 * hydro.size),
+        cost_estimate=cost(60 * hydro.size * wide, 2 * hydro.size),
     )(hydro, load_panels, *pieces)
     arrived = lax.all_to_all(parts, "gy", 0, 0, axis_index_groups=[places_along_gy(n_gy)], tiled=True)
     (*payloads, fourth) = lax.optimization_barrier((*payloads, fourth))

time: 30.1 us -> 29 us (0.963)
  waiting for transfers between devices: 5.34 us -> 4.04 us
    ppermute x6, waiting for transfers between devices: 2.8 us -> 1.7 us  [exchange(): return lax.ppermute(x, 'gx', [(i, target(i, step, n)) for i in range(n)])]
    all_to_all x1, waiting for transfers between devices: 1.55 us -> 0.65 us  [on_device(): lax.all_to_all(parts, 'gy', 0, 0, axis_index_groups=[places_along_gy(n_gy...]
    ppermute x4, waiting for transfers between devices: 1 us -> 1.68 us  [exchange_sides(): return lax.ppermute(x, ('gx', 'gy'), pairs)]
    ppermute x6, starting transfers between devices: 4.95 us -> 5.33 us  [exchange(): return lax.ppermute(x, 'gx', [(i, target(i, step, n)) for i in range(n)])]
  transfers between devices with their start and end apart: 11 -> 11, of which waited for: 5 -> 4; matrix products, arithmetic and copies ran while one was open for 0% -> 0% of each run, Pallas kernels for 22% -> 22%
where the time goes in v10:
time: 29 us; the launch traced here: 28.7 us
  starting transfers between devices  14.5 us (50%)
  Pallas kernels  9.41 us (32%)
  waiting for transfers between devices  4.04 us (14%)
  between operations  0.7 us (2%)
    all_to_all x1, starting transfers between devices, on_device(): lax.all_to_all(parts, 'gy', 0, 0, axis_index_groups=[places_along_gy(n_gy...  6.41 us
    ppermute x6, starting transfers between devices, exchange(): return lax.ppermute(x, 'gx', [(i, target(i, step, n)) for i in range(n)])  5.33 us
    pallas_call x1, Pallas kernels, on_device(): pl.pallas_call(functools.partial(interior_kernel, rows, cols, (n_gx, n_gy...  3.34 us
    ppermute x4, starting transfers between devices, exchange_sides(): return lax.ppermute(x, ('gx', 'gy'), pairs)  2.81 us
    pallas_call x1, Pallas kernels, on_device(): pl.pallas_call(functools.partial(panels_kernel, rows, cols, early, late),...  1.9 us
    ppermute x6, waiting for transfers between devices, exchange(): return lax.ppermute(x, 'gx', [(i, target(i, step, n)) for i in range(n)])  1.7 us
    ppermute x4, waiting for transfers between devices, exchange_sides(): return lax.ppermute(x, ('gx', 'gy'), pairs)  1.68 us
    pallas_call x1, Pallas kernels, on_device(): pl.pallas_call(functools.partial(edges_kernel, rows, cols, late), name='e...  1.13 us
  transfers between devices with their start and end apart: 11, of which 4 were waited for; matrix products, arithmetic and copies ran while one was open for 0% of the time, Pallas kernels for 22%

profile of v10, /device:TPU:0, one launch (start us, length us, event | category | flops | bytes accessed | tf_op | source)
XLA Modules:
  0.0 28.7 jit_solution(2107670607030875427)
XLA Ops:
  0.6 1.9 %panels.1 = (bf16[32,256]{1,0:T(8,128)(2,1)S(1)}, bf16[1024,128]{1,0:T(8,128)(2,1)S(1)}, bf16[4,256,128]{2,1,0:T(8,128)(2,1)S(1)}, bf16[4,256,128]{2,1,0:T(8,128...) custom-call(s32[2,2,4]{2,1,0:T(2,128)} %joints_far.3, bf16[4,256,128]{2,1,0:T(8,128)(2,1)} %bitcast.9, ...), custom_call_target="tpu_custom_call" | custom-call | flops 16777216 | bytes 524288 | tf_op jit(solution)/shard_map/panels/pallas_call | solution.py:403
  2.5 2.4 %collective-permute-start.2 = (bf16[32,256]{1,0:T(8,128)(2,1)S(1)}, bf16[32,256]{1,0:T(8,128)(2,1)S(1)}, u32[]{:S(2)}, u32[]{:S(2)}) collective-permute-start(bf16[32,256]{1,0:T(8,128)(2,1)S(1)} %get-tuple-element.48.refs_0_), channel_id=1, source_target_pairs={{0,24},{8,16},{16,8},{24,0},{1,25},{9,17},{17,9},{25,1},{2,26},{10... | collective-permute-start | bytes 49160 | tf_op jit(solution)/shard_map/ppermute | solution.py:100
  5.0 0.6 %collective-permute-start.1 = (bf16[32,256]{1,0:T(8,128)(2,1)S(1)}, bf16[32,256]{1,0:T(8,128)(2,1)S(1)}, u32[]{:S(2)}, u32[]{:S(2)}) collective-permute-start(bf16[32,256]{1,0:T(8,128)(2,1)S(1)} %get-tuple-element.48.refs_0_), channel_id=1, source_target_pairs={{0,16},{8,24},{16,0},{24,8},{1,17},{9,25},{17,1},{25,9},{2,18},{10... | collective-permute-start | bytes 49160 | tf_op jit(solution)/shard_map/ppermute | solution.py:100
  5.6 0.0 collective-permute-start
  5.7 0.5 %collective-permute-start.3 = (bf16[1024,128]{1,0:T(8,128)(2,1)S(1)}, bf16[1024,128]{1,0:T(8,128)(2,1)S(1)}, u32[]{:S(2)}, u32[]{:S(2)}) collective-permute-start(bf16[1024,128]{1,0:T(8,128)(2,1)S(1)} %get-tuple-element.52), channel_id=1, source_target_pairs={{0,8},{1,2},{2,1},{3,4},{4,3},{5,6},{6,5},{7,15},{8,0},{9,10},{10,... | collective-permute-start | bytes 786440 | tf_op jit(solution)/shard_map/ppermute | solution.py:115
  6.1 0.0 copy-start.1
  6.1 1.1 %edges.1 = (bf16[32,256]{1,0:T(8,128)(2,1)S(1)}, bf16[1024,128]{1,0:T(8,128)(2,1)}, bf16[1024,128]{1,0:T(8,128)(2,1)S(1)}, bf16[1024,128]{1,0:T(8,128)(2,1)S(1)}) custom-call(bf16[4,256,128]{2,1,0:T(8,128)(2,1)S(1)} %get-tuple-element.40.motion, bf16[4,256,128]{2,1,0:T(8,128)(2,1)S(1)} %get-tuple-element.41.load, ...), custom_call_target="tpu_custom_call" | custom-call | flops 3019898880 | bytes 1310720 | tf_op jit(solution)/shard_map/edges/pallas_call | solution.py:424
  7.3 0.0 collective-permute-done.2.refs_3_
  7.3 1.5 %collective-permute-done.1.refs_2_ = bf16[32,256]{1,0:T(8,128)(2,1)S(1)} collective-permute-done((bf16[32,256]{1,0:T(8,128)(2,1)S(1)}, bf16[32,256]{1,0:T(8,128)(2,1)S(1)}, u32[]{:S(2)}, u32[]{:S(2)}) %collective-permute-start.1) | collective-permute-done | bytes 16416 | tf_op jit(solution)/shard_map/ppermute | solution.py:100
  8.7 0.0 collective-permute-done.refs_1_
  8.7 0.0 copy-done.1
  8.7 1.0 %pressure.1 = bf16[8,64,256]{2,1,0:T(8,128)(2,1)} custom-call(bf16[2,256,128]{2,1,0:T(8,128)(2,1)S(1)} %copy-done.1, bf16[32,256]{1,0:T(8,128)(2,1)S(1)} %get-tuple-element.47.load_panels, bf16[32,256]{1,0:T(8,128)(2,1)S(1)} %get-tuple-element.48.refs_0_, bf16[32,256]{1,0:T(8,128)(2,1)S(1)} %collective-permute-done.refs_1_, ...), custom_call_target="tpu_custom_call" | custom-call | flops 1006632960 | bytes 131072 | tf_op jit(solution)/shard_map/pressure/pallas_call | solution.py:436
  9.7 6.4 %all-to-all-start = ((bf16[8,64,256]{2,1,0:T(8,128)(2,1)}), bf16[8,64,256]{2,1,0:T(8,128)(2,1)S(1)}, u32[]{:S(2)}, u32[]{:S(2)}) async-start(bf16[8,64,256]{2,1,0:T(8,128)(2,1)} %pressure.1), calls=%async_computation | async-start | bytes 524288 | tf_op jit(solution)/shard_map/all_to_all | solution.py:446
  16.1 0.0 collective-permute-done.3.refs_1_
  16.2 0.0 collective-permute-start.4
  16.2 0.9 %collective-permute-start.5 = (bf16[1024,128]{1,0:T(8,128)(2,1)S(1)}, bf16[1024,128]{1,0:T(8,128)(2,1)S(1)}, u32[]{:S(2)}, u32[]{:S(2)}) collective-permute-start(bf16[1024,128]{1,0:T(8,128)(2,1)S(1)} %get-tuple-element.63), channel_id=1, source_target_pairs={{0,24},{1,25},{2,26},{3,27},{4,28},{5,29},{6,30},{7,31},{8,16},{9,... | collective-permute-start | bytes 786440 | tf_op jit(solution)/shard_map/ppermute | solution.py:115
  17.0 1.5 %collective-permute-start.6 = (bf16[1024,128]{1,0:T(8,128)(2,1)S(1)}, bf16[1024,128]{1,0:T(8,128)(2,1)S(1)}, u32[]{:S(2)}, u32[]{:S(2)}) collective-permute-start(bf16[1024,128]{1,0:T(8,128)(2,1)S(1)} %get-tuple-element.64), channel_id=1, source_target_pairs={{0,1},{1,0},{2,3},{3,2},{4,5},{5,4},{6,7},{7,6},{8,9},{9,8},{10,11... | collective-permute-start | bytes 786440 | tf_op jit(solution)/shard_map/ppermute | solution.py:115
  18.5 3.3 %interior.1 = (f32[4,256,128]{2,1,0:T(8,128)S(1)}, f32[4,256,128]{2,1,0:T(8,128)S(1)}, f32[4,256,128]{2,1,0:T(8,128)}, bf16[6,2,128,128]{3,2,1,0:T(8,128)(2,1)S(1)}) custom-call(s32[2,2,4]{2,1,0:T(2,128)} %joints_far.3, bf16[4,256,128]{2,1,0:T(8,128)(2,1)} %bitcast.10, bf16[4,256,128]{2,1,0:T(8,128)(2,1)} %bitcast.12, bf16[4,256,128]{2,1,0:T(8,128)(2,1)} %bitcast.13, ...), custom_call_target="tpu_custom_call" | custom-call | flops 402653184 | bytes 3670016 | tf_op jit(solution)/shard_map/interior/pallas_call | solution.py:452
  21.9 0.7 %all-to-all-done.arrived = bf16[8,64,256]{2,1,0:T(8,128)(2,1)S(1)} async-done(((bf16[8,64,256]{2,1,0:T(8,128)(2,1)}), bf16[8,64,256]{2,1,0:T(8,128)(2,1)S(1)}, u32[]{:S(2)}, u32[]{:S(2)}) %all-to-all-start) | async-done | bytes 262176 | tf_op jit(solution)/shard_map/all_to_all | solution.py:446
  22.5 0.3 %reaction.1 = (f32[32,256]{1,0:T(8,128)S(1)}, f32[32,256]{1,0:T(8,128)S(1)}, f32[32,256]{1,0:T(8,128)S(1)}, f32[32,256]{1,0:T(8,128)S(1)}) custom-call(bf16[2,256,128]{2,1,0:T(8,128)(2,1)S(1)} %copy-done.1, bf16[8,64,256]{2,1,0:T(8,128)(2,1)S(1)} %all-to-all-done.arrived), custom_call_target="tpu_custom_call" | custom-call | flops 33554432 | bytes 131072 | tf_op jit(solution)/shard_map/reaction/pallas_call | solution.py:472
  22.8 0.0 copy-start
  22.8 1.4 %collective-permute-start.7 = (f32[32,256]{1,0:T(8,128)S(1)}, f32[32,256]{1,0:T(8,128)S(1)}, u32[]{:S(2)}, u32[]{:S(2)}) collective-permute-start(f32[32,256]{1,0:T(8,128)S(1)} %get-tuple-element.68), channel_id=1, source_target_pairs={{0,16},{8,24},{16,0},{24,8},{1,17},{9,25},{17,1},{25,9},{2,18},{10... | collective-permute-start | bytes 98312 | tf_op jit(solution)/shard_map/ppermute | solution.py:100
  24.3 0.0 collective-permute-start.8
  24.3 0.0 collective-permute-done.4.refs_0_
  24.3 0.8 %collective-permute-start.9 = (f32[32,256]{1,0:T(8,128)S(1)}, f32[32,256]{1,0:T(8,128)S(1)}, u32[]{:S(2)}, u32[]{:S(2)}) collective-permute-start(f32[32,256]{1,0:T(8,128)S(1)} %get-tuple-element.70), channel_id=1, source_target_pairs={{0,8},{8,0},{16,24},{24,16},{1,9},{9,1},{17,25},{25,17},{2,10},{10... | collective-permute-start | bytes 98312 | tf_op jit(solution)/shard_map/ppermute | solution.py:100
  25.1 0.0 collective-permute-done.5.refs_1_
  25.1 1.7 %collective-permute-done.6.refs_2_ = bf16[1024,128]{1,0:T(8,128)(2,1)S(1)} collective-permute-done((bf16[1024,128]{1,0:T(8,128)(2,1)S(1)}, bf16[1024,128]{1,0:T(8,128)(2,1)S(1)}, u32[]{:S(2)}, u32[]{:S(2)}) %collective-permute-start.6) | collective-permute-done | bytes 262176 | tf_op jit(solution)/shard_map/ppermute | solution.py:115
  26.7 0.6 %boundary.1 = (f32[4,256,128]{2,1,0:T(8,128)S(1)}, f32[4,256,128]{2,1,0:T(8,128)S(1)}) custom-call(bf16[32,512]{1,0:T(8,128)(2,1)S(1)} %get-tuple-element.39.maps, bf16[6,2,128,128]{3,2,1,0:T(8,128)(2,1)S(1)} %get-tuple-element.58.coupling, f32[4,256,128]{2,1,0:T(8,128)S(1)} %get-tuple-element.59.residual, f32[4,256,128]{2,1,0:T(8,128)S(1)} %get-tuple-element.60.multiplier, ...), custom_call_target="tpu_custom_call" | custom-call | flops 268435456 | bytes 3014656 | tf_op jit(solution)/shard_map/boundary/pallas_call | solution.py:484
  27.3 0.0 collective-permute-done.7.refs_0_
  27.4 0.2 collective-permute-done.8.refs_1_
  27.6 0.0 collective-permute-done.9.refs_2_
  27.6 0.0 copy-done
  27.6 1.1 %final.1 = (f32[4,256,128]{2,1,0:T(8,128)}, f32[4,256,128]{2,1,0:T(8,128)}, f32[2,2]{1,0:T(2,128)}) custom-call(bf16[32,512]{1,0:T(8,128)(2,1)S(1)} %get-tuple-element.39.maps, f32[4,256,128]{2,1,0:T(8,128)S(1)} %get-tuple-element.65.residual, f32[4,256,128]{2,1,0:T(8,128)S(1)} %get-tuple-element.66.multiplier, f32[4,256,128]{2,1,0:T(8,128)S(1)} %copy-done, ...), custom_call_target="tpu_custom_call" | custom-call | flops 16777216 | bytes 2621440 | tf_op jit(solution)/shard_map/final/pallas_call | solution.py:494
Async XLA Ops:
  2.5 4.7 %collective-permute-start.2 = (bf16[32,256]{1,0:T(8,128)(2,1)S(1)}, bf16[32,256]{1,0:T(8,128)(2,1)S(1)}, u32[]{:S(2)}, u32[]{:S(2)}) collective-permute-start(bf16[32,256]{1,0:T(8,128)(2,1)S(1)} %get-tuple-element.48.refs_0_), channel_id=1, source_target_pairs={{0,24},{8,16},{16,8},{24,0},{1,25},{9,17},{17,9},{25,1},{2,26},{10... | collective-permute-start | bytes 49160 | tf_op jit(solution)/shard_map/ppermute | solution.py:100
  5.0 3.7 %collective-permute-start.1 = (bf16[32,256]{1,0:T(8,128)(2,1)S(1)}, bf16[32,256]{1,0:T(8,128)(2,1)S(1)}, u32[]{:S(2)}, u32[]{:S(2)}) collective-permute-start(bf16[32,256]{1,0:T(8,128)(2,1)S(1)} %get-tuple-element.48.refs_0_), channel_id=1, source_target_pairs={{0,16},{8,24},{16,0},{24,8},{1,17},{9,25},{17,1},{25,9},{2,18},{10... | collective-permute-start | bytes 49160 | tf_op jit(solution)/shard_map/ppermute | solution.py:100
  5.6 3.1 %collective-permute-start = (bf16[32,256]{1,0:T(8,128)(2,1)S(1)}, bf16[32,256]{1,0:T(8,128)(2,1)S(1)}, u32[]{:S(2)}, u32[]{:S(2)}) collective-permute-start(bf16[32,256]{1,0:T(8,128)(2,1)S(1)} %get-tuple-element.48.refs_0_), channel_id=1, source_target_pairs={{0,8},{8,0},{16,24},{24,16},{1,9},{9,1},{17,25},{25,17},{2,10},{10... | collective-permute-start | bytes 49160 | tf_op jit(solution)/shard_map/ppermute | solution.py:100
  5.7 10.5 %collective-permute-start.3 = (bf16[1024,128]{1,0:T(8,128)(2,1)S(1)}, bf16[1024,128]{1,0:T(8,128)(2,1)S(1)}, u32[]{:S(2)}, u32[]{:S(2)}) collective-permute-start(bf16[1024,128]{1,0:T(8,128)(2,1)S(1)} %get-tuple-element.52), channel_id=1, source_target_pairs={{0,8},{1,2},{2,1},{3,4},{4,3},{5,6},{6,5},{7,15},{8,0},{9,10},{10,... | collective-permute-start | bytes 786440 | tf_op jit(solution)/shard_map/ppermute | solution.py:115
  6.1 2.6 %copy-start.1 = (bf16[2,256,128]{2,1,0:T(8,128)(2,1)S(1)}, bf16[2,256,128]{2,1,0:T(8,128)(2,1)}, u32[]{:S(2)}) copy-start(bf16[2,256,128]{2,1,0:T(8,128)(2,1)} %hydro_ref.3) | copy-start | bytes 393220
  9.7 12.8 %all-to-all-start = ((bf16[8,64,256]{2,1,0:T(8,128)(2,1)}), bf16[8,64,256]{2,1,0:T(8,128)(2,1)S(1)}, u32[]{:S(2)}, u32[]{:S(2)}) async-start(bf16[8,64,256]{2,1,0:T(8,128)(2,1)} %pressure.1), calls=%async_computation | async-start | bytes 524288 | tf_op jit(solution)/shard_map/all_to_all | solution.py:446
  16.2 8.1 %collective-permute-start.4 = (bf16[1024,128]{1,0:T(8,128)(2,1)}, bf16[1024,128]{1,0:T(8,128)(2,1)S(1)}, u32[]{:S(2)}, u32[]{:S(2)}) collective-permute-start(bf16[1024,128]{1,0:T(8,128)(2,1)} %get-tuple-element.62), channel_id=1, source_target_pairs={{0,8},{1,9},{2,10},{3,11},{4,12},{5,13},{6,14},{7,15},{8,0},{9,1},... | collective-permute-start | bytes 786440 | tf_op jit(solution)/shard_map/ppermute | solution.py:115
  16.2 8.9 %collective-permute-start.5 = (bf16[1024,128]{1,0:T(8,128)(2,1)S(1)}, bf16[1024,128]{1,0:T(8,128)(2,1)S(1)}, u32[]{:S(2)}, u32[]{:S(2)}) collective-permute-start(bf16[1024,128]{1,0:T(8,128)(2,1)S(1)} %get-tuple-element.63), channel_id=1, source_target_pairs={{0,24},{1,25},{2,26},{3,27},{4,28},{5,29},{6,30},{7,31},{8,16},{9,... | collective-permute-start | bytes 786440 | tf_op jit(solution)/shard_map/ppermute | solution.py:115
  17.0 9.7 %collective-permute-start.6 = (bf16[1024,128]{1,0:T(8,128)(2,1)S(1)}, bf16[1024,128]{1,0:T(8,128)(2,1)S(1)}, u32[]{:S(2)}, u32[]{:S(2)}) collective-permute-start(bf16[1024,128]{1,0:T(8,128)(2,1)S(1)} %get-tuple-element.64), channel_id=1, source_target_pairs={{0,1},{1,0},{2,3},{3,2},{4,5},{5,4},{6,7},{7,6},{8,9},{9,8},{10,11... | collective-permute-start | bytes 786440 | tf_op jit(solution)/shard_map/ppermute | solution.py:115
  22.8 4.8 %copy-start = (f32[4,256,128]{2,1,0:T(8,128)S(1)}, f32[4,256,128]{2,1,0:T(8,128)}, u32[]{:S(2)}) copy-start(f32[4,256,128]{2,1,0:T(8,128)} %get-tuple-element.67.own) | copy-start | bytes 1572868
  22.8 4.5 %collective-permute-start.7 = (f32[32,256]{1,0:T(8,128)S(1)}, f32[32,256]{1,0:T(8,128)S(1)}, u32[]{:S(2)}, u32[]{:S(2)}) collective-permute-start(f32[32,256]{1,0:T(8,128)S(1)} %get-tuple-element.68), channel_id=1, source_target_pairs={{0,16},{8,24},{16,0},{24,8},{1,17},{9,25},{17,1},{25,9},{2,18},{10... | collective-permute-start | bytes 98312 | tf_op jit(solution)/shard_map/ppermute | solution.py:100
  24.3 3.3 %collective-permute-start.8 = (f32[32,256]{1,0:T(8,128)S(1)}, f32[32,256]{1,0:T(8,128)S(1)}, u32[]{:S(2)}, u32[]{:S(2)}) collective-permute-start(f32[32,256]{1,0:T(8,128)S(1)} %get-tuple-element.69), channel_id=1, source_target_pairs={{0,24},{8,16},{16,8},{24,0},{1,25},{9,17},{17,9},{25,1},{2,26},{10... | collective-permute-start | bytes 98312 | tf_op jit(solution)/shard_map/ppermute | solution.py:100
  24.3 3.3 %collective-permute-start.9 = (f32[32,256]{1,0:T(8,128)S(1)}, f32[32,256]{1,0:T(8,128)S(1)}, u32[]{:S(2)}, u32[]{:S(2)}) collective-permute-start(f32[32,256]{1,0:T(8,128)S(1)} %get-tuple-element.70), channel_id=1, source_target_pairs={{0,8},{8,0},{16,24},{24,16},{1,9},{9,1},{17,25},{25,17},{2,10},{10... | collective-permute-start | bytes 98312 | tf_op jit(solution)/shard_map/ppermute | solution.py:100

commit v11 on v10

--- a/solution.py
+++ b/solution.py
@@ -479,7 +479,7 @@
         compiler_params=params(16),
         cost_estimate=cost(2 * hydro.size * wide, 2 * hydro.size),
     )(hydro, arrived)
-    reactions = [exchange(reaction_parts[step], step) for step in reversed(range(1, n_gx))] + [reaction_parts[0]]
+    reactions = [exchange(reaction_parts[step], step) for step in [*range(2, n_gx), 1]] + [reaction_parts[0]]
 
     residual, multiplier = pl.pallas_call(
         functools.partial(boundary_kernel, rows, cols, (n_gx, n_gy), lift, late),

time: 29 us -> 28.7 us (0.990)
  transfers between devices with their start and end apart: 11 -> 11, of which waited for: 4 -> 3; matrix products, arithmetic and copies ran while one was open for 0% -> 0% of each run, Pallas kernels for 22% -> 22%
where the time goes in v11:
time: 28.7 us; the launch traced here: 28.5 us
  starting transfers between devices  14.3 us (50%)
  Pallas kernels  9.41 us (33%)
  waiting for transfers between devices  4.07 us (14%)
  between operations  0.72 us (3%)
    all_to_all x1, starting transfers between devices, on_device(): lax.all_to_all(parts, 'gy', 0, 0, axis_index_groups=[places_along_gy(n_gy...  6.41 us
    ppermute x6, starting transfers between devices, exchange(): return lax.ppermute(x, 'gx', [(i, target(i, step, n)) for i in range(n)])  5.05 us
    pallas_call x1, Pallas kernels, on_device(): pl.pallas_call(functools.partial(interior_kernel, rows, cols, (n_gx, n_gy...  3.34 us
    ppermute x4, starting transfers between devices, exchange_sides(): return lax.ppermute(x, ('gx', 'gy'), pairs)  2.81 us
    ppermute x4, waiting for transfers between devices, exchange_sides(): return lax.ppermute(x, ('gx', 'gy'), pairs)  1.96 us
    pallas_call x1, Pallas kernels, on_device(): pl.pallas_call(functools.partial(panels_kernel, rows, cols, early, late),...  1.9 us
    ppermute x6, waiting for transfers between devices, exchange(): return lax.ppermute(x, 'gx', [(i, target(i, step, n)) for i in range(n)])  1.46 us
    pallas_call x1, Pallas kernels, on_device(): pl.pallas_call(functools.partial(edges_kernel, rows, cols, late), name='e...  1.13 us
  transfers between devices with their start and end apart: 11, of which 3 were waited for; matrix products, arithmetic and copies ran while one was open for 0% of the time, Pallas kernels for 22%

profile of v11, /device:TPU:0, one launch (start us, length us, event | category | flops | bytes accessed | tf_op | source)
XLA Modules:
  0.0 28.5 jit_solution(8563785644101120519)
XLA Ops:
  0.6 1.9 %panels.1 = (bf16[32,256]{1,0:T(8,128)(2,1)S(1)}, bf16[1024,128]{1,0:T(8,128)(2,1)S(1)}, bf16[4,256,128]{2,1,0:T(8,128)(2,1)S(1)}, bf16[4,256,128]{2,1,0:T(8,128...) custom-call(s32[2,2,4]{2,1,0:T(2,128)} %joints_far.3, bf16[4,256,128]{2,1,0:T(8,128)(2,1)} %bitcast.9, ...), custom_call_target="tpu_custom_call" | custom-call | flops 16777216 | bytes 524288 | tf_op jit(solution)/shard_map/panels/pallas_call | solution.py:403
  2.5 2.4 %collective-permute-start.2 = (bf16[32,256]{1,0:T(8,128)(2,1)S(1)}, bf16[32,256]{1,0:T(8,128)(2,1)S(1)}, u32[]{:S(2)}, u32[]{:S(2)}) collective-permute-start(bf16[32,256]{1,0:T(8,128)(2,1)S(1)} %get-tuple-element.48.refs_0_), channel_id=1, source_target_pairs={{0,24},{8,16},{16,8},{24,0},{1,25},{9,17},{17,9},{25,1},{2,26},{10... | collective-permute-start | bytes 49160 | tf_op jit(solution)/shard_map/ppermute | solution.py:100
  5.0 0.6 %collective-permute-start.1 = (bf16[32,256]{1,0:T(8,128)(2,1)S(1)}, bf16[32,256]{1,0:T(8,128)(2,1)S(1)}, u32[]{:S(2)}, u32[]{:S(2)}) collective-permute-start(bf16[32,256]{1,0:T(8,128)(2,1)S(1)} %get-tuple-element.48.refs_0_), channel_id=1, source_target_pairs={{0,16},{8,24},{16,0},{24,8},{1,17},{9,25},{17,1},{25,9},{2,18},{10... | collective-permute-start | bytes 49160 | tf_op jit(solution)/shard_map/ppermute | solution.py:100
  5.6 0.0 collective-permute-start
  5.7 0.5 %collective-permute-start.3 = (bf16[1024,128]{1,0:T(8,128)(2,1)S(1)}, bf16[1024,128]{1,0:T(8,128)(2,1)S(1)}, u32[]{:S(2)}, u32[]{:S(2)}) collective-permute-start(bf16[1024,128]{1,0:T(8,128)(2,1)S(1)} %get-tuple-element.52), channel_id=1, source_target_pairs={{0,8},{1,2},{2,1},{3,4},{4,3},{5,6},{6,5},{7,15},{8,0},{9,10},{10,... | collective-permute-start | bytes 786440 | tf_op jit(solution)/shard_map/ppermute | solution.py:115
  6.1 0.0 copy-start.1
  6.1 1.1 %edges.1 = (bf16[32,256]{1,0:T(8,128)(2,1)S(1)}, bf16[1024,128]{1,0:T(8,128)(2,1)}, bf16[1024,128]{1,0:T(8,128)(2,1)S(1)}, bf16[1024,128]{1,0:T(8,128)(2,1)S(1)}) custom-call(bf16[4,256,128]{2,1,0:T(8,128)(2,1)S(1)} %get-tuple-element.40.motion, bf16[4,256,128]{2,1,0:T(8,128)(2,1)S(1)} %get-tuple-element.41.load, ...), custom_call_target="tpu_custom_call" | custom-call | flops 3019898880 | bytes 1310720 | tf_op jit(solution)/shard_map/edges/pallas_call | solution.py:424
  7.3 0.0 collective-permute-done.2.refs_3_
  7.3 1.5 %collective-permute-done.1.refs_2_ = bf16[32,256]{1,0:T(8,128)(2,1)S(1)} collective-permute-done((bf16[32,256]{1,0:T(8,128)(2,1)S(1)}, bf16[32,256]{1,0:T(8,128)(2,1)S(1)}, u32[]{:S(2)}, u32[]{:S(2)}) %collective-permute-start.1) | collective-permute-done | bytes 16416 | tf_op jit(solution)/shard_map/ppermute | solution.py:100
  8.7 0.0 collective-permute-done.refs_1_
  8.7 0.0 copy-done.1
  8.7 1.0 %pressure.1 = bf16[8,64,256]{2,1,0:T(8,128)(2,1)} custom-call(bf16[2,256,128]{2,1,0:T(8,128)(2,1)S(1)} %copy-done.1, bf16[32,256]{1,0:T(8,128)(2,1)S(1)} %get-tuple-element.47.load_panels, bf16[32,256]{1,0:T(8,128)(2,1)S(1)} %get-tuple-element.48.refs_0_, bf16[32,256]{1,0:T(8,128)(2,1)S(1)} %collective-permute-done.refs_1_, ...), custom_call_target="tpu_custom_call" | custom-call | flops 1006632960 | bytes 131072 | tf_op jit(solution)/shard_map/pressure/pallas_call | solution.py:436
  9.7 6.4 %all-to-all-start = ((bf16[8,64,256]{2,1,0:T(8,128)(2,1)}), bf16[8,64,256]{2,1,0:T(8,128)(2,1)S(1)}, u32[]{:S(2)}, u32[]{:S(2)}) async-start(bf16[8,64,256]{2,1,0:T(8,128)(2,1)} %pressure.1), calls=%async_computation | async-start | bytes 524288 | tf_op jit(solution)/shard_map/all_to_all | solution.py:446
  16.1 0.0 collective-permute-done.3.refs_1_
  16.2 0.0 collective-permute-start.4
  16.2 0.9 %collective-permute-start.5 = (bf16[1024,128]{1,0:T(8,128)(2,1)S(1)}, bf16[1024,128]{1,0:T(8,128)(2,1)S(1)}, u32[]{:S(2)}, u32[]{:S(2)}) collective-permute-start(bf16[1024,128]{1,0:T(8,128)(2,1)S(1)} %get-tuple-element.63), channel_id=1, source_target_pairs={{0,24},{1,25},{2,26},{3,27},{4,28},{5,29},{6,30},{7,31},{8,16},{9,... | collective-permute-start | bytes 786440 | tf_op jit(solution)/shard_map/ppermute | solution.py:115
  17.0 1.5 %collective-permute-start.6 = (bf16[1024,128]{1,0:T(8,128)(2,1)S(1)}, bf16[1024,128]{1,0:T(8,128)(2,1)S(1)}, u32[]{:S(2)}, u32[]{:S(2)}) collective-permute-start(bf16[1024,128]{1,0:T(8,128)(2,1)S(1)} %get-tuple-element.64), channel_id=1, source_target_pairs={{0,1},{1,0},{2,3},{3,2},{4,5},{5,4},{6,7},{7,6},{8,9},{9,8},{10,11... | collective-permute-start | bytes 786440 | tf_op jit(solution)/shard_map/ppermute | solution.py:115
  18.5 3.3 %interior.1 = (f32[4,256,128]{2,1,0:T(8,128)S(1)}, f32[4,256,128]{2,1,0:T(8,128)S(1)}, f32[4,256,128]{2,1,0:T(8,128)}, bf16[6,2,128,128]{3,2,1,0:T(8,128)(2,1)S(1)}) custom-call(s32[2,2,4]{2,1,0:T(2,128)} %joints_far.3, bf16[4,256,128]{2,1,0:T(8,128)(2,1)} %bitcast.10, bf16[4,256,128]{2,1,0:T(8,128)(2,1)} %bitcast.12, bf16[4,256,128]{2,1,0:T(8,128)(2,1)} %bitcast.13, ...), custom_call_target="tpu_custom_call" | custom-call | flops 402653184 | bytes 3670016 | tf_op jit(solution)/shard_map/interior/pallas_call | solution.py:452
  21.9 0.7 %all-to-all-done.arrived = bf16[8,64,256]{2,1,0:T(8,128)(2,1)S(1)} async-done(((bf16[8,64,256]{2,1,0:T(8,128)(2,1)}), bf16[8,64,256]{2,1,0:T(8,128)(2,1)S(1)}, u32[]{:S(2)}, u32[]{:S(2)}) %all-to-all-start) | async-done | bytes 262176 | tf_op jit(solution)/shard_map/all_to_all | solution.py:446
  22.5 0.3 %reaction.1 = (f32[32,256]{1,0:T(8,128)S(1)}, f32[32,256]{1,0:T(8,128)S(1)}, f32[32,256]{1,0:T(8,128)S(1)}, f32[32,256]{1,0:T(8,128)S(1)}) custom-call(bf16[2,256,128]{2,1,0:T(8,128)(2,1)S(1)} %copy-done.1, bf16[8,64,256]{2,1,0:T(8,128)(2,1)S(1)} %all-to-all-done.arrived), custom_call_target="tpu_custom_call" | custom-call | flops 33554432 | bytes 131072 | tf_op jit(solution)/shard_map/reaction/pallas_call | solution.py:472
  22.8 0.0 copy-start
  22.8 0.1 collective-permute-start.7
  22.9 1.4 %collective-permute-start.8 = (f32[32,256]{1,0:T(8,128)S(1)}, f32[32,256]{1,0:T(8,128)S(1)}, u32[]{:S(2)}, u32[]{:S(2)}) collective-permute-start(f32[32,256]{1,0:T(8,128)S(1)} %get-tuple-element.69), channel_id=1, source_target_pairs={{0,16},{8,24},{16,0},{24,8},{1,17},{9,25},{17,1},{25,9},{2,18},{10... | collective-permute-start | bytes 98312 | tf_op jit(solution)/shard_map/ppermute | solution.py:100
  24.3 0.0 collective-permute-done.4.refs_0_
  24.3 0.4 %collective-permute-start.9 = (f32[32,256]{1,0:T(8,128)S(1)}, f32[32,256]{1,0:T(8,128)S(1)}, u32[]{:S(2)}, u32[]{:S(2)}) collective-permute-start(f32[32,256]{1,0:T(8,128)S(1)} %get-tuple-element.70), channel_id=1, source_target_pairs={{0,8},{8,0},{16,24},{24,16},{1,9},{9,1},{17,25},{25,17},{2,10},{10... | collective-permute-start | bytes 98312 | tf_op jit(solution)/shard_map/ppermute | solution.py:100
  24.8 0.0 collective-permute-done.5.refs_1_
  24.8 1.9 %collective-permute-done.6.refs_2_ = bf16[1024,128]{1,0:T(8,128)(2,1)S(1)} collective-permute-done((bf16[1024,128]{1,0:T(8,128)(2,1)S(1)}, bf16[1024,128]{1,0:T(8,128)(2,1)S(1)}, u32[]{:S(2)}, u32[]{:S(2)}) %collective-permute-start.6) | collective-permute-done | bytes 262176 | tf_op jit(solution)/shard_map/ppermute | solution.py:115
  26.7 0.6 %boundary.1 = (f32[4,256,128]{2,1,0:T(8,128)S(1)}, f32[4,256,128]{2,1,0:T(8,128)S(1)}) custom-call(bf16[32,512]{1,0:T(8,128)(2,1)S(1)} %get-tuple-element.39.maps, bf16[6,2,128,128]{3,2,1,0:T(8,128)(2,1)S(1)} %get-tuple-element.58.coupling, f32[4,256,128]{2,1,0:T(8,128)S(1)} %get-tuple-element.59.residual, f32[4,256,128]{2,1,0:T(8,128)S(1)} %get-tuple-element.60.multiplier, ...), custom_call_target="tpu_custom_call" | custom-call | flops 268435456 | bytes 3014656 | tf_op jit(solution)/shard_map/boundary/pallas_call | solution.py:484
  27.3 0.0 collective-permute-done.7.refs_0_
  27.4 0.0 collective-permute-done.8.refs_1_
  27.4 0.0 collective-permute-done.9.refs_2_
  27.4 0.0 copy-done
  27.4 1.1 %final.1 = (f32[4,256,128]{2,1,0:T(8,128)}, f32[4,256,128]{2,1,0:T(8,128)}, f32[2,2]{1,0:T(2,128)}) custom-call(bf16[32,512]{1,0:T(8,128)(2,1)S(1)} %get-tuple-element.39.maps, f32[4,256,128]{2,1,0:T(8,128)S(1)} %get-tuple-element.65.residual, f32[4,256,128]{2,1,0:T(8,128)S(1)} %get-tuple-element.66.multiplier, f32[4,256,128]{2,1,0:T(8,128)S(1)} %copy-done, ...), custom_call_target="tpu_custom_call" | custom-call | flops 16777216 | bytes 2621440 | tf_op jit(solution)/shard_map/final/pallas_call | solution.py:494
Async XLA Ops:
  2.5 4.7 %collective-permute-start.2 = (bf16[32,256]{1,0:T(8,128)(2,1)S(1)}, bf16[32,256]{1,0:T(8,128)(2,1)S(1)}, u32[]{:S(2)}, u32[]{:S(2)}) collective-permute-start(bf16[32,256]{1,0:T(8,128)(2,1)S(1)} %get-tuple-element.48.refs_0_), channel_id=1, source_target_pairs={{0,24},{8,16},{16,8},{24,0},{1,25},{9,17},{17,9},{25,1},{2,26},{10... | collective-permute-start | bytes 49160 | tf_op jit(solution)/shard_map/ppermute | solution.py:100
  5.0 3.7 %collective-permute-start.1 = (bf16[32,256]{1,0:T(8,128)(2,1)S(1)}, bf16[32,256]{1,0:T(8,128)(2,1)S(1)}, u32[]{:S(2)}, u32[]{:S(2)}) collective-permute-start(bf16[32,256]{1,0:T(8,128)(2,1)S(1)} %get-tuple-element.48.refs_0_), channel_id=1, source_target_pairs={{0,16},{8,24},{16,0},{24,8},{1,17},{9,25},{17,1},{25,9},{2,18},{10... | collective-permute-start | bytes 49160 | tf_op jit(solution)/shard_map/ppermute | solution.py:100
  5.6 3.1 %collective-permute-start = (bf16[32,256]{1,0:T(8,128)(2,1)S(1)}, bf16[32,256]{1,0:T(8,128)(2,1)S(1)}, u32[]{:S(2)}, u32[]{:S(2)}) collective-permute-start(bf16[32,256]{1,0:T(8,128)(2,1)S(1)} %get-tuple-element.48.refs_0_), channel_id=1, source_target_pairs={{0,8},{8,0},{16,24},{24,16},{1,9},{9,1},{17,25},{25,17},{2,10},{10... | collective-permute-start | bytes 49160 | tf_op jit(solution)/shard_map/ppermute | solution.py:100
  5.7 10.5 %collective-permute-start.3 = (bf16[1024,128]{1,0:T(8,128)(2,1)S(1)}, bf16[1024,128]{1,0:T(8,128)(2,1)S(1)}, u32[]{:S(2)}, u32[]{:S(2)}) collective-permute-start(bf16[1024,128]{1,0:T(8,128)(2,1)S(1)} %get-tuple-element.52), channel_id=1, source_target_pairs={{0,8},{1,2},{2,1},{3,4},{4,3},{5,6},{6,5},{7,15},{8,0},{9,10},{10,... | collective-permute-start | bytes 786440 | tf_op jit(solution)/shard_map/ppermute | solution.py:115
  6.1 2.6 %copy-start.1 = (bf16[2,256,128]{2,1,0:T(8,128)(2,1)S(1)}, bf16[2,256,128]{2,1,0:T(8,128)(2,1)}, u32[]{:S(2)}) copy-start(bf16[2,256,128]{2,1,0:T(8,128)(2,1)} %hydro_ref.3) | copy-start | bytes 393220
  9.7 12.8 %all-to-all-start = ((bf16[8,64,256]{2,1,0:T(8,128)(2,1)}), bf16[8,64,256]{2,1,0:T(8,128)(2,1)S(1)}, u32[]{:S(2)}, u32[]{:S(2)}) async-start(bf16[8,64,256]{2,1,0:T(8,128)(2,1)} %pressure.1), calls=%async_computation | async-start | bytes 524288 | tf_op jit(solution)/shard_map/all_to_all | solution.py:446
  16.2 8.2 %collective-permute-start.4 = (bf16[1024,128]{1,0:T(8,128)(2,1)}, bf16[1024,128]{1,0:T(8,128)(2,1)S(1)}, u32[]{:S(2)}, u32[]{:S(2)}) collective-permute-start(bf16[1024,128]{1,0:T(8,128)(2,1)} %get-tuple-element.62), channel_id=1, source_target_pairs={{0,8},{1,9},{2,10},{3,11},{4,12},{5,13},{6,14},{7,15},{8,0},{9,1},... | collective-permute-start | bytes 786440 | tf_op jit(solution)/shard_map/ppermute | solution.py:115
  16.2 8.6 %collective-permute-start.5 = (bf16[1024,128]{1,0:T(8,128)(2,1)S(1)}, bf16[1024,128]{1,0:T(8,128)(2,1)S(1)}, u32[]{:S(2)}, u32[]{:S(2)}) collective-permute-start(bf16[1024,128]{1,0:T(8,128)(2,1)S(1)} %get-tuple-element.63), channel_id=1, source_target_pairs={{0,24},{1,25},{2,26},{3,27},{4,28},{5,29},{6,30},{7,31},{8,16},{9,... | collective-permute-start | bytes 786440 | tf_op jit(solution)/shard_map/ppermute | solution.py:115
  17.0 9.7 %collective-permute-start.6 = (bf16[1024,128]{1,0:T(8,128)(2,1)S(1)}, bf16[1024,128]{1,0:T(8,128)(2,1)S(1)}, u32[]{:S(2)}, u32[]{:S(2)}) collective-permute-start(bf16[1024,128]{1,0:T(8,128)(2,1)S(1)} %get-tuple-element.64), channel_id=1, source_target_pairs={{0,1},{1,0},{2,3},{3,2},{4,5},{5,4},{6,7},{7,6},{8,9},{9,8},{10,11... | collective-permute-start | bytes 786440 | tf_op jit(solution)/shard_map/ppermute | solution.py:115
  22.8 4.5 %copy-start = (f32[4,256,128]{2,1,0:T(8,128)S(1)}, f32[4,256,128]{2,1,0:T(8,128)}, u32[]{:S(2)}) copy-start(f32[4,256,128]{2,1,0:T(8,128)} %get-tuple-element.67.own) | copy-start | bytes 1572868
  22.8 4.5 %collective-permute-start.7 = (f32[32,256]{1,0:T(8,128)S(1)}, f32[32,256]{1,0:T(8,128)S(1)}, u32[]{:S(2)}, u32[]{:S(2)}) collective-permute-start(f32[32,256]{1,0:T(8,128)S(1)} %get-tuple-element.68), channel_id=1, source_target_pairs={{0,24},{8,16},{16,8},{24,0},{1,25},{9,17},{17,9},{25,1},{2,26},{10... | collective-permute-start | bytes 98312 | tf_op jit(solution)/shard_map/ppermute | solution.py:100
  22.9 4.4 %collective-permute-start.8 = (f32[32,256]{1,0:T(8,128)S(1)}, f32[32,256]{1,0:T(8,128)S(1)}, u32[]{:S(2)}, u32[]{:S(2)}) collective-permute-start(f32[32,256]{1,0:T(8,128)S(1)} %get-tuple-element.69), channel_id=1, source_target_pairs={{0,16},{8,24},{16,0},{24,8},{1,17},{9,25},{17,1},{25,9},{2,18},{10... | collective-permute-start | bytes 98312 | tf_op jit(solution)/shard_map/ppermute | solution.py:100
  24.3 3.0 %collective-permute-start.9 = (f32[32,256]{1,0:T(8,128)S(1)}, f32[32,256]{1,0:T(8,128)S(1)}, u32[]{:S(2)}, u32[]{:S(2)}) collective-permute-start(f32[32,256]{1,0:T(8,128)S(1)} %get-tuple-element.70), channel_id=1, source_target_pairs={{0,8},{8,0},{16,24},{24,16},{1,9},{9,1},{17,25},{25,17},{2,10},{10... | collective-permute-start | bytes 98312 | tf_op jit(solution)/shard_map/ppermute | solution.py:100

commit v12 on v11

--- a/solution.py
+++ b/solution.py
@@ -444,7 +444,8 @@
         cost_estimate=cost(60 * hydro.size * wide, 2 * hydro.size),
     )(hydro, load_panels, *pieces)
     arrived = lax.all_to_all(parts, "gy", 0, 0, axis_index_groups=[places_along_gy(n_gy)], tiled=True)
-    (*payloads, fourth) = lax.optimization_barrier((*payloads, fourth))
+    payloads = list(payloads)
+    payloads[0], fourth = lax.optimization_barrier((payloads[0], fourth))
     third = exchange_sides(payloads[2], 1, 1)
     second = exchange_sides(payloads[1], 0, 2)
     first = exchange_sides(payloads[0], 0, 1)

time: 28.7 us -> 28.7 us (level)
  starting transfers between devices: 14.3 us -> 14 us
  waiting for transfers between devices: 4.07 us -> 4.37 us
where the time goes in v12:
time: 28.7 us; the launch traced here: 28.5 us
  starting transfers between devices  14 us (49%)
  Pallas kernels  9.4 us (33%)
  waiting for transfers between devices  4.37 us (15%)
  between operations  0.73 us (3%)
    all_to_all x1, starting transfers between devices, on_device(): lax.all_to_all(parts, 'gy', 0, 0, axis_index_groups=[places_along_gy(n_gy...  6.41 us
    ppermute x6, starting transfers between devices, exchange(): return lax.ppermute(x, 'gx', [(i, target(i, step, n)) for i in range(n)])  5.04 us
    pallas_call x1, Pallas kernels, on_device(): pl.pallas_call(functools.partial(interior_kernel, rows, cols, (n_gx, n_gy...  3.34 us
    ppermute x4, starting transfers between devices, exchange_sides(): return lax.ppermute(x, ('gx', 'gy'), pairs)  2.54 us
    ppermute x4, waiting for transfers between devices, exchange_sides(): return lax.ppermute(x, ('gx', 'gy'), pairs)  1.96 us
    pallas_call x1, Pallas kernels, on_device(): pl.pallas_call(functools.partial(panels_kernel, rows, cols, early, late),...  1.9 us
    ppermute x6, waiting for transfers between devices, exchange(): return lax.ppermute(x, 'gx', [(i, target(i, step, n)) for i in range(n)])  1.47 us
    pallas_call x1, Pallas kernels, on_device(): pl.pallas_call(functools.partial(edges_kernel, rows, cols, late), name='e...  1.13 us
  transfers between devices with their start and end apart: 11, of which 3 were waited for; matrix products, arithmetic and copies ran while one was open for 0% of the time, Pallas kernels for 22%

profile of v12, /device:TPU:0, one launch (start us, length us, event | category | flops | bytes accessed | tf_op | source)
XLA Modules:
  0.0 28.5 jit_solution(16740745306467400449)
XLA Ops:
  0.6 1.9 %panels.1 = (bf16[32,256]{1,0:T(8,128)(2,1)S(1)}, bf16[1024,128]{1,0:T(8,128)(2,1)S(1)}, bf16[4,256,128]{2,1,0:T(8,128)(2,1)S(1)}, bf16[4,256,128]{2,1,0:T(8,128...) custom-call(s32[2,2,4]{2,1,0:T(2,128)} %joints_far.3, bf16[4,256,128]{2,1,0:T(8,128)(2,1)} %bitcast.9, ...), custom_call_target="tpu_custom_call" | custom-call | flops 16777216 | bytes 524288 | tf_op jit(solution)/shard_map/panels/pallas_call | solution.py:403
  2.5 2.4 %collective-permute-start.2 = (bf16[32,256]{1,0:T(8,128)(2,1)S(1)}, bf16[32,256]{1,0:T(8,128)(2,1)S(1)}, u32[]{:S(2)}, u32[]{:S(2)}) collective-permute-start(bf16[32,256]{1,0:T(8,128)(2,1)S(1)} %get-tuple-element.46.refs_0_), channel_id=1, source_target_pairs={{0,24},{8,16},{16,8},{24,0},{1,25},{9,17},{17,9},{25,1},{2,26},{10... | collective-permute-start | bytes 49160 | tf_op jit(solution)/shard_map/ppermute | solution.py:100
  5.0 0.6 %collective-permute-start.1 = (bf16[32,256]{1,0:T(8,128)(2,1)S(1)}, bf16[32,256]{1,0:T(8,128)(2,1)S(1)}, u32[]{:S(2)}, u32[]{:S(2)}) collective-permute-start(bf16[32,256]{1,0:T(8,128)(2,1)S(1)} %get-tuple-element.46.refs_0_), channel_id=1, source_target_pairs={{0,16},{8,24},{16,0},{24,8},{1,17},{9,25},{17,1},{25,9},{2,18},{10... | collective-permute-start | bytes 49160 | tf_op jit(solution)/shard_map/ppermute | solution.py:100
  5.6 0.0 collective-permute-start
  5.7 0.5 %collective-permute-start.3 = (bf16[1024,128]{1,0:T(8,128)(2,1)S(1)}, bf16[1024,128]{1,0:T(8,128)(2,1)S(1)}, u32[]{:S(2)}, u32[]{:S(2)}) collective-permute-start(bf16[1024,128]{1,0:T(8,128)(2,1)S(1)} %get-tuple-element.48), channel_id=1, source_target_pairs={{0,8},{1,2},{2,1},{3,4},{4,3},{5,6},{6,5},{7,15},{8,0},{9,10},{10,... | collective-permute-start | bytes 786440 | tf_op jit(solution)/shard_map/ppermute | solution.py:115
  6.1 0.0 copy-start.1
  6.1 1.1 %edges.1 = (bf16[32,256]{1,0:T(8,128)(2,1)S(1)}, bf16[1024,128]{1,0:T(8,128)(2,1)S(1)}, bf16[1024,128]{1,0:T(8,128)(2,1)}, bf16[1024,128]{1,0:T(8,128)(2,1)S(1)}) custom-call(bf16[4,256,128]{2,1,0:T(8,128)(2,1)S(1)} %get-tuple-element.38.motion, bf16[4,256,128]{2,1,0:T(8,128)(2,1)S(1)} %get-tuple-element.39.load, ...), custom_call_target="tpu_custom_call" | custom-call | flops 3019898880 | bytes 1310720 | tf_op jit(solution)/shard_map/edges/pallas_call | solution.py:424
  7.3 0.0 collective-permute-done.2.refs_3_
  7.3 1.5 %collective-permute-done.1.refs_2_ = bf16[32,256]{1,0:T(8,128)(2,1)S(1)} collective-permute-done((bf16[32,256]{1,0:T(8,128)(2,1)S(1)}, bf16[32,256]{1,0:T(8,128)(2,1)S(1)}, u32[]{:S(2)}, u32[]{:S(2)}) %collective-permute-start.1) | collective-permute-done | bytes 16416 | tf_op jit(solution)/shard_map/ppermute | solution.py:100
  8.7 0.0 collective-permute-done.refs_1_
  8.7 0.0 copy-done.1
  8.7 1.0 %pressure.1 = bf16[8,64,256]{2,1,0:T(8,128)(2,1)} custom-call(bf16[2,256,128]{2,1,0:T(8,128)(2,1)S(1)} %copy-done.1, bf16[32,256]{1,0:T(8,128)(2,1)S(1)} %get-tuple-element.45.load_panels, bf16[32,256]{1,0:T(8,128)(2,1)S(1)} %get-tuple-element.46.refs_0_, bf16[32,256]{1,0:T(8,128)(2,1)S(1)} %collective-permute-done.refs_1_, ...), custom_call_target="tpu_custom_call" | custom-call | flops 1006632960 | bytes 131072 | tf_op jit(solution)/shard_map/pressure/pallas_call | solution.py:436
  9.7 6.4 %all-to-all-start = ((bf16[8,64,256]{2,1,0:T(8,128)(2,1)}), bf16[8,64,256]{2,1,0:T(8,128)(2,1)S(1)}, u32[]{:S(2)}, u32[]{:S(2)}) async-start(bf16[8,64,256]{2,1,0:T(8,128)(2,1)} %pressure.1), calls=%async_computation | async-start | bytes 524288 | tf_op jit(solution)/shard_map/all_to_all | solution.py:446
  16.1 0.0 collective-permute-start.5
  16.2 1.5 %collective-permute-start.6 = (bf16[1024,128]{1,0:T(8,128)(2,1)S(1)}, bf16[1024,128]{1,0:T(8,128)(2,1)S(1)}, u32[]{:S(2)}, u32[]{:S(2)}) collective-permute-start(bf16[1024,128]{1,0:T(8,128)(2,1)S(1)} %get-tuple-element.60), channel_id=1, source_target_pairs={{0,1},{1,0},{2,3},{3,2},{4,5},{5,4},{6,7},{7,6},{8,9},{9,8},{10,11... | collective-permute-start | bytes 786440 | tf_op jit(solution)/shard_map/ppermute | solution.py:115
  17.6 0.0 collective-permute-done.3.refs_1_
  17.6 0.6 %collective-permute-start.4 = (bf16[1024,128]{1,0:T(8,128)(2,1)S(1)}, bf16[1024,128]{1,0:T(8,128)(2,1)S(1)}, u32[]{:S(2)}, u32[]{:S(2)}) collective-permute-start(bf16[1024,128]{1,0:T(8,128)(2,1)S(1)} %get-tuple-element.58), channel_id=1, source_target_pairs={{0,8},{1,9},{2,10},{3,11},{4,12},{5,13},{6,14},{7,15},{8,0},{9,1},... | collective-permute-start | bytes 786440 | tf_op jit(solution)/shard_map/ppermute | solution.py:115
  18.2 3.3 %interior.1 = (f32[4,256,128]{2,1,0:T(8,128)S(1)}, f32[4,256,128]{2,1,0:T(8,128)S(1)}, f32[4,256,128]{2,1,0:T(8,128)}, bf16[6,2,128,128]{3,2,1,0:T(8,128)(2,1)S(1)}) custom-call(s32[2,2,4]{2,1,0:T(2,128)} %joints_far.3, bf16[4,256,128]{2,1,0:T(8,128)(2,1)} %bitcast.10, bf16[4,256,128]{2,1,0:T(8,128)(2,1)} %bitcast.12, bf16[4,256,128]{2,1,0:T(8,128)(2,1)} %bitcast.13, ...), custom_call_target="tpu_custom_call" | custom-call | flops 402653184 | bytes 3670016 | tf_op jit(solution)/shard_map/interior/pallas_call | solution.py:453
  21.6 0.9 %all-to-all-done.arrived = bf16[8,64,256]{2,1,0:T(8,128)(2,1)S(1)} async-done(((bf16[8,64,256]{2,1,0:T(8,128)(2,1)}), bf16[8,64,256]{2,1,0:T(8,128)(2,1)S(1)}, u32[]{:S(2)}, u32[]{:S(2)}) %all-to-all-start) | async-done | bytes 262176 | tf_op jit(solution)/shard_map/all_to_all | solution.py:446
  22.5 0.3 %reaction.1 = (f32[32,256]{1,0:T(8,128)S(1)}, f32[32,256]{1,0:T(8,128)S(1)}, f32[32,256]{1,0:T(8,128)S(1)}, f32[32,256]{1,0:T(8,128)S(1)}) custom-call(bf16[2,256,128]{2,1,0:T(8,128)(2,1)S(1)} %copy-done.1, bf16[8,64,256]{2,1,0:T(8,128)(2,1)S(1)} %all-to-all-done.arrived), custom_call_target="tpu_custom_call" | custom-call | flops 33554432 | bytes 131072 | tf_op jit(solution)/shard_map/reaction/pallas_call | solution.py:473
  22.8 0.0 copy-start
  22.8 0.1 collective-permute-start.7
  22.9 1.4 %collective-permute-start.8 = (f32[32,256]{1,0:T(8,128)S(1)}, f32[32,256]{1,0:T(8,128)S(1)}, u32[]{:S(2)}, u32[]{:S(2)}) collective-permute-start(f32[32,256]{1,0:T(8,128)S(1)} %get-tuple-element.65), channel_id=1, source_target_pairs={{0,16},{8,24},{16,0},{24,8},{1,17},{9,25},{17,1},{25,9},{2,18},{10... | collective-permute-start | bytes 98312 | tf_op jit(solution)/shard_map/ppermute | solution.py:100
  24.3 0.0 collective-permute-done.5.refs_1_
  24.3 0.4 %collective-permute-start.9 = (f32[32,256]{1,0:T(8,128)S(1)}, f32[32,256]{1,0:T(8,128)S(1)}, u32[]{:S(2)}, u32[]{:S(2)}) collective-permute-start(f32[32,256]{1,0:T(8,128)S(1)} %get-tuple-element.66), channel_id=1, source_target_pairs={{0,8},{8,0},{16,24},{24,16},{1,9},{9,1},{17,25},{25,17},{2,10},{10... | collective-permute-start | bytes 98312 | tf_op jit(solution)/shard_map/ppermute | solution.py:100
  24.8 2.0 %collective-permute-done.6.refs_2_ = bf16[1024,128]{1,0:T(8,128)(2,1)S(1)} collective-permute-done((bf16[1024,128]{1,0:T(8,128)(2,1)S(1)}, bf16[1024,128]{1,0:T(8,128)(2,1)S(1)}, u32[]{:S(2)}, u32[]{:S(2)}) %collective-permute-start.6) | collective-permute-done | bytes 262176 | tf_op jit(solution)/shard_map/ppermute | solution.py:115
  26.7 0.0 collective-permute-done.4.refs_0_
  26.7 0.6 %boundary.1 = (f32[4,256,128]{2,1,0:T(8,128)S(1)}, f32[4,256,128]{2,1,0:T(8,128)S(1)}) custom-call(bf16[32,512]{1,0:T(8,128)(2,1)S(1)} %get-tuple-element.37.maps, bf16[6,2,128,128]{3,2,1,0:T(8,128)(2,1)S(1)} %get-tuple-element.54.coupling, f32[4,256,128]{2,1,0:T(8,128)S(1)} %get-tuple-element.55.residual, f32[4,256,128]{2,1,0:T(8,128)S(1)} %get-tuple-element.56.multiplier, ...), custom_call_target="tpu_custom_call" | custom-call | flops 268435456 | bytes 3014656 | tf_op jit(solution)/shard_map/boundary/pallas_call | solution.py:485
  27.3 0.0 collective-permute-done.7.refs_0_
  27.4 0.0 collective-permute-done.8.refs_1_
  27.4 0.0 collective-permute-done.9.refs_2_
  27.4 0.0 copy-done
  27.4 1.1 %final.1 = (f32[4,256,128]{2,1,0:T(8,128)}, f32[4,256,128]{2,1,0:T(8,128)}, f32[2,2]{1,0:T(2,128)}) custom-call(bf16[32,512]{1,0:T(8,128)(2,1)S(1)} %get-tuple-element.37.maps, f32[4,256,128]{2,1,0:T(8,128)S(1)} %get-tuple-element.61.residual, f32[4,256,128]{2,1,0:T(8,128)S(1)} %get-tuple-element.62.multiplier, f32[4,256,128]{2,1,0:T(8,128)S(1)} %copy-done, ...), custom_call_target="tpu_custom_call" | custom-call | flops 16777216 | bytes 2621440 | tf_op jit(solution)/shard_map/final/pallas_call | solution.py:495
Async XLA Ops:
  2.5 4.7 %collective-permute-start.2 = (bf16[32,256]{1,0:T(8,128)(2,1)S(1)}, bf16[32,256]{1,0:T(8,128)(2,1)S(1)}, u32[]{:S(2)}, u32[]{:S(2)}) collective-permute-start(bf16[32,256]{1,0:T(8,128)(2,1)S(1)} %get-tuple-element.46.refs_0_), channel_id=1, source_target_pairs={{0,24},{8,16},{16,8},{24,0},{1,25},{9,17},{17,9},{25,1},{2,26},{10... | collective-permute-start | bytes 49160 | tf_op jit(solution)/shard_map/ppermute | solution.py:100
  5.0 3.7 %collective-permute-start.1 = (bf16[32,256]{1,0:T(8,128)(2,1)S(1)}, bf16[32,256]{1,0:T(8,128)(2,1)S(1)}, u32[]{:S(2)}, u32[]{:S(2)}) collective-permute-start(bf16[32,256]{1,0:T(8,128)(2,1)S(1)} %get-tuple-element.46.refs_0_), channel_id=1, source_target_pairs={{0,16},{8,24},{16,0},{24,8},{1,17},{9,25},{17,1},{25,9},{2,18},{10... | collective-permute-start | bytes 49160 | tf_op jit(solution)/shard_map/ppermute | solution.py:100
  5.6 3.1 %collective-permute-start = (bf16[32,256]{1,0:T(8,128)(2,1)S(1)}, bf16[32,256]{1,0:T(8,128)(2,1)S(1)}, u32[]{:S(2)}, u32[]{:S(2)}) collective-permute-start(bf16[32,256]{1,0:T(8,128)(2,1)S(1)} %get-tuple-element.46.refs_0_), channel_id=1, source_target_pairs={{0,8},{8,0},{16,24},{24,16},{1,9},{9,1},{17,25},{25,17},{2,10},{10... | collective-permute-start | bytes 49160 | tf_op jit(solution)/shard_map/ppermute | solution.py:100
  5.7 12.0 %collective-permute-start.3 = (bf16[1024,128]{1,0:T(8,128)(2,1)S(1)}, bf16[1024,128]{1,0:T(8,128)(2,1)S(1)}, u32[]{:S(2)}, u32[]{:S(2)}) collective-permute-start(bf16[1024,128]{1,0:T(8,128)(2,1)S(1)} %get-tuple-element.48), channel_id=1, source_target_pairs={{0,8},{1,2},{2,1},{3,4},{4,3},{5,6},{6,5},{7,15},{8,0},{9,10},{10,... | collective-permute-start | bytes 786440 | tf_op jit(solution)/shard_map/ppermute | solution.py:115
  6.1 2.6 %copy-start.1 = (bf16[2,256,128]{2,1,0:T(8,128)(2,1)S(1)}, bf16[2,256,128]{2,1,0:T(8,128)(2,1)}, u32[]{:S(2)}) copy-start(bf16[2,256,128]{2,1,0:T(8,128)(2,1)} %hydro_ref.3) | copy-start | bytes 393220
  9.7 12.8 %all-to-all-start = ((bf16[8,64,256]{2,1,0:T(8,128)(2,1)}), bf16[8,64,256]{2,1,0:T(8,128)(2,1)S(1)}, u32[]{:S(2)}, u32[]{:S(2)}) async-start(bf16[8,64,256]{2,1,0:T(8,128)(2,1)} %pressure.1), calls=%async_computation | async-start | bytes 524288 | tf_op jit(solution)/shard_map/all_to_all | solution.py:446
  16.1 8.2 %collective-permute-start.5 = (bf16[1024,128]{1,0:T(8,128)(2,1)}, bf16[1024,128]{1,0:T(8,128)(2,1)S(1)}, u32[]{:S(2)}, u32[]{:S(2)}) collective-permute-start(bf16[1024,128]{1,0:T(8,128)(2,1)} %get-tuple-element.59), channel_id=1, source_target_pairs={{0,24},{1,25},{2,26},{3,27},{4,28},{5,29},{6,30},{7,31},{8,16},{9,... | collective-permute-start | bytes 786440 | tf_op jit(solution)/shard_map/ppermute | solution.py:115
  16.2 10.6 %collective-permute-start.6 = (bf16[1024,128]{1,0:T(8,128)(2,1)S(1)}, bf16[1024,128]{1,0:T(8,128)(2,1)S(1)}, u32[]{:S(2)}, u32[]{:S(2)}) collective-permute-start(bf16[1024,128]{1,0:T(8,128)(2,1)S(1)} %get-tuple-element.60), channel_id=1, source_target_pairs={{0,1},{1,0},{2,3},{3,2},{4,5},{5,4},{6,7},{7,6},{8,9},{9,8},{10,11... | collective-permute-start | bytes 786440 | tf_op jit(solution)/shard_map/ppermute | solution.py:115
  17.6 9.1 %collective-permute-start.4 = (bf16[1024,128]{1,0:T(8,128)(2,1)S(1)}, bf16[1024,128]{1,0:T(8,128)(2,1)S(1)}, u32[]{:S(2)}, u32[]{:S(2)}) collective-permute-start(bf16[1024,128]{1,0:T(8,128)(2,1)S(1)} %get-tuple-element.58), channel_id=1, source_target_pairs={{0,8},{1,9},{2,10},{3,11},{4,12},{5,13},{6,14},{7,15},{8,0},{9,1},... | collective-permute-start | bytes 786440 | tf_op jit(solution)/shard_map/ppermute | solution.py:115
  22.8 4.5 %copy-start = (f32[4,256,128]{2,1,0:T(8,128)S(1)}, f32[4,256,128]{2,1,0:T(8,128)}, u32[]{:S(2)}) copy-start(f32[4,256,128]{2,1,0:T(8,128)} %get-tuple-element.63.own) | copy-start | bytes 1572868
  22.8 4.5 %collective-permute-start.7 = (f32[32,256]{1,0:T(8,128)S(1)}, f32[32,256]{1,0:T(8,128)S(1)}, u32[]{:S(2)}, u32[]{:S(2)}) collective-permute-start(f32[32,256]{1,0:T(8,128)S(1)} %get-tuple-element.64), channel_id=1, source_target_pairs={{0,24},{8,16},{16,8},{24,0},{1,25},{9,17},{17,9},{25,1},{2,26},{10... | collective-permute-start | bytes 98312 | tf_op jit(solution)/shard_map/ppermute | solution.py:100
  22.9 4.4 %collective-permute-start.8 = (f32[32,256]{1,0:T(8,128)S(1)}, f32[32,256]{1,0:T(8,128)S(1)}, u32[]{:S(2)}, u32[]{:S(2)}) collective-permute-start(f32[32,256]{1,0:T(8,128)S(1)} %get-tuple-element.65), channel_id=1, source_target_pairs={{0,16},{8,24},{16,0},{24,8},{1,17},{9,25},{17,1},{25,9},{2,18},{10... | collective-permute-start | bytes 98312 | tf_op jit(solution)/shard_map/ppermute | solution.py:100
  24.3 3.0 %collective-permute-start.9 = (f32[32,256]{1,0:T(8,128)S(1)}, f32[32,256]{1,0:T(8,128)S(1)}, u32[]{:S(2)}, u32[]{:S(2)}) collective-permute-start(f32[32,256]{1,0:T(8,128)S(1)} %get-tuple-element.66), channel_id=1, source_target_pairs={{0,8},{8,0},{16,24},{24,16},{1,9},{9,1},{17,25},{25,17},{2,10},{10... | collective-permute-start | bytes 98312 | tf_op jit(solution)/shard_map/ppermute | solution.py:100
